TPU v7x, 32 devices: a whole 2x2x4 slice. The times are simulated.
32 devices in a mesh: parts: 2 (over y), az: 4 (over z), date: 2 (over x), rg: 2 (over core).
Axes of the slice: x: 2, y: 2, z: 4, core: 2. Of those that a mesh axis runs over, the one named last changes fastest.
Arguments:
- image_stack: float32 [2, 4, 256, 512], P(None, ('parts', 'date'), 'az', 'rg'), parts along dimension 1, may hold values from -6 to 6
- tap_weights: float32 [8, 4, 256], P(None, ('parts', 'date'), 'az'), parts along dimension 1, may hold values from -0.25 to 0.75
- offsets: int32 [4, 256], P(('parts', 'date'), 'az'), parts along dimension 0, may hold values from -12 to 12, as said below
- matchings: int32 [3, 2], replicated, may hold values from 0 to 1, each once within a row
Outputs:
- filtered: float32 [3, 2, 4, 256, 512], P(None, None, ('parts', 'date'), 'az', 'rg'), parts along dimension 2
There are 2 independent parts, one for each index of `parts`. A program takes and returns all parts, laid end to end along the dimension named above; an argument that names none is the same for every part. Nothing has to cross between parts.
Inputs may be any that keep to these rules, and one draw needn't show every extreme that they name: `offsets`: both ends of the range occur in every draw. `matchings`: each row names every date once.
All inputs are finite; a program needn't handle non-finite values.
Results may differ from a plain program's by a relative error of at most 0.0045.
Values may be sent and summed in bfloat16 or wider, within the bound.
No kernel may reach another device: no remote copies, remote signals or barrier semaphores. Data moves between devices by JAX's collectives and lax.ppermute only.
A program may use at most 64 MiB of HBM per device.

v0:
```python
import math

import jax
import jax.numpy as jnp
from jax import lax
from jax.sharding import PartitionSpec as P

TAPS = 8
SHIFT_MAX = 12
PATCH = 64


def extended(value, sides, width):
    for axis, dim in sides:
        peers, length = (lax.axis_size(axis), value.shape[dim])
        up = [(i, (i + 1) % peers) for i in range(peers - 1)]
        down = [(j, i) for i, j in up]
        last = lax.slice_in_dim(value, length - width, length, axis=dim)
        leading = lax.slice_in_dim(value, 0, width, axis=dim)
        before = lax.ppermute(last, axis, up)
        after = lax.ppermute(leading, axis, down)
        value = jnp.concatenate([before, value, after], axis=dim)
    return value


def fourier_table(sine_sign, table_scale):
    freq_ids = jnp.arange(PATCH, dtype=jnp.int32)
    phase_ids = freq_ids[:, None] * freq_ids[None, :] % PATCH
    angles = phase_ids.astype(jnp.float32) * (2.0 * math.pi / PATCH)
    cosine = jnp.cos(angles) * table_scale
    sine_part = jnp.sin(angles) * (sine_sign * table_scale)
    upper_rows = jnp.concatenate([cosine, -sine_part], axis=1)
    bottom = jnp.concatenate([sine_part, cosine], axis=1)
    return jnp.concatenate([upper_rows, bottom], axis=0).astype(jnp.bfloat16)


def filter_all(ifg_wide, forward_table, inverse_table, window):
    half_patch = PATCH // 2
    match_count, _, date_dev, wide_lines, wide_samples = ifg_wide.shape
    row_blocks = wide_lines // half_patch
    col_blocks = wide_samples // half_patch
    forward_split = forward_table.reshape(2, PATCH, 2 * PATCH)
    first_half = forward_split[:, :half_patch]
    second_half = forward_split[:, half_patch:]
    line_blocks = ifg_wide.reshape(match_count, 2, date_dev, row_blocks, half_patch, wide_samples)
    line_sum = jnp.einsum(
        "mcdbuw,cuo->mdbow",
        line_blocks[:, :, :, :-1],
        first_half,
        preferred_element_type=jnp.float32,
    )
    line_sum = line_sum + jnp.einsum(
        "mcdbuw,cuo->mdbow",
        line_blocks[:, :, :, 1:],
        second_half,
        preferred_element_type=jnp.float32,
    )
    line_spectra = line_sum.astype(jnp.bfloat16)
    range_blocks = line_spectra.reshape(
        match_count, date_dev, row_blocks - 1, 2, PATCH, col_blocks, half_patch
    )
    spectrum = jnp.einsum(
        "mdrclqv,cvf->mdrlqf",
        range_blocks[:, :, :, :, :, :-1],
        first_half,
        preferred_element_type=jnp.float32,
    )
    spectrum = spectrum + jnp.einsum(
        "mdrclqv,cvf->mdrlqf",
        range_blocks[:, :, :, :, :, 1:],
        second_half,
        preferred_element_type=jnp.float32,
    )
    spec_real = spectrum[..., :PATCH]
    spec_imag = spectrum[..., PATCH:]
    power_spec = spec_real * spec_real + spec_imag * spec_imag
    smooth = power_spec + jnp.roll(power_spec, 1, 3) + jnp.roll(power_spec, -1, 3)
    smooth = smooth + jnp.roll(smooth, 1, 5) + jnp.roll(smooth, -1, 5)
    ref_power = PATCH * PATCH * 1.0
    gain_map = jnp.power((smooth / 9.0 + ref_power) / ref_power, 0.25)
    shaped = jnp.concatenate([spec_real * gain_map, spec_imag * gain_map], axis=-1).astype(
        jnp.bfloat16
    )
    range_back = jnp.einsum(
        "mdrlqk,kj->mdrlqj", shaped, inverse_table, preferred_element_type=jnp.float32
    ).astype(jnp.bfloat16)
    range_back = range_back.reshape(
        match_count, date_dev, row_blocks - 1, PATCH, col_blocks - 1, 2, PATCH
    )
    inverse_split = inverse_table.reshape(2, PATCH, 2, PATCH)
    lines_back = jnp.einsum(
        "mdrlqcs,clex->medrxqs", range_back, inverse_split, preferred_element_type=jnp.float32
    )
    weighted = lines_back * window[:, None, None] * window[None, None, :]
    joined_cols = weighted[..., :-1, half_patch:] + weighted[..., 1:, :half_patch]
    joined_cols = joined_cols.reshape(match_count, 2, date_dev, row_blocks - 1, PATCH, -1)
    joined_rows = joined_cols[:, :, :, :-1, half_patch:] + joined_cols[:, :, :, 1:, :half_patch]
    return joined_rows.reshape(match_count, 2, date_dev, (row_blocks - 2) * half_patch, -1)


def cross_product(own_tile, partners):
    own_real = own_tile[0].astype(jnp.float32)
    own_imag = own_tile[1].astype(jnp.float32)
    other_real = partners[:, 0].astype(jnp.float32)
    other_imag = partners[:, 1].astype(jnp.float32)
    real_part = own_real[None] * other_real + own_imag[None] * other_imag
    imag_part = own_imag[None] * other_real - own_real[None] * other_imag
    return jnp.stack([real_part, imag_part], axis=1).astype(jnp.bfloat16)


def per_device(image_stack, tap_weights, offsets, matchings):
    date_dev = image_stack.shape[1]
    line_count = image_stack.shape[2]
    rim_width = SHIFT_MAX + TAPS // 2
    half_patch = PATCH // 2
    wide_stack = extended(image_stack, (("az", 2),), rim_width)
    line_ids = jnp.arange(line_count, dtype=jnp.int32)
    wide_ids = jnp.arange(line_count + 2 * rim_width, dtype=jnp.int32)
    band_matrix = jnp.zeros((date_dev, line_count, line_count + 2 * rim_width), jnp.float32)
    for tap_index in range(TAPS):
        target = line_ids[None, :] + offsets + (tap_index - (TAPS // 2 - 1) + rim_width)
        band_matrix = band_matrix + jnp.where(
            wide_ids[None, None, :] == target[:, :, None], tap_weights[tap_index][:, :, None], 0.0
        )
    resampled = jnp.einsum(
        "dij,cdjs->cdis",
        band_matrix,
        wide_stack,
        precision=lax.Precision.HIGHEST,
        preferred_element_type=jnp.float32,
    ).astype(jnp.bfloat16)
    wanted = lax.dynamic_slice_in_dim(matchings, lax.axis_index("date") * date_dev, date_dev, 1)
    tile_wide = extended(resampled, (("az", 2), ("rg", 3)), half_patch)
    shard_piece = lax.all_gather(tile_wide, "date", axis=1, tiled=True)
    piece_dates = shard_piece.shape[1]
    slot_ids = jnp.arange(piece_dates, dtype=jnp.int32)
    select = (wanted[:, :, None] == slot_ids[None, None, :]).astype(jnp.bfloat16)
    picked = jnp.einsum("mdj,cjls->mcdls", select, shard_piece, preferred_element_type=jnp.bfloat16)
    ifg_wide = cross_product(tile_wide, picked)
    forward_table = fourier_table(1.0, 1.0)
    inverse_table = fourier_table(-1.0, 1.0 / PATCH)
    window = jnp.sin(math.pi * (jnp.arange(PATCH, dtype=jnp.float32) + 0.5) / PATCH) ** 2
    return filter_all(ifg_wide, forward_table, inverse_table, window)


def solution(mesh):
    placed = (
        P(None, ("parts", "date"), "az", "rg"),
        P(None, ("parts", "date"), "az"),
        P(("parts", "date"), "az"),
        P(),
    )
    return jax.shard_map(
        per_device,
        mesh=mesh,
        in_specs=placed,
        out_specs=P(None, None, ("parts", "date"), "az", "rg"),
        check_vma=False,
    )
```

profile of v0, /device:TPU:0, one launch (start us, length us, event | category | flops | bytes accessed | tf_op | source)
XLA Modules:
  0.0 57.9 jit_solution(10740422156659371928)
XLA Ops:
  0.0 0.8 %fusion.105 = (f32[2,1,16,256]{3,2,0,1:T(8,128)S(1)}, f32[2,1,16,256]{3,2,0,1:T(8,128)S(1)}) fusion(f32[2,1,64,256]{3,2,0,1:T(8,128)} %bitcast.176), kind=kLoop, calls=%fused_computation.165 | loop fusion | bytes 131072 | tf_op jit(solution)/shard_map/slice | solution.py:18
  0.8 4.9 %collective-permute-start = (f32[2,1,16,256]{3,2,0,1:T(8,128)S(1)}, f32[2,1,16,256]{3,2,0,1:T(8,128)S(1)}, u32[]{:S(2)}, u32[]{:S(2)}) collective-permute-start(f32[2,1,16,256]{3,2,0,1:T(8,128)S(1)} %get-tuple-element.23), channel_id=1, source_target_pairs={{0,4},{4,8},{8,12},{1,5},{5,9},{9,13},{2,6},{6,10},{10,14},{3,7},{... | collective-permute-start | bytes 98312 | tf_op jit(solution)/shard_map/ppermute | solution.py:20
  5.7 1.3 %collective-permute-start.1 = (f32[2,1,16,256]{3,2,0,1:T(8,128)S(1)}, f32[2,1,16,256]{3,2,0,1:T(8,128)S(1)}, u32[]{:S(2)}, u32[]{:S(2)}) collective-permute-start(f32[2,1,16,256]{3,2,0,1:T(8,128)S(1)} %get-tuple-element.24), channel_id=1, source_target_pairs={{4,0},{8,4},{12,8},{5,1},{9,5},{13,9},{6,2},{10,6},{14,10},{7,3},{... | collective-permute-start | bytes 98312 | tf_op jit(solution)/shard_map/ppermute | solution.py:21
  7.0 0.1 negate_convert_fusion
  7.2 0.1 fusion.85
  7.3 0.2 broadcast_multiply_fusion
  7.5 0.1 fusion.86
  7.6 0.8 %slice_bitcast_fusion.9 = (f32[64]{0:T(128)S(1)}, f32[64]{0:T(128)S(1)}, f32[64]{0:T(128)S(1)}, f32[64]{0:T(128)S(1)}, f32[64]{0:T(128)S(1)}, /*index=5*/f32[64]{0:T(128)S(1)}, f32[64]{0:T(128)S(1)}, f32[64]{0:T(128)S(1)}) fusion(f32[8,1,64]{2,1,0:T(1,128)} %param.5), kind=kLoop, calls=%fused_computation.151 | loop fusion | bytes 4096 | tf_op jit(solution)/shard_map/jit(_where)/broadcast_in_dim | solution.py:122
  8.4 0.7 %add_bitcast_fusion.7 = (s32[64]{0:T(128)S(1)}, s32[64]{0:T(128)S(1)}, s32[64]{0:T(128)S(1)}, s32[64]{0:T(128)S(1)}, s32[64]{0:T(128)S(1)}, /*index=5*/s32[64]{0:T(128)S(1)}, s32[64]{0:T(128)S(1)}, s32[64]{0:T(128)S(1)}) fusion(s32[1,64]{1,0:T(1,128)} %param.6), kind=kLoop, calls=%fused_computation.152 | loop fusion | flops 576 | bytes 2304 | tf_op jit(solution)/shard_map/add | solution.py:121
  9.3 2.3 %collective-permute-done.1 = f32[2,1,16,256]{3,2,0,1:T(8,128)S(1)} collective-permute-done((f32[2,1,16,256]{3,2,0,1:T(8,128)S(1)}, f32[2,1,16,256]{3,2,0,1:T(8,128)S(1)}, u32[]{:S(2)}, u32[]{:S(2)}) %collective-permute-start.1) | collective-permute-done | bytes 32800 | tf_op jit(solution)/shard_map/ppermute | solution.py:21
  11.5 1.3 %fusion.17 = bf16[2,1,64,256]{3,2,0,1:T(8,128)(2,1)S(1)} fusion(f32[2,1,16,256]{3,2,0,1:T(8,128)S(1)} %collective-permute-done.1, f32[2,1,64,256]{3,2,0,1:T(8,128)} %bitcast.177, f32[2,1,16,256]{3,2,0,1:T(8,128)S(1)} %collective-permute-done, f32[64]{0:T(128)S(1)} %get-tuple-element.33, s32[64]{0:T(128)S(1)} %get-tuple-element.42, ...), kind=kOutput, calls=%fused_computation.31 | convolution fusion | flops 38021120 | bytes 266240 | tf_op jit(solution)/shard_map/dij,cdjs->cdis/dot_general | solution.py:125
  12.9 3.5 %collective-permute-start.2 = (bf16[2,1,32,256]{3,2,0,1:T(8,128)(2,1)S(1)}, bf16[2,1,32,256]{3,2,0,1:T(8,128)(2,1)S(1)}, u32[]{:S(2)}, u32[]{:S(2)}) collective-permute-start(bf16[2,1,32,256]{3,2,0,1:T(8,128)(2,1)S(1)} %get-tuple-element.25), channel_id=1, source_target_pairs={{0,4},{4,8},{8,12},{1,5},{5,9},{9,13},{2,6},{6,10},{10,14},{3,7},{... | collective-permute-start | bytes 98312 | tf_op jit(solution)/shard_map/ppermute | solution.py:20
  16.4 1.3 %collective-permute-start.3 = (bf16[2,1,32,256]{3,2,0,1:T(8,128)(2,1)S(1)}, bf16[2,1,32,256]{3,2,0,1:T(8,128)(2,1)S(1)}, u32[]{:S(2)}, u32[]{:S(2)}) collective-permute-start(bf16[2,1,32,256]{3,2,0,1:T(8,128)(2,1)S(1)} %get-tuple-element.26), channel_id=1, source_target_pairs={{4,0},{8,4},{12,8},{5,1},{9,5},{13,9},{6,2},{10,6},{14,10},{7,3},{... | collective-permute-start | bytes 98312 | tf_op jit(solution)/shard_map/ppermute | solution.py:21
  17.7 0.2 collective-permute-done.2
  17.9 4.2 %collective-permute-done.3 = bf16[2,1,32,256]{3,2,0,1:T(8,128)(2,1)S(1)} collective-permute-done((bf16[2,1,32,256]{3,2,0,1:T(8,128)(2,1)S(1)}, bf16[2,1,32,256]{3,2,0,1:T(8,128)(2,1)S(1)}, u32[]{:S(2)}, u32[]{:S(2)}) %collective-permute-start.3) | collective-permute-done | bytes 32800 | tf_op jit(solution)/shard_map/ppermute | solution.py:21
  22.2 0.1 fusion.104
  22.3 1.3 %collective-permute-start.4 = (bf16[2,1,128,32]{3,2,0,1:T(8,128)(2,1)S(1)}, bf16[2,1,128,32]{3,2,0,1:T(8,128)(2,1)S(1)}, u32[]{:S(2)}, u32[]{:S(2)}) collective-permute-start(bf16[2,1,128,32]{3,2,0,1:T(8,128)(2,1)S(1)} %get-tuple-element.21), channel_id=1, source_target_pairs={{0,1},{2,3},{4,5},{6,7},{8,9},{10,11},{12,13},{14,15},{16,17},{18,... | collective-permute-start | bytes 49160 | tf_op jit(solution)/shard_map/ppermute | solution.py:20
  23.6 1.3 %collective-permute-start.5 = (bf16[2,1,128,32]{3,2,0,1:T(8,128)(2,1)S(1)}, bf16[2,1,128,32]{3,2,0,1:T(8,128)(2,1)S(1)}, u32[]{:S(2)}, u32[]{:S(2)}) collective-permute-start(bf16[2,1,128,32]{3,2,0,1:T(8,128)(2,1)S(1)} %get-tuple-element.22), channel_id=1, source_target_pairs={{1,0},{3,2},{5,4},{7,6},{9,8},{11,10},{13,12},{15,14},{17,16},{19,... | collective-permute-start | bytes 49160 | tf_op jit(solution)/shard_map/ppermute | solution.py:21
  24.9 0.1 convert_element_type.93
  25.0 1.7 %collective-permute-done.5 = bf16[2,1,128,32]{3,2,0,1:T(8,128)(2,1)S(1)} collective-permute-done((bf16[2,1,128,32]{3,2,0,1:T(8,128)(2,1)S(1)}, bf16[2,1,128,32]{3,2,0,1:T(8,128)(2,1)S(1)}, u32[]{:S(2)}, u32[]{:S(2)}) %collective-permute-start.5) | collective-permute-done | bytes 16416 | tf_op jit(solution)/shard_map/ppermute | solution.py:21
  26.7 0.1 pad_maximum_fusion.1
  26.9 0.2 copy.53
  27.1 6.9 %all_gather.3 = bf16[2,2,128,320]{2,3,0,1:T(8,128)(2,1)S(1)} all-gather(bf16[2,1,128,320]{2,3,0,1:T(8,128)(2,1)S(1)} %copy.53), channel_id=1, replica_groups=mesh['parts'=2,'az'=4,'date'=2,'rg'=2] {'date'}, dimensions={1}, use_global_device_ids=true | all-gather | bytes 491520 | tf_op jit(solution)/shard_map/all_gather | solution.py:134
  34.0 0.6 fusion.29
  34.7 0.1 copy.52
  34.8 0.1 copy.56
  34.9 0.2 fusion.21
  35.1 0.2 copy.57
  35.3 0.2 copy.58
  35.5 0.4 fusion.24
  36.0 0.4 fusion.16
  36.4 0.9 %reshape.882 = bf16[3,1,3,2,64,10,32]{4,3,6,5,2,0,1:T(2,128)(2,1)S(1)} reshape(bf16[3,1,3,128,320]{3,4,2,0,1:T(8,128)(2,1)S(1)} %fusion.16) | data formatting | bytes 1474560 | tf_op jit(solution)/shard_map/reshape | solution.py:59
  37.3 2.7 %fusion.103 = (bf16[3,1,3,2,64,9,32]{4,3,6,5,2,0,1:T(2,128)(2,1)S(1)}, bf16[3,1,3,2,64,9,32]{4,3,6,5,2,0,1:T(2,128)(2,1)S(1)}) fusion(bf16[3,1,3,2,64,10,32]{4,3,6,5,2,0,1:T(2,128)(2,1)S(1)} %reshape.882), kind=kLoop, calls=%fused_computation.163 | loop fusion | bytes 2654208 | tf_op jit(solution)/shard_map/slice | solution.py:70
  40.0 0.5 fusion.15
  40.5 0.5 fusion.8
  41.1 0.8 %multiply_add_fusion = f32[3,1,3,64,9,64]{5,3,4,2,0,1:T(8,128)S(1)} fusion(f32[3,1,3,64,9,128]{5,3,4,2,0,1:T(8,128)S(1)} %fusion.8), kind=kLoop, calls=%fused_computation.15 | loop fusion | flops 995328 | bytes 3981312 | tf_op jit(solution)/shard_map/add | solution.py:76
  41.8 0.8 %fusion.101 = (f32[3,1,3,63,9,64]{5,3,4,2,0,1:T(8,128)S(1)}, f32[3,1,3,63,9,64]{5,3,4,2,0,1:T(8,128)S(1)}) fusion(f32[3,1,3,64,9,64]{5,3,4,2,0,1:T(8,128)S(1)} %multiply_add_fusion), kind=kLoop, calls=%fused_computation.161 | loop fusion | bytes 5225472 | tf_op jit(solution)/shard_map/jit(_roll_static)/slice | solution.py:77
  42.7 1.5 %fusion.2 = f32[3,1,3,64,9,64]{5,3,4,2,0,1:T(8,128)S(1)} fusion(f32[3,1,3,63,9,64]{5,3,4,2,0,1:T(8,128)S(1)} %get-tuple-element.12, f32[3,1,3,1,9,64]{5,3,4,2,0,1:T(1,128)S(1)} %get-tuple-element.14, f32[3,1,3,1,9,64]{5,3,4,2,0,1:T(1,128)S(1)} %get-tuple-element.13, f32[3,1,3,63,9,64]{5,3,4,2,0,1:T(8,128)S(1)} %get-tuple-element.11, ...), kind=kLoop, calls=%fused_computation.4 | loop fusion | flops 2322432 | bytes 6635520 | tf_op jit(solution)/shard_map/add | solution.py:77
  44.2 1.0 %fusion.100 = (f32[3,1,3,64,9,63]{5,3,4,2,0,1:T(8,128)S(1)}, f32[3,1,3,64,9,63]{5,3,4,2,0,1:T(8,128)S(1)}) fusion(f32[3,1,3,64,9,64]{5,3,4,2,0,1:T(8,128)S(1)} %fusion.2), kind=kLoop, calls=%fused_computation.160 | loop fusion | bytes 5225472 | tf_op jit(solution)/shard_map/jit(_roll_static)/slice | solution.py:78
  45.2 1.1 %fusion.99 = (f32[3,1,3,64,9,1]{5,3,4,2,0,1:T(8,128)S(1)}, f32[3,1,3,64,9,1]{5,3,4,2,0,1:T(8,128)S(1)}) fusion(f32[3,1,3,64,9,64]{5,3,4,2,0,1:T(8,128)S(1)} %fusion.2), kind=kLoop, calls=%fused_computation.159 | loop fusion | bytes 82944 | tf_op jit(solution)/shard_map/jit(_roll_static)/slice | solution.py:78
  46.3 2.2 %fusion.10 = (bf16[3,3,64,9,64]{4,2,3,1,0:T(8,128)(2,1)S(1)}, f32[3,1,3,64,9,64]{5,3,4,2,0,1:T(8,128)S(1)}) fusion(f32[3,1,3,64,9,128]{5,3,4,2,0,1:T(8,128)S(1)} %fusion.8, f32[3,1,3,64,9,1]{5,3,4,2,0,1:T(8,128)S(1)} %get-tuple-element.8, f32[3,1,3,64,9,63]{5,3,4,2,0,1:T(8,128)S(1)} %get-tuple-element.10, f32[3,1,3,64,9,64]{5,3,4,2,0,1:T(8,128)S(1)} %fusion.2, ...), kind=kLoop, calls=%fused_computation.21 | loop fusion | flops 2985984 | bytes 7299072 | tf_op jit(solution)/shard_map/concatenate | solution.py:81
  48.5 0.8 %fusion.11 = bf16[3,3,64,9,64]{4,2,3,1,0:T(8,128)(2,1)S(1)} fusion(f32[3,1,3,64,9,64]{5,3,4,2,0,1:T(8,128)S(1)} %get-tuple-element.6, f32[3,1,3,64,9,128]{5,3,4,2,0,1:T(8,128)S(1)} %fusion.8), kind=kLoop, calls=%fused_computation.22 | loop fusion | flops 663552 | bytes 3317760 | tf_op jit(solution)/shard_map/concatenate | solution.py:81
  49.3 1.9 %convolution_convert_fusion = bf16[3,3,64,9,128]{4,2,3,1,0:T(8,128)(2,1)} fusion(bf16[3,3,64,9,64]{4,2,3,1,0:T(8,128)(2,1)S(1)} %fusion.11, bf16[3,3,64,9,64]{4,2,3,1,0:T(8,128)(2,1)S(1)} %get-tuple-element.5, bf16[128,128]{1,0:T(8,128)(2,1)S(1)} %maximum_convert_fusion), kind=kOutput, calls=%fused_computation.17 | convolution fusion | flops 173187072 | bytes 2686976 | tf_op jit(solution)/shard_map/mdrlqk,kj->mdrlqj/dot_general | solution.py:84
  51.2 3.1 %copy.80 = bf16[3,3,64,9,128]{2,4,3,1,0:T(8,128)(2,1)S(1)} copy(bf16[3,3,64,9,128]{4,2,3,1,0:T(8,128)(2,1)} %convolution_convert_fusion) | data formatting | bytes 2654208 | tf_op jit(solution)/shard_map/reshape.46
  54.3 1.3 %fusion.1 = f32[3,2,1,3,64,9,64]{4,6,5,3,0,1,2:T(8,128)S(1)} fusion(f32[64]{0:T(128)S(1)} %sine_multiply_fusion, bf16[3,3,64,9,2,64,1]{2,5,4,3,1,0,6:T(8,128)(2,1)S(1)} %bitcast.165, bf16[2,64,2,64,1,1,1]{3,2,1,0,6,5,4:T(2,128)(2,1)S(1)} %bitcast.175), kind=kOutput, calls=%fused_computation.2 | convolution fusion | flops 171196416 | bytes 4014336 | tf_op jit(solution)/shard_map/mdrlqcs,clex->medrxqs/dot_general | solution.py:91
  55.7 0.5 slice_add_fusion
  56.2 0.5 slice_add_fusion.1
  56.7 1.2 %copy.65 = f32[3,2,1,2,32,256]{5,4,3,1,0,2:T(8,128)} copy(f32[3,2,1,2,32,256]{4,5,3,0,1,2:T(8,128)S(1)} %slice_add_fusion.1) | data formatting | bytes 786432 | tf_op jit(solution)/shard_map/add | solution.py:97
  (13 shorter events, 0.4 us)
Async XLA Ops:
  0.0 24.9 %copy-start = (s32[3,2]{0,1:T(2,128)S(1)}, s32[3,2]{0,1:T(2,128)}, u32[]{:S(2)}) copy-start(s32[3,2]{0,1:T(2,128)} %param.7) | copy-start | bytes 76
  0.8 8.4 %collective-permute-start = (f32[2,1,16,256]{3,2,0,1:T(8,128)S(1)}, f32[2,1,16,256]{3,2,0,1:T(8,128)S(1)}, u32[]{:S(2)}, u32[]{:S(2)}) collective-permute-start(f32[2,1,16,256]{3,2,0,1:T(8,128)S(1)} %get-tuple-element.23), channel_id=1, source_target_pairs={{0,4},{4,8},{8,12},{1,5},{5,9},{9,13},{2,6},{6,10},{10,14},{3,7},{... | collective-permute-start | bytes 98312 | tf_op jit(solution)/shard_map/ppermute | solution.py:20
  5.7 5.8 %collective-permute-start.1 = (f32[2,1,16,256]{3,2,0,1:T(8,128)S(1)}, f32[2,1,16,256]{3,2,0,1:T(8,128)S(1)}, u32[]{:S(2)}, u32[]{:S(2)}) collective-permute-start(f32[2,1,16,256]{3,2,0,1:T(8,128)S(1)} %get-tuple-element.24), channel_id=1, source_target_pairs={{4,0},{8,4},{12,8},{5,1},{9,5},{13,9},{6,2},{10,6},{14,10},{7,3},{... | collective-permute-start | bytes 98312 | tf_op jit(solution)/shard_map/ppermute | solution.py:21
  12.9 5.1 %collective-permute-start.2 = (bf16[2,1,32,256]{3,2,0,1:T(8,128)(2,1)S(1)}, bf16[2,1,32,256]{3,2,0,1:T(8,128)(2,1)S(1)}, u32[]{:S(2)}, u32[]{:S(2)}) collective-permute-start(bf16[2,1,32,256]{3,2,0,1:T(8,128)(2,1)S(1)} %get-tuple-element.25), channel_id=1, source_target_pairs={{0,4},{4,8},{8,12},{1,5},{5,9},{9,13},{2,6},{6,10},{10,14},{3,7},{... | collective-permute-start | bytes 98312 | tf_op jit(solution)/shard_map/ppermute | solution.py:20
  16.4 5.8 %collective-permute-start.3 = (bf16[2,1,32,256]{3,2,0,1:T(8,128)(2,1)S(1)}, bf16[2,1,32,256]{3,2,0,1:T(8,128)(2,1)S(1)}, u32[]{:S(2)}, u32[]{:S(2)}) collective-permute-start(bf16[2,1,32,256]{3,2,0,1:T(8,128)(2,1)S(1)} %get-tuple-element.26), channel_id=1, source_target_pairs={{4,0},{8,4},{12,8},{5,1},{9,5},{13,9},{6,2},{10,6},{14,10},{7,3},{... | collective-permute-start | bytes 98312 | tf_op jit(solution)/shard_map/ppermute | solution.py:21
  22.3 2.7 %collective-permute-start.4 = (bf16[2,1,128,32]{3,2,0,1:T(8,128)(2,1)S(1)}, bf16[2,1,128,32]{3,2,0,1:T(8,128)(2,1)S(1)}, u32[]{:S(2)}, u32[]{:S(2)}) collective-permute-start(bf16[2,1,128,32]{3,2,0,1:T(8,128)(2,1)S(1)} %get-tuple-element.21), channel_id=1, source_target_pairs={{0,1},{2,3},{4,5},{6,7},{8,9},{10,11},{12,13},{14,15},{16,17},{18,... | collective-permute-start | bytes 49160 | tf_op jit(solution)/shard_map/ppermute | solution.py:20
  23.6 3.1 %collective-permute-start.5 = (bf16[2,1,128,32]{3,2,0,1:T(8,128)(2,1)S(1)}, bf16[2,1,128,32]{3,2,0,1:T(8,128)(2,1)S(1)}, u32[]{:S(2)}, u32[]{:S(2)}) collective-permute-start(bf16[2,1,128,32]{3,2,0,1:T(8,128)(2,1)S(1)} %get-tuple-element.22), channel_id=1, source_target_pairs={{1,0},{3,2},{5,4},{7,6},{9,8},{11,10},{13,12},{15,14},{17,16},{19,... | collective-permute-start | bytes 49160 | tf_op jit(solution)/shard_map/ppermute | solution.py:21
where the time goes:
time: 58.3 us; the launch traced here: 57.9 us
  starting transfers between devices  13.6 us (23%)
  local copies, waits for them, and re-layouts  13.4 us (23%)
  waiting for transfers between devices  8.46 us (15%)
  other arithmetic  8.09 us (14%)
  matrix products  7.06 us (12%)
  blocking collectives  6.94 us (12%)
    ppermute x3, starting transfers between devices, extended(): before = lax.ppermute(last, axis, up)  9.69 us
    ppermute x3, waiting for transfers between devices, extended(): after = lax.ppermute(leading, axis, down)  8.23 us
    all_gather x1, blocking collectives, per_device(): shard_piece = lax.all_gather(tile_wide, 'date', axis=1, tiled=True)  6.94 us
    ppermute x3, starting transfers between devices, extended(): after = lax.ppermute(leading, axis, down)  3.88 us
    another operation x3, local copies, waits for them, and re-layouts  3.56 us
    concatenate x2, other arithmetic, filter_all(): jnp.concatenate([spec_real * gain_map, spec_imag * gain_map], axis=-1)  3 us
    slice x1, local copies, waits for them, and re-layouts, filter_all(): range_blocks[:, :, :, :, :, 1:]  2.7 us
    slice x2, local copies, waits for them, and re-layouts, filter_all(): smooth = smooth + jnp.roll(smooth, 1, 5) + jnp.roll(smooth, -1, 5)  2.03 us
  transfers between devices with their start and end apart: 6, of which 4 were waited for; matrix products, arithmetic and copies ran while one was open for 4% of the time, Pallas kernels for 0%

commit v1 on v0

v1 whole, which is shorter than its diff:
```python
import math

import jax
import jax.numpy as jnp
import numpy as np
from jax import lax
from jax.experimental import pallas as pl
from jax.experimental.pallas import tpu as pltpu
from jax.sharding import PartitionSpec as P

TAPS = 8
SHIFT_MAX = 12
PATCH = 64
HALF = PATCH // 2
RIM = SHIFT_MAX + TAPS // 2
REACH = HALF + RIM
LANES = 128
VMEM_LIMIT = 48 * 1024 * 1024

VMEM = pl.BlockSpec(memory_space=pltpu.VMEM)
SMEM = pl.BlockSpec(memory_space=pltpu.SMEM)
PARAMS = pltpu.CompilerParams(vmem_limit_bytes=VMEM_LIMIT)


def fourier_table(sine_sign, table_scale):
    freq_ids = np.arange(PATCH)
    phase_ids = (freq_ids[:, None] * freq_ids[None, :]) % PATCH
    angles = phase_ids * (2.0 * math.pi / PATCH)
    cosine = np.cos(angles) * table_scale
    sine_part = np.sin(angles) * (sine_sign * table_scale)
    top = np.concatenate([cosine, -sine_part], axis=1)
    bottom = np.concatenate([sine_part, cosine], axis=1)
    return np.concatenate([top, bottom], axis=0).astype(np.float32)


def paired(table):
    split = table.reshape(2, PATCH, 2, PATCH)
    wide = np.zeros((2, 2, PATCH, 2, 2, PATCH), np.float32)
    for slot in range(2):
        wide[:, slot, :, :, slot, :] = split
    return wide.reshape(4 * PATCH, 4 * PATCH)


def line_table(forward, row_patches):
    wide_lines = (row_patches + 1) * HALF
    table = np.zeros((row_patches, 2 * PATCH, 2, wide_lines), np.float32)
    transposed = forward.T.reshape(2 * PATCH, 2, PATCH)
    for row in range(row_patches):
        table[row, :, :, row * HALF : row * HALF + PATCH] = transposed
    return table.reshape(row_patches * 2 * PATCH, 2 * wide_lines)


def window_table():
    window = np.sin(math.pi * (np.arange(PATCH) + 0.5) / PATCH) ** 2
    return np.tile(np.outer(window, window), (2, 2)).astype(np.float32)


def ring_table():
    ring = np.zeros((LANES, LANES), np.float32)
    for lane in range(LANES):
        base = lane // PATCH * PATCH
        for step in (-1, 0, 1):
            ring[base + (lane + step) % PATCH, lane] = 1.0
    return ring


def pack_kernel(image_ref, taps_ref, offsets_ref, first_ref, last_ref):
    lines = image_ref.shape[1]
    width = image_ref.shape[2]
    taps = taps_ref[...]
    taps_high = taps.astype(jnp.bfloat16).astype(jnp.float32)
    taps_low = taps - taps_high
    shifts = jnp.broadcast_to(offsets_ref[...].astype(jnp.float32), (TAPS, lines))

    def write(out_ref, line_start, tap_start):
        for part in range(2):
            rows = image_ref[part, line_start : line_start + REACH, :]
            out_ref[part * REACH : (part + 1) * REACH, :] = rows.astype(jnp.bfloat16)
        cut = slice(tap_start, tap_start + HALF)
        filler = jnp.zeros((TAPS, width - 3 * HALF), jnp.float32)
        block = jnp.concatenate([taps_high[:, cut], taps_low[:, cut], shifts[:, cut], filler], axis=1)
        block = jnp.concatenate([block, jnp.zeros_like(block)], axis=0)
        out_ref[2 * REACH :, :] = block.astype(jnp.bfloat16)

    write(first_ref, 0, 0)
    write(last_ref, lines - REACH, lines - HALF)


def resample_kernel(image_ref, taps_ref, offsets_ref, above_ref, below_ref, tile_ref, edge_ref):
    lines = image_ref.shape[1]
    width = image_ref.shape[2]
    wide = lines + 2 * HALF

    def unpacked(ref):
        block = ref[2 * REACH :, : LANES].astype(jnp.float32)[:TAPS]
        return block[:, :HALF] + block[:, HALF : 2 * HALF], block[:1, 2 * HALF : 3 * HALF]

    above_taps, above_shift = unpacked(above_ref)
    below_taps, below_shift = unpacked(below_ref)
    taps = jnp.concatenate([above_taps, taps_ref[...], below_taps], axis=1)
    own_shift = offsets_ref[...].astype(jnp.float32)
    shift = jnp.concatenate([above_shift, own_shift, below_shift], axis=1).astype(jnp.int32)

    def band(source_lines):
        count = source_lines.shape[0]
        place = lax.broadcasted_iota(jnp.int32, (count, wide), 1) - HALF
        tap_ids = source_lines - place - shift + (TAPS // 2 - 1)
        total = jnp.zeros((count, wide), jnp.float32)
        for tap in range(TAPS):
            total = jnp.where(tap_ids == tap, taps[tap : tap + 1, :], total)
        return total

    own_ids = lax.broadcasted_iota(jnp.int32, (lines, wide), 0)
    rim_ids = lax.broadcasted_iota(jnp.int32, (2 * REACH, wide), 0)
    rim_ids = jnp.where(rim_ids < REACH, rim_ids - REACH, rim_ids - REACH + lines)
    own_band = band(own_ids)
    rim_band = band(rim_ids)
    rim_high = rim_band.astype(jnp.bfloat16)
    rim_low = (rim_band - rim_high.astype(jnp.float32)).astype(jnp.bfloat16)
    rim_both = jnp.concatenate([rim_high, rim_low], axis=0)
    over_rows = (((0,), (0,)), ((), ()))
    side = lax.axis_index("rg")
    edges = []
    for part in range(2):
        own = lax.dot_general(
            own_band,
            image_ref[part],
            over_rows,
            precision=lax.Precision.HIGHEST,
            preferred_element_type=jnp.float32,
        )
        cut = slice(part * REACH, (part + 1) * REACH)
        rim = jnp.concatenate([above_ref[cut, :], below_ref[cut, :]], axis=0)
        rim = jnp.concatenate([rim, rim], axis=0)
        total = own + lax.dot_general(rim_both, rim, over_rows, preferred_element_type=jnp.float32)
        tile_ref[part * wide : (part + 1) * wide, :] = total.astype(jnp.bfloat16)
        edge = jnp.where(side == 0, total[:, width - HALF :], total[:, :HALF])
        edges += [edge[: wide // 2], edge[wide // 2 :]]
    edge_ref[...] = jnp.concatenate(edges, axis=1).astype(jnp.bfloat16)


def cross(own_parts, other_parts):
    own_real, own_imag = own_parts
    other_real, other_imag = other_parts
    real = own_real * other_real + own_imag * other_imag
    imag = own_imag * other_real - own_real * other_imag
    return real, imag


def filter_kernel(
    match_ref,
    line_ref,
    forward_ref,
    inverse_ref,
    back_ref,
    window_ref,
    ring_ref,
    *refs,
):
    slots = (len(refs) - 3) // 2
    out_ref, spectrum_ref, filtered_ref = refs[-3:]
    match_count, _, _, lines, width = out_ref.shape
    wide = lines + 2 * HALF
    row_patches = lines // HALF + 1
    side = lax.axis_index("rg")
    date = lax.axis_index("date")
    dates = match_ref.shape[1]
    window = window_ref[...]
    back = back_ref[...]

    def tile_parts(slot):
        tile = refs[2 * slot][...].astype(jnp.float32)
        edge = refs[2 * slot + 1][...].astype(jnp.float32)
        cuts = [edge[:, i * HALF : (i + 1) * HALF] for i in range(4)]
        edge_real = jnp.concatenate(cuts[:2], axis=0)
        edge_imag = jnp.concatenate(cuts[2:], axis=0)
        return (tile[:wide], tile[wide:]), (edge_real, edge_imag)

    own_tile, own_edge = tile_parts(0)
    for slot in range(slots):
        other_tile, other_edge = (own_tile, own_edge) if slot == 0 else tile_parts(slot)
        mid = jnp.concatenate(cross(own_tile, other_tile), axis=0)
        rim = jnp.concatenate(cross(own_edge, other_edge), axis=0)
        before = jnp.where(side == 0, 0.0, rim)
        after = jnp.where(side == 0, rim, 0.0)
        filler = jnp.zeros((2 * wide, LANES - 2 * HALF), jnp.float32)
        shifted = jnp.concatenate([before, mid, after, filler], axis=1).astype(jnp.bfloat16)
        both = jnp.concatenate([mid.astype(jnp.bfloat16), shifted], axis=1)
        chunks = both.shape[1] // LANES
        line_spectra = jnp.dot(
            line_ref[...], both, preferred_element_type=jnp.float32
        ).astype(jnp.bfloat16)
        pieces = []
        for row in range(row_patches):
            top = row * 2 * PATCH
            for chunk in range(chunks):
                cut = slice(chunk * LANES, (chunk + 1) * LANES)
                pieces.append(
                    jnp.concatenate(
                        [
                            line_spectra[top : top + PATCH, cut],
                            line_spectra[top + PATCH : top + 2 * PATCH, cut],
                        ],
                        axis=1,
                    )
                )
        patches = jnp.concatenate(pieces, axis=0)
        spectrum_ref[...] = jnp.dot(
            patches, forward_ref[...], preferred_element_type=jnp.float32
        )
        pieces = []
        for block in range(row_patches * chunks):
            rows = slice(block * PATCH, (block + 1) * PATCH)
            real = spectrum_ref[rows, :LANES]
            imag = spectrum_ref[rows, LANES:]
            power = real * real + imag * imag
            power = power + pltpu.roll(power, 1, 0) + pltpu.roll(power, PATCH - 1, 0)
            smooth = jnp.dot(
                power.astype(jnp.bfloat16), ring_ref[...], preferred_element_type=jnp.float32
            )
            gain = lax.rsqrt(lax.rsqrt(smooth * (1.0 / (9.0 * PATCH * PATCH)) + 1.0))
            pieces.append(
                jnp.concatenate([real * gain, imag * gain], axis=1).astype(jnp.bfloat16)
            )
        shaped = jnp.concatenate(pieces, axis=0)
        range_back = jnp.dot(
            shaped, inverse_ref[...], preferred_element_type=jnp.float32
        ).astype(jnp.bfloat16)
        for chunk in range(chunks):
            totals = [[None] * (row_patches - 1) for _ in range(2)]
            for row in range(row_patches):
                top = (row * chunks + chunk) * PATCH
                block = range_back[top : top + PATCH]
                stacked = jnp.concatenate([block[:, :LANES], block[:, LANES:]], axis=0)
                patch_out = jnp.dot(back, stacked, preferred_element_type=jnp.float32) * window
                for part in range(2):
                    upper = patch_out[part * PATCH : part * PATCH + HALF]
                    lower = patch_out[part * PATCH + HALF : (part + 1) * PATCH]
                    if row > 0:
                        totals[part][row - 1] = totals[part][row - 1] + upper
                    if row < row_patches - 1:
                        totals[part][row] = lower
            for part in range(2):
                spectrum_ref[part * lines : (part + 1) * lines, :LANES] = jnp.concatenate(
                    totals[part], axis=0
                )
            filtered_ref[chunk] = spectrum_ref[: 2 * lines, :LANES]
        mids = width // LANES
        mid = jnp.concatenate([filtered_ref[i] for i in range(mids)], axis=1)
        moved = jnp.concatenate([filtered_ref[i] for i in range(mids, chunks)], axis=1)
        result = mid + moved[:, HALF : HALF + width]
        for match in range(match_count):
            wanted = match_ref[match, date]
            here = lax.rem(wanted - date + dates, dates) == slot

            @pl.when(here)
            def _():
                for part in range(2):
                    out_ref[match, part, 0] = result[part * lines : (part + 1) * lines]


def per_device(image_stack, tap_weights, offsets, matchings):
    _, _, lines, width = image_stack.shape
    match_count = matchings.shape[0]
    image = image_stack.reshape(2, lines, width)
    taps = tap_weights.reshape(TAPS, lines)
    message = jax.ShapeDtypeStruct((2 * REACH + 16, width), jnp.bfloat16)
    first, last = pl.pallas_call(
        pack_kernel,
        out_shape=(message, message),
        in_specs=[VMEM] * 3,
        out_specs=(VMEM, VMEM),
        compiler_params=PARAMS,
        name="pack",
    )(image, taps, offsets)
    peers = lax.axis_size("az")
    up = [(i, i + 1) for i in range(peers - 1)]
    down = [(j, i) for i, j in up]
    above = lax.ppermute(last, "az", up)
    below = lax.ppermute(first, "az", down)
    wide = lines + 2 * HALF
    tile, edge = pl.pallas_call(
        resample_kernel,
        out_shape=(
            jax.ShapeDtypeStruct((2 * wide, width), jnp.bfloat16),
            jax.ShapeDtypeStruct((wide // 2, 4 * HALF), jnp.bfloat16),
        ),
        in_specs=[VMEM] * 5,
        out_specs=(VMEM, VMEM),
        compiler_params=PARAMS,
        name="resample",
    )(image, taps, offsets, above, below)
    dates = lax.axis_size("date")
    received = []
    for slot in range(dates):
        if slot > 0:
            pairs = [((i + slot) % dates, i) for i in range(dates)]
            received.append(lax.ppermute(tile, "date", pairs))
        else:
            received.append(tile)
        crossed = [
            (((i + slot) % dates) * 2 + 1 - j, i * 2 + j) for i in range(dates) for j in range(2)
        ]
        received.append(lax.ppermute(edge, ("date", "rg"), crossed))
    row_patches = lines // HALF + 1
    forward = fourier_table(1.0, 1.0)
    inverse = fourier_table(-1.0, 1.0 / PATCH)
    chunks = (width + width + LANES) // LANES
    back = inverse.reshape(2, PATCH, 2, PATCH).transpose(2, 3, 0, 1).reshape(2 * PATCH, 2 * PATCH)
    tables = [
        jnp.asarray(line_table(forward, row_patches), jnp.bfloat16),
        jnp.asarray(paired(forward), jnp.bfloat16),
        jnp.asarray(paired(inverse), jnp.bfloat16),
        jnp.asarray(back, jnp.bfloat16),
        jnp.asarray(window_table()),
        jnp.asarray(ring_table(), jnp.bfloat16),
    ]
    return pl.pallas_call(
        filter_kernel,
        out_shape=jax.ShapeDtypeStruct((match_count, 2, 1, lines, width), jnp.float32),
        in_specs=[SMEM] + [VMEM] * (len(tables) + len(received)),
        out_specs=VMEM,
        scratch_shapes=[
            pltpu.VMEM((row_patches * chunks * PATCH, 2 * LANES), jnp.float32),
            pltpu.VMEM((chunks, 2 * lines, LANES), jnp.float32),
        ],
        compiler_params=PARAMS,
        name="goldstein",
    )(matchings, *tables, *received)


def solution(mesh):
    placed = (
        P(None, ("parts", "date"), "az", "rg"),
        P(None, ("parts", "date"), "az"),
        P(("parts", "date"), "az"),
        P(),
    )
    return jax.shard_map(
        per_device,
        mesh=mesh,
        in_specs=placed,
        out_specs=P(None, None, ("parts", "date"), "az", "rg"),
        check_vma=False,
    )
```

time: 58.3 us -> 26.8 us (0.46)
  local copies, waits for them, and re-layouts: 13.4 us -> 4.77 us
  other arithmetic: 8.09 us -> 0 us
  matrix products: 7.06 us -> 0 us
  blocking collectives: 6.94 us -> 0 us
  Pallas kernels: 0 us -> 5.19 us
  starting transfers between devices: 13.6 us -> 8.68 us
  waiting for transfers between devices: 8.46 us -> 7.68 us
    dot_general x8 -> x0, matrix products: 7.06 us -> none  [the longest x1 1.93 us: filter_all(): jnp.einsum('mdrlqk,kj->mdrlqj', shaped, inverse_table, preferred_element_...]
    all_gather x1 -> x0, blocking collectives: 6.94 us -> none  [per_device(): shard_piece = lax.all_gather(tile_wide, 'date', axis=1, tiled=True)]
    slice x8 -> x0, local copies, waits for them, and re-layouts: 6.48 us -> none  [the longest x1 2.7 us: filter_all(): range_blocks[:, :, :, :, :, 1:]]
    pallas_call x0 -> x3, Pallas kernels: none -> 5.19 us  [the longest x1 4.38 us: per_device(): pl.pallas_call(filter_kernel, out_shape=jax.ShapeDtypeStruct((match_count...]
    ppermute x6 -> x5, starting transfers between devices: 13.6 us -> 8.68 us  [the longest x1 5.05 us: per_device(): above = lax.ppermute(last, 'az', up)]
    unnamed x2 -> x21, local copies, waits for them, and re-layouts: 0.01 us -> 4.77 us
    add x5 -> x0, other arithmetic: 3.94 us -> none  [the longest x1 1.5 us: filter_all(): power_spec + jnp.roll(power_spec, 1, 3) + jnp.roll(power_spec, -1, 3)]
    another operation x3 -> x0, local copies, waits for them, and re-layouts: 3.56 us -> none
  transfers between devices with their start and end apart: 6 -> 5, of which waited for: 4 -> 4; matrix products, arithmetic and copies ran while one was open for 4% -> 0% of each run, Pallas kernels for 0% -> 0%
where the time goes in v1:
time: 26.8 us; the launch traced here: 26.4 us
  starting transfers between devices  8.68 us (32%)
  waiting for transfers between devices  7.68 us (29%)
  Pallas kernels  5.19 us (19%)
  local copies, waits for them, and re-layouts  4.77 us (18%)
    ppermute x1, starting transfers between devices, per_device(): above = lax.ppermute(last, 'az', up)  5.05 us
    unnamed x21, local copies, waits for them, and re-layouts  4.77 us
    ppermute x1, waiting for transfers between devices, per_device(): below = lax.ppermute(first, 'az', down)  4.41 us
    pallas_call x1, Pallas kernels, per_device(): pl.pallas_call(filter_kernel, out_shape=jax.ShapeDtypeStruct((match_count...  4.38 us
    ppermute x2, waiting for transfers between devices, per_device(): received.append(lax.ppermute(edge, ('date', 'rg'), crossed))  2.58 us
    ppermute x1, starting transfers between devices, per_device(): received.append(lax.ppermute(tile, 'date', pairs))  1.56 us
    ppermute x1, starting transfers between devices, per_device(): below = lax.ppermute(first, 'az', down)  1.42 us
    pallas_call x1, Pallas kernels, per_device(): pl.pallas_call(resample_kernel, out_shape=(jax.ShapeDtypeStruct((2 * wide...  0.74 us
  transfers between devices with their start and end apart: 5, of which 4 were waited for; matrix products, arithmetic and copies ran while one was open for 0% of the time, Pallas kernels for 0%

profile of v1, /device:TPU:0, one launch (start us, length us, event | category | flops | bytes accessed | tf_op | source)
XLA Modules:
  0.0 26.4 jit_solution(11323200145841469915)
XLA Ops:
  0.0 0.0 copy-start.8
  0.0 0.7 %copy-done.8 = s32[1,64]{1,0:T(1,128)S(1)} copy-done((s32[1,64]{1,0:T(1,128)S(1)}, s32[1,64]{1,0:T(1,128)}, u32[]{:S(2)}) %copy-start.8) | copy-done | bytes 280
  0.7 0.0 copy-start
  0.7 0.9 %copy-done = f32[2,1,64,256]{3,2,1,0:T(8,128)S(1)} copy-done((f32[2,1,64,256]{3,2,1,0:T(8,128)S(1)}, f32[2,1,64,256]{3,2,1,0:T(8,128)}, u32[]{:S(2)}) %copy-start) | copy-done | bytes 131096
  1.6 0.0 copy-start.7
  1.6 0.7 %copy-done.7 = f32[8,1,64]{2,1,0:T(1,128)S(1)} copy-done((f32[8,1,64]{2,1,0:T(1,128)S(1)}, f32[8,1,64]{2,1,0:T(1,128)}, u32[]{:S(2)}) %copy-start.7) | copy-done | bytes 2072
  2.2 0.0 copy-start.9
  2.3 0.0 copy-start.1
  2.3 0.1 pack.1
  2.3 0.0 copy-start.2
  2.3 5.1 %collective-permute-start = (bf16[112,256]{1,0:T(8,128)(2,1)S(1)}, bf16[112,256]{1,0:T(8,128)(2,1)S(1)}, u32[]{:S(2)}, u32[]{:S(2)}) collective-permute-start(bf16[112,256]{1,0:T(8,128)(2,1)S(1)} %get-tuple-element.9), channel_id=1, source_target_pairs={{0,4},{4,8},{8,12},{1,5},{5,9},{9,13},{2,6},{6,10},{10,14},{3,7},{... | collective-permute-start | bytes 172040 | tf_op jit(solution)/shard_map/ppermute | solution.py:279
  7.4 0.0 copy-start.4
  7.4 1.4 %collective-permute-start.1 = (bf16[112,256]{1,0:T(8,128)(2,1)S(1)}, bf16[112,256]{1,0:T(8,128)(2,1)S(1)}, u32[]{:S(2)}, u32[]{:S(2)}) collective-permute-start(bf16[112,256]{1,0:T(8,128)(2,1)S(1)} %get-tuple-element.10), channel_id=1, source_target_pairs={{4,0},{8,4},{12,8},{5,1},{9,5},{13,9},{6,2},{10,6},{14,10},{7,3},{... | collective-permute-start | bytes 172040 | tf_op jit(solution)/shard_map/ppermute | solution.py:280
  8.8 0.4 %collective-permute-done.above_ref = bf16[112,256]{1,0:T(8,128)(2,1)S(1)} collective-permute-done((bf16[112,256]{1,0:T(8,128)(2,1)S(1)}, bf16[112,256]{1,0:T(8,128)(2,1)S(1)}, u32[]{:S(2)}, u32[]{:S(2)}) %collective-permute-start) | collective-permute-done | bytes 57376 | tf_op jit(solution)/shard_map/ppermute | solution.py:279
  9.2 4.4 %collective-permute-done.1.below_ref = bf16[112,256]{1,0:T(8,128)(2,1)S(1)} collective-permute-done((bf16[112,256]{1,0:T(8,128)(2,1)S(1)}, bf16[112,256]{1,0:T(8,128)(2,1)S(1)}, u32[]{:S(2)}, u32[]{:S(2)}) %collective-permute-start.1) | collective-permute-done | bytes 57376 | tf_op jit(solution)/shard_map/ppermute | solution.py:280
  13.6 0.7 %resample.1 = (bf16[256,256]{1,0:T(8,128)(2,1)S(1)}, bf16[64,128]{1,0:T(8,128)(2,1)S(1)}) custom-call(f32[2,64,256]{2,1,0:T(8,128)S(1)} %bitcast.3, f32[8,64]{1,0:T(8,128)S(1)} %bitcast.5, s32[1,64]{1,0:T(1,128)S(1)} %copy-done.8, bf16[112,256]{1,0:T(8,128)(2,1)S(1)} %collective-permute-done.above_ref, bf16[112,256]{1,0:T(8,128)(2,1)S(1)} %collective-permute-done.1.below_ref), custom_call_target="tpu_custom_call" | custom-call | tf_op jit(solution)/shard_map/resample/pallas_call | solution.py:282
  14.4 1.6 %collective-permute-start.3 = (bf16[256,256]{1,0:T(8,128)(2,1)S(1)}, bf16[256,256]{1,0:T(8,128)(2,1)S(1)}, u32[]{:S(2)}, u32[]{:S(2)}) collective-permute-start(bf16[256,256]{1,0:T(8,128)(2,1)S(1)} %get-tuple-element.11.refs_0_), channel_id=1, source_target_pairs={{2,0},{0,2},{3,1},{1,3},{6,4},{4,6},{7,5},{5,7},{10,8},{8,10},{11,... | collective-permute-start | bytes 393224 | tf_op jit(solution)/shard_map/ppermute | solution.py:298
  15.9 0.0 collective-permute-start.4
  15.9 0.6 %collective-permute-start.2 = (bf16[64,128]{1,0:T(8,128)(2,1)S(1)}, bf16[64,128]{1,0:T(8,128)(2,1)S(1)}, u32[]{:S(2)}, u32[]{:S(2)}) collective-permute-start(bf16[64,128]{1,0:T(8,128)(2,1)S(1)} %get-tuple-element.12), channel_id=1, source_target_pairs={{1,0},{0,1},{3,2},{2,3},{5,4},{4,5},{7,6},{6,7},{9,8},{8,9},{11,10... | collective-permute-start | bytes 49160 | tf_op jit(solution)/shard_map/ppermute | solution.py:304
  16.6 0.0 copy-done.9
  16.6 0.1 copy.11.match_ref
  16.7 2.6 %collective-permute-done.4.refs_3_ = bf16[64,128]{1,0:T(8,128)(2,1)S(1)} collective-permute-done((bf16[64,128]{1,0:T(8,128)(2,1)S(1)}, bf16[64,128]{1,0:T(8,128)(2,1)S(1)}, u32[]{:S(2)}, u32[]{:S(2)}) %collective-permute-start.4) | collective-permute-done | bytes 16416 | tf_op jit(solution)/shard_map/ppermute | solution.py:304
  19.2 0.0 collective-permute-done.2.refs_1_
  19.2 0.3 %collective-permute-done.3.refs_2_ = bf16[256,256]{1,0:T(8,128)(2,1)S(1)} collective-permute-done((bf16[256,256]{1,0:T(8,128)(2,1)S(1)}, bf16[256,256]{1,0:T(8,128)(2,1)S(1)}, u32[]{:S(2)}, u32[]{:S(2)}) %collective-permute-start.3) | collective-permute-done | bytes 131104 | tf_op jit(solution)/shard_map/ppermute | solution.py:298
  19.6 0.0 copy-done.1
  19.6 0.0 copy-done.2
  19.6 0.0 copy-done.4
  19.6 0.0 copy-start.3
  19.6 0.9 %copy-done.3 = bf16[256,256]{1,0:T(8,128)(2,1)S(1)} copy-done((bf16[256,256]{1,0:T(8,128)(2,1)S(1)}, bf16[256,256]{1,0:T(8,128)(2,1)}, u32[]{:S(2)}) %copy-start.3) | copy-done | bytes 131096
  20.5 0.0 copy-start.5
  20.5 0.8 %copy-done.5 = bf16[128,128]{1,0:T(8,128)(2,1)S(1)} copy-done((bf16[128,128]{1,0:T(8,128)(2,1)S(1)}, bf16[128,128]{1,0:T(8,128)(2,1)}, u32[]{:S(2)}) %copy-start.5) | copy-done | bytes 32792
  21.2 0.0 copy-start.6
  21.2 0.8 %copy-done.6 = bf16[128,128]{1,0:T(8,128)(2,1)S(1)} copy-done((bf16[128,128]{1,0:T(8,128)(2,1)S(1)}, bf16[128,128]{1,0:T(8,128)(2,1)}, u32[]{:S(2)}) %copy-start.6) | copy-done | bytes 32792
  22.0 4.4 %goldstein.1 = f32[3,2,1,64,256]{4,3,2,1,0:T(8,128)} custom-call(s32[3,2]{1,0:T(4,128)S(1)} %copy.11.match_ref, bf16[384,256]{1,0:T(8,128)(2,1)S(1)} %copy-done.1, bf16[256,256]{1,0:T(8,128)(2,1)S(1)} %copy-done.3, bf16[256,256]{1,0:T(8,128)(2,1)S(1)} %copy-done.2, bf16[128,128]{1,0:T(8,128)(2,1)S(1)} %copy-done.6, f32[128,128]{1,0:T(8,128)S(1)} %copy-done.4, ...), custom_call_target="tpu_custom_call" | custom-call | tf_op jit(solution)/shard_map/goldstein/pallas_call | solution.py:318
Async XLA Ops:
  0.0 0.7 %copy-start.8 = (s32[1,64]{1,0:T(1,128)S(1)}, s32[1,64]{1,0:T(1,128)}, u32[]{:S(2)}) copy-start(s32[1,64]{1,0:T(1,128)} %offsets_ref.3) | copy-start | bytes 772
  0.7 0.9 %copy-start = (f32[2,1,64,256]{3,2,1,0:T(8,128)S(1)}, f32[2,1,64,256]{3,2,1,0:T(8,128)}, u32[]{:S(2)}) copy-start(f32[2,1,64,256]{3,2,1,0:T(8,128)} %param.10) | copy-start | bytes 393220
  1.6 0.7 %copy-start.7 = (f32[8,1,64]{2,1,0:T(1,128)S(1)}, f32[8,1,64]{2,1,0:T(1,128)}, u32[]{:S(2)}) copy-start(f32[8,1,64]{2,1,0:T(1,128)} %param.11) | copy-start | bytes 6148
  2.2 14.3 %copy-start.9 = (s32[3,2]{0,1:T(2,128)S(1)}, s32[3,2]{0,1:T(2,128)}, u32[]{:S(2)}) copy-start(s32[3,2]{0,1:T(2,128)} %param.13) | copy-start | bytes 76
  2.3 17.3 %copy-start.1 = (bf16[384,256]{1,0:T(8,128)(2,1)S(1)}, bf16[384,256]{1,0:T(8,128)(2,1)}, u32[]{:S(2)}) copy-start(bf16[384,256]{1,0:T(8,128)(2,1)} %constant.12.clone.line_ref) | copy-start | bytes 589828
  2.3 17.2 %copy-start.2 = (bf16[256,256]{1,0:T(8,128)(2,1)S(1)}, bf16[256,256]{1,0:T(8,128)(2,1)}, u32[]{:S(2)}) copy-start(bf16[256,256]{1,0:T(8,128)(2,1)} %constant.14.clone.inverse_ref) | copy-start | bytes 393220
  2.3 6.9 %collective-permute-start = (bf16[112,256]{1,0:T(8,128)(2,1)S(1)}, bf16[112,256]{1,0:T(8,128)(2,1)S(1)}, u32[]{:S(2)}, u32[]{:S(2)}) collective-permute-start(bf16[112,256]{1,0:T(8,128)(2,1)S(1)} %get-tuple-element.9), channel_id=1, source_target_pairs={{0,4},{4,8},{8,12},{1,5},{5,9},{9,13},{2,6},{6,10},{10,14},{3,7},{... | collective-permute-start | bytes 172040 | tf_op jit(solution)/shard_map/ppermute | solution.py:279
  7.4 12.2 %copy-start.4 = (f32[128,128]{1,0:T(8,128)S(1)}, f32[128,128]{1,0:T(8,128)}, u32[]{:S(2)}) copy-start(f32[128,128]{1,0:T(8,128)} %constant.16.clone.window_ref) | copy-start | bytes 196612
  7.4 6.2 %collective-permute-start.1 = (bf16[112,256]{1,0:T(8,128)(2,1)S(1)}, bf16[112,256]{1,0:T(8,128)(2,1)S(1)}, u32[]{:S(2)}, u32[]{:S(2)}) collective-permute-start(bf16[112,256]{1,0:T(8,128)(2,1)S(1)} %get-tuple-element.10), channel_id=1, source_target_pairs={{4,0},{8,4},{12,8},{5,1},{9,5},{13,9},{6,2},{10,6},{14,10},{7,3},{... | collective-permute-start | bytes 172040 | tf_op jit(solution)/shard_map/ppermute | solution.py:280
  14.4 5.2 %collective-permute-start.3 = (bf16[256,256]{1,0:T(8,128)(2,1)S(1)}, bf16[256,256]{1,0:T(8,128)(2,1)S(1)}, u32[]{:S(2)}, u32[]{:S(2)}) collective-permute-start(bf16[256,256]{1,0:T(8,128)(2,1)S(1)} %get-tuple-element.11.refs_0_), channel_id=1, source_target_pairs={{2,0},{0,2},{3,1},{1,3},{6,4},{4,6},{7,5},{5,7},{10,8},{8,10},{11,... | collective-permute-start | bytes 393224 | tf_op jit(solution)/shard_map/ppermute | solution.py:298
  15.9 3.3 %collective-permute-start.4 = (bf16[64,128]{1,0:T(8,128)(2,1)S(1)}, bf16[64,128]{1,0:T(8,128)(2,1)S(1)}, u32[]{:S(2)}, u32[]{:S(2)}) collective-permute-start(bf16[64,128]{1,0:T(8,128)(2,1)S(1)} %get-tuple-element.12), channel_id=1, source_target_pairs={{3,0},{2,1},{1,2},{0,3},{7,4},{6,5},{5,6},{4,7},{11,8},{10,9},{9,1... | collective-permute-start | bytes 49160 | tf_op jit(solution)/shard_map/ppermute | solution.py:304
  15.9 3.3 %collective-permute-start.2 = (bf16[64,128]{1,0:T(8,128)(2,1)S(1)}, bf16[64,128]{1,0:T(8,128)(2,1)S(1)}, u32[]{:S(2)}, u32[]{:S(2)}) collective-permute-start(bf16[64,128]{1,0:T(8,128)(2,1)S(1)} %get-tuple-element.12), channel_id=1, source_target_pairs={{1,0},{0,1},{3,2},{2,3},{5,4},{4,5},{7,6},{6,7},{9,8},{8,9},{11,10... | collective-permute-start | bytes 49160 | tf_op jit(solution)/shard_map/ppermute | solution.py:304
  19.6 0.9 %copy-start.3 = (bf16[256,256]{1,0:T(8,128)(2,1)S(1)}, bf16[256,256]{1,0:T(8,128)(2,1)}, u32[]{:S(2)}) copy-start(bf16[256,256]{1,0:T(8,128)(2,1)} %constant.13.clone.forward_ref) | copy-start | bytes 393220
  20.5 0.8 %copy-start.5 = (bf16[128,128]{1,0:T(8,128)(2,1)S(1)}, bf16[128,128]{1,0:T(8,128)(2,1)}, u32[]{:S(2)}) copy-start(bf16[128,128]{1,0:T(8,128)(2,1)} %constant.17.clone.ring_ref) | copy-start | bytes 98308
  21.2 0.8 %copy-start.6 = (bf16[128,128]{1,0:T(8,128)(2,1)S(1)}, bf16[128,128]{1,0:T(8,128)(2,1)}, u32[]{:S(2)}) copy-start(bf16[128,128]{1,0:T(8,128)(2,1)} %constant.15.clone.back_ref) | copy-start | bytes 98308

commit v2 on v1

v2 whole, which is shorter than its diff:
```python
import math

import jax
import jax.numpy as jnp
import numpy as np
from jax import lax
from jax.experimental import pallas as pl
from jax.experimental.pallas import tpu as pltpu
from jax.sharding import PartitionSpec as P

TAPS = 8
SHIFT_MAX = 12
PATCH = 64
HALF = PATCH // 2
RIM = SHIFT_MAX + TAPS // 2
REACH = HALF + RIM
LANES = 128
VMEM_LIMIT = 48 * 1024 * 1024

VMEM = pl.BlockSpec(memory_space=pltpu.VMEM)
SMEM = pl.BlockSpec(memory_space=pltpu.SMEM)
PARAMS = pltpu.CompilerParams(vmem_limit_bytes=VMEM_LIMIT)


def fourier_table(sine_sign, table_scale):
    freq_ids = np.arange(PATCH)
    phase_ids = (freq_ids[:, None] * freq_ids[None, :]) % PATCH
    angles = phase_ids * (2.0 * math.pi / PATCH)
    cosine = np.cos(angles) * table_scale
    sine_part = np.sin(angles) * (sine_sign * table_scale)
    top = np.concatenate([cosine, -sine_part], axis=1)
    bottom = np.concatenate([sine_part, cosine], axis=1)
    return np.concatenate([top, bottom], axis=0).astype(np.float32)


def paired(table):
    split = table.reshape(2, PATCH, 2, PATCH)
    wide = np.zeros((2, 2, PATCH, 2, 2, PATCH), np.float32)
    for slot in range(2):
        wide[:, slot, :, :, slot, :] = split
    return wide.reshape(4 * PATCH, 4 * PATCH)


def line_table(forward, row_patches):
    wide_lines = (row_patches + 1) * HALF
    table = np.zeros((row_patches, 2 * PATCH, 2, wide_lines), np.float32)
    transposed = forward.T.reshape(2 * PATCH, 2, PATCH)
    for row in range(row_patches):
        table[row, :, :, row * HALF : row * HALF + PATCH] = transposed
    return table.reshape(row_patches * 2 * PATCH, 2 * wide_lines)


def window_table():
    window = np.sin(math.pi * (np.arange(PATCH) + 0.5) / PATCH) ** 2
    return np.tile(np.outer(window, window), (2, 2)).astype(np.float32)


def ring_table():
    ring = np.zeros((LANES, LANES), np.float32)
    for lane in range(LANES):
        base = lane // PATCH * PATCH
        for step in (-1, 0, 1):
            ring[base + (lane + step) % PATCH, lane] = 1.0
    return ring


def edge_of(other_ref, part, side, lines):
    width = other_ref.shape[2]
    return jnp.where(
        side == 0, other_ref[part, lines, :HALF], other_ref[part, lines, width - HALF :]
    )


def pack_kernel(image_ref, other_ref, taps_ref, offsets_ref, first_ref, last_ref):
    lines = image_ref.shape[1]
    width = image_ref.shape[2]
    side = lax.axis_index("rg")
    taps = taps_ref[...]
    taps_high = taps.astype(jnp.bfloat16).astype(jnp.float32)
    taps_low = taps - taps_high
    shifts = jnp.broadcast_to(offsets_ref[...].astype(jnp.float32), (TAPS, lines))

    def write(out_ref, line_start, tap_start):
        rows = slice(line_start, line_start + REACH)
        for part in range(2):
            cut = slice(part * REACH, (part + 1) * REACH)
            out_ref[cut, :] = image_ref[part, rows, :].astype(jnp.bfloat16)
        edges = jnp.concatenate([edge_of(other_ref, part, side, rows) for part in range(2)], axis=0)
        cut = slice(tap_start, tap_start + HALF)
        block = jnp.concatenate([taps_high[:, cut], taps_low[:, cut], shifts[:, cut]], axis=1)
        block = jnp.concatenate([block, jnp.zeros((HALF - TAPS, 3 * HALF), jnp.float32)], axis=0)
        cuts = [edges[i * HALF : (i + 1) * HALF] for i in range(3)]
        filler = jnp.zeros((HALF, width - 6 * HALF), jnp.float32)
        block = jnp.concatenate([block, *cuts, filler], axis=1)
        out_ref[2 * REACH :, :] = block.astype(jnp.bfloat16)

    write(first_ref, 0, 0)
    write(last_ref, lines - REACH, lines - HALF)


def resample_kernel(
    image_ref, other_ref, taps_ref, offsets_ref, above_ref, below_ref, tile_ref
):
    lines = image_ref.shape[1]
    width = image_ref.shape[2]
    wide = lines + 2 * HALF
    side = lax.axis_index("rg")

    def unpacked(ref):
        block = ref[2 * REACH :, :].astype(jnp.float32)
        head = block[:TAPS]
        edges = [block[:, i * HALF : (i + 1) * HALF] for i in range(3, 6)]
        return (
            head[:, :HALF] + head[:, HALF : 2 * HALF],
            head[:1, 2 * HALF : 3 * HALF],
            jnp.concatenate(edges, axis=0),
        )

    above_taps, above_shift, above_edge = unpacked(above_ref)
    below_taps, below_shift, below_edge = unpacked(below_ref)
    taps = jnp.concatenate([above_taps, taps_ref[...], below_taps], axis=1)
    own_shift = offsets_ref[...].astype(jnp.float32)
    shift = jnp.concatenate([above_shift, own_shift, below_shift], axis=1).astype(jnp.int32)

    def band(source_lines):
        count = source_lines.shape[0]
        place = lax.broadcasted_iota(jnp.int32, (count, wide), 1) - HALF
        tap_ids = source_lines - place - shift + (TAPS // 2 - 1)
        total = jnp.zeros((count, wide), jnp.float32)
        for tap in range(TAPS):
            total = jnp.where(tap_ids == tap, taps[tap : tap + 1, :], total)
        return total

    own_ids = lax.broadcasted_iota(jnp.int32, (lines, wide), 0)
    rim_ids = lax.broadcasted_iota(jnp.int32, (2 * REACH, wide), 0)
    rim_ids = jnp.where(rim_ids < REACH, rim_ids - REACH, rim_ids - REACH + lines)
    own_band = band(own_ids)
    rim_band = band(rim_ids)
    rim_high = rim_band.astype(jnp.bfloat16)
    rim_low = (rim_band - rim_high.astype(jnp.float32)).astype(jnp.bfloat16)
    rim_both = jnp.concatenate([rim_high, rim_low], axis=0)
    over_rows = (((0,), (0,)), ((), ()))
    edges = []
    for part in range(2):
        edge = edge_of(other_ref, part, side, slice(0, lines))
        own = lax.dot_general(
            own_band,
            jnp.concatenate([image_ref[part], edge], axis=1),
            over_rows,
            precision=lax.Precision.HIGHEST,
            preferred_element_type=jnp.float32,
        )
        cut = slice(part * REACH, (part + 1) * REACH)
        rim = jnp.concatenate([above_ref[cut, :], below_ref[cut, :]], axis=0)
        rim_edge = jnp.concatenate([above_edge[cut], below_edge[cut]], axis=0).astype(jnp.bfloat16)
        rim = jnp.concatenate([rim, rim_edge], axis=1)
        rim = jnp.concatenate([rim, rim], axis=0)
        total = own + lax.dot_general(rim_both, rim, over_rows, preferred_element_type=jnp.float32)
        tile_ref[part * wide : (part + 1) * wide, :] = total[:, :width].astype(jnp.bfloat16)
        rows = wide // 4
        edges += [total[i * rows : (i + 1) * rows, width:] for i in range(4)]
    tile_ref[2 * wide :, :] = jnp.concatenate(edges, axis=1).astype(jnp.bfloat16)


def cross(own_parts, other_parts):
    own_real, own_imag = own_parts
    other_real, other_imag = other_parts
    real = own_real * other_real + own_imag * other_imag
    imag = own_imag * other_real - own_real * other_imag
    return real, imag


def tile_parts(tile_ref, wide):
    tile = tile_ref[: 2 * wide, :].astype(jnp.float32)
    edge = tile_ref[2 * wide :, :].astype(jnp.float32)
    cuts = [edge[:, i * HALF : (i + 1) * HALF] for i in range(8)]
    edge_real = jnp.concatenate(cuts[:4], axis=0)
    edge_imag = jnp.concatenate(cuts[4:], axis=0)
    return (tile[:wide], tile[wide:]), (edge_real, edge_imag)


def filtered_of(own_ref, other_ref, table_ref, spectrum_ref, filtered_ref, lines):
    width = own_ref.shape[1]
    wide = lines + 2 * HALF
    row_patches = lines // HALF + 1
    side = lax.axis_index("rg")
    tables = split_tables(table_ref, row_patches)
    line_table_of, forward, inverse, back, ring, window = tables
    own_tile, own_edge = tile_parts(own_ref, wide)
    other_tile, other_edge = tile_parts(other_ref, wide)
    mid = jnp.concatenate(cross(own_tile, other_tile), axis=0)
    rim = jnp.concatenate(cross(own_edge, other_edge), axis=0)
    before = jnp.where(side == 0, 0.0, rim)
    after = jnp.where(side == 0, rim, 0.0)
    filler = jnp.zeros((2 * wide, LANES - 2 * HALF), jnp.float32)
    shifted = jnp.concatenate([before, mid, after, filler], axis=1).astype(jnp.bfloat16)
    both = jnp.concatenate([mid.astype(jnp.bfloat16), shifted], axis=1)
    chunks = both.shape[1] // LANES
    line_spectra = jnp.dot(line_table_of, both, preferred_element_type=jnp.float32)
    line_spectra = line_spectra.astype(jnp.bfloat16)
    pieces = []
    for row in range(row_patches):
        top = row * 2 * PATCH
        for chunk in range(chunks):
            cut = slice(chunk * LANES, (chunk + 1) * LANES)
            real = line_spectra[top : top + PATCH, cut]
            imag = line_spectra[top + PATCH : top + 2 * PATCH, cut]
            pieces.append(jnp.concatenate([real, imag], axis=1))
    patches = jnp.concatenate(pieces, axis=0)
    spectrum_ref[...] = jnp.dot(patches, forward, preferred_element_type=jnp.float32)
    pieces = []
    for block in range(row_patches * chunks):
        rows = slice(block * PATCH, (block + 1) * PATCH)
        real = spectrum_ref[rows, :LANES]
        imag = spectrum_ref[rows, LANES:]
        power = real * real + imag * imag
        power = power + pltpu.roll(power, 1, 0) + pltpu.roll(power, PATCH - 1, 0)
        smooth = jnp.dot(power.astype(jnp.bfloat16), ring, preferred_element_type=jnp.float32)
        gain = lax.rsqrt(lax.rsqrt(smooth * (1.0 / (9.0 * PATCH * PATCH)) + 1.0))
        pieces.append(jnp.concatenate([real * gain, imag * gain], axis=1).astype(jnp.bfloat16))
    shaped = jnp.concatenate(pieces, axis=0)
    range_back = jnp.dot(shaped, inverse, preferred_element_type=jnp.float32)
    range_back = range_back.astype(jnp.bfloat16)
    for chunk in range(chunks):
        totals = [[None] * (row_patches - 1) for _ in range(2)]
        for row in range(row_patches):
            top = (row * chunks + chunk) * PATCH
            block = range_back[top : top + PATCH]
            stacked = jnp.concatenate([block[:, :LANES], block[:, LANES:]], axis=0)
            patch_out = jnp.dot(back, stacked, preferred_element_type=jnp.float32) * window
            for part in range(2):
                upper = patch_out[part * PATCH : part * PATCH + HALF]
                lower = patch_out[part * PATCH + HALF : (part + 1) * PATCH]
                if row > 0:
                    totals[part][row - 1] = totals[part][row - 1] + upper
                if row < row_patches - 1:
                    totals[part][row] = lower
        for part in range(2):
            for row in range(row_patches - 1):
                top = part * lines + row * HALF
                filtered_ref[chunk, top : top + HALF] = totals[part][row]
    mids = width // LANES
    mid = jnp.concatenate([filtered_ref[i] for i in range(mids)], axis=1)
    moved = jnp.concatenate([filtered_ref[i] for i in range(mids, chunks)], axis=1)
    return mid + moved[:, HALF : HALF + width]


def own_kernel(table_ref, own_ref, out_ref, spectrum_ref, filtered_ref):
    lines = out_ref.shape[0] // 2
    out_ref[...] = filtered_of(own_ref, own_ref, table_ref, spectrum_ref, filtered_ref, lines)


def other_kernel(match_ref, table_ref, filtered_own_ref, own_ref, *refs):
    out_ref, spectrum_ref, filtered_ref = refs[-3:]
    match_count, _, _, lines, _ = out_ref.shape
    date = lax.axis_index("date")
    dates = match_ref.shape[1]

    def store(slot, result):
        for match in range(match_count):
            here = lax.rem(match_ref[match, date] - date + dates, dates) == slot

            @pl.when(here)
            def _():
                for part in range(2):
                    out_ref[match, part, 0] = result[part * lines : (part + 1) * lines]

    store(0, filtered_own_ref[...])
    for slot, other_ref in enumerate(refs[:-3], 1):
        store(slot, filtered_of(own_ref, other_ref, table_ref, spectrum_ref, filtered_ref, lines))


def all_tables(row_patches):
    forward = fourier_table(1.0, 1.0)
    inverse = fourier_table(-1.0, 1.0 / PATCH)
    back = inverse.reshape(2, PATCH, 2, PATCH).transpose(2, 3, 0, 1).reshape(2 * PATCH, 2 * PATCH)
    window = window_table()[:PATCH, :PATCH]
    splits = []
    for _ in range(3):
        splits.append(window.astype(jnp.bfloat16).astype(np.float32))
        window = window - splits[-1]
    rows = [
        line_table(forward, row_patches),
        paired(forward),
        paired(inverse),
        np.concatenate([back, ring_table()], axis=1),
        np.concatenate([*splits, np.zeros_like(window)], axis=1),
    ]
    return np.concatenate(rows, axis=0).astype(jnp.bfloat16)


def split_tables(table_ref, row_patches):
    at = row_patches * 2 * PATCH
    line_table_of = table_ref[:at, :]
    forward = table_ref[at : at + 4 * PATCH, :]
    at += 4 * PATCH
    inverse = table_ref[at : at + 4 * PATCH, :]
    at += 4 * PATCH
    back = table_ref[at : at + LANES, :LANES]
    ring = table_ref[at : at + LANES, LANES:]
    at += LANES
    splits = table_ref[at : at + PATCH, :].astype(jnp.float32)
    window = splits[:, :PATCH] + splits[:, PATCH : 2 * PATCH] + splits[:, 2 * PATCH : 3 * PATCH]
    window = jnp.concatenate([window, window], axis=1)
    window = jnp.concatenate([window, window], axis=0)
    return line_table_of, forward, inverse, back, ring, window


def per_device(image_stack, tap_weights, offsets, matchings):
    _, _, lines, width = image_stack.shape
    match_count = matchings.shape[0]
    wide = lines + 2 * HALF
    row_patches = lines // HALF + 1
    other = lax.ppermute(image_stack, "rg", [(0, 1), (1, 0)]).reshape(2, lines, width)
    image = image_stack.reshape(2, lines, width)
    taps = tap_weights.reshape(TAPS, lines)
    message = jax.ShapeDtypeStruct((2 * REACH + HALF, width), jnp.bfloat16)
    first, last = pl.pallas_call(
        pack_kernel,
        out_shape=(message, message),
        in_specs=[VMEM] * 4,
        out_specs=(VMEM, VMEM),
        compiler_params=PARAMS,
        name="pack",
    )(image, other, taps, offsets)
    peers = lax.axis_size("az")
    up = [(i, i + 1) for i in range(peers - 1)]
    down = [(j, i) for i, j in up]
    above = lax.ppermute(last, "az", up)
    below = lax.ppermute(first, "az", down)
    tile = pl.pallas_call(
        resample_kernel,
        out_shape=jax.ShapeDtypeStruct((2 * wide + wide // 4, width), jnp.bfloat16),
        in_specs=[VMEM] * 6,
        out_specs=VMEM,
        compiler_params=PARAMS,
        name="resample",
    )(image, other, taps, offsets, above, below)
    dates = lax.axis_size("date")
    others = [
        lax.ppermute(tile, "date", [((i + slot) % dates, i) for i in range(dates)])
        for slot in range(1, dates)
    ]
    chunks = (width + width + LANES) // LANES
    tables = jnp.asarray(all_tables(row_patches))
    scratch = [
        pltpu.VMEM((row_patches * chunks * PATCH, 2 * LANES), jnp.float32),
        pltpu.VMEM((chunks, 2 * lines, LANES), jnp.float32),
    ]
    filtered_own = pl.pallas_call(
        own_kernel,
        out_shape=jax.ShapeDtypeStruct((2 * lines, width), jnp.float32),
        in_specs=[VMEM] * 2,
        out_specs=VMEM,
        scratch_shapes=scratch,
        compiler_params=PARAMS,
        name="filter_own",
    )(tables, tile)
    return pl.pallas_call(
        other_kernel,
        out_shape=jax.ShapeDtypeStruct((match_count, 2, 1, lines, width), jnp.float32),
        in_specs=[SMEM] + [VMEM] * (3 + len(others)),
        out_specs=VMEM,
        scratch_shapes=scratch,
        compiler_params=PARAMS,
        name="filter_other",
    )(matchings, tables, filtered_own, tile, *others)


def solution(mesh):
    placed = (
        P(None, ("parts", "date"), "az", "rg"),
        P(None, ("parts", "date"), "az"),
        P(("parts", "date"), "az"),
        P(),
    )
    return jax.shard_map(
        per_device,
        mesh=mesh,
        in_specs=placed,
        out_specs=P(None, None, ("parts", "date"), "az", "rg"),
        check_vma=False,
    )
```

time: 26.8 us -> 25.5 us (0.951)
  local copies, waits for them, and re-layouts: 4.77 us -> 3.69 us
  waiting for transfers between devices: 7.68 us -> 8.23 us
  starting transfers between devices: 8.68 us -> 8.14 us
    unnamed x21 -> x15, local copies, waits for them, and re-layouts: 4.77 us -> 3.69 us
    ppermute x3 -> x2, waiting for transfers between devices: 2.9 us -> 3.37 us  [the longest x1 2.18 us: per_device(): lax.ppermute(tile, 'date', [((i + slot) % dates, i) for i in range(dates)])]
    ppermute x3 -> x2, starting transfers between devices: 2.21 us -> 2.01 us  [the longest x1 1.56 us: per_device(): lax.ppermute(tile, 'date', [((i + slot) % dates, i) for i in range(dates)])]
    pallas_call x2 -> x3, Pallas kernels: 5.12 us -> 4.97 us  [the longest x1 2.78 us: per_device(): pl.pallas_call(other_kernel, out_shape=jax.ShapeDtypeStruct((match_count,...]
  transfers between devices with their start and end apart: 5 -> 4, of which waited for: 4 -> 4; matrix products, arithmetic and copies ran while one was open for 0% -> 0% of each run, Pallas kernels for 0% -> 5%
where the time goes in v2:
time: 25.5 us; the launch traced here: 25.2 us
  waiting for transfers between devices  8.23 us (32%)
  starting transfers between devices  8.14 us (32%)
  Pallas kernels  5.12 us (20%)
  local copies, waits for them, and re-layouts  3.69 us (14%)
    ppermute x1, starting transfers between devices, per_device(): above = lax.ppermute(last, 'az', up)  4.84 us
    ppermute x1, waiting for transfers between devices, per_device(): below = lax.ppermute(first, 'az', down)  4.27 us
    unnamed x15, local copies, waits for them, and re-layouts  3.69 us
    pallas_call x1, Pallas kernels, per_device(): pl.pallas_call(other_kernel, out_shape=jax.ShapeDtypeStruct((match_count,...  2.78 us
    ppermute x1, waiting for transfers between devices, per_device(): lax.ppermute(tile, 'date', [((i + slot) % dates, i) for i in range(dates)])  2.18 us
    ppermute x1, starting transfers between devices, per_device(): lax.ppermute(tile, 'date', [((i + slot) % dates, i) for i in range(dates)])  1.56 us
    pallas_call x1, Pallas kernels, per_device(): pl.pallas_call(own_kernel, out_shape=jax.ShapeDtypeStruct((2 * lines, wid...  1.37 us
    ppermute x1, starting transfers between devices, per_device(): below = lax.ppermute(first, 'az', down)  1.29 us
  transfers between devices with their start and end apart: 4, of which 4 were waited for; matrix products, arithmetic and copies ran while one was open for 0% of the time, Pallas kernels for 5%

profile of v2, /device:TPU:0, one launch (start us, length us, event | category | flops | bytes accessed | tf_op | source)
XLA Modules:
  0.0 25.2 jit_solution(1370664214522309076)
XLA Ops:
  0.0 0.0 copy-start
  0.0 0.5 %collective-permute-start = (f32[2,1,64,256]{3,2,0,1:T(8,128)}, f32[2,1,64,256]{3,2,0,1:T(8,128)S(1)}, u32[]{:S(2)}, u32[]{:S(2)}) collective-permute-start(f32[2,1,64,256]{3,2,0,1:T(8,128)} %bitcast.4), channel_id=1, source_target_pairs={{0,1},{1,0},{2,3},{3,2},{4,5},{5,4},{6,7},{7,6},{8,9},{9,8},{10,11... | collective-permute-start | bytes 393224 | tf_op jit(solution)/shard_map/ppermute | solution.py:314
  0.5 1.2 %collective-permute-done = f32[2,1,64,256]{3,2,0,1:T(8,128)S(1)} collective-permute-done((f32[2,1,64,256]{3,2,0,1:T(8,128)}, f32[2,1,64,256]{3,2,0,1:T(8,128)S(1)}, u32[]{:S(2)}, u32[]{:S(2)}) %collective-permute-start) | collective-permute-done | bytes 131104 | tf_op jit(solution)/shard_map/ppermute | solution.py:314
  1.7 0.0 copy-start.1
  1.7 0.9 %copy-done.1 = f32[2,1,64,256]{3,2,1,0:T(8,128)S(1)} copy-done((f32[2,1,64,256]{3,2,1,0:T(8,128)S(1)}, f32[2,1,64,256]{3,2,1,0:T(8,128)}, u32[]{:S(2)}) %copy-start.1) | copy-done | bytes 131096
  2.6 0.0 copy-start.2
  2.6 0.7 %copy-done.2 = f32[8,1,64]{2,1,0:T(1,128)S(1)} copy-done((f32[8,1,64]{2,1,0:T(1,128)S(1)}, f32[8,1,64]{2,1,0:T(1,128)}, u32[]{:S(2)}) %copy-start.2) | copy-done | bytes 2072
  3.2 0.0 copy-start.4
  3.2 0.7 %copy-done.4 = s32[1,64]{1,0:T(1,128)S(1)} copy-done((s32[1,64]{1,0:T(1,128)S(1)}, s32[1,64]{1,0:T(1,128)}, u32[]{:S(2)}) %copy-start.4) | copy-done | bytes 280
  3.9 0.2 pack.1
  4.1 4.8 %collective-permute-start.1 = (bf16[128,256]{1,0:T(8,128)(2,1)S(1)}, bf16[128,256]{1,0:T(8,128)(2,1)S(1)}, u32[]{:S(2)}, u32[]{:S(2)}) collective-permute-start(bf16[128,256]{1,0:T(8,128)(2,1)S(1)} %get-tuple-element.7), channel_id=1, source_target_pairs={{0,4},{4,8},{8,12},{1,5},{5,9},{9,13},{2,6},{6,10},{10,14},{3,7},{... | collective-permute-start | bytes 196616 | tf_op jit(solution)/shard_map/ppermute | solution.py:329
  8.9 1.3 %collective-permute-start.2 = (bf16[128,256]{1,0:T(8,128)(2,1)S(1)}, bf16[128,256]{1,0:T(8,128)(2,1)S(1)}, u32[]{:S(2)}, u32[]{:S(2)}) collective-permute-start(bf16[128,256]{1,0:T(8,128)(2,1)S(1)} %get-tuple-element.8), channel_id=1, source_target_pairs={{4,0},{8,4},{12,8},{5,1},{9,5},{13,9},{6,2},{10,6},{14,10},{7,3},{... | collective-permute-start | bytes 196616 | tf_op jit(solution)/shard_map/ppermute | solution.py:330
  10.2 0.6 %collective-permute-done.1.above_ref = bf16[128,256]{1,0:T(8,128)(2,1)S(1)} collective-permute-done((bf16[128,256]{1,0:T(8,128)(2,1)S(1)}, bf16[128,256]{1,0:T(8,128)(2,1)S(1)}, u32[]{:S(2)}, u32[]{:S(2)}) %collective-permute-start.1) | collective-permute-done | bytes 65568 | tf_op jit(solution)/shard_map/ppermute | solution.py:329
  10.8 4.3 %collective-permute-done.2.below_ref = bf16[128,256]{1,0:T(8,128)(2,1)S(1)} collective-permute-done((bf16[128,256]{1,0:T(8,128)(2,1)S(1)}, bf16[128,256]{1,0:T(8,128)(2,1)S(1)}, u32[]{:S(2)}, u32[]{:S(2)}) %collective-permute-start.2) | collective-permute-done | bytes 65568 | tf_op jit(solution)/shard_map/ppermute | solution.py:330
  15.1 0.0 copy-start.3
  15.1 0.7 %copy-done.3 = f32[8,1,64]{2,1,0:T(1,128)S(1)} copy-done((f32[8,1,64]{2,1,0:T(1,128)S(1)}, f32[8,1,64]{2,1,0:T(1,128)}, u32[]{:S(2)}) %copy-start.3) | copy-done | bytes 2072
  15.8 0.0 copy-start.5
  15.8 0.7 %copy-done.5 = s32[1,64]{1,0:T(1,128)S(1)} copy-done((s32[1,64]{1,0:T(1,128)S(1)}, s32[1,64]{1,0:T(1,128)}, u32[]{:S(2)}) %copy-start.5) | copy-done | bytes 280
  16.4 0.0 copy-start.6
  16.4 0.8 %resample.1.own_ref = bf16[288,256]{1,0:T(8,128)(2,1)S(1)} custom-call(f32[2,64,256]{2,1,0:T(8,128)S(1)} %bitcast.6, f32[2,64,256]{2,1,0:T(8,128)S(1)} %bitcast.8, f32[8,64]{1,0:T(8,128)S(1)} %bitcast.10, s32[1,64]{1,0:T(1,128)S(1)} %copy-done.5, bf16[128,256]{1,0:T(8,128)(2,1)S(1)} %collective-permute-done.1.above_ref, ...), custom_call_target="tpu_custom_call" | custom-call | tf_op jit(solution)/shard_map/resample/pallas_call | solution.py:331
  17.2 1.6 %collective-permute-start.3 = (bf16[288,256]{1,0:T(8,128)(2,1)S(1)}, bf16[288,256]{1,0:T(8,128)(2,1)S(1)}, u32[]{:S(2)}, u32[]{:S(2)}) collective-permute-start(bf16[288,256]{1,0:T(8,128)(2,1)S(1)} %resample.1.own_ref), channel_id=1, source_target_pairs={{2,0},{0,2},{3,1},{1,3},{6,4},{4,6},{7,5},{5,7},{10,8},{8,10},{11,... | collective-permute-start | bytes 442376 | tf_op jit(solution)/shard_map/ppermute | solution.py:341
  18.8 0.0 copy-done.6
  18.8 0.1 copy.7.match_ref
  18.9 0.0 copy-done
  18.9 1.4 %filter_own.1.filtered_own_ref = f32[128,256]{1,0:T(8,128)S(1)} custom-call(bf16[1088,256]{1,0:T(8,128)(2,1)S(1)} %copy-done, bf16[288,256]{1,0:T(8,128)(2,1)S(1)} %resample.1.own_ref), custom_call_target="tpu_custom_call" | custom-call | tf_op jit(solution)/shard_map/filter_own/pallas_call | solution.py:350
  20.3 2.2 %collective-permute-done.3.refs_0_ = bf16[288,256]{1,0:T(8,128)(2,1)S(1)} collective-permute-done((bf16[288,256]{1,0:T(8,128)(2,1)S(1)}, bf16[288,256]{1,0:T(8,128)(2,1)S(1)}, u32[]{:S(2)}, u32[]{:S(2)}) %collective-permute-start.3) | collective-permute-done | bytes 147488 | tf_op jit(solution)/shard_map/ppermute | solution.py:341
  22.4 2.8 %filter_other.1 = f32[3,2,1,64,256]{4,3,2,1,0:T(8,128)} custom-call(s32[3,2]{1,0:T(4,128)S(1)} %copy.7.match_ref, bf16[1088,256]{1,0:T(8,128)(2,1)S(1)} %copy-done, f32[128,256]{1,0:T(8,128)S(1)} %filter_own.1.filtered_own_ref, bf16[288,256]{1,0:T(8,128)(2,1)S(1)} %resample.1.own_ref, bf16[288,256]{1,0:T(8,128)(2,1)S(1)} %collective-permute-done.3.refs_0_), custom_call_target="tpu_custom_call" | custom-call | tf_op jit(solution)/shard_map/filter_other/pallas_call | solution.py:359
Async XLA Ops:
  0.0 18.9 %copy-start = (bf16[1088,256]{1,0:T(8,128)(2,1)S(1)}, bf16[1088,256]{1,0:T(8,128)(2,1)}, u32[]{:S(2)}) copy-start(bf16[1088,256]{1,0:T(8,128)(2,1)} %constant.2.clone.table_ref) | copy-start | bytes 1671172
  0.0 1.6 %collective-permute-start = (f32[2,1,64,256]{3,2,0,1:T(8,128)}, f32[2,1,64,256]{3,2,0,1:T(8,128)S(1)}, u32[]{:S(2)}, u32[]{:S(2)}) collective-permute-start(f32[2,1,64,256]{3,2,0,1:T(8,128)} %bitcast.4), channel_id=1, source_target_pairs={{0,1},{1,0},{2,3},{3,2},{4,5},{5,4},{6,7},{7,6},{8,9},{9,8},{10,11... | collective-permute-start | bytes 393224 | tf_op jit(solution)/shard_map/ppermute | solution.py:314
  1.7 0.9 %copy-start.1 = (f32[2,1,64,256]{3,2,1,0:T(8,128)S(1)}, f32[2,1,64,256]{3,2,1,0:T(8,128)}, u32[]{:S(2)}) copy-start(f32[2,1,64,256]{3,2,1,0:T(8,128)} %param.5) | copy-start | bytes 393220
  2.6 0.7 %copy-start.2 = (f32[8,1,64]{2,1,0:T(1,128)S(1)}, f32[8,1,64]{2,1,0:T(1,128)}, u32[]{:S(2)}) copy-start(f32[8,1,64]{2,1,0:T(1,128)} %param.6) | copy-start | bytes 6148
  3.2 0.7 %copy-start.4 = (s32[1,64]{1,0:T(1,128)S(1)}, s32[1,64]{1,0:T(1,128)}, u32[]{:S(2)}) copy-start(s32[1,64]{1,0:T(1,128)} %offsets_ref.3) | copy-start | bytes 772
  4.1 6.7 %collective-permute-start.1 = (bf16[128,256]{1,0:T(8,128)(2,1)S(1)}, bf16[128,256]{1,0:T(8,128)(2,1)S(1)}, u32[]{:S(2)}, u32[]{:S(2)}) collective-permute-start(bf16[128,256]{1,0:T(8,128)(2,1)S(1)} %get-tuple-element.7), channel_id=1, source_target_pairs={{0,4},{4,8},{8,12},{1,5},{5,9},{9,13},{2,6},{6,10},{10,14},{3,7},{... | collective-permute-start | bytes 196616 | tf_op jit(solution)/shard_map/ppermute | solution.py:329
  8.9 6.2 %collective-permute-start.2 = (bf16[128,256]{1,0:T(8,128)(2,1)S(1)}, bf16[128,256]{1,0:T(8,128)(2,1)S(1)}, u32[]{:S(2)}, u32[]{:S(2)}) collective-permute-start(bf16[128,256]{1,0:T(8,128)(2,1)S(1)} %get-tuple-element.8), channel_id=1, source_target_pairs={{4,0},{8,4},{12,8},{5,1},{9,5},{13,9},{6,2},{10,6},{14,10},{7,3},{... | collective-permute-start | bytes 196616 | tf_op jit(solution)/shard_map/ppermute | solution.py:330
  15.1 0.7 %copy-start.3 = (f32[8,1,64]{2,1,0:T(1,128)S(1)}, f32[8,1,64]{2,1,0:T(1,128)}, u32[]{:S(2)}) copy-start(f32[8,1,64]{2,1,0:T(1,128)} %param.6) | copy-start | bytes 6148
  15.8 0.7 %copy-start.5 = (s32[1,64]{1,0:T(1,128)S(1)}, s32[1,64]{1,0:T(1,128)}, u32[]{:S(2)}) copy-start(s32[1,64]{1,0:T(1,128)} %offsets_ref.3) | copy-start | bytes 772
  16.4 2.4 %copy-start.6 = (s32[3,2]{0,1:T(2,128)S(1)}, s32[3,2]{0,1:T(2,128)}, u32[]{:S(2)}) copy-start(s32[3,2]{0,1:T(2,128)} %param.8) | copy-start | bytes 76
  17.2 5.2 %collective-permute-start.3 = (bf16[288,256]{1,0:T(8,128)(2,1)S(1)}, bf16[288,256]{1,0:T(8,128)(2,1)S(1)}, u32[]{:S(2)}, u32[]{:S(2)}) collective-permute-start(bf16[288,256]{1,0:T(8,128)(2,1)S(1)} %resample.1.own_ref), channel_id=1, source_target_pairs={{2,0},{0,2},{3,1},{1,3},{6,4},{4,6},{7,5},{5,7},{10,8},{8,10},{11,... | collective-permute-start | bytes 442376 | tf_op jit(solution)/shard_map/ppermute | solution.py:341

commit v3 on v2

--- a/solution.py
+++ b/solution.py
@@ -19,6 +19,7 @@
 
 VMEM = pl.BlockSpec(memory_space=pltpu.VMEM)
 SMEM = pl.BlockSpec(memory_space=pltpu.SMEM)
+HBM = pl.BlockSpec(memory_space=pltpu.HBM)
 PARAMS = pltpu.CompilerParams(vmem_limit_bytes=VMEM_LIMIT)
 
 
@@ -71,7 +72,18 @@
     )
 
 
-def pack_kernel(image_ref, other_ref, taps_ref, offsets_ref, first_ref, last_ref):
+def load_kernel(*refs):
+    count = (len(refs) - 1) // 2
+    copies = [
+        pltpu.make_async_copy(refs[i], refs[count + i], refs[-1].at[i]) for i in range(count)
+    ]
+    for copy in copies:
+        copy.start()
+    for copy in copies:
+        copy.wait()
+
+
+def pack_kernel(image_ref, other_ref, taps_ref, offsets_ref, even_ref, odd_ref):
     lines = image_ref.shape[1]
     width = image_ref.shape[2]
     side = lax.axis_index("rg")
@@ -94,20 +106,33 @@
         block = jnp.concatenate([block, *cuts, filler], axis=1)
         out_ref[2 * REACH :, :] = block.astype(jnp.bfloat16)
 
-    write(first_ref, 0, 0)
-    write(last_ref, lines - REACH, lines - HALF)
+    parity = lax.rem(lax.axis_index("az"), 2)
+
+    @pl.when(parity == 0)
+    def _():
+        write(even_ref, lines - REACH, lines - HALF)
+        write(odd_ref, 0, 0)
+
+    @pl.when(parity == 1)
+    def _():
+        write(even_ref, 0, 0)
+        write(odd_ref, lines - REACH, lines - HALF)
 
 
 def resample_kernel(
-    image_ref, other_ref, taps_ref, offsets_ref, above_ref, below_ref, tile_ref
+    image_ref, other_ref, taps_ref, offsets_ref, even_ref, odd_ref, tile_ref
 ):
     lines = image_ref.shape[1]
     width = image_ref.shape[2]
     wide = lines + 2 * HALF
     side = lax.axis_index("rg")
 
-    def unpacked(ref):
-        block = ref[2 * REACH :, :].astype(jnp.float32)
+    parity = lax.rem(lax.axis_index("az"), 2)
+    above = jnp.where(parity == 0, odd_ref[...], even_ref[...])
+    below = jnp.where(parity == 0, even_ref[...], odd_ref[...])
+
+    def unpacked(message):
+        block = message[2 * REACH :, :].astype(jnp.float32)
         head = block[:TAPS]
         edges = [block[:, i * HALF : (i + 1) * HALF] for i in range(3, 6)]
         return (
@@ -116,8 +141,8 @@
             jnp.concatenate(edges, axis=0),
         )
 
-    above_taps, above_shift, above_edge = unpacked(above_ref)
-    below_taps, below_shift, below_edge = unpacked(below_ref)
+    above_taps, above_shift, above_edge = unpacked(above)
+    below_taps, below_shift, below_edge = unpacked(below)
     taps = jnp.concatenate([above_taps, taps_ref[...], below_taps], axis=1)
     own_shift = offsets_ref[...].astype(jnp.float32)
     shift = jnp.concatenate([above_shift, own_shift, below_shift], axis=1).astype(jnp.int32)
@@ -151,7 +176,7 @@
             preferred_element_type=jnp.float32,
         )
         cut = slice(part * REACH, (part + 1) * REACH)
-        rim = jnp.concatenate([above_ref[cut, :], below_ref[cut, :]], axis=0)
+        rim = jnp.concatenate([above[cut, :], below[cut, :]], axis=0)
         rim_edge = jnp.concatenate([above_edge[cut], below_edge[cut]], axis=0).astype(jnp.bfloat16)
         rim = jnp.concatenate([rim, rim_edge], axis=1)
         rim = jnp.concatenate([rim, rim], axis=0)
@@ -251,23 +276,28 @@
 
 
 def other_kernel(match_ref, table_ref, filtered_own_ref, own_ref, *refs):
-    out_ref, spectrum_ref, filtered_ref = refs[-3:]
+    out_ref, result_ref, spectrum_ref, filtered_ref, sems = refs[-5:]
     match_count, _, _, lines, _ = out_ref.shape
     date = lax.axis_index("date")
     dates = match_ref.shape[1]
 
-    def store(slot, result):
-        for match in range(match_count):
-            here = lax.rem(match_ref[match, date] - date + dates, dates) == slot
-
-            @pl.when(here)
-            def _():
-                for part in range(2):
-                    out_ref[match, part, 0] = result[part * lines : (part + 1) * lines]
-
-    store(0, filtered_own_ref[...])
-    for slot, other_ref in enumerate(refs[:-3], 1):
-        store(slot, filtered_of(own_ref, other_ref, table_ref, spectrum_ref, filtered_ref, lines))
+    def keep(slot, result):
+        for part in range(2):
+            result_ref[slot, part] = result[part * lines : (part + 1) * lines]
+
+    keep(0, filtered_own_ref[...])
+    for slot, other_ref in enumerate(refs[:-5], 1):
+        keep(slot, filtered_of(own_ref, other_ref, table_ref, spectrum_ref, filtered_ref, lines))
+    copies = []
+    for match in range(match_count):
+        slot = lax.rem(match_ref[match, date] - date + dates, dates)
+        copies.append(
+            pltpu.make_async_copy(result_ref.at[slot], out_ref.at[match, :, 0], sems.at[match])
+        )
+    for copy in copies:
+        copy.start()
+    for copy in copies:
+        copy.wait()
 
 
 def all_tables(row_patches):
@@ -312,10 +342,23 @@
     wide = lines + 2 * HALF
     row_patches = lines // HALF + 1
     other = lax.ppermute(image_stack, "rg", [(0, 1), (1, 0)]).reshape(2, lines, width)
-    image = image_stack.reshape(2, lines, width)
-    taps = tap_weights.reshape(TAPS, lines)
+    arguments = (
+        image_stack.reshape(2, lines, width),
+        tap_weights.reshape(TAPS, lines),
+        offsets,
+    )
+    loaded = pl.pallas_call(
+        load_kernel,
+        out_shape=tuple(jax.ShapeDtypeStruct(a.shape, a.dtype) for a in arguments),
+        in_specs=[HBM] * 3,
+        out_specs=(VMEM,) * 3,
+        scratch_shapes=[pltpu.SemaphoreType.DMA((3,))],
+        compiler_params=PARAMS,
+        name="load",
+    )(*arguments)
+    image, taps, offsets = loaded
     message = jax.ShapeDtypeStruct((2 * REACH + HALF, width), jnp.bfloat16)
-    first, last = pl.pallas_call(
+    even, odd = pl.pallas_call(
         pack_kernel,
         out_shape=(message, message),
         in_specs=[VMEM] * 4,
@@ -324,10 +367,12 @@
         name="pack",
     )(image, other, taps, offsets)
     peers = lax.axis_size("az")
-    up = [(i, i + 1) for i in range(peers - 1)]
-    down = [(j, i) for i, j in up]
-    above = lax.ppermute(last, "az", up)
-    below = lax.ppermute(first, "az", down)
+
+    def swapped(value, start):
+        pairs = [(i, i + 1) for i in range(start, peers - 1, 2)]
+        return lax.ppermute(value, "az", pairs + [(j, i) for i, j in pairs])
+
+    even, odd = swapped(even, 0), swapped(odd, 1)
     tile = pl.pallas_call(
         resample_kernel,
         out_shape=jax.ShapeDtypeStruct((2 * wide + wide // 4, width), jnp.bfloat16),
@@ -335,7 +380,7 @@
         out_specs=VMEM,
         compiler_params=PARAMS,
         name="resample",
-    )(image, other, taps, offsets, above, below)
+    )(image, other, taps, offsets, even, odd)
     dates = lax.axis_size("date")
     others = [
         lax.ppermute(tile, "date", [((i + slot) % dates, i) for i in range(dates)])
@@ -360,8 +405,12 @@
         other_kernel,
         out_shape=jax.ShapeDtypeStruct((match_count, 2, 1, lines, width), jnp.float32),
         in_specs=[SMEM] + [VMEM] * (3 + len(others)),
-        out_specs=VMEM,
-        scratch_shapes=scratch,
+        out_specs=HBM,
+        scratch_shapes=[
+            pltpu.VMEM((dates, 2, lines, width), jnp.float32),
+            *scratch,
+            pltpu.SemaphoreType.DMA((match_count,)),
+        ],
         compiler_params=PARAMS,
         name="filter_other",
     )(matchings, tables, filtered_own, tile, *others)

time: 25.5 us -> 19.6 us (0.77)
  the two profiles are of different devices: /device:TPU:0 before, /device:TPU:8 now
where the time goes in v3:
time: 19.6 us; the launch traced here: 19.4 us
  starting transfers between devices  6.79 us (35%)
  Pallas kernels  5.27 us (27%)
  waiting for transfers between devices  4.85 us (25%)
  local copies, waits for them, and re-layouts  2.4 us (12%)
    ppermute x2, starting transfers between devices, swapped(): return lax.ppermute(value, 'az', pairs + [(j, i) for i, j in pairs])  5.23 us
    pallas_call x1, Pallas kernels, per_device(): pl.pallas_call(other_kernel, out_shape=jax.ShapeDtypeStruct((match_count,...  2.73 us
    ppermute x1, waiting for transfers between devices, per_device(): lax.ppermute(tile, 'date', [((i + slot) % dates, i) for i in range(dates)])  2.45 us
    unnamed x11, local copies, waits for them, and re-layouts  2.4 us
    ppermute x2, waiting for transfers between devices, swapped(): return lax.ppermute(value, 'az', pairs + [(j, i) for i, j in pairs])  2.4 us
    ppermute x1, starting transfers between devices, per_device(): lax.ppermute(tile, 'date', [((i + slot) % dates, i) for i in range(dates)])  1.56 us
    pallas_call x1, Pallas kernels, per_device(): pl.pallas_call(own_kernel, out_shape=jax.ShapeDtypeStruct((2 * lines, wid...  1.37 us
    pallas_call x1, Pallas kernels, per_device(): pl.pallas_call(resample_kernel, out_shape=jax.ShapeDtypeStruct((2 * wide...  0.82 us
  transfers between devices with their start and end apart: 4, of which 2 were waited for; matrix products, arithmetic and copies ran while one was open for 0% of the time, Pallas kernels for 8%

profile of v3, /device:TPU:8, one launch (start us, length us, event | category | flops | bytes accessed | tf_op | source)
XLA Modules:
  0.0 19.4 jit_solution(12591909790877775147)
XLA Ops:
  0.0 0.0 copy-start
  0.0 0.0 collective-permute-start
  0.0 0.0 copy-start.1
  0.0 1.0 %copy-done.1 = f32[2,1,64,256]{3,2,1,0:T(8,128)S(1)} copy-done((f32[2,1,64,256]{3,2,1,0:T(8,128)S(1)}, f32[2,1,64,256]{3,2,1,0:T(8,128)}, u32[]{:S(2)}) %copy-start.1) | copy-done | bytes 131096
  1.0 0.0 copy-start.2
  1.0 0.7 %copy-done.2 = f32[8,1,64]{2,1,0:T(1,128)S(1)} copy-done((f32[8,1,64]{2,1,0:T(1,128)S(1)}, f32[8,1,64]{2,1,0:T(1,128)}, u32[]{:S(2)}) %copy-start.2) | copy-done | bytes 2072
  1.7 0.0 copy-start.3
  1.7 0.7 %copy-done.3 = s32[1,64]{1,0:T(1,128)S(1)} copy-done((s32[1,64]{1,0:T(1,128)S(1)}, s32[1,64]{1,0:T(1,128)}, u32[]{:S(2)}) %copy-start.3) | copy-done | bytes 280
  2.3 0.2 load.1
  2.5 0.0 collective-permute-done
  2.5 0.2 pack.1
  2.7 0.1 collective-permute-start.1
  2.8 0.0 copy-start.4
  2.8 5.2 %collective-permute-start.2 = (bf16[128,256]{1,0:T(8,128)(2,1)S(1)}, bf16[128,256]{1,0:T(8,128)(2,1)S(1)}, u32[]{:S(2)}, u32[]{:S(2)}) collective-permute-start(bf16[128,256]{1,0:T(8,128)(2,1)S(1)} %get-tuple-element.14), channel_id=1, source_target_pairs={{4,8},{8,4},{5,9},{9,5},{6,10},{10,6},{7,11},{11,7},{20,24},{24,20... | collective-permute-start | bytes 196616 | tf_op jit(solution)/shard_map/ppermute | solution.py:373
  7.9 0.0 collective-permute-done.1.even_ref
  7.9 2.4 %collective-permute-done.2.odd_ref = bf16[128,256]{1,0:T(8,128)(2,1)S(1)} collective-permute-done((bf16[128,256]{1,0:T(8,128)(2,1)S(1)}, bf16[128,256]{1,0:T(8,128)(2,1)S(1)}, u32[]{:S(2)}, u32[]{:S(2)}) %collective-permute-start.2) | collective-permute-done | bytes 65568 | tf_op jit(solution)/shard_map/ppermute | solution.py:373
  10.3 0.8 %resample.1.own_ref = bf16[288,256]{1,0:T(8,128)(2,1)S(1)} custom-call(f32[2,64,256]{2,1,0:T(8,128)S(1)} %get-tuple-element.10.image_ref, f32[2,64,256]{2,1,0:T(8,128)S(1)} %bitcast.5, f32[8,64]{1,0:T(8,128)S(1)} %get-tuple-element.11.taps_ref, s32[1,64]{1,0:T(1,128)S(1)} %get-tuple-element.12.offsets_ref, ...), custom_call_target="tpu_custom_call" | custom-call | tf_op jit(solution)/shard_map/resample/pallas_call | solution.py:376
  11.2 1.6 %collective-permute-start.3 = (bf16[288,256]{1,0:T(8,128)(2,1)S(1)}, bf16[288,256]{1,0:T(8,128)(2,1)S(1)}, u32[]{:S(2)}, u32[]{:S(2)}) collective-permute-start(bf16[288,256]{1,0:T(8,128)(2,1)S(1)} %resample.1.own_ref), channel_id=1, source_target_pairs={{2,0},{0,2},{3,1},{1,3},{6,4},{4,6},{7,5},{5,7},{10,8},{8,10},{11,... | collective-permute-start | bytes 442376 | tf_op jit(solution)/shard_map/ppermute | solution.py:386
  12.7 0.0 copy-done.4
  12.7 0.1 copy.7.match_ref
  12.8 0.0 copy-done
  12.8 1.4 %filter_own.1.filtered_own_ref = f32[128,256]{1,0:T(8,128)S(1)} custom-call(bf16[1088,256]{1,0:T(8,128)(2,1)S(1)} %copy-done, bf16[288,256]{1,0:T(8,128)(2,1)S(1)} %resample.1.own_ref), custom_call_target="tpu_custom_call" | custom-call | tf_op jit(solution)/shard_map/filter_own/pallas_call | solution.py:395
  14.2 2.4 %collective-permute-done.3.refs_0_ = bf16[288,256]{1,0:T(8,128)(2,1)S(1)} collective-permute-done((bf16[288,256]{1,0:T(8,128)(2,1)S(1)}, bf16[288,256]{1,0:T(8,128)(2,1)S(1)}, u32[]{:S(2)}, u32[]{:S(2)}) %collective-permute-start.3) | collective-permute-done | bytes 147488 | tf_op jit(solution)/shard_map/ppermute | solution.py:386
  16.6 2.7 %filter_other.1 = f32[3,2,1,64,256]{4,3,2,1,0:T(8,128)} custom-call(s32[3,2]{1,0:T(4,128)S(1)} %copy.7.match_ref, bf16[1088,256]{1,0:T(8,128)(2,1)S(1)} %copy-done, f32[128,256]{1,0:T(8,128)S(1)} %filter_own.1.filtered_own_ref, bf16[288,256]{1,0:T(8,128)(2,1)S(1)} %resample.1.own_ref, bf16[288,256]{1,0:T(8,128)(2,1)S(1)} %collective-permute-done.3.refs_0_), custom_call_target="tpu_custom_call" | custom-call | tf_op jit(solution)/shard_map/filter_other/pallas_call | solution.py:404
Async XLA Ops:
  0.0 12.8 %copy-start = (bf16[1088,256]{1,0:T(8,128)(2,1)S(1)}, bf16[1088,256]{1,0:T(8,128)(2,1)}, u32[]{:S(2)}) copy-start(bf16[1088,256]{1,0:T(8,128)(2,1)} %constant.2.clone.table_ref) | copy-start | bytes 1671172
  0.0 2.5 %collective-permute-start = (f32[2,1,64,256]{3,2,0,1:T(8,128)}, f32[2,1,64,256]{3,2,0,1:T(8,128)S(1)}, u32[]{:S(2)}, u32[]{:S(2)}) collective-permute-start(f32[2,1,64,256]{3,2,0,1:T(8,128)} %bitcast.6), channel_id=1, source_target_pairs={{0,1},{1,0},{2,3},{3,2},{4,5},{5,4},{6,7},{7,6},{8,9},{9,8},{10,11... | collective-permute-start | bytes 393224 | tf_op jit(solution)/shard_map/ppermute | solution.py:344
  0.0 1.0 %copy-start.1 = (f32[2,1,64,256]{3,2,1,0:T(8,128)S(1)}, f32[2,1,64,256]{3,2,1,0:T(8,128)}, u32[]{:S(2)}) copy-start(f32[2,1,64,256]{3,2,1,0:T(8,128)} %param.5) | copy-start | bytes 393220
  1.0 0.7 %copy-start.2 = (f32[8,1,64]{2,1,0:T(1,128)S(1)}, f32[8,1,64]{2,1,0:T(1,128)}, u32[]{:S(2)}) copy-start(f32[8,1,64]{2,1,0:T(1,128)} %param.6) | copy-start | bytes 6148
  1.7 0.7 %copy-start.3 = (s32[1,64]{1,0:T(1,128)S(1)}, s32[1,64]{1,0:T(1,128)}, u32[]{:S(2)}) copy-start(s32[1,64]{1,0:T(1,128)} %refs_2_.1) | copy-start | bytes 772
  2.7 5.3 %collective-permute-start.1 = (bf16[128,256]{1,0:T(8,128)(2,1)S(1)}, bf16[128,256]{1,0:T(8,128)(2,1)S(1)}, u32[]{:S(2)}, u32[]{:S(2)}) collective-permute-start(bf16[128,256]{1,0:T(8,128)(2,1)S(1)} %get-tuple-element.13), channel_id=1, source_target_pairs={{0,4},{8,12},{4,0},{12,8},{1,5},{9,13},{5,1},{13,9},{2,6},{10,14},... | collective-permute-start | bytes 196616 | tf_op jit(solution)/shard_map/ppermute | solution.py:373
  2.8 10.0 %copy-start.4 = (s32[3,2]{0,1:T(2,128)S(1)}, s32[3,2]{0,1:T(2,128)}, u32[]{:S(2)}) copy-start(s32[3,2]{0,1:T(2,128)} %param.8) | copy-start | bytes 76
  2.8 7.6 %collective-permute-start.2 = (bf16[128,256]{1,0:T(8,128)(2,1)S(1)}, bf16[128,256]{1,0:T(8,128)(2,1)S(1)}, u32[]{:S(2)}, u32[]{:S(2)}) collective-permute-start(bf16[128,256]{1,0:T(8,128)(2,1)S(1)} %get-tuple-element.14), channel_id=1, source_target_pairs={{4,8},{8,4},{5,9},{9,5},{6,10},{10,6},{7,11},{11,7},{20,24},{24,20... | collective-permute-start | bytes 196616 | tf_op jit(solution)/shard_map/ppermute | solution.py:373
  11.2 5.5 %collective-permute-start.3 = (bf16[288,256]{1,0:T(8,128)(2,1)S(1)}, bf16[288,256]{1,0:T(8,128)(2,1)S(1)}, u32[]{:S(2)}, u32[]{:S(2)}) collective-permute-start(bf16[288,256]{1,0:T(8,128)(2,1)S(1)} %resample.1.own_ref), channel_id=1, source_target_pairs={{2,0},{0,2},{3,1},{1,3},{6,4},{4,6},{7,5},{5,7},{10,8},{8,10},{11,... | collective-permute-start | bytes 442376 | tf_op jit(solution)/shard_map/ppermute | solution.py:386

commit v4 on v3

--- a/solution.py
+++ b/solution.py
@@ -65,126 +65,125 @@
     return ring
 
 
-def edge_of(other_ref, part, side, lines):
-    width = other_ref.shape[2]
-    return jnp.where(
-        side == 0, other_ref[part, lines, :HALF], other_ref[part, lines, width - HALF :]
-    )
-
-
-def load_kernel(*refs):
-    count = (len(refs) - 1) // 2
-    copies = [
-        pltpu.make_async_copy(refs[i], refs[count + i], refs[-1].at[i]) for i in range(count)
-    ]
-    for copy in copies:
-        copy.start()
-    for copy in copies:
-        copy.wait()
-
-
-def pack_kernel(image_ref, other_ref, taps_ref, offsets_ref, even_ref, odd_ref):
+def load_kernel(image_ref, kernel_ref, image_out, kernel_out):
+    image_out[...] = image_ref[...]
+    kernel_out[...] = kernel_ref[...]
+
+
+def faces_below():
+    return lax.rem(lax.axis_index("az") + lax.axis_index("rg"), 2) == 0
+
+
+def all_samples(image_ref, other_ref, part, lines):
+    mine = image_ref[part, lines, :]
+    other = other_ref[part, lines, :]
+    side = lax.axis_index("rg")
+    left = jnp.where(side == 0, mine, other)
+    right = jnp.where(side == 0, other, mine)
+    return jnp.concatenate([left, right], axis=1)
+
+
+def pack_kernel(image_ref, other_ref, kernel_ref, out_ref):
+    lines = image_ref.shape[1]
+    samples = 2 * image_ref.shape[2]
+    below = faces_below()
+    taps = kernel_ref[:TAPS, :]
+    shifts = jnp.broadcast_to(kernel_ref[TAPS : TAPS + 1, :], taps.shape)
+    taps_high = taps.astype(jnp.bfloat16).astype(jnp.float32)
+    taps_low = taps - taps_high
+
+    def write(line_start, tap_start):
+        for part in range(2):
+            rows = all_samples(image_ref, other_ref, part, slice(line_start, line_start + REACH))
+            out_ref[part * REACH : (part + 1) * REACH, :] = rows.astype(jnp.bfloat16)
+        cut = slice(tap_start, tap_start + HALF)
+        filler = jnp.zeros((TAPS, samples - 3 * HALF), jnp.float32)
+        block = jnp.concatenate([taps_high[:, cut], taps_low[:, cut], shifts[:, cut], filler], axis=1)
+        block = jnp.concatenate([block, jnp.zeros_like(block)], axis=0)
+        out_ref[2 * REACH :, :] = block.astype(jnp.bfloat16)
+
+    @pl.when(below)
+    def _():
+        write(lines - REACH, lines - HALF)
+
+    @pl.when(jnp.logical_not(below))
+    def _():
+        write(0, 0)
+
+
+def resample_kernel(image_ref, other_ref, kernel_ref, message_ref, keep_ref, send_ref):
     lines = image_ref.shape[1]
     width = image_ref.shape[2]
+    half = lines // 2 + HALF
+    below = faces_below()
     side = lax.axis_index("rg")
-    taps = taps_ref[...]
-    taps_high = taps.astype(jnp.bfloat16).astype(jnp.float32)
-    taps_low = taps - taps_high
-    shifts = jnp.broadcast_to(offsets_ref[...].astype(jnp.float32), (TAPS, lines))
-
-    def write(out_ref, line_start, tap_start):
-        rows = slice(line_start, line_start + REACH)
-        for part in range(2):
-            cut = slice(part * REACH, (part + 1) * REACH)
-            out_ref[cut, :] = image_ref[part, rows, :].astype(jnp.bfloat16)
-        edges = jnp.concatenate([edge_of(other_ref, part, side, rows) for part in range(2)], axis=0)
-        cut = slice(tap_start, tap_start + HALF)
-        block = jnp.concatenate([taps_high[:, cut], taps_low[:, cut], shifts[:, cut]], axis=1)
-        block = jnp.concatenate([block, jnp.zeros((HALF - TAPS, 3 * HALF), jnp.float32)], axis=0)
-        cuts = [edges[i * HALF : (i + 1) * HALF] for i in range(3)]
-        filler = jnp.zeros((HALF, width - 6 * HALF), jnp.float32)
-        block = jnp.concatenate([block, *cuts, filler], axis=1)
-        out_ref[2 * REACH :, :] = block.astype(jnp.bfloat16)
-
-    parity = lax.rem(lax.axis_index("az"), 2)
-
-    @pl.when(parity == 0)
-    def _():
-        write(even_ref, lines - REACH, lines - HALF)
-        write(odd_ref, 0, 0)
-
-    @pl.when(parity == 1)
-    def _():
-        write(even_ref, 0, 0)
-        write(odd_ref, lines - REACH, lines - HALF)
-
-
-def resample_kernel(
-    image_ref, other_ref, taps_ref, offsets_ref, even_ref, odd_ref, tile_ref
-):
-    lines = image_ref.shape[1]
-    width = image_ref.shape[2]
-    wide = lines + 2 * HALF
-    side = lax.axis_index("rg")
-
-    parity = lax.rem(lax.axis_index("az"), 2)
-    above = jnp.where(parity == 0, odd_ref[...], even_ref[...])
-    below = jnp.where(parity == 0, even_ref[...], odd_ref[...])
-
-    def unpacked(message):
-        block = message[2 * REACH :, :].astype(jnp.float32)
-        head = block[:TAPS]
-        edges = [block[:, i * HALF : (i + 1) * HALF] for i in range(3, 6)]
-        return (
-            head[:, :HALF] + head[:, HALF : 2 * HALF],
-            head[:1, 2 * HALF : 3 * HALF],
-            jnp.concatenate(edges, axis=0),
-        )
-
-    above_taps, above_shift, above_edge = unpacked(above)
-    below_taps, below_shift, below_edge = unpacked(below)
-    taps = jnp.concatenate([above_taps, taps_ref[...], below_taps], axis=1)
-    own_shift = offsets_ref[...].astype(jnp.float32)
-    shift = jnp.concatenate([above_shift, own_shift, below_shift], axis=1).astype(jnp.int32)
-
-    def band(source_lines):
-        count = source_lines.shape[0]
-        place = lax.broadcasted_iota(jnp.int32, (count, wide), 1) - HALF
-        tap_ids = source_lines - place - shift + (TAPS // 2 - 1)
-        total = jnp.zeros((count, wide), jnp.float32)
+    head = message_ref[2 * REACH :, :LANES].astype(jnp.float32)[:TAPS]
+    rim_taps = head[:, :HALF] + head[:, HALF : 2 * HALF]
+    rim_shift = head[:1, 2 * HALF : 3 * HALF]
+
+    def per_line(own, rim):
+        lower = jnp.concatenate([own[:, lines - (half - HALF) :], rim], axis=1)
+        upper = jnp.concatenate([rim, own[:, : half - HALF]], axis=1)
+        return jnp.where(below, lower, upper)
+
+    taps = per_line(kernel_ref[:TAPS, :], rim_taps)
+    shift = per_line(kernel_ref[TAPS : TAPS + 1, :], rim_shift).astype(jnp.int32)
+    first_line = jnp.where(below, lines + HALF - half, -HALF)
+    first_rim = jnp.where(below, lines, -REACH)
+
+    def band(count, first_source):
+        source = lax.broadcasted_iota(jnp.int32, (count, half), 0) + first_source
+        place = lax.broadcasted_iota(jnp.int32, (count, half), 1) + first_line
+        tap_ids = source - place - shift + (TAPS // 2 - 1)
+        total = jnp.zeros((count, half), jnp.float32)
         for tap in range(TAPS):
             total = jnp.where(tap_ids == tap, taps[tap : tap + 1, :], total)
         return total
 
-    own_ids = lax.broadcasted_iota(jnp.int32, (lines, wide), 0)
-    rim_ids = lax.broadcasted_iota(jnp.int32, (2 * REACH, wide), 0)
-    rim_ids = jnp.where(rim_ids < REACH, rim_ids - REACH, rim_ids - REACH + lines)
-    own_band = band(own_ids)
-    rim_band = band(rim_ids)
+    own_band = band(lines, 0)
+    rim_band = band(REACH, first_rim)
     rim_high = rim_band.astype(jnp.bfloat16)
     rim_low = (rim_band - rim_high.astype(jnp.float32)).astype(jnp.bfloat16)
     rim_both = jnp.concatenate([rim_high, rim_low], axis=0)
     over_rows = (((0,), (0,)), ((), ()))
-    edges = []
+    mine, others = [], []
     for part in range(2):
-        edge = edge_of(other_ref, part, side, slice(0, lines))
         own = lax.dot_general(
             own_band,
-            jnp.concatenate([image_ref[part], edge], axis=1),
+            all_samples(image_ref, other_ref, part, slice(0, lines)),
             over_rows,
             precision=lax.Precision.HIGHEST,
             preferred_element_type=jnp.float32,
         )
-        cut = slice(part * REACH, (part + 1) * REACH)
-        rim = jnp.concatenate([above[cut, :], below[cut, :]], axis=0)
-        rim_edge = jnp.concatenate([above_edge[cut], below_edge[cut]], axis=0).astype(jnp.bfloat16)
-        rim = jnp.concatenate([rim, rim_edge], axis=1)
+        rim = message_ref[part * REACH : (part + 1) * REACH, :]
         rim = jnp.concatenate([rim, rim], axis=0)
         total = own + lax.dot_general(rim_both, rim, over_rows, preferred_element_type=jnp.float32)
-        tile_ref[part * wide : (part + 1) * wide, :] = total[:, :width].astype(jnp.bfloat16)
-        rows = wide // 4
-        edges += [total[i * rows : (i + 1) * rows, width:] for i in range(4)]
-    tile_ref[2 * wide :, :] = jnp.concatenate(edges, axis=1).astype(jnp.bfloat16)
+        left, right = total[:, :width], total[:, width:]
+        left_edge, right_edge = right[:, :HALF], left[:, width - HALF :]
+        mine.append((jnp.where(side == 0, left, right), jnp.where(side == 0, left_edge, right_edge)))
+        others.append((jnp.where(side == 0, right, left), jnp.where(side == 0, right_edge, left_edge)))
+    rows = half // 4
+    for out_ref, parts in ((keep_ref, mine), (send_ref, others)):
+        edges = []
+        for part, (tile, edge) in enumerate(parts):
+            out_ref[part * half : (part + 1) * half, :] = tile.astype(jnp.bfloat16)
+            edges += [edge[i * rows : (i + 1) * rows] for i in range(4)]
+        out_ref[2 * half :, :] = jnp.concatenate(edges, axis=1).astype(jnp.bfloat16)
+
+
+def join_kernel(mine_ref, other_ref, tile_ref):
+    rows = mine_ref.shape[0]
+    below = faces_below()
+
+    @pl.when(below)
+    def _():
+        tile_ref[:rows, :] = other_ref[...]
+        tile_ref[rows:, :] = mine_ref[...]
+
+    @pl.when(jnp.logical_not(below))
+    def _():
+        tile_ref[:rows, :] = mine_ref[...]
+        tile_ref[rows:, :] = other_ref[...]
 
 
 def cross(own_parts, other_parts):
@@ -196,12 +195,20 @@
 
 
 def tile_parts(tile_ref, wide):
-    tile = tile_ref[: 2 * wide, :].astype(jnp.float32)
-    edge = tile_ref[2 * wide :, :].astype(jnp.float32)
-    cuts = [edge[:, i * HALF : (i + 1) * HALF] for i in range(8)]
-    edge_real = jnp.concatenate(cuts[:4], axis=0)
-    edge_imag = jnp.concatenate(cuts[4:], axis=0)
-    return (tile[:wide], tile[wide:]), (edge_real, edge_imag)
+    half = wide // 2
+    step = tile_ref.shape[0] // 2
+    parts, edges = [], []
+    for part in range(2):
+        tops = [at * step + part * half for at in range(2)]
+        pieces = [tile_ref[top : top + half, :].astype(jnp.float32) for top in tops]
+        parts.append(jnp.concatenate(pieces, axis=0))
+        pieces = []
+        for at in range(2):
+            block = tile_ref[at * step + 2 * half : (at + 1) * step, :].astype(jnp.float32)
+            for i in range(4 * part, 4 * part + 4):
+                pieces.append(block[:, i * HALF : (i + 1) * HALF])
+        edges.append(jnp.concatenate(pieces, axis=0))
+    return parts, edges
 
 
 def filtered_of(own_ref, other_ref, table_ref, spectrum_ref, filtered_ref, lines):
@@ -342,45 +349,54 @@
     wide = lines + 2 * HALF
     row_patches = lines // HALF + 1
     other = lax.ppermute(image_stack, "rg", [(0, 1), (1, 0)]).reshape(2, lines, width)
-    arguments = (
-        image_stack.reshape(2, lines, width),
-        tap_weights.reshape(TAPS, lines),
-        offsets,
+    image = image_stack.reshape(2, lines, width)
+    kernel = jnp.concatenate(
+        [
+            tap_weights.reshape(TAPS, lines),
+            offsets.astype(jnp.float32),
+            jnp.zeros((TAPS - 1, lines), jnp.float32),
+        ],
+        axis=0,
     )
-    loaded = pl.pallas_call(
+    image, kernel = pl.pallas_call(
         load_kernel,
-        out_shape=tuple(jax.ShapeDtypeStruct(a.shape, a.dtype) for a in arguments),
-        in_specs=[HBM] * 3,
-        out_specs=(VMEM,) * 3,
-        scratch_shapes=[pltpu.SemaphoreType.DMA((3,))],
+        out_shape=tuple(jax.ShapeDtypeStruct(a.shape, a.dtype) for a in (image, kernel)),
+        in_specs=[VMEM] * 2,
+        out_specs=(VMEM,) * 2,
         compiler_params=PARAMS,
         name="load",
-    )(*arguments)
-    image, taps, offsets = loaded
-    message = jax.ShapeDtypeStruct((2 * REACH + HALF, width), jnp.bfloat16)
-    even, odd = pl.pallas_call(
+    )(image, kernel)
+    message = pl.pallas_call(
         pack_kernel,
-        out_shape=(message, message),
+        out_shape=jax.ShapeDtypeStruct((2 * REACH + 2 * TAPS, 2 * width), jnp.bfloat16),
+        in_specs=[VMEM] * 3,
+        out_specs=VMEM,
+        compiler_params=PARAMS,
+        name="pack",
+    )(image, other, kernel)
+    peers = lax.axis_size("az")
+    pairs = [
+        (2 * i + core, 2 * (i + 1) + core) for core in range(2) for i in range(core, peers - 1, 2)
+    ]
+    message = lax.ppermute(message, ("az", "rg"), pairs + [(j, i) for i, j in pairs])
+    half = jax.ShapeDtypeStruct((wide + wide // 8, width), jnp.bfloat16)
+    mine, theirs = pl.pallas_call(
+        resample_kernel,
+        out_shape=(half, half),
         in_specs=[VMEM] * 4,
         out_specs=(VMEM, VMEM),
         compiler_params=PARAMS,
-        name="pack",
-    )(image, other, taps, offsets)
-    peers = lax.axis_size("az")
-
-    def swapped(value, start):
-        pairs = [(i, i + 1) for i in range(start, peers - 1, 2)]
-        return lax.ppermute(value, "az", pairs + [(j, i) for i, j in pairs])
-
-    even, odd = swapped(even, 0), swapped(odd, 1)
+        name="resample",
+    )(image, other, kernel, message)
+    theirs = lax.ppermute(theirs, "rg", [(0, 1), (1, 0)])
     tile = pl.pallas_call(
-        resample_kernel,
-        out_shape=jax.ShapeDtypeStruct((2 * wide + wide // 4, width), jnp.bfloat16),
-        in_specs=[VMEM] * 6,
+        join_kernel,
+        out_shape=jax.ShapeDtypeStruct((2 * half.shape[0], width), jnp.bfloat16),
+        in_specs=[VMEM] * 2,
         out_specs=VMEM,
         compiler_params=PARAMS,
-        name="resample",
-    )(image, other, taps, offsets, even, odd)
+        name="join",
+    )(mine, theirs)
     dates = lax.axis_size("date")
     others = [
         lax.ppermute(tile, "date", [((i + slot) % dates, i) for i in range(dates)])

time: 19.6 us -> 20.8 us (1.061)
  the two profiles are of different devices: /device:TPU:8 before, /device:TPU:0 now
where the time goes in v4:
time: 20.8 us; the launch traced here: 20.6 us
  starting transfers between devices  7.56 us (36%)
  waiting for transfers between devices  6.7 us (32%)
  Pallas kernels  4.94 us (24%)
  local copies, waits for them, and re-layouts  1.29 us (6%)
    ppermute x1, starting transfers between devices, per_device(): lax.ppermute(message, ('az', 'rg'), pairs + [(j, i) for i, j in pairs])  5.06 us
    ppermute x1, waiting for transfers between devices, per_device(): lax.ppermute(message, ('az', 'rg'), pairs + [(j, i) for i, j in pairs])  2.76 us
    pallas_call x1, Pallas kernels, per_device(): pl.pallas_call(other_kernel, out_shape=jax.ShapeDtypeStruct((match_count,...  2.73 us
    ppermute x1, waiting for transfers between devices, per_device(): lax.ppermute(tile, 'date', [((i + slot) % dates, i) for i in range(dates)])  2.69 us
    ppermute x1, starting transfers between devices, per_device(): lax.ppermute(tile, 'date', [((i + slot) % dates, i) for i in range(dates)])  1.99 us
    pallas_call x1, Pallas kernels, per_device(): pl.pallas_call(own_kernel, out_shape=jax.ShapeDtypeStruct((2 * lines, wid...  1.37 us
    ppermute x1, waiting for transfers between devices, per_device(): theirs = lax.ppermute(theirs, 'rg', [(0, 1), (1, 0)])  1.25 us
    unnamed x11, local copies, waits for them, and re-layouts  1.21 us
  transfers between devices with their start and end apart: 4, of which 3 were waited for; matrix products, arithmetic and copies ran while one was open for 1% of the time, Pallas kernels for 7%

profile of v4, /device:TPU:0, one launch (start us, length us, event | category | flops | bytes accessed | tf_op | source)
XLA Modules:
  0.0 20.6 jit_solution(3617011918300148422)
XLA Ops:
  0.0 0.0 copy-start.4
  0.0 0.0 copy-start.2
  0.0 0.5 %collective-permute-start = (f32[2,1,64,256]{3,2,0,1:T(8,128)}, f32[2,1,64,256]{3,2,0,1:T(8,128)S(1)}, u32[]{:S(2)}, u32[]{:S(2)}) collective-permute-start(f32[2,1,64,256]{3,2,0,1:T(8,128)} %bitcast.6), channel_id=1, source_target_pairs={{0,1},{1,0},{2,3},{3,2},{4,5},{5,4},{6,7},{7,6},{8,9},{9,8},{10,11... | collective-permute-start | bytes 393224 | tf_op jit(solution)/shard_map/ppermute | solution.py:351
  0.5 0.2 copy-done.4
  0.7 0.1 pad.2.clone
  0.7 0.0 copy-done.2
  0.7 0.1 maximum_maximum_fusion.kernel_ref
  0.8 0.0 copy-start.1
  0.8 0.9 %copy-done.1 = f32[2,1,64,256]{3,2,1,0:T(8,128)S(1)} copy-done((f32[2,1,64,256]{3,2,1,0:T(8,128)S(1)}, f32[2,1,64,256]{3,2,1,0:T(8,128)}, u32[]{:S(2)}) %copy-start.1) | copy-done | bytes 131096
  1.7 0.0 copy-start
  1.7 0.0 collective-permute-done
  1.8 0.1 pack.1
  1.8 5.1 %collective-permute-start.1 = (bf16[112,512]{1,0:T(8,128)(2,1)S(1)}, bf16[112,512]{1,0:T(8,128)(2,1)S(1)}, u32[]{:S(2)}, u32[]{:S(2)}) collective-permute-start(bf16[112,512]{1,0:T(8,128)(2,1)S(1)} %pack.1), channel_id=1, source_target_pairs={{0,4},{8,12},{5,9},{4,0},{12,8},{9,5},{2,6},{10,14},{7,11},{6,2},{... | collective-permute-start | bytes 344072 | tf_op jit(solution)/shard_map/ppermute | solution.py:381
  6.9 2.8 %collective-permute-done.1.message_ref = bf16[112,512]{1,0:T(8,128)(2,1)S(1)} collective-permute-done((bf16[112,512]{1,0:T(8,128)(2,1)S(1)}, bf16[112,512]{1,0:T(8,128)(2,1)S(1)}, u32[]{:S(2)}, u32[]{:S(2)}) %collective-permute-start.1) | collective-permute-done | bytes 114720 | tf_op jit(solution)/shard_map/ppermute | solution.py:381
  9.7 0.7 %resample.1 = (bf16[144,256]{1,0:T(8,128)(2,1)S(1)}, bf16[144,256]{1,0:T(8,128)(2,1)S(1)}) custom-call(f32[2,64,256]{2,1,0:T(8,128)S(1)} %get-tuple-element.9.image_ref, f32[2,64,256]{2,1,0:T(8,128)S(1)} %bitcast.5, f32[16,64]{1,0:T(8,128)S(1)} %get-tuple-element.10.kernel_ref, bf16[112,512]{1,0:T(8,128)(2,1)S(1)} %collective-permute-done.1.message_ref), custom_call_target="tpu_custom_call" | custom-call | tf_op jit(solution)/shard_map/resample/pallas_call | solution.py:383
  10.4 0.1 collective-permute-start.2
  10.5 1.3 %collective-permute-done.2.other_ref = bf16[144,256]{1,0:T(8,128)(2,1)S(1)} collective-permute-done((bf16[144,256]{1,0:T(8,128)(2,1)S(1)}, bf16[144,256]{1,0:T(8,128)(2,1)S(1)}, u32[]{:S(2)}, u32[]{:S(2)}) %collective-permute-start.2) | collective-permute-done | bytes 73760 | tf_op jit(solution)/shard_map/ppermute | solution.py:391
  11.7 0.0 copy-start.3
  11.7 2.0 %collective-permute-start.3 = (bf16[288,256]{1,0:T(8,128)(2,1)S(1)}, bf16[288,256]{1,0:T(8,128)(2,1)S(1)}, u32[]{:S(2)}, u32[]{:S(2)}) collective-permute-start(bf16[288,256]{1,0:T(8,128)(2,1)S(1)} %join.1.own_ref), channel_id=1, source_target_pairs={{2,0},{0,2},{3,1},{1,3},{6,4},{4,6},{7,5},{5,7},{10,8},{8,10},{11,... | collective-permute-start | bytes 442376 | tf_op jit(solution)/shard_map/ppermute | solution.py:402
  13.7 0.0 copy-done.3
  13.7 0.1 copy.7.match_ref
  13.8 0.0 copy-done
  13.8 1.4 %filter_own.1.filtered_own_ref = f32[128,256]{1,0:T(8,128)S(1)} custom-call(bf16[1088,256]{1,0:T(8,128)(2,1)S(1)} %copy-done, bf16[288,256]{1,0:T(8,128)(2,1)S(1)} %join.1.own_ref), custom_call_target="tpu_custom_call" | custom-call | tf_op jit(solution)/shard_map/filter_own/pallas_call | solution.py:411
  15.2 2.7 %collective-permute-done.3.refs_0_ = bf16[288,256]{1,0:T(8,128)(2,1)S(1)} collective-permute-done((bf16[288,256]{1,0:T(8,128)(2,1)S(1)}, bf16[288,256]{1,0:T(8,128)(2,1)S(1)}, u32[]{:S(2)}, u32[]{:S(2)}) %collective-permute-start.3) | collective-permute-done | bytes 147488 | tf_op jit(solution)/shard_map/ppermute | solution.py:402
  17.9 2.7 %filter_other.1 = f32[3,2,1,64,256]{4,3,2,1,0:T(8,128)} custom-call(s32[3,2]{1,0:T(4,128)S(1)} %copy.7.match_ref, bf16[1088,256]{1,0:T(8,128)(2,1)S(1)} %copy-done, f32[128,256]{1,0:T(8,128)S(1)} %filter_own.1.filtered_own_ref, bf16[288,256]{1,0:T(8,128)(2,1)S(1)} %join.1.own_ref, bf16[288,256]{1,0:T(8,128)(2,1)S(1)} %collective-permute-done.3.refs_0_), custom_call_target="tpu_custom_call" | custom-call | tf_op jit(solution)/shard_map/filter_other/pallas_call | solution.py:420
  (4 shorter events, 0.0 us)
Async XLA Ops:
  0.0 0.7 %copy-start.4 = (s32[1,64]{1,0:T(1,128)S(1)}, s32[1,64]{1,0:T(1,128)}, u32[]{:S(2)}) copy-start(s32[1,64]{1,0:T(1,128)} %param.7) | copy-start | bytes 772
  0.0 0.7 %copy-start.2 = (f32[8,1,64]{2,1,0:T(1,128)S(1)}, f32[8,1,64]{2,1,0:T(1,128)}, u32[]{:S(2)}) copy-start(f32[8,1,64]{2,1,0:T(1,128)} %param.6) | copy-start | bytes 6148
  0.0 1.7 %collective-permute-start = (f32[2,1,64,256]{3,2,0,1:T(8,128)}, f32[2,1,64,256]{3,2,0,1:T(8,128)S(1)}, u32[]{:S(2)}, u32[]{:S(2)}) collective-permute-start(f32[2,1,64,256]{3,2,0,1:T(8,128)} %bitcast.6), channel_id=1, source_target_pairs={{0,1},{1,0},{2,3},{3,2},{4,5},{5,4},{6,7},{7,6},{8,9},{9,8},{10,11... | collective-permute-start | bytes 393224 | tf_op jit(solution)/shard_map/ppermute | solution.py:351
  0.8 0.9 %copy-start.1 = (f32[2,1,64,256]{3,2,1,0:T(8,128)S(1)}, f32[2,1,64,256]{3,2,1,0:T(8,128)}, u32[]{:S(2)}) copy-start(f32[2,1,64,256]{3,2,1,0:T(8,128)} %param.5) | copy-start | bytes 393220
  1.7 12.1 %copy-start = (bf16[1088,256]{1,0:T(8,128)(2,1)S(1)}, bf16[1088,256]{1,0:T(8,128)(2,1)}, u32[]{:S(2)}) copy-start(bf16[1088,256]{1,0:T(8,128)(2,1)} %constant.4.clone.table_ref) | copy-start | bytes 1671172
  1.8 7.8 %collective-permute-start.1 = (bf16[112,512]{1,0:T(8,128)(2,1)S(1)}, bf16[112,512]{1,0:T(8,128)(2,1)S(1)}, u32[]{:S(2)}, u32[]{:S(2)}) collective-permute-start(bf16[112,512]{1,0:T(8,128)(2,1)S(1)} %pack.1), channel_id=1, source_target_pairs={{0,4},{8,12},{5,9},{4,0},{12,8},{9,5},{2,6},{10,14},{7,11},{6,2},{... | collective-permute-start | bytes 344072 | tf_op jit(solution)/shard_map/ppermute | solution.py:381
  10.4 1.3 %collective-permute-start.2 = (bf16[144,256]{1,0:T(8,128)(2,1)S(1)}, bf16[144,256]{1,0:T(8,128)(2,1)S(1)}, u32[]{:S(2)}, u32[]{:S(2)}) collective-permute-start(bf16[144,256]{1,0:T(8,128)(2,1)S(1)} %get-tuple-element.12), channel_id=1, source_target_pairs={{0,1},{1,0},{2,3},{3,2},{4,5},{5,4},{6,7},{7,6},{8,9},{9,8},{10,11... | collective-permute-start | bytes 221192 | tf_op jit(solution)/shard_map/ppermute | solution.py:391
  11.7 2.0 %copy-start.3 = (s32[3,2]{0,1:T(2,128)S(1)}, s32[3,2]{0,1:T(2,128)}, u32[]{:S(2)}) copy-start(s32[3,2]{0,1:T(2,128)} %param.8) | copy-start | bytes 76
  11.7 6.2 %collective-permute-start.3 = (bf16[288,256]{1,0:T(8,128)(2,1)S(1)}, bf16[288,256]{1,0:T(8,128)(2,1)S(1)}, u32[]{:S(2)}, u32[]{:S(2)}) collective-permute-start(bf16[288,256]{1,0:T(8,128)(2,1)S(1)} %join.1.own_ref), channel_id=1, source_target_pairs={{2,0},{0,2},{3,1},{1,3},{6,4},{4,6},{7,5},{5,7},{10,8},{8,10},{11,... | collective-permute-start | bytes 442376 | tf_op jit(solution)/shard_map/ppermute | solution.py:402

commit v5 on v3

--- a/solution.py
+++ b/solution.py
@@ -72,25 +72,19 @@
     )
 
 
-def load_kernel(*refs):
-    count = (len(refs) - 1) // 2
-    copies = [
-        pltpu.make_async_copy(refs[i], refs[count + i], refs[-1].at[i]) for i in range(count)
-    ]
-    for copy in copies:
-        copy.start()
-    for copy in copies:
-        copy.wait()
-
-
-def pack_kernel(image_ref, other_ref, taps_ref, offsets_ref, even_ref, odd_ref):
+def load_kernel(image_ref, kernel_ref, image_out, kernel_out):
+    image_out[...] = image_ref[...]
+    kernel_out[...] = kernel_ref[...]
+
+
+def pack_kernel(image_ref, other_ref, kernel_ref, even_ref, odd_ref):
     lines = image_ref.shape[1]
     width = image_ref.shape[2]
     side = lax.axis_index("rg")
-    taps = taps_ref[...]
+    taps = kernel_ref[:TAPS, :]
     taps_high = taps.astype(jnp.bfloat16).astype(jnp.float32)
     taps_low = taps - taps_high
-    shifts = jnp.broadcast_to(offsets_ref[...].astype(jnp.float32), (TAPS, lines))
+    shifts = jnp.broadcast_to(kernel_ref[TAPS : TAPS + 1, :], (TAPS, lines))
 
     def write(out_ref, line_start, tap_start):
         rows = slice(line_start, line_start + REACH)
@@ -119,17 +113,18 @@
         write(odd_ref, lines - REACH, lines - HALF)
 
 
-def resample_kernel(
-    image_ref, other_ref, taps_ref, offsets_ref, even_ref, odd_ref, tile_ref
-):
+def resample_kernel(image_ref, other_ref, kernel_ref, even_ref, odd_ref, tile_ref):
     lines = image_ref.shape[1]
     width = image_ref.shape[2]
     wide = lines + 2 * HALF
     side = lax.axis_index("rg")
 
-    parity = lax.rem(lax.axis_index("az"), 2)
+    place = lax.axis_index("az")
+    parity = lax.rem(place, 2)
     above = jnp.where(parity == 0, odd_ref[...], even_ref[...])
     below = jnp.where(parity == 0, even_ref[...], odd_ref[...])
+    above = jnp.where(place == 0, jnp.zeros_like(above), above)
+    below = jnp.where(place == lax.axis_size("az") - 1, jnp.zeros_like(below), below)
 
     def unpacked(message):
         block = message[2 * REACH :, :].astype(jnp.float32)
@@ -143,8 +138,8 @@
 
     above_taps, above_shift, above_edge = unpacked(above)
     below_taps, below_shift, below_edge = unpacked(below)
-    taps = jnp.concatenate([above_taps, taps_ref[...], below_taps], axis=1)
-    own_shift = offsets_ref[...].astype(jnp.float32)
+    taps = jnp.concatenate([above_taps, kernel_ref[:TAPS, :], below_taps], axis=1)
+    own_shift = kernel_ref[TAPS : TAPS + 1, :]
     shift = jnp.concatenate([above_shift, own_shift, below_shift], axis=1).astype(jnp.int32)
 
     def band(source_lines):
@@ -342,45 +337,49 @@
     wide = lines + 2 * HALF
     row_patches = lines // HALF + 1
     other = lax.ppermute(image_stack, "rg", [(0, 1), (1, 0)]).reshape(2, lines, width)
-    arguments = (
-        image_stack.reshape(2, lines, width),
-        tap_weights.reshape(TAPS, lines),
-        offsets,
+    image = image_stack.reshape(2, lines, width)
+    kernel = jnp.concatenate(
+        [
+            tap_weights.reshape(TAPS, lines),
+            offsets.astype(jnp.float32),
+            jnp.zeros((TAPS - 1, lines), jnp.float32),
+        ],
+        axis=0,
     )
-    loaded = pl.pallas_call(
+    image, kernel = pl.pallas_call(
         load_kernel,
-        out_shape=tuple(jax.ShapeDtypeStruct(a.shape, a.dtype) for a in arguments),
-        in_specs=[HBM] * 3,
-        out_specs=(VMEM,) * 3,
-        scratch_shapes=[pltpu.SemaphoreType.DMA((3,))],
+        out_shape=tuple(jax.ShapeDtypeStruct(a.shape, a.dtype) for a in (image, kernel)),
+        in_specs=[VMEM] * 2,
+        out_specs=(VMEM,) * 2,
         compiler_params=PARAMS,
         name="load",
-    )(*arguments)
-    image, taps, offsets = loaded
+    )(image, kernel)
     message = jax.ShapeDtypeStruct((2 * REACH + HALF, width), jnp.bfloat16)
     even, odd = pl.pallas_call(
         pack_kernel,
         out_shape=(message, message),
-        in_specs=[VMEM] * 4,
+        in_specs=[VMEM] * 3,
         out_specs=(VMEM, VMEM),
         compiler_params=PARAMS,
         name="pack",
-    )(image, other, taps, offsets)
+    )(image, other, kernel)
     peers = lax.axis_size("az")
 
     def swapped(value, start):
         pairs = [(i, i + 1) for i in range(start, peers - 1, 2)]
-        return lax.ppermute(value, "az", pairs + [(j, i) for i, j in pairs])
+        paired_up = {i for pair in pairs for i in pair}
+        alone = [(i, i) for i in range(peers) if i not in paired_up]
+        return lax.ppermute(value, "az", pairs + [(j, i) for i, j in pairs] + alone)
 
     even, odd = swapped(even, 0), swapped(odd, 1)
     tile = pl.pallas_call(
         resample_kernel,
         out_shape=jax.ShapeDtypeStruct((2 * wide + wide // 4, width), jnp.bfloat16),
-        in_specs=[VMEM] * 6,
+        in_specs=[VMEM] * 5,
         out_specs=VMEM,
         compiler_params=PARAMS,
         name="resample",
-    )(image, other, taps, offsets, even, odd)
+    )(image, other, kernel, even, odd)
     dates = lax.axis_size("date")
     others = [
         lax.ppermute(tile, "date", [((i + slot) % dates, i) for i in range(dates)])

time: 19.6 us -> 19.6 us (level)
  the two profiles are of different devices: /device:TPU:8 before, /device:TPU:10 now
where the time goes in v5:
time: 19.6 us; the launch traced here: 19.4 us
  starting transfers between devices  5.85 us (30%)
  waiting for transfers between devices  5.81 us (30%)
  Pallas kernels  5.11 us (26%)
  other arithmetic  1.48 us (8%)
  local copies, waits for them, and re-layouts  1.08 us (6%)
    ppermute x2, starting transfers between devices, swapped(): return lax.ppermute(value, 'az', pairs + [(j, i) for i, j in pairs] + alone)  5.25 us
    ppermute x1, waiting for transfers between devices, per_device(): lax.ppermute(tile, 'date', [((i + slot) % dates, i) for i in range(dates)])  3.41 us
    pallas_call x1, Pallas kernels, per_device(): pl.pallas_call(other_kernel, out_shape=jax.ShapeDtypeStruct((match_count,...  2.73 us
    ppermute x2, waiting for transfers between devices, swapped(): return lax.ppermute(value, 'az', pairs + [(j, i) for i, j in pairs] + alone)  2.4 us
    pallas_call x1, Pallas kernels, per_device(): pl.pallas_call(own_kernel, out_shape=jax.ShapeDtypeStruct((2 * lines, wid...  1.37 us
    unnamed x7, local copies, waits for them, and re-layouts  1 us
    pallas_call x1, Pallas kernels, per_device(): pl.pallas_call(resample_kernel, out_shape=jax.ShapeDtypeStruct((2 * wide...  0.82 us
    concatenate x1, other arithmetic, per_device(): jnp.concatenate([tap_weights.reshape(TAPS, lines), offsets.astype(jnp.flo...  0.76 us
  transfers between devices with their start and end apart: 4, of which 2 were waited for; matrix products, arithmetic and copies ran while one was open for 8% of the time, Pallas kernels for 7%

profile of v5, /device:TPU:10, one launch (start us, length us, event | category | flops | bytes accessed | tf_op | source)
XLA Modules:
  0.0 19.4 jit_solution(5506305763656865201)
XLA Ops:
  0.0 0.0 copy-start
  0.0 0.0 collective-permute-start
  0.0 0.7 %convert_element_type.3 = f32[1,64]{1,0:T(1,128)S(1)} convert(s32[1,64]{1,0:T(1,128)} %param.7) | non-fusion elementwise | flops 64 | bytes 512 | tf_op jit(solution)/shard_map/convert_element_type | solution.py:344
  0.7 0.1 pad.2.clone
  0.8 0.8 %maximum_maximum_fusion.kernel_ref = f32[16,64]{1,0:T(8,128)S(1)} fusion(f32[1,64]{1,0:T(1,128)S(1)} %convert_element_type.3, f32[8,64]{1,0:T(8,128)} %bitcast.8, f32[16]{0:T(128)S(1)} %pad.2.clone), kind=kLoop, calls=%fused_computation | loop fusion | flops 2048 | bytes 6464 | tf_op jit(solution)/shard_map/concatenate | solution.py:341
  1.6 0.0 copy-start.1
  1.6 0.9 %copy-done.1 = f32[2,1,64,256]{3,2,1,0:T(8,128)S(1)} copy-done((f32[2,1,64,256]{3,2,1,0:T(8,128)S(1)}, f32[2,1,64,256]{3,2,1,0:T(8,128)}, u32[]{:S(2)}) %copy-start.1) | copy-done | bytes 131096
  2.5 0.0 collective-permute-done
  2.5 0.2 pack.1
  2.7 0.5 %collective-permute-start.1 = (bf16[128,256]{1,0:T(8,128)(2,1)S(1)}, bf16[128,256]{1,0:T(8,128)(2,1)S(1)}, u32[]{:S(2)}, u32[]{:S(2)}) collective-permute-start(bf16[128,256]{1,0:T(8,128)(2,1)S(1)} %get-tuple-element.11), channel_id=1, source_target_pairs={{0,4},{8,12},{4,0},{12,8},{1,5},{9,13},{5,1},{13,9},{2,6},{10,14},... | collective-permute-start | bytes 196616 | tf_op jit(solution)/shard_map/ppermute | solution.py:372
  3.2 0.0 copy-start.2
  3.2 4.7 %collective-permute-start.2 = (bf16[128,256]{1,0:T(8,128)(2,1)S(1)}, bf16[128,256]{1,0:T(8,128)(2,1)S(1)}, u32[]{:S(2)}, u32[]{:S(2)}) collective-permute-start(bf16[128,256]{1,0:T(8,128)(2,1)S(1)} %get-tuple-element.12), channel_id=1, source_target_pairs={{4,8},{8,4},{0,0},{12,12},{5,9},{9,5},{1,1},{13,13},{6,10},{10,6},... | collective-permute-start | bytes 196616 | tf_op jit(solution)/shard_map/ppermute | solution.py:372
  7.9 0.0 collective-permute-done.1.even_ref
  7.9 2.4 %collective-permute-done.2.odd_ref = bf16[128,256]{1,0:T(8,128)(2,1)S(1)} collective-permute-done((bf16[128,256]{1,0:T(8,128)(2,1)S(1)}, bf16[128,256]{1,0:T(8,128)(2,1)S(1)}, u32[]{:S(2)}, u32[]{:S(2)}) %collective-permute-start.2) | collective-permute-done | bytes 65568 | tf_op jit(solution)/shard_map/ppermute | solution.py:372
  10.3 0.8 %resample.1.own_ref = bf16[288,256]{1,0:T(8,128)(2,1)S(1)} custom-call(f32[2,64,256]{2,1,0:T(8,128)S(1)} %get-tuple-element.9.image_ref, f32[2,64,256]{2,1,0:T(8,128)S(1)} %bitcast.5, f32[16,64]{1,0:T(8,128)S(1)} %get-tuple-element.10.kernel_ref, bf16[128,256]{1,0:T(8,128)(2,1)S(1)} %collective-permute-done.1.even_ref, ...), custom_call_target="tpu_custom_call" | custom-call | tf_op jit(solution)/shard_map/resample/pallas_call | solution.py:375
  11.2 0.6 %collective-permute-start.3 = (bf16[288,256]{1,0:T(8,128)(2,1)S(1)}, bf16[288,256]{1,0:T(8,128)(2,1)S(1)}, u32[]{:S(2)}, u32[]{:S(2)}) collective-permute-start(bf16[288,256]{1,0:T(8,128)(2,1)S(1)} %resample.1.own_ref), channel_id=1, source_target_pairs={{2,0},{0,2},{3,1},{1,3},{6,4},{4,6},{7,5},{5,7},{10,8},{8,10},{11,... | collective-permute-start | bytes 442376 | tf_op jit(solution)/shard_map/ppermute | solution.py:385
  11.8 0.0 copy-done.2
  11.8 0.1 copy.7.match_ref
  11.9 0.0 copy-done
  11.9 1.4 %filter_own.1.filtered_own_ref = f32[128,256]{1,0:T(8,128)S(1)} custom-call(bf16[1088,256]{1,0:T(8,128)(2,1)S(1)} %copy-done, bf16[288,256]{1,0:T(8,128)(2,1)S(1)} %resample.1.own_ref), custom_call_target="tpu_custom_call" | custom-call | tf_op jit(solution)/shard_map/filter_own/pallas_call | solution.py:394
  13.2 3.4 %collective-permute-done.3.refs_0_ = bf16[288,256]{1,0:T(8,128)(2,1)S(1)} collective-permute-done((bf16[288,256]{1,0:T(8,128)(2,1)S(1)}, bf16[288,256]{1,0:T(8,128)(2,1)S(1)}, u32[]{:S(2)}, u32[]{:S(2)}) %collective-permute-start.3) | collective-permute-done | bytes 147488 | tf_op jit(solution)/shard_map/ppermute | solution.py:385
  16.6 2.7 %filter_other.1 = f32[3,2,1,64,256]{4,3,2,1,0:T(8,128)} custom-call(s32[3,2]{1,0:T(4,128)S(1)} %copy.7.match_ref, bf16[1088,256]{1,0:T(8,128)(2,1)S(1)} %copy-done, f32[128,256]{1,0:T(8,128)S(1)} %filter_own.1.filtered_own_ref, bf16[288,256]{1,0:T(8,128)(2,1)S(1)} %resample.1.own_ref, bf16[288,256]{1,0:T(8,128)(2,1)S(1)} %collective-permute-done.3.refs_0_), custom_call_target="tpu_custom_call" | custom-call | tf_op jit(solution)/shard_map/filter_other/pallas_call | solution.py:403
  (2 shorter events, 0.0 us)
Async XLA Ops:
  0.0 11.9 %copy-start = (bf16[1088,256]{1,0:T(8,128)(2,1)S(1)}, bf16[1088,256]{1,0:T(8,128)(2,1)}, u32[]{:S(2)}) copy-start(bf16[1088,256]{1,0:T(8,128)(2,1)} %constant.4.clone.table_ref) | copy-start | bytes 1671172
  0.0 2.5 %collective-permute-start = (f32[2,1,64,256]{3,2,0,1:T(8,128)}, f32[2,1,64,256]{3,2,0,1:T(8,128)S(1)}, u32[]{:S(2)}, u32[]{:S(2)}) collective-permute-start(f32[2,1,64,256]{3,2,0,1:T(8,128)} %bitcast.6), channel_id=1, source_target_pairs={{0,1},{1,0},{2,3},{3,2},{4,5},{5,4},{6,7},{7,6},{8,9},{9,8},{10,11... | collective-permute-start | bytes 393224 | tf_op jit(solution)/shard_map/ppermute | solution.py:339
  1.6 0.9 %copy-start.1 = (f32[2,1,64,256]{3,2,1,0:T(8,128)S(1)}, f32[2,1,64,256]{3,2,1,0:T(8,128)}, u32[]{:S(2)}) copy-start(f32[2,1,64,256]{3,2,1,0:T(8,128)} %param.5) | copy-start | bytes 393220
  2.7 5.3 %collective-permute-start.1 = (bf16[128,256]{1,0:T(8,128)(2,1)S(1)}, bf16[128,256]{1,0:T(8,128)(2,1)S(1)}, u32[]{:S(2)}, u32[]{:S(2)}) collective-permute-start(bf16[128,256]{1,0:T(8,128)(2,1)S(1)} %get-tuple-element.11), channel_id=1, source_target_pairs={{0,4},{8,12},{4,0},{12,8},{1,5},{9,13},{5,1},{13,9},{2,6},{10,14},... | collective-permute-start | bytes 196616 | tf_op jit(solution)/shard_map/ppermute | solution.py:372
  3.2 8.6 %copy-start.2 = (s32[3,2]{0,1:T(2,128)S(1)}, s32[3,2]{0,1:T(2,128)}, u32[]{:S(2)}) copy-start(s32[3,2]{0,1:T(2,128)} %param.8) | copy-start | bytes 76
  3.2 7.1 %collective-permute-start.2 = (bf16[128,256]{1,0:T(8,128)(2,1)S(1)}, bf16[128,256]{1,0:T(8,128)(2,1)S(1)}, u32[]{:S(2)}, u32[]{:S(2)}) collective-permute-start(bf16[128,256]{1,0:T(8,128)(2,1)S(1)} %get-tuple-element.12), channel_id=1, source_target_pairs={{4,8},{8,4},{0,0},{12,12},{5,9},{9,5},{1,1},{13,13},{6,10},{10,6},... | collective-permute-start | bytes 196616 | tf_op jit(solution)/shard_map/ppermute | solution.py:372
  11.2 5.5 %collective-permute-start.3 = (bf16[288,256]{1,0:T(8,128)(2,1)S(1)}, bf16[288,256]{1,0:T(8,128)(2,1)S(1)}, u32[]{:S(2)}, u32[]{:S(2)}) collective-permute-start(bf16[288,256]{1,0:T(8,128)(2,1)S(1)} %resample.1.own_ref), channel_id=1, source_target_pairs={{2,0},{0,2},{3,1},{1,3},{6,4},{4,6},{7,5},{5,7},{10,8},{8,10},{11,... | collective-permute-start | bytes 442376 | tf_op jit(solution)/shard_map/ppermute | solution.py:385

commit v6 on v3

--- a/solution.py
+++ b/solution.py
@@ -127,9 +127,12 @@
     wide = lines + 2 * HALF
     side = lax.axis_index("rg")
 
-    parity = lax.rem(lax.axis_index("az"), 2)
+    place = lax.axis_index("az")
+    parity = lax.rem(place, 2)
     above = jnp.where(parity == 0, odd_ref[...], even_ref[...])
     below = jnp.where(parity == 0, even_ref[...], odd_ref[...])
+    above = jnp.where(place == 0, jnp.zeros_like(above), above)
+    below = jnp.where(place == lax.axis_size("az") - 1, jnp.zeros_like(below), below)
 
     def unpacked(message):
         block = message[2 * REACH :, :].astype(jnp.float32)
@@ -347,16 +350,15 @@
         tap_weights.reshape(TAPS, lines),
         offsets,
     )
-    loaded = pl.pallas_call(
+    image, taps, offsets = pl.pallas_call(
         load_kernel,
-        out_shape=tuple(jax.ShapeDtypeStruct(a.shape, a.dtype) for a in arguments),
+        out_shape=tuple(pltpu.VMEM(a.shape, a.dtype) for a in arguments),
         in_specs=[HBM] * 3,
         out_specs=(VMEM,) * 3,
         scratch_shapes=[pltpu.SemaphoreType.DMA((3,))],
         compiler_params=PARAMS,
         name="load",
-    )(*arguments)
-    image, taps, offsets = loaded
+    )(*(pltpu.with_memory_space_constraint(a, pltpu.HBM) for a in arguments))
     message = jax.ShapeDtypeStruct((2 * REACH + HALF, width), jnp.bfloat16)
     even, odd = pl.pallas_call(
         pack_kernel,
@@ -369,7 +371,7 @@
     peers = lax.axis_size("az")
 
     def swapped(value, start):
-        pairs = [(i, i + 1) for i in range(start, peers - 1, 2)]
+        pairs = [(i, (i + 1) % peers) for i in range(start, peers, 2)]
         return lax.ppermute(value, "az", pairs + [(j, i) for i, j in pairs])
 
     even, odd = swapped(even, 0), swapped(odd, 1)

time: 19.6 us -> 19.9 us (1.015)
  the two profiles are of different devices: /device:TPU:8 before, /device:TPU:0 now
where the time goes in v6:
time: 19.9 us; the launch traced here: 19.8 us
  starting transfers between devices  7.48 us (38%)
  waiting for transfers between devices  6.17 us (31%)
  Pallas kernels  6.01 us (30%)
    ppermute x2, starting transfers between devices, swapped(): return lax.ppermute(value, 'az', pairs + [(j, i) for i, j in pairs])  5.47 us
    ppermute x2, waiting for transfers between devices, swapped(): return lax.ppermute(value, 'az', pairs + [(j, i) for i, j in pairs])  3.74 us
    pallas_call x1, Pallas kernels, per_device(): pl.pallas_call(other_kernel, out_shape=jax.ShapeDtypeStruct((match_count,...  2.73 us
    ppermute x1, waiting for transfers between devices, per_device(): lax.ppermute(tile, 'date', [((i + slot) % dates, i) for i in range(dates)])  2.17 us
    ppermute x1, starting transfers between devices, per_device(): lax.ppermute(tile, 'date', [((i + slot) % dates, i) for i in range(dates)])  1.56 us
    pallas_call x1, Pallas kernels, per_device(): pl.pallas_call(own_kernel, out_shape=jax.ShapeDtypeStruct((2 * lines, wid...  1.37 us
    pallas_call x1, Pallas kernels, per_device(): pl.pallas_call(load_kernel, out_shape=tuple((pltpu.VMEM(a.shape, a.dtype)...  0.93 us
    pallas_call x1, Pallas kernels, per_device(): pl.pallas_call(resample_kernel, out_shape=jax.ShapeDtypeStruct((2 * wide...  0.82 us
  transfers between devices with their start and end apart: 4, of which 3 were waited for; matrix products, arithmetic and copies ran while one was open for 0% of the time, Pallas kernels for 12%

profile of v6, /device:TPU:0, one launch (start us, length us, event | category | flops | bytes accessed | tf_op | source)
XLA Modules:
  0.0 19.8 jit_solution(4043003803130306253)
XLA Ops:
  0.0 0.0 copy-start
  0.0 0.5 %collective-permute-start = (f32[2,1,64,256]{3,2,0,1:T(8,128)}, f32[2,1,64,256]{3,2,0,1:T(8,128)S(1)}, u32[]{:S(2)}, u32[]{:S(2)}) collective-permute-start(f32[2,1,64,256]{3,2,0,1:T(8,128)} %bitcast.6), channel_id=1, source_target_pairs={{0,1},{1,0},{2,3},{3,2},{4,5},{5,4},{6,7},{7,6},{8,9},{9,8},{10,11... | collective-permute-start | bytes 393224 | tf_op jit(solution)/shard_map/ppermute | solution.py:347
  0.5 0.9 %load.1 = (f32[2,64,256]{2,1,0:T(8,128)S(1)}, f32[8,64]{1,0:T(8,128)S(1)}, s32[1,64]{1,0:T(1,128)S(1)}) custom-call(f32[2,64,256]{2,1,0:T(8,128)} %bitcast.7, f32[8,64]{1,0:T(8,128)} %bitcast.8, s32[1,64]{1,0:T(1,128)} %refs_2_.1), custom_call_target="tpu_custom_call" | custom-call | tf_op jit(solution)/shard_map/load/pallas_call | solution.py:353
  1.4 0.3 %collective-permute-done = f32[2,1,64,256]{3,2,0,1:T(8,128)S(1)} collective-permute-done((f32[2,1,64,256]{3,2,0,1:T(8,128)}, f32[2,1,64,256]{3,2,0,1:T(8,128)S(1)}, u32[]{:S(2)}, u32[]{:S(2)}) %collective-permute-start) | collective-permute-done | bytes 131104 | tf_op jit(solution)/shard_map/ppermute | solution.py:347
  1.7 0.2 pack.1
  1.8 3.0 %collective-permute-start.1 = (bf16[128,256]{1,0:T(8,128)(2,1)S(1)}, bf16[128,256]{1,0:T(8,128)(2,1)S(1)}, u32[]{:S(2)}, u32[]{:S(2)}) collective-permute-start(bf16[128,256]{1,0:T(8,128)(2,1)S(1)} %get-tuple-element.13), channel_id=1, source_target_pairs={{0,4},{8,12},{4,0},{12,8},{1,5},{9,13},{5,1},{13,9},{2,6},{10,14},... | collective-permute-start | bytes 196616 | tf_op jit(solution)/shard_map/ppermute | solution.py:375
  4.8 0.0 copy-start.1
  4.8 2.5 %collective-permute-start.2 = (bf16[128,256]{1,0:T(8,128)(2,1)S(1)}, bf16[128,256]{1,0:T(8,128)(2,1)S(1)}, u32[]{:S(2)}, u32[]{:S(2)}) collective-permute-start(bf16[128,256]{1,0:T(8,128)(2,1)S(1)} %get-tuple-element.14), channel_id=1, source_target_pairs={{4,8},{12,0},{8,4},{0,12},{5,9},{13,1},{9,5},{1,13},{6,10},{14,2},... | collective-permute-start | bytes 196616 | tf_op jit(solution)/shard_map/ppermute | solution.py:375
  7.3 0.0 collective-permute-done.1.even_ref
  7.3 3.7 %collective-permute-done.2.odd_ref = bf16[128,256]{1,0:T(8,128)(2,1)S(1)} collective-permute-done((bf16[128,256]{1,0:T(8,128)(2,1)S(1)}, bf16[128,256]{1,0:T(8,128)(2,1)S(1)}, u32[]{:S(2)}, u32[]{:S(2)}) %collective-permute-start.2) | collective-permute-done | bytes 65568 | tf_op jit(solution)/shard_map/ppermute | solution.py:375
  11.0 0.8 %resample.1.own_ref = bf16[288,256]{1,0:T(8,128)(2,1)S(1)} custom-call(f32[2,64,256]{2,1,0:T(8,128)S(1)} %get-tuple-element.10.image_ref, f32[2,64,256]{2,1,0:T(8,128)S(1)} %bitcast.5, f32[8,64]{1,0:T(8,128)S(1)} %get-tuple-element.11.taps_ref, s32[1,64]{1,0:T(1,128)S(1)} %get-tuple-element.12.offsets_ref, ...), custom_call_target="tpu_custom_call" | custom-call | tf_op jit(solution)/shard_map/resample/pallas_call | solution.py:378
  11.9 1.6 %collective-permute-start.3 = (bf16[288,256]{1,0:T(8,128)(2,1)S(1)}, bf16[288,256]{1,0:T(8,128)(2,1)S(1)}, u32[]{:S(2)}, u32[]{:S(2)}) collective-permute-start(bf16[288,256]{1,0:T(8,128)(2,1)S(1)} %resample.1.own_ref), channel_id=1, source_target_pairs={{2,0},{0,2},{3,1},{1,3},{6,4},{4,6},{7,5},{5,7},{10,8},{8,10},{11,... | collective-permute-start | bytes 442376 | tf_op jit(solution)/shard_map/ppermute | solution.py:388
  13.4 0.0 copy-done.1
  13.4 0.1 copy.7.match_ref
  13.5 0.0 copy-done
  13.5 1.4 %filter_own.1.filtered_own_ref = f32[128,256]{1,0:T(8,128)S(1)} custom-call(bf16[1088,256]{1,0:T(8,128)(2,1)S(1)} %copy-done, bf16[288,256]{1,0:T(8,128)(2,1)S(1)} %resample.1.own_ref), custom_call_target="tpu_custom_call" | custom-call | tf_op jit(solution)/shard_map/filter_own/pallas_call | solution.py:397
  14.9 2.2 %collective-permute-done.3.refs_0_ = bf16[288,256]{1,0:T(8,128)(2,1)S(1)} collective-permute-done((bf16[288,256]{1,0:T(8,128)(2,1)S(1)}, bf16[288,256]{1,0:T(8,128)(2,1)S(1)}, u32[]{:S(2)}, u32[]{:S(2)}) %collective-permute-start.3) | collective-permute-done | bytes 147488 | tf_op jit(solution)/shard_map/ppermute | solution.py:388
  17.1 2.7 %filter_other.1 = f32[3,2,1,64,256]{4,3,2,1,0:T(8,128)} custom-call(s32[3,2]{1,0:T(4,128)S(1)} %copy.7.match_ref, bf16[1088,256]{1,0:T(8,128)(2,1)S(1)} %copy-done, f32[128,256]{1,0:T(8,128)S(1)} %filter_own.1.filtered_own_ref, bf16[288,256]{1,0:T(8,128)(2,1)S(1)} %resample.1.own_ref, bf16[288,256]{1,0:T(8,128)(2,1)S(1)} %collective-permute-done.3.refs_0_), custom_call_target="tpu_custom_call" | custom-call | tf_op jit(solution)/shard_map/filter_other/pallas_call | solution.py:406
Async XLA Ops:
  0.0 13.5 %copy-start = (bf16[1088,256]{1,0:T(8,128)(2,1)S(1)}, bf16[1088,256]{1,0:T(8,128)(2,1)}, u32[]{:S(2)}) copy-start(bf16[1088,256]{1,0:T(8,128)(2,1)} %constant.2.clone.table_ref) | copy-start | bytes 1671172
  0.0 1.6 %collective-permute-start = (f32[2,1,64,256]{3,2,0,1:T(8,128)}, f32[2,1,64,256]{3,2,0,1:T(8,128)S(1)}, u32[]{:S(2)}, u32[]{:S(2)}) collective-permute-start(f32[2,1,64,256]{3,2,0,1:T(8,128)} %bitcast.6), channel_id=1, source_target_pairs={{0,1},{1,0},{2,3},{3,2},{4,5},{5,4},{6,7},{7,6},{8,9},{9,8},{10,11... | collective-permute-start | bytes 393224 | tf_op jit(solution)/shard_map/ppermute | solution.py:347
  1.8 5.5 %collective-permute-start.1 = (bf16[128,256]{1,0:T(8,128)(2,1)S(1)}, bf16[128,256]{1,0:T(8,128)(2,1)S(1)}, u32[]{:S(2)}, u32[]{:S(2)}) collective-permute-start(bf16[128,256]{1,0:T(8,128)(2,1)S(1)} %get-tuple-element.13), channel_id=1, source_target_pairs={{0,4},{8,12},{4,0},{12,8},{1,5},{9,13},{5,1},{13,9},{2,6},{10,14},... | collective-permute-start | bytes 196616 | tf_op jit(solution)/shard_map/ppermute | solution.py:375
  4.8 8.6 %copy-start.1 = (s32[3,2]{0,1:T(2,128)S(1)}, s32[3,2]{0,1:T(2,128)}, u32[]{:S(2)}) copy-start(s32[3,2]{0,1:T(2,128)} %param.8) | copy-start | bytes 76
  4.8 6.2 %collective-permute-start.2 = (bf16[128,256]{1,0:T(8,128)(2,1)S(1)}, bf16[128,256]{1,0:T(8,128)(2,1)S(1)}, u32[]{:S(2)}, u32[]{:S(2)}) collective-permute-start(bf16[128,256]{1,0:T(8,128)(2,1)S(1)} %get-tuple-element.14), channel_id=1, source_target_pairs={{4,8},{12,0},{8,4},{0,12},{5,9},{13,1},{9,5},{1,13},{6,10},{14,2},... | collective-permute-start | bytes 196616 | tf_op jit(solution)/shard_map/ppermute | solution.py:375
  11.9 5.2 %collective-permute-start.3 = (bf16[288,256]{1,0:T(8,128)(2,1)S(1)}, bf16[288,256]{1,0:T(8,128)(2,1)S(1)}, u32[]{:S(2)}, u32[]{:S(2)}) collective-permute-start(bf16[288,256]{1,0:T(8,128)(2,1)S(1)} %resample.1.own_ref), channel_id=1, source_target_pairs={{2,0},{0,2},{3,1},{1,3},{6,4},{4,6},{7,5},{5,7},{10,8},{8,10},{11,... | collective-permute-start | bytes 442376 | tf_op jit(solution)/shard_map/ppermute | solution.py:388

commit v7 on v6

--- a/solution.py
+++ b/solution.py
@@ -371,8 +371,14 @@
     peers = lax.axis_size("az")
 
     def swapped(value, start):
-        pairs = [(i, (i + 1) % peers) for i in range(start, peers, 2)]
-        return lax.ppermute(value, "az", pairs + [(j, i) for i, j in pairs])
+        paired = {i: i + 1 for i in range(start, peers - 1, 2)}
+        paired.update({j: i for i, j in paired.items()})
+        pairs = [
+            (2 * i + core, 2 * paired[i] + core if i in paired else 2 * i + 1 - core)
+            for i in range(peers)
+            for core in range(2)
+        ]
+        return lax.ppermute(value, ("az", "rg"), pairs)
 
     even, odd = swapped(even, 0), swapped(odd, 1)
     tile = pl.pallas_call(

time: 19.9 us -> 16.5 us (0.83)
  starting transfers between devices: 7.48 us -> 5.29 us
  waiting for transfers between devices: 6.17 us -> 4.79 us
    ppermute x2, starting transfers between devices: 5.47 us -> 3 us  [swapped(): return lax.ppermute(value, ('az', 'rg'), pairs)]
    ppermute x2, waiting for transfers between devices: 3.74 us -> 2.4 us  [swapped(): return lax.ppermute(value, ('az', 'rg'), pairs)]
    ppermute x1, starting transfers between devices: 1.56 us -> 1.84 us  [per_device(): lax.ppermute(tile, 'date', [((i + slot) % dates, i) for i in range(dates)])]
  transfers between devices with their start and end apart: 4 -> 4, of which waited for: 3 -> 3; matrix products, arithmetic and copies ran while one was open for 0% -> 1% of each run, Pallas kernels for 12% -> 14%
where the time goes in v7:
time: 16.5 us; the launch traced here: 16.2 us
  Pallas kernels  6.02 us (36%)
  starting transfers between devices  5.29 us (32%)
  waiting for transfers between devices  4.79 us (29%)
    ppermute x2, starting transfers between devices, swapped(): return lax.ppermute(value, ('az', 'rg'), pairs)  3 us
    pallas_call x1, Pallas kernels, per_device(): pl.pallas_call(other_kernel, out_shape=jax.ShapeDtypeStruct((match_count,...  2.73 us
    ppermute x2, waiting for transfers between devices, swapped(): return lax.ppermute(value, ('az', 'rg'), pairs)  2.4 us
    ppermute x1, waiting for transfers between devices, per_device(): lax.ppermute(tile, 'date', [((i + slot) % dates, i) for i in range(dates)])  2.14 us
    ppermute x1, starting transfers between devices, per_device(): lax.ppermute(tile, 'date', [((i + slot) % dates, i) for i in range(dates)])  1.84 us
    pallas_call x1, Pallas kernels, per_device(): pl.pallas_call(own_kernel, out_shape=jax.ShapeDtypeStruct((2 * lines, wid...  1.37 us
    pallas_call x1, Pallas kernels, per_device(): pl.pallas_call(load_kernel, out_shape=tuple((pltpu.VMEM(a.shape, a.dtype)...  0.93 us
    pallas_call x1, Pallas kernels, per_device(): pl.pallas_call(resample_kernel, out_shape=jax.ShapeDtypeStruct((2 * wide...  0.83 us
  transfers between devices with their start and end apart: 4, of which 3 were waited for; matrix products, arithmetic and copies ran while one was open for 1% of the time, Pallas kernels for 14%

profile of v7, /device:TPU:0, one launch (start us, length us, event | category | flops | bytes accessed | tf_op | source)
XLA Modules:
  0.0 16.2 jit_solution(10304504212519772217)
XLA Ops:
  0.0 0.0 copy-start
  0.0 0.5 %collective-permute-start = (f32[2,1,64,256]{3,2,0,1:T(8,128)}, f32[2,1,64,256]{3,2,0,1:T(8,128)S(1)}, u32[]{:S(2)}, u32[]{:S(2)}) collective-permute-start(f32[2,1,64,256]{3,2,0,1:T(8,128)} %bitcast.6), channel_id=1, source_target_pairs={{0,1},{1,0},{2,3},{3,2},{4,5},{5,4},{6,7},{7,6},{8,9},{9,8},{10,11... | collective-permute-start | bytes 393224 | tf_op jit(solution)/shard_map/ppermute | solution.py:347
  0.5 0.9 %load.1 = (f32[2,64,256]{2,1,0:T(8,128)S(1)}, f32[8,64]{1,0:T(8,128)S(1)}, s32[1,64]{1,0:T(1,128)S(1)}) custom-call(f32[2,64,256]{2,1,0:T(8,128)} %bitcast.7, f32[8,64]{1,0:T(8,128)} %bitcast.8, s32[1,64]{1,0:T(1,128)} %refs_2_.1), custom_call_target="tpu_custom_call" | custom-call | tf_op jit(solution)/shard_map/load/pallas_call | solution.py:353
  1.4 0.3 %collective-permute-done = f32[2,1,64,256]{3,2,0,1:T(8,128)S(1)} collective-permute-done((f32[2,1,64,256]{3,2,0,1:T(8,128)}, f32[2,1,64,256]{3,2,0,1:T(8,128)S(1)}, u32[]{:S(2)}, u32[]{:S(2)}) %collective-permute-start) | collective-permute-done | bytes 131104 | tf_op jit(solution)/shard_map/ppermute | solution.py:347
  1.7 0.2 pack.1
  1.8 3.0 %collective-permute-start.1 = (bf16[128,256]{1,0:T(8,128)(2,1)S(1)}, bf16[128,256]{1,0:T(8,128)(2,1)S(1)}, u32[]{:S(2)}, u32[]{:S(2)}) collective-permute-start(bf16[128,256]{1,0:T(8,128)(2,1)S(1)} %get-tuple-element.13), channel_id=1, source_target_pairs={{0,4},{1,5},{4,0},{5,1},{8,12},{9,13},{12,8},{13,9},{2,6},{3,7},{6... | collective-permute-start | bytes 196616 | tf_op jit(solution)/shard_map/ppermute | solution.py:381
  4.8 0.0 copy-start.1
  4.8 0.0 collective-permute-start.2
  4.8 2.4 %collective-permute-done.1.even_ref = bf16[128,256]{1,0:T(8,128)(2,1)S(1)} collective-permute-done((bf16[128,256]{1,0:T(8,128)(2,1)S(1)}, bf16[128,256]{1,0:T(8,128)(2,1)S(1)}, u32[]{:S(2)}, u32[]{:S(2)}) %collective-permute-start.1) | collective-permute-done | bytes 65568 | tf_op jit(solution)/shard_map/ppermute | solution.py:381
  7.2 0.0 collective-permute-done.2.odd_ref
  7.2 0.8 %resample.1.own_ref = bf16[288,256]{1,0:T(8,128)(2,1)S(1)} custom-call(f32[2,64,256]{2,1,0:T(8,128)S(1)} %get-tuple-element.10.image_ref, f32[2,64,256]{2,1,0:T(8,128)S(1)} %bitcast.5, f32[8,64]{1,0:T(8,128)S(1)} %get-tuple-element.11.taps_ref, s32[1,64]{1,0:T(1,128)S(1)} %get-tuple-element.12.offsets_ref, ...), custom_call_target="tpu_custom_call" | custom-call | tf_op jit(solution)/shard_map/resample/pallas_call | solution.py:384
  8.1 1.8 %collective-permute-start.3 = (bf16[288,256]{1,0:T(8,128)(2,1)S(1)}, bf16[288,256]{1,0:T(8,128)(2,1)S(1)}, u32[]{:S(2)}, u32[]{:S(2)}) collective-permute-start(bf16[288,256]{1,0:T(8,128)(2,1)S(1)} %resample.1.own_ref), channel_id=1, source_target_pairs={{2,0},{0,2},{3,1},{1,3},{6,4},{4,6},{7,5},{5,7},{10,8},{8,10},{11,... | collective-permute-start | bytes 442376 | tf_op jit(solution)/shard_map/ppermute | solution.py:394
  9.9 0.0 copy-done.1
  9.9 0.1 copy.7.match_ref
  10.0 0.0 copy-done
  10.0 1.4 %filter_own.1.filtered_own_ref = f32[128,256]{1,0:T(8,128)S(1)} custom-call(bf16[1088,256]{1,0:T(8,128)(2,1)S(1)} %copy-done, bf16[288,256]{1,0:T(8,128)(2,1)S(1)} %resample.1.own_ref), custom_call_target="tpu_custom_call" | custom-call | tf_op jit(solution)/shard_map/filter_own/pallas_call | solution.py:403
  11.4 2.1 %collective-permute-done.3.refs_0_ = bf16[288,256]{1,0:T(8,128)(2,1)S(1)} collective-permute-done((bf16[288,256]{1,0:T(8,128)(2,1)S(1)}, bf16[288,256]{1,0:T(8,128)(2,1)S(1)}, u32[]{:S(2)}, u32[]{:S(2)}) %collective-permute-start.3) | collective-permute-done | bytes 147488 | tf_op jit(solution)/shard_map/ppermute | solution.py:394
  13.5 2.7 %filter_other.1 = f32[3,2,1,64,256]{4,3,2,1,0:T(8,128)} custom-call(s32[3,2]{1,0:T(4,128)S(1)} %copy.7.match_ref, bf16[1088,256]{1,0:T(8,128)(2,1)S(1)} %copy-done, f32[128,256]{1,0:T(8,128)S(1)} %filter_own.1.filtered_own_ref, bf16[288,256]{1,0:T(8,128)(2,1)S(1)} %resample.1.own_ref, bf16[288,256]{1,0:T(8,128)(2,1)S(1)} %collective-permute-done.3.refs_0_), custom_call_target="tpu_custom_call" | custom-call | tf_op jit(solution)/shard_map/filter_other/pallas_call | solution.py:412
Async XLA Ops:
  0.0 10.0 %copy-start = (bf16[1088,256]{1,0:T(8,128)(2,1)S(1)}, bf16[1088,256]{1,0:T(8,128)(2,1)}, u32[]{:S(2)}) copy-start(bf16[1088,256]{1,0:T(8,128)(2,1)} %constant.2.clone.table_ref) | copy-start | bytes 1671172
  0.0 1.6 %collective-permute-start = (f32[2,1,64,256]{3,2,0,1:T(8,128)}, f32[2,1,64,256]{3,2,0,1:T(8,128)S(1)}, u32[]{:S(2)}, u32[]{:S(2)}) collective-permute-start(f32[2,1,64,256]{3,2,0,1:T(8,128)} %bitcast.6), channel_id=1, source_target_pairs={{0,1},{1,0},{2,3},{3,2},{4,5},{5,4},{6,7},{7,6},{8,9},{9,8},{10,11... | collective-permute-start | bytes 393224 | tf_op jit(solution)/shard_map/ppermute | solution.py:347
  1.8 5.4 %collective-permute-start.1 = (bf16[128,256]{1,0:T(8,128)(2,1)S(1)}, bf16[128,256]{1,0:T(8,128)(2,1)S(1)}, u32[]{:S(2)}, u32[]{:S(2)}) collective-permute-start(bf16[128,256]{1,0:T(8,128)(2,1)S(1)} %get-tuple-element.13), channel_id=1, source_target_pairs={{0,4},{1,5},{4,0},{5,1},{8,12},{9,13},{12,8},{13,9},{2,6},{3,7},{6... | collective-permute-start | bytes 196616 | tf_op jit(solution)/shard_map/ppermute | solution.py:381
  4.8 5.1 %copy-start.1 = (s32[3,2]{0,1:T(2,128)S(1)}, s32[3,2]{0,1:T(2,128)}, u32[]{:S(2)}) copy-start(s32[3,2]{0,1:T(2,128)} %param.8) | copy-start | bytes 76
  4.8 2.4 %collective-permute-start.2 = (bf16[128,256]{1,0:T(8,128)(2,1)S(1)}, bf16[128,256]{1,0:T(8,128)(2,1)S(1)}, u32[]{:S(2)}, u32[]{:S(2)}) collective-permute-start(bf16[128,256]{1,0:T(8,128)(2,1)S(1)} %get-tuple-element.14), channel_id=1, source_target_pairs={{0,1},{1,0},{4,8},{5,9},{8,4},{9,5},{12,13},{13,12},{2,3},{3,2},{6... | collective-permute-start | bytes 196616 | tf_op jit(solution)/shard_map/ppermute | solution.py:381
  8.1 5.5 %collective-permute-start.3 = (bf16[288,256]{1,0:T(8,128)(2,1)S(1)}, bf16[288,256]{1,0:T(8,128)(2,1)S(1)}, u32[]{:S(2)}, u32[]{:S(2)}) collective-permute-start(bf16[288,256]{1,0:T(8,128)(2,1)S(1)} %resample.1.own_ref), channel_id=1, source_target_pairs={{2,0},{0,2},{3,1},{1,3},{6,4},{4,6},{7,5},{5,7},{10,8},{8,10},{11,... | collective-permute-start | bytes 442376 | tf_op jit(solution)/shard_map/ppermute | solution.py:394

commit v8 on v7

v8 whole, which is shorter than its diff:
```python
import functools
import math

import jax
import jax.numpy as jnp
import numpy as np
from jax import lax
from jax.experimental import pallas as pl
from jax.experimental.pallas import tpu as pltpu
from jax.sharding import PartitionSpec as P

TAPS = 8
SHIFT_MAX = 12
PATCH = 64
HALF = PATCH // 2
RIM = SHIFT_MAX + TAPS // 2
REACH = HALF + RIM
LANES = 128
EDGE_ROWS = 16
VMEM_LIMIT = 48 * 1024 * 1024

VMEM = pl.BlockSpec(memory_space=pltpu.VMEM)
SMEM = pl.BlockSpec(memory_space=pltpu.SMEM)
HBM = pl.BlockSpec(memory_space=pltpu.HBM)
PARAMS = pltpu.CompilerParams(vmem_limit_bytes=VMEM_LIMIT)


def fourier_table(sine_sign, table_scale):
    freq_ids = np.arange(PATCH)
    phase_ids = (freq_ids[:, None] * freq_ids[None, :]) % PATCH
    angles = phase_ids * (2.0 * math.pi / PATCH)
    cosine = np.cos(angles) * table_scale
    sine_part = np.sin(angles) * (sine_sign * table_scale)
    top = np.concatenate([cosine, -sine_part], axis=1)
    bottom = np.concatenate([sine_part, cosine], axis=1)
    return np.concatenate([top, bottom], axis=0).astype(np.float32)


def paired(table):
    split = table.reshape(2, PATCH, 2, PATCH)
    wide = np.zeros((2, 2, PATCH, 2, 2, PATCH), np.float32)
    for slot in range(2):
        wide[:, slot, :, :, slot, :] = split
    return wide.reshape(4 * PATCH, 4 * PATCH)


def line_table(forward, order):
    return forward.T.reshape(2 * PATCH, 2, PATCH)[:, :, order].reshape(2 * PATCH, 2 * PATCH)


def window_table():
    window = np.sin(math.pi * (np.arange(PATCH) + 0.5) / PATCH) ** 2
    return np.tile(np.outer(window, window), (2, 2)).astype(np.float32)


def ring_table():
    ring = np.zeros((LANES, LANES), np.float32)
    for lane in range(LANES):
        base = lane // PATCH * PATCH
        for step in (-1, 0, 1):
            ring[base + (lane + step) % PATCH, lane] = 1.0
    return ring


def edge_of(other_ref, part, side, lines):
    width = other_ref.shape[2]
    return jnp.where(
        side == 0, other_ref[part, lines, :HALF], other_ref[part, lines, width - HALF :]
    )


def load_kernel(*refs):
    count = (len(refs) - 1) // 2
    copies = [
        pltpu.make_async_copy(refs[i], refs[count + i], refs[-1].at[i]) for i in range(count)
    ]
    for copy in copies:
        copy.start()
    for copy in copies:
        copy.wait()


def pack_kernel(image_ref, other_ref, taps_ref, offsets_ref, even_ref, odd_ref):
    lines = image_ref.shape[1]
    width = image_ref.shape[2]
    side = lax.axis_index("rg")
    taps = taps_ref[...]
    taps_high = taps.astype(jnp.bfloat16).astype(jnp.float32)
    taps_low = taps - taps_high
    shifts = jnp.broadcast_to(offsets_ref[...].astype(jnp.float32), (TAPS, lines))

    def write(out_ref, line_start, tap_start):
        rows = slice(line_start, line_start + REACH)
        for part in range(2):
            cut = slice(part * REACH, (part + 1) * REACH)
            out_ref[cut, :] = image_ref[part, rows, :].astype(jnp.bfloat16)
        edges = jnp.concatenate([edge_of(other_ref, part, side, rows) for part in range(2)], axis=0)
        cut = slice(tap_start, tap_start + HALF)
        block = jnp.concatenate([taps_high[:, cut], taps_low[:, cut], shifts[:, cut]], axis=1)
        block = jnp.concatenate([block, jnp.zeros((HALF - TAPS, 3 * HALF), jnp.float32)], axis=0)
        cuts = [edges[i * HALF : (i + 1) * HALF] for i in range(3)]
        filler = jnp.zeros((HALF, width - 6 * HALF), jnp.float32)
        block = jnp.concatenate([block, *cuts, filler], axis=1)
        out_ref[2 * REACH :, :] = block.astype(jnp.bfloat16)

    parity = lax.rem(lax.axis_index("az"), 2)

    @pl.when(parity == 0)
    def _():
        write(even_ref, lines - REACH, lines - HALF)
        write(odd_ref, 0, 0)

    @pl.when(parity == 1)
    def _():
        write(even_ref, 0, 0)
        write(odd_ref, lines - REACH, lines - HALF)


def is_above(turn):
    return lax.rem(lax.axis_index("az") + turn, 2) == 1


def band(taps, shift, first_line, source):
    count, lines = source.shape
    tap_ids = source - (lax.broadcasted_iota(jnp.int32, (count, lines), 1) + first_line)
    tap_ids = tap_ids - shift + (TAPS // 2 - 1)
    total = jnp.zeros((count, lines), jnp.float32)
    for tap in range(TAPS):
        total = jnp.where(tap_ids == tap, taps[tap : tap + 1, :], total)
    return total


def high_low(value):
    high = value.astype(jnp.bfloat16)
    low = (value - high.astype(jnp.float32)).astype(jnp.bfloat16)
    return jnp.concatenate([high, low], axis=0)


def apply_band(weights, rows):
    over_rows = (((0,), (0,)), ((), ()))
    rows = jnp.concatenate([rows, rows], axis=0)
    return lax.dot_general(high_low(weights), rows, over_rows, preferred_element_type=jnp.float32)


def write_piece(out_ref, parts, width):
    lines = parts[0].shape[0]
    edges = []
    for part, value in enumerate(parts):
        out_ref[part * lines : (part + 1) * lines, :] = value[:, :width].astype(jnp.bfloat16)
        for at in range(0, lines, EDGE_ROWS):
            edges.append(value[at : at + EDGE_ROWS, width:])
    edges.append(jnp.zeros((EDGE_ROWS, width - len(edges) * HALF), jnp.float32))
    out_ref[2 * lines :, :] = jnp.concatenate(edges, axis=1).astype(jnp.bfloat16)


def read_piece(ref):
    lines = (ref.shape[0] - EDGE_ROWS) // 2
    block = ref[2 * lines :, :].astype(jnp.float32)
    steps = lines // EDGE_ROWS
    parts = []
    for part in range(2):
        tile = ref[part * lines : (part + 1) * lines, :].astype(jnp.float32)
        slots = range(part * steps, (part + 1) * steps)
        edge = jnp.concatenate([block[:, i * HALF : (i + 1) * HALF] for i in slots], axis=0)
        parts.append((tile, edge))
    return parts


def inner_kernel(image_ref, other_ref, taps_ref, offsets_ref, out_ref):
    lines = image_ref.shape[1]
    width = image_ref.shape[2]
    side = lax.axis_index("rg")
    cut = slice(RIM, lines - RIM)
    source = lax.broadcasted_iota(jnp.int32, (lines, lines - 2 * RIM), 0)
    weights = band(taps_ref[:, cut], offsets_ref[:, cut], RIM, source)
    weights = jnp.concatenate([weights, weights], axis=0)
    parts = []
    for part in range(2):
        edge = edge_of(other_ref, part, side, slice(0, lines))
        rows = high_low(jnp.concatenate([image_ref[part], edge], axis=1))
        parts.append(apply_band(weights, rows))
    write_piece(out_ref, parts, width)


def side_kernel(turn, image_ref, other_ref, taps_ref, offsets_ref, message_ref, *refs):
    out_ref = refs[-1]
    lines = image_ref.shape[1]
    width = image_ref.shape[2]
    side = lax.axis_index("rg")
    place = lax.axis_index("az")
    above = is_above(turn)
    alone = jnp.where(above, place == 0, place == lax.axis_size("az") - 1)
    message = message_ref[...]
    message = jnp.where(alone, jnp.zeros_like(message), message)
    block = message[2 * REACH :, :].astype(jnp.float32)
    head = block[:TAPS]
    rim_taps = head[:, :HALF] + head[:, HALF : 2 * HALF]
    rim_shift = head[:1, 2 * HALF : 3 * HALF]
    rim_edges = [block[:, i * HALF : (i + 1) * HALF] for i in range(3, 6)]
    rim_edges = jnp.concatenate(rim_edges, axis=0).astype(jnp.bfloat16)

    def per_line(own, rim):
        upper = jnp.concatenate([rim, own[:, :RIM]], axis=1)
        lower = jnp.concatenate([own[:, lines - RIM :], rim], axis=1)
        return jnp.where(above, upper, lower)

    taps = per_line(taps_ref[...], rim_taps)
    shift = per_line(offsets_ref[...].astype(jnp.float32), rim_shift).astype(jnp.int32)
    first_line = jnp.where(above, -HALF, lines - RIM)
    near = 2 * RIM
    first_own = jnp.where(above, 0, lines - near)
    first_rim = jnp.where(above, -REACH, lines)
    source = lax.broadcasted_iota(jnp.int32, (REACH + near, REACH), 0)
    source = jnp.where(source < REACH, source + first_rim, source - REACH + first_own)
    weights = band(taps, shift, first_line, source)
    weights = jnp.concatenate([weights, weights[REACH:]], axis=0)
    parts = []
    for part in range(2):
        upper, lower = slice(0, near), slice(lines - near, lines)
        edge = jnp.where(
            above, edge_of(other_ref, part, side, upper), edge_of(other_ref, part, side, lower)
        )
        own = jnp.where(above, image_ref[part, upper, :], image_ref[part, lower, :])
        own = high_low(jnp.concatenate([own, edge], axis=1))
        cut = slice(part * REACH, (part + 1) * REACH)
        rim = jnp.concatenate([message[cut, :], rim_edges[cut]], axis=1)
        parts.append(apply_band(weights, jnp.concatenate([rim, own], axis=0)))
    write_piece(out_ref, parts, width)


def cross(own_parts, other_parts):
    own_real, own_imag = own_parts
    other_real, other_imag = other_parts
    real = own_real * other_real + own_imag * other_imag
    imag = own_imag * other_real - own_real * other_imag
    return real, imag


def interferogram(own_pieces, other_pieces, cuts):
    side = lax.axis_index("rg")

    def lines_of(pieces, part, which):
        return jnp.concatenate([cut(piece[part][which]) for piece, cut in zip(pieces, cuts)], axis=0)

    def both(which):
        own = [lines_of(own_pieces, part, which) for part in range(2)]
        other = [lines_of(other_pieces, part, which) for part in range(2)]
        return jnp.concatenate(cross(own, other), axis=0)

    mid, rim = both(0), both(1)
    before = jnp.where(side == 0, 0.0, rim)
    after = jnp.where(side == 0, rim, 0.0)
    filler = jnp.zeros((mid.shape[0], LANES - 2 * HALF), jnp.float32)
    shifted = jnp.concatenate([before, mid, after, filler], axis=1).astype(jnp.bfloat16)
    return jnp.concatenate([mid.astype(jnp.bfloat16), shifted], axis=1)


def side_cuts(above):
    return [
        lambda value: value,
        lambda value: jnp.where(above, value[:RIM], value[value.shape[0] - RIM :]),
    ]


def middle_cuts(above):
    def near(flag):
        return lambda value: jnp.where(flag, value[value.shape[0] - RIM :], value[:RIM])

    return [near(above), lambda value: value, near(jnp.logical_not(above))]


def patch_row(both, line_table_of, tables, spectrum_ref):
    forward, inverse, ring = tables
    chunks = both.shape[1] // LANES
    line_spectra = jnp.dot(line_table_of, both, preferred_element_type=jnp.float32)
    line_spectra = line_spectra.astype(jnp.bfloat16)
    pieces = []
    for chunk in range(chunks):
        cut = slice(chunk * LANES, (chunk + 1) * LANES)
        pieces.append(jnp.concatenate([line_spectra[:PATCH, cut], line_spectra[PATCH:, cut]], axis=1))
    patches = jnp.concatenate(pieces, axis=0)
    spectrum_ref[...] = jnp.dot(patches, forward, preferred_element_type=jnp.float32)
    pieces = []
    for chunk in range(chunks):
        rows = slice(chunk * PATCH, (chunk + 1) * PATCH)
        real = spectrum_ref[rows, :LANES]
        imag = spectrum_ref[rows, LANES:]
        power = real * real + imag * imag
        power = power + pltpu.roll(power, 1, 0) + pltpu.roll(power, PATCH - 1, 0)
        smooth = jnp.dot(power.astype(jnp.bfloat16), ring, preferred_element_type=jnp.float32)
        gain = lax.rsqrt(lax.rsqrt(smooth * (1.0 / (9.0 * PATCH * PATCH)) + 1.0))
        pieces.append(jnp.concatenate([real * gain, imag * gain], axis=1).astype(jnp.bfloat16))
    shaped = jnp.concatenate(pieces, axis=0)
    range_back = jnp.dot(shaped, inverse, preferred_element_type=jnp.float32)
    range_back = range_back.astype(jnp.bfloat16)
    stacked = []
    for chunk in range(chunks):
        block = range_back[chunk * PATCH : (chunk + 1) * PATCH]
        stacked.append(jnp.concatenate([block[:, :LANES], block[:, LANES:]], axis=0))
    return stacked


def lines_back(stacked, back, window, width):
    pieces = [jnp.dot(back, s, preferred_element_type=jnp.float32) * window for s in stacked]
    mids = width // LANES
    mid = jnp.concatenate(pieces[:mids], axis=1)
    moved = jnp.concatenate(pieces[mids:], axis=1)
    return mid + moved[:, HALF : HALF + width]


def all_tables():
    forward = fourier_table(1.0, 1.0)
    inverse = fourier_table(-1.0, 1.0 / PATCH)
    back = inverse.reshape(2, PATCH, 2, PATCH).transpose(2, 3, 0, 1)
    back = back.reshape(2, 2, HALF, 2 * PATCH).transpose(1, 0, 2, 3).reshape(2 * PATCH, 2 * PATCH)
    window = window_table()[:PATCH, :PATCH]
    splits = []
    for _ in range(3):
        splits.append(window.astype(jnp.bfloat16).astype(np.float32))
        window = window - splits[-1]
    natural = np.arange(PATCH)
    rotated = np.concatenate([natural[RIM:], natural[:RIM]])
    swapped = np.concatenate([natural[PATCH - RIM :], natural[RIM : PATCH - RIM], natural[:RIM]])
    side = [line_table(forward, order) for order in (natural, rotated)]
    middle = [line_table(forward, order) for order in (natural, swapped)]
    rows = [
        np.concatenate([np.concatenate(side, axis=0), np.concatenate(middle, axis=0)], axis=1),
        paired(forward),
        paired(inverse),
        np.concatenate([back, ring_table()], axis=1),
        np.concatenate([*splits, np.zeros_like(window)], axis=1),
    ]
    return np.concatenate(rows, axis=0).astype(jnp.bfloat16)


class Tables:
    def __init__(self, ref):
        self.ref = ref
        size = 4 * PATCH
        self.back_at, self.window_at = 3 * size, 3 * size + LANES
        ring = ref[self.back_at : self.back_at + LANES, LANES:]
        self.core = ref[size : 2 * size, :], ref[2 * size : 3 * size, :], ring

    def line(self, above, lanes):
        start = pl.multiple_of(jnp.where(above, 0, 2 * PATCH), 2 * PATCH)
        return self.ref[pl.ds(start, 2 * PATCH), lanes * LANES : (lanes + 1) * LANES]

    def back(self, half):
        start = pl.multiple_of(self.back_at + half * PATCH, PATCH)
        return self.ref[pl.ds(start, PATCH), :LANES]

    def window(self, half):
        start = pl.multiple_of(self.window_at + half * HALF, HALF)
        splits = self.ref[pl.ds(start, HALF), :].astype(jnp.float32)
        window = splits[:, :PATCH] + splits[:, PATCH : 2 * PATCH] + splits[:, 2 * PATCH : 3 * PATCH]
        window = jnp.concatenate([window, window], axis=1)
        return jnp.concatenate([window, window], axis=0)


def half_of(turn):
    return jnp.where(is_above(turn), 0, 1)


def side_row(turn, own, other, tables, spectrum_ref, width):
    above = is_above(turn)
    both = interferogram(own, other, side_cuts(above))
    stacked = patch_row(both, tables.line(above, 0), tables.core, spectrum_ref)
    half = 1 - half_of(turn)
    return lines_back(stacked, tables.back(half), tables.window(half), width)


def middle_row(own, other, tables, spectrum_ref, width):
    above = is_above(0)
    both = interferogram(own, other, middle_cuts(above))
    stacked = patch_row(both, tables.line(above, 1), tables.core, spectrum_ref)
    back = jnp.concatenate([tables.back(half_of(turn)) for turn in range(2)], axis=0)
    window = jnp.concatenate([tables.window(half_of(turn)) for turn in range(2)], axis=0)
    return lines_back(stacked, back, window, width)


def keep(result_ref, result, turn):
    start = pl.multiple_of(half_of(turn) * HALF, HALF)
    for part in range(2):
        result_ref[part, pl.ds(start, HALF), :] = result[part * HALF : (part + 1) * HALF]


def rest_of(own, other, first, tables, spectrum_ref, result_ref, width):
    middle = middle_row(own, other, tables, spectrum_ref, width)
    keep(result_ref, middle[: 2 * HALF] + first, 0)
    second = side_row(1, [own[2], own[1]], [other[2], other[1]], tables, spectrum_ref, width)
    keep(result_ref, middle[2 * HALF :] + second, 1)


def own_kernel(table_ref, first_ref, inner_ref, second_ref, out_ref, spectrum_ref):
    width = first_ref.shape[1]
    own = [read_piece(ref) for ref in (first_ref, inner_ref, second_ref)]
    tables = Tables(table_ref)
    first = side_row(0, own[:2], own[:2], tables, spectrum_ref, width)
    rest_of(own, own, first, tables, spectrum_ref, out_ref, width)


def other_first_kernel(table_ref, first_ref, inner_ref, *refs):
    count = (len(refs) - 1) // 3
    spectrum_ref = refs[-1]
    own = [read_piece(ref) for ref in (first_ref, inner_ref)]
    tables = Tables(table_ref)
    for at in range(count):
        other = [read_piece(ref) for ref in refs[2 * at : 2 * at + 2]]
        result = side_row(0, own, other, tables, spectrum_ref, first_ref.shape[1])
        refs[2 * count + at][...] = result


def other_rest_kernel(
    match_ref, table_ref, filtered_own_ref, first_ref, inner_ref, second_ref, *refs
):
    out_ref, result_ref, spectrum_ref, sems = refs[-4:]
    match_count = out_ref.shape[0]
    date = lax.axis_index("date")
    dates = match_ref.shape[1]
    own = [read_piece(ref) for ref in (first_ref, inner_ref, second_ref)]
    tables = Tables(table_ref)
    result_ref[0] = filtered_own_ref[...]
    for slot in range(1, dates):
        *pieces, done_ref = refs[4 * slot - 4 : 4 * slot]
        other = [read_piece(ref) for ref in pieces]
        rest_of(
            own,
            other,
            done_ref[...],
            tables,
            spectrum_ref,
            result_ref.at[slot],
            first_ref.shape[1],
        )
    copies = []
    for match in range(match_count):
        slot = lax.rem(match_ref[match, date] - date + dates, dates)
        copies.append(
            pltpu.make_async_copy(result_ref.at[slot], out_ref.at[match, :, 0], sems.at[match])
        )
    for copy in copies:
        copy.start()
    for copy in copies:
        copy.wait()


def per_device(image_stack, tap_weights, offsets, matchings):
    _, _, lines, width = image_stack.shape
    match_count = matchings.shape[0]
    other = lax.ppermute(image_stack, "rg", [(0, 1), (1, 0)]).reshape(2, lines, width)
    arguments = (
        image_stack.reshape(2, lines, width),
        tap_weights.reshape(TAPS, lines),
        offsets,
    )
    raw = pl.pallas_call(
        load_kernel,
        out_shape=tuple(pltpu.VMEM(a.shape, a.dtype) for a in arguments),
        in_specs=[HBM] * 3,
        out_specs=(VMEM,) * 3,
        scratch_shapes=[pltpu.SemaphoreType.DMA((3,))],
        compiler_params=PARAMS,
        name="load",
    )(*(pltpu.with_memory_space_constraint(a, pltpu.HBM) for a in arguments))
    raw = (raw[0], other, *raw[1:])
    message = jax.ShapeDtypeStruct((2 * REACH + HALF, width), jnp.bfloat16)
    messages = pl.pallas_call(
        pack_kernel,
        out_shape=(message, message),
        in_specs=[VMEM] * 4,
        out_specs=(VMEM, VMEM),
        compiler_params=PARAMS,
        name="pack",
    )(*raw)
    peers = lax.axis_size("az")

    def swapped(value, start):
        paired_with = {i: i + 1 for i in range(start, peers - 1, 2)}
        paired_with.update({j: i for i, j in paired_with.items()})
        pairs = [
            (2 * i + core, 2 * paired_with[i] + core if i in paired_with else 2 * i + 1 - core)
            for i in range(peers)
            for core in range(2)
        ]
        return lax.ppermute(value, ("az", "rg"), pairs)

    messages = [swapped(messages[turn], turn) for turn in range(2)]
    inner = pl.pallas_call(
        inner_kernel,
        out_shape=jax.ShapeDtypeStruct((2 * (lines - 2 * RIM) + EDGE_ROWS, width), jnp.bfloat16),
        in_specs=[VMEM] * 4,
        out_specs=VMEM,
        compiler_params=PARAMS,
        name="inner",
    )(*raw)
    dates = lax.axis_size("date")

    def from_date(piece, slot):
        return lax.ppermute(piece, "date", [((i + slot) % dates, i) for i in range(dates)])

    slots = range(1, dates)
    inners = [from_date(inner, slot) for slot in slots]
    sides = []
    for turn in range(2):
        made = (*inners, *sides) if turn else (inner,)
        call = pl.pallas_call(
            functools.partial(side_kernel, turn),
            out_shape=jax.ShapeDtypeStruct((2 * REACH + EDGE_ROWS, width), jnp.bfloat16),
            in_specs=[VMEM] * (5 + len(made)),
            out_specs=VMEM,
            compiler_params=PARAMS,
            name="side_" + "ab"[turn],
        )
        sides.append(call(*raw, messages[turn], *made))
    own = (sides[0], inner, sides[1])
    firsts = [from_date(sides[0], slot) for slot in slots]
    seconds = [from_date(sides[1], slot) for slot in slots]
    tables = jnp.asarray(all_tables())
    chunks = (width + width + LANES) // LANES
    spectrum = pltpu.VMEM((chunks * PATCH, 2 * LANES), jnp.float32)
    filtered_own = pl.pallas_call(
        own_kernel,
        out_shape=jax.ShapeDtypeStruct((2, lines, width), jnp.float32),
        in_specs=[VMEM] * 4,
        out_specs=VMEM,
        scratch_shapes=[spectrum],
        compiler_params=PARAMS,
        name="filter_own",
    )(tables, *own)
    pieces = [piece for pair in zip(firsts, inners) for piece in pair]
    done = pl.pallas_call(
        other_first_kernel,
        out_shape=[jax.ShapeDtypeStruct((2 * HALF, width), jnp.float32)] * len(firsts),
        in_specs=[VMEM] * (3 + len(pieces)),
        out_specs=[VMEM] * len(firsts),
        scratch_shapes=[spectrum],
        compiler_params=PARAMS,
        name="filter_first",
    )(tables, *own[:2], *pieces)
    pieces = [piece for group in zip(firsts, inners, seconds, done) for piece in group]
    return pl.pallas_call(
        other_rest_kernel,
        out_shape=jax.ShapeDtypeStruct((match_count, 2, 1, lines, width), jnp.float32),
        in_specs=[SMEM] + [VMEM] * (5 + len(pieces)),
        out_specs=HBM,
        scratch_shapes=[
            pltpu.VMEM((dates, 2, lines, width), jnp.float32),
            spectrum,
            pltpu.SemaphoreType.DMA((match_count,)),
        ],
        compiler_params=PARAMS,
        name="filter_rest",
    )(matchings, tables, filtered_own, *own, *pieces)


def solution(mesh):
    placed = (
        P(None, ("parts", "date"), "az", "rg"),
        P(None, ("parts", "date"), "az"),
        P(("parts", "date"), "az"),
        P(),
    )
    return jax.shard_map(
        per_device,
        mesh=mesh,
        in_specs=placed,
        out_specs=P(None, None, ("parts", "date"), "az", "rg"),
        check_vma=False,
    )
```

time: 16.5 us -> 18.1 us (1.097)
  waiting for transfers between devices: 4.79 us -> 0.78 us
  Pallas kernels: 6.02 us -> 8.88 us
  starting transfers between devices: 5.29 us -> 8.01 us
    pallas_call x3 -> x6, Pallas kernels: 4.93 us -> 7.79 us  [the longest x1 3.11 us: per_device(): pl.pallas_call(other_rest_kernel, out_shape=jax.ShapeDtypeStruct((match_c...]
    ppermute x1 -> x3, starting transfers between devices: 1.84 us -> 4.56 us  [from_date(): lax.ppermute(piece, 'date', [((i + slot) % dates, i) for i in range(dates)])]
    ppermute x1 -> x3, waiting for transfers between devices: 2.14 us -> 0.01 us  [from_date(): lax.ppermute(piece, 'date', [((i + slot) % dates, i) for i in range(dates)])]
    ppermute x2, waiting for transfers between devices: 2.4 us -> 0.52 us  [swapped(): return lax.ppermute(value, ('az', 'rg'), pairs)]
  transfers between devices with their start and end apart: 4 -> 6, of which waited for: 3 -> 2; matrix products, arithmetic and copies ran while one was open for 1% -> 1% of each run, Pallas kernels for 14% -> 32%
where the time goes in v8:
time: 18.1 us; the launch traced here: 17.8 us
  Pallas kernels  8.88 us (49%)
  starting transfers between devices  8.01 us (44%)
  waiting for transfers between devices  0.78 us (4%)
    ppermute x3, starting transfers between devices, from_date(): lax.ppermute(piece, 'date', [((i + slot) % dates, i) for i in range(dates)])  4.56 us
    pallas_call x1, Pallas kernels, per_device(): pl.pallas_call(other_rest_kernel, out_shape=jax.ShapeDtypeStruct((match_c...  3.11 us
    ppermute x2, starting transfers between devices, swapped(): return lax.ppermute(value, ('az', 'rg'), pairs)  3 us
    pallas_call x1, Pallas kernels, per_device(): pl.pallas_call(own_kernel, out_shape=jax.ShapeDtypeStruct((2, lines, widt...  2.24 us
    pallas_call x1, Pallas kernels, per_device(): pl.pallas_call(other_first_kernel, out_shape=[jax.ShapeDtypeStruct((2 * H...  1.15 us
    pallas_call x2, Pallas kernels, per_device(): sides.append(call(*raw, messages[turn], *made))  0.94 us
    pallas_call x1, Pallas kernels, per_device(): pl.pallas_call(load_kernel, out_shape=tuple((pltpu.VMEM(a.shape, a.dtype)...  0.93 us
    ppermute x2, waiting for transfers between devices, swapped(): return lax.ppermute(value, ('az', 'rg'), pairs)  0.52 us
  transfers between devices with their start and end apart: 6, of which 2 were waited for; matrix products, arithmetic and copies ran while one was open for 1% of the time, Pallas kernels for 32%

profile of v8, /device:TPU:0, one launch (start us, length us, event | category | flops | bytes accessed | tf_op | source)
XLA Modules:
  0.0 17.8 jit_solution(16840945158868785749)
XLA Ops:
  0.0 0.5 %collective-permute-start = (f32[2,1,64,256]{3,2,0,1:T(8,128)}, f32[2,1,64,256]{3,2,0,1:T(8,128)S(1)}, u32[]{:S(2)}, u32[]{:S(2)}) collective-permute-start(f32[2,1,64,256]{3,2,0,1:T(8,128)} %bitcast.8), channel_id=1, source_target_pairs={{0,1},{1,0},{2,3},{3,2},{4,5},{5,4},{6,7},{7,6},{8,9},{9,8},{10,11... | collective-permute-start | bytes 393224 | tf_op jit(solution)/shard_map/ppermute | solution.py:450
  0.5 0.9 %load.1 = (f32[2,64,256]{2,1,0:T(8,128)S(1)}, f32[8,64]{1,0:T(8,128)S(1)}, s32[1,64]{1,0:T(1,128)S(1)}) custom-call(f32[2,64,256]{2,1,0:T(8,128)} %bitcast.9, f32[8,64]{1,0:T(8,128)} %bitcast.10, s32[1,64]{1,0:T(1,128)} %refs_2_.1), custom_call_target="tpu_custom_call" | custom-call | tf_op jit(solution)/shard_map/load/pallas_call | solution.py:456
  1.4 0.3 %collective-permute-done = f32[2,1,64,256]{3,2,0,1:T(8,128)S(1)} collective-permute-done((f32[2,1,64,256]{3,2,0,1:T(8,128)}, f32[2,1,64,256]{3,2,0,1:T(8,128)S(1)}, u32[]{:S(2)}, u32[]{:S(2)}) %collective-permute-start) | collective-permute-done | bytes 131104 | tf_op jit(solution)/shard_map/ppermute | solution.py:450
  1.7 0.2 pack.1
  1.8 3.0 %collective-permute-start.1 = (bf16[128,256]{1,0:T(8,128)(2,1)S(1)}, bf16[128,256]{1,0:T(8,128)(2,1)S(1)}, u32[]{:S(2)}, u32[]{:S(2)}) collective-permute-start(bf16[128,256]{1,0:T(8,128)(2,1)S(1)} %get-tuple-element.13), channel_id=1, source_target_pairs={{0,4},{1,5},{4,0},{5,1},{8,12},{9,13},{12,8},{13,9},{2,6},{3,7},{6... | collective-permute-start | bytes 196616 | tf_op jit(solution)/shard_map/ppermute | solution.py:485
  4.8 0.0 collective-permute-start.2
  4.8 0.3 %inner.1.refs_0_.inner_ref = bf16[80,256]{1,0:T(8,128)(2,1)S(1)} custom-call(f32[2,64,256]{2,1,0:T(8,128)S(1)} %get-tuple-element.10.image_ref, f32[2,64,256]{2,1,0:T(8,128)S(1)} %bitcast.5, f32[8,64]{1,0:T(8,128)S(1)} %get-tuple-element.11.taps_ref, s32[1,64]{1,0:T(1,128)S(1)} %get-tuple-element.12.offsets_ref), custom_call_target="tpu_custom_call" | custom-call | tf_op jit(solution)/shard_map/inner/pallas_call | solution.py:488
  5.2 0.0 copy-start
  5.2 1.5 %collective-permute-start.3 = (bf16[80,256]{1,0:T(8,128)(2,1)S(1)}, bf16[80,256]{1,0:T(8,128)(2,1)S(1)}, u32[]{:S(2)}, u32[]{:S(2)}) collective-permute-start(bf16[80,256]{1,0:T(8,128)(2,1)S(1)} %inner.1.refs_0_.inner_ref), channel_id=1, source_target_pairs={{2,0},{0,2},{3,1},{1,3},{6,4},{4,6},{7,5},{5,7},{10,8},{8,10},{11,... | collective-permute-start | bytes 122888 | tf_op jit(solution)/shard_map/ppermute | solution.py:499
  6.7 0.5 %collective-permute-done.1.message_ref = bf16[128,256]{1,0:T(8,128)(2,1)S(1)} collective-permute-done((bf16[128,256]{1,0:T(8,128)(2,1)S(1)}, bf16[128,256]{1,0:T(8,128)(2,1)S(1)}, u32[]{:S(2)}, u32[]{:S(2)}) %collective-permute-start.1) | collective-permute-done | bytes 65568 | tf_op jit(solution)/shard_map/ppermute | solution.py:485
  7.2 0.5 %side_a.1.refs_1_.first_ref = bf16[112,256]{1,0:T(8,128)(2,1)S(1)} custom-call(f32[2,64,256]{2,1,0:T(8,128)S(1)} %get-tuple-element.10.image_ref, f32[2,64,256]{2,1,0:T(8,128)S(1)} %bitcast.6, f32[8,64]{1,0:T(8,128)S(1)} %get-tuple-element.11.taps_ref, s32[1,64]{1,0:T(1,128)S(1)} %get-tuple-element.12.offsets_ref, ...), custom_call_target="tpu_custom_call" | custom-call | tf_op jit(solution)/shard_map/side_a/pallas_call | solution.py:514
  7.7 0.0 copy-start.1
  7.7 1.8 %collective-permute-start.4 = (bf16[112,256]{1,0:T(8,128)(2,1)S(1)}, bf16[112,256]{1,0:T(8,128)(2,1)S(1)}, u32[]{:S(2)}, u32[]{:S(2)}) collective-permute-start(bf16[112,256]{1,0:T(8,128)(2,1)S(1)} %side_a.1.refs_1_.first_ref), channel_id=1, source_target_pairs={{2,0},{0,2},{3,1},{1,3},{6,4},{4,6},{7,5},{5,7},{10,8},{8,10},{11,... | collective-permute-start | bytes 172040 | tf_op jit(solution)/shard_map/ppermute | solution.py:499
  9.5 0.0 collective-permute-done.3.refs_0_.refs_1_
  9.5 0.0 collective-permute-done.2.message_ref
  9.5 0.5 %side_b.1.second_ref = bf16[112,256]{1,0:T(8,128)(2,1)S(1)} custom-call(f32[2,64,256]{2,1,0:T(8,128)S(1)} %get-tuple-element.10.image_ref, f32[2,64,256]{2,1,0:T(8,128)S(1)} %bitcast.7, f32[8,64]{1,0:T(8,128)S(1)} %get-tuple-element.11.taps_ref, s32[1,64]{1,0:T(1,128)S(1)} %get-tuple-element.12.offsets_ref, ...), custom_call_target="tpu_custom_call" | custom-call | tf_op jit(solution)/shard_map/side_b/pallas_call | solution.py:514
  10.0 1.2 %collective-permute-start.5 = (bf16[112,256]{1,0:T(8,128)(2,1)S(1)}, bf16[112,256]{1,0:T(8,128)(2,1)S(1)}, u32[]{:S(2)}, u32[]{:S(2)}) collective-permute-start(bf16[112,256]{1,0:T(8,128)(2,1)S(1)} %side_b.1.second_ref), channel_id=1, source_target_pairs={{2,0},{0,2},{3,1},{1,3},{6,4},{4,6},{7,5},{5,7},{10,8},{8,10},{11,... | collective-permute-start | bytes 172040 | tf_op jit(solution)/shard_map/ppermute | solution.py:499
  11.2 0.0 copy-done.1
  11.2 0.1 copy.7.match_ref
  11.3 0.0 copy-done
  11.3 2.2 %filter_own.1.filtered_own_ref = f32[2,64,256]{2,1,0:T(8,128)S(1)} custom-call(bf16[960,256]{1,0:T(8,128)(2,1)S(1)} %copy-done, bf16[112,256]{1,0:T(8,128)(2,1)S(1)} %side_a.1.refs_1_.first_ref, bf16[80,256]{1,0:T(8,128)(2,1)S(1)} %inner.1.refs_0_.inner_ref, bf16[112,256]{1,0:T(8,128)(2,1)S(1)} %side_b.1.second_ref), custom_call_target="tpu_custom_call" | custom-call | tf_op jit(solution)/shard_map/filter_own/pallas_call | solution.py:521
  13.5 0.0 collective-permute-done.4.refs_0_
  13.6 1.2 %filter_first.1.refs_3_ = f32[64,256]{1,0:T(8,128)S(1)} custom-call(bf16[960,256]{1,0:T(8,128)(2,1)S(1)} %copy-done, bf16[112,256]{1,0:T(8,128)(2,1)S(1)} %side_a.1.refs_1_.first_ref, bf16[80,256]{1,0:T(8,128)(2,1)S(1)} %inner.1.refs_0_.inner_ref, bf16[112,256]{1,0:T(8,128)(2,1)S(1)} %collective-permute-done.4.refs_0_, ...), custom_call_target="tpu_custom_call" | custom-call | tf_op jit(solution)/shard_map/filter_first/pallas_call | solution.py:531
  14.7 0.0 collective-permute-done.5.refs_2_
  14.7 3.1 %filter_rest.1 = f32[3,2,1,64,256]{4,3,2,1,0:T(8,128)} custom-call(s32[3,2]{1,0:T(4,128)S(1)} %copy.7.match_ref, bf16[960,256]{1,0:T(8,128)(2,1)S(1)} %copy-done, f32[2,64,256]{2,1,0:T(8,128)S(1)} %filter_own.1.filtered_own_ref, bf16[112,256]{1,0:T(8,128)(2,1)S(1)} %side_a.1.refs_1_.first_ref, bf16[80,256]{1,0:T(8,128)(2,1)S(1)} %inner.1.refs_0_.inner_ref, ...), custom_call_target="tpu_custom_call" | custom-call | tf_op jit(solution)/shard_map/filter_rest/pallas_call | solution.py:541
Async XLA Ops:
  0.0 1.6 %collective-permute-start = (f32[2,1,64,256]{3,2,0,1:T(8,128)}, f32[2,1,64,256]{3,2,0,1:T(8,128)S(1)}, u32[]{:S(2)}, u32[]{:S(2)}) collective-permute-start(f32[2,1,64,256]{3,2,0,1:T(8,128)} %bitcast.8), channel_id=1, source_target_pairs={{0,1},{1,0},{2,3},{3,2},{4,5},{5,4},{6,7},{7,6},{8,9},{9,8},{10,11... | collective-permute-start | bytes 393224 | tf_op jit(solution)/shard_map/ppermute | solution.py:450
  1.8 5.4 %collective-permute-start.1 = (bf16[128,256]{1,0:T(8,128)(2,1)S(1)}, bf16[128,256]{1,0:T(8,128)(2,1)S(1)}, u32[]{:S(2)}, u32[]{:S(2)}) collective-permute-start(bf16[128,256]{1,0:T(8,128)(2,1)S(1)} %get-tuple-element.13), channel_id=1, source_target_pairs={{0,4},{1,5},{4,0},{5,1},{8,12},{9,13},{12,8},{13,9},{2,6},{3,7},{6... | collective-permute-start | bytes 196616 | tf_op jit(solution)/shard_map/ppermute | solution.py:485
  4.8 4.7 %collective-permute-start.2 = (bf16[128,256]{1,0:T(8,128)(2,1)S(1)}, bf16[128,256]{1,0:T(8,128)(2,1)S(1)}, u32[]{:S(2)}, u32[]{:S(2)}) collective-permute-start(bf16[128,256]{1,0:T(8,128)(2,1)S(1)} %get-tuple-element.14), channel_id=1, source_target_pairs={{0,1},{1,0},{4,8},{5,9},{8,4},{9,5},{12,13},{13,12},{2,3},{3,2},{6... | collective-permute-start | bytes 196616 | tf_op jit(solution)/shard_map/ppermute | solution.py:485
  5.2 6.1 %copy-start = (bf16[960,256]{1,0:T(8,128)(2,1)S(1)}, bf16[960,256]{1,0:T(8,128)(2,1)}, u32[]{:S(2)}) copy-start(bf16[960,256]{1,0:T(8,128)(2,1)} %constant.2.clone.table_ref) | copy-start | bytes 1474564
  5.2 4.3 %collective-permute-start.3 = (bf16[80,256]{1,0:T(8,128)(2,1)S(1)}, bf16[80,256]{1,0:T(8,128)(2,1)S(1)}, u32[]{:S(2)}, u32[]{:S(2)}) collective-permute-start(bf16[80,256]{1,0:T(8,128)(2,1)S(1)} %inner.1.refs_0_.inner_ref), channel_id=1, source_target_pairs={{2,0},{0,2},{3,1},{1,3},{6,4},{4,6},{7,5},{5,7},{10,8},{8,10},{11,... | collective-permute-start | bytes 122888 | tf_op jit(solution)/shard_map/ppermute | solution.py:499
  7.7 3.5 %copy-start.1 = (s32[3,2]{0,1:T(2,128)S(1)}, s32[3,2]{0,1:T(2,128)}, u32[]{:S(2)}) copy-start(s32[3,2]{0,1:T(2,128)} %param.8) | copy-start | bytes 76
  7.7 5.9 %collective-permute-start.4 = (bf16[112,256]{1,0:T(8,128)(2,1)S(1)}, bf16[112,256]{1,0:T(8,128)(2,1)S(1)}, u32[]{:S(2)}, u32[]{:S(2)}) collective-permute-start(bf16[112,256]{1,0:T(8,128)(2,1)S(1)} %side_a.1.refs_1_.first_ref), channel_id=1, source_target_pairs={{2,0},{0,2},{3,1},{1,3},{6,4},{4,6},{7,5},{5,7},{10,8},{8,10},{11,... | collective-permute-start | bytes 172040 | tf_op jit(solution)/shard_map/ppermute | solution.py:499
  10.0 4.7 %collective-permute-start.5 = (bf16[112,256]{1,0:T(8,128)(2,1)S(1)}, bf16[112,256]{1,0:T(8,128)(2,1)S(1)}, u32[]{:S(2)}, u32[]{:S(2)}) collective-permute-start(bf16[112,256]{1,0:T(8,128)(2,1)S(1)} %side_b.1.second_ref), channel_id=1, source_target_pairs={{2,0},{0,2},{3,1},{1,3},{6,4},{4,6},{7,5},{5,7},{10,8},{8,10},{11,... | collective-permute-start | bytes 172040 | tf_op jit(solution)/shard_map/ppermute | solution.py:499

commit v9 on v7

v9 whole, which is shorter than its diff:
```python
import functools
import math

import jax
import jax.numpy as jnp
import numpy as np
from jax import lax
from jax.experimental import pallas as pl
from jax.experimental.pallas import tpu as pltpu
from jax.sharding import PartitionSpec as P

TAPS = 8
SHIFT_MAX = 12
PATCH = 64
HALF = PATCH // 2
RIM = SHIFT_MAX + TAPS // 2
REACH = HALF + RIM
LANES = 128
EDGE_STEP = 16
VMEM_LIMIT = 48 * 1024 * 1024

VMEM = pl.BlockSpec(memory_space=pltpu.VMEM)
SMEM = pl.BlockSpec(memory_space=pltpu.SMEM)
HBM = pl.BlockSpec(memory_space=pltpu.HBM)
PARAMS = pltpu.CompilerParams(vmem_limit_bytes=VMEM_LIMIT)


def fourier_table(sine_sign, table_scale):
    freq_ids = np.arange(PATCH)
    phase_ids = (freq_ids[:, None] * freq_ids[None, :]) % PATCH
    angles = phase_ids * (2.0 * math.pi / PATCH)
    cosine = np.cos(angles) * table_scale
    sine_part = np.sin(angles) * (sine_sign * table_scale)
    top = np.concatenate([cosine, -sine_part], axis=1)
    bottom = np.concatenate([sine_part, cosine], axis=1)
    return np.concatenate([top, bottom], axis=0).astype(np.float32)


def paired(table):
    split = table.reshape(2, PATCH, 2, PATCH)
    wide = np.zeros((2, 2, PATCH, 2, 2, PATCH), np.float32)
    for slot in range(2):
        wide[:, slot, :, :, slot, :] = split
    return wide.reshape(4 * PATCH, 4 * PATCH)


def line_table(forward, row_patches):
    wide_lines = (row_patches + 1) * HALF
    table = np.zeros((row_patches, 2 * PATCH, 2, wide_lines), np.float32)
    transposed = forward.T.reshape(2 * PATCH, 2, PATCH)
    for row in range(row_patches):
        table[row, :, :, row * HALF : row * HALF + PATCH] = transposed
    return table.reshape(row_patches * 2 * PATCH, 2 * wide_lines)


def window_table():
    window = np.sin(math.pi * (np.arange(PATCH) + 0.5) / PATCH) ** 2
    return np.tile(np.outer(window, window), (2, 2)).astype(np.float32)


def ring_table():
    ring = np.zeros((LANES, LANES), np.float32)
    for lane in range(LANES):
        base = lane // PATCH * PATCH
        for step in (-1, 0, 1):
            ring[base + (lane + step) % PATCH, lane] = 1.0
    return ring


def edge_of(other_ref, part, side, lines):
    width = other_ref.shape[2]
    return jnp.where(
        side == 0, other_ref[part, lines, :HALF], other_ref[part, lines, width - HALF :]
    )


def load_kernel(*refs):
    count = (len(refs) - 1) // 2
    copies = [
        pltpu.make_async_copy(refs[i], refs[count + i], refs[-1].at[i]) for i in range(count)
    ]
    for copy in copies:
        copy.start()
    for copy in copies:
        copy.wait()


def pack_kernel(image_ref, other_ref, taps_ref, offsets_ref, even_ref, odd_ref):
    lines = image_ref.shape[1]
    width = image_ref.shape[2]
    side = lax.axis_index("rg")
    taps = taps_ref[...]
    taps_high = taps.astype(jnp.bfloat16).astype(jnp.float32)
    taps_low = taps - taps_high
    shifts = jnp.broadcast_to(offsets_ref[...].astype(jnp.float32), (TAPS, lines))

    def write(out_ref, line_start, tap_start):
        rows = slice(line_start, line_start + REACH)
        for part in range(2):
            cut = slice(part * REACH, (part + 1) * REACH)
            out_ref[cut, :] = image_ref[part, rows, :].astype(jnp.bfloat16)
        edges = jnp.concatenate([edge_of(other_ref, part, side, rows) for part in range(2)], axis=0)
        cut = slice(tap_start, tap_start + HALF)
        block = jnp.concatenate([taps_high[:, cut], taps_low[:, cut], shifts[:, cut]], axis=1)
        block = jnp.concatenate([block, jnp.zeros((HALF - TAPS, 3 * HALF), jnp.float32)], axis=0)
        cuts = [edges[i * HALF : (i + 1) * HALF] for i in range(3)]
        filler = jnp.zeros((HALF, width - 6 * HALF), jnp.float32)
        block = jnp.concatenate([block, *cuts, filler], axis=1)
        out_ref[2 * REACH :, :] = block.astype(jnp.bfloat16)

    parity = lax.rem(lax.axis_index("az"), 2)

    @pl.when(parity == 0)
    def _():
        write(even_ref, lines - REACH, lines - HALF)
        write(odd_ref, 0, 0)

    @pl.when(parity == 1)
    def _():
        write(even_ref, 0, 0)
        write(odd_ref, lines - REACH, lines - HALF)


def is_above(turn):
    return lax.rem(lax.axis_index("az") + turn, 2) == 1


def band(taps, shift, first_line, source):
    count, lines = source.shape
    tap_ids = source - (lax.broadcasted_iota(jnp.int32, (count, lines), 1) + first_line)
    tap_ids = tap_ids - shift + (TAPS // 2 - 1)
    total = jnp.zeros((count, lines), jnp.float32)
    for tap in range(TAPS):
        total = jnp.where(tap_ids == tap, taps[tap : tap + 1, :], total)
    return total


def high_low(value):
    high = value.astype(jnp.bfloat16)
    low = (value - high.astype(jnp.float32)).astype(jnp.bfloat16)
    return jnp.concatenate([high, low], axis=0)


def apply_band(weights, rows):
    over_rows = (((0,), (0,)), ((), ()))
    rows = jnp.concatenate([rows, rows], axis=0)
    return lax.dot_general(high_low(weights), rows, over_rows, preferred_element_type=jnp.float32)


def edge_rows(lines, width):
    rows = EDGE_STEP
    while 2 * lines // rows * HALF > width:
        rows *= 2
    return rows


def piece_shape(lines, width):
    return jax.ShapeDtypeStruct((2 * lines + edge_rows(lines, width), width), jnp.bfloat16)


def write_piece(out_ref, parts, width):
    lines = parts[0].shape[0]
    rows = edge_rows(lines, width)
    for part, value in enumerate(parts):
        out_ref[part * lines : (part + 1) * lines, :] = value[:, :width].astype(jnp.bfloat16)
    edges = jnp.concatenate([value[:, width:] for value in parts], axis=0)
    slots = [edges[at : at + rows] for at in range(0, 2 * lines, rows)]
    slots.append(jnp.zeros((rows, width - len(slots) * HALF), jnp.float32))
    out_ref[2 * lines :, :] = jnp.concatenate(slots, axis=1).astype(jnp.bfloat16)


def read_piece(ref, lines):
    rows = ref.shape[0] - 2 * lines
    block = ref[2 * lines :, :].astype(jnp.float32)
    slots = [block[:, i * HALF : (i + 1) * HALF] for i in range(2 * lines // rows)]
    edges = jnp.concatenate(slots, axis=0)
    tiles = ref[: 2 * lines, :].astype(jnp.float32)
    return [(v[:lines], v[lines:]) for v in (tiles, edges)]


def inner_kernel(image_ref, other_ref, taps_ref, offsets_ref, out_ref):
    lines = image_ref.shape[1]
    width = image_ref.shape[2]
    side = lax.axis_index("rg")
    cut = slice(RIM, lines - RIM)
    source = lax.broadcasted_iota(jnp.int32, (lines, lines - 2 * RIM), 0)
    weights = band(taps_ref[:, cut], offsets_ref[:, cut], RIM, source)
    weights = jnp.concatenate([weights, weights], axis=0)
    for part in range(2):
        edge = edge_of(other_ref, part, side, slice(0, lines))
        rows = high_low(jnp.concatenate([image_ref[part], edge], axis=1))
        out_ref[part] = apply_band(weights, rows)


def side_kernel(turn, image_ref, other_ref, taps_ref, offsets_ref, message_ref, *refs):
    out_ref = refs[-1]
    lines = image_ref.shape[1]
    width = image_ref.shape[2]
    side = lax.axis_index("rg")
    place = lax.axis_index("az")
    above = is_above(turn)
    alone = jnp.where(above, place == 0, place == lax.axis_size("az") - 1)
    message = message_ref[...]
    message = jnp.where(alone, jnp.zeros_like(message), message)
    block = message[2 * REACH :, :].astype(jnp.float32)
    head = block[:TAPS]
    rim_taps = head[:, :HALF] + head[:, HALF : 2 * HALF]
    rim_shift = head[:1, 2 * HALF : 3 * HALF]
    rim_edges = [block[:, i * HALF : (i + 1) * HALF] for i in range(3, 6)]
    rim_edges = jnp.concatenate(rim_edges, axis=0).astype(jnp.bfloat16)

    def per_line(own, rim):
        upper = jnp.concatenate([rim, own[:, :RIM]], axis=1)
        lower = jnp.concatenate([own[:, lines - RIM :], rim], axis=1)
        return jnp.where(above, upper, lower)

    taps = per_line(taps_ref[...], rim_taps)
    shift = per_line(offsets_ref[...].astype(jnp.float32), rim_shift).astype(jnp.int32)
    first_line = jnp.where(above, -HALF, lines - RIM)
    near = 2 * RIM
    first_own = jnp.where(above, 0, lines - near)
    first_rim = jnp.where(above, -REACH, lines)
    source = lax.broadcasted_iota(jnp.int32, (REACH + near, REACH), 0)
    source = jnp.where(source < REACH, source + first_rim, source - REACH + first_own)
    weights = band(taps, shift, first_line, source)
    weights = jnp.concatenate([weights, weights[REACH:]], axis=0)
    parts = []
    for part in range(2):
        upper, lower = slice(0, near), slice(lines - near, lines)
        edge = jnp.where(
            above, edge_of(other_ref, part, side, upper), edge_of(other_ref, part, side, lower)
        )
        own = jnp.where(above, image_ref[part, upper, :], image_ref[part, lower, :])
        own = high_low(jnp.concatenate([own, edge], axis=1))
        cut = slice(part * REACH, (part + 1) * REACH)
        rim = jnp.concatenate([message[cut, :], rim_edges[cut]], axis=1)
        total = apply_band(weights, jnp.concatenate([rim, own], axis=0))
        if turn == 0:
            total = jnp.concatenate([total, refs[0][part]], axis=0)
        parts.append(total)
    write_piece(out_ref, parts, width)


def cross(own_parts, other_parts):
    own_real, own_imag = own_parts
    other_real, other_imag = other_parts
    real = own_real * other_real + own_imag * other_imag
    imag = own_imag * other_real - own_real * other_imag
    return real, imag


def tile_of(first_ref, second_ref, lines):
    first = read_piece(first_ref, REACH + lines - 2 * RIM)
    second = read_piece(second_ref, REACH)
    return [
        tuple(jnp.concatenate([a, b], axis=0) for a, b in zip(*which))
        for which in zip(first, second)
    ]


def filtered_of(own_refs, other_refs, table_ref, spectrum_ref, lines):
    width = own_refs[0].shape[1]
    wide = lines + 2 * HALF
    row_patches = lines // HALF + 1
    side = lax.axis_index("rg")
    line_table_of, forward, inverse, back, ring, window = split_tables(table_ref, row_patches)
    own_tile, own_edge = tile_of(*own_refs, lines)
    other_tile, other_edge = tile_of(*other_refs, lines)
    mid = jnp.concatenate(cross(own_tile, other_tile), axis=0)
    rim = jnp.concatenate(cross(own_edge, other_edge), axis=0)
    before = jnp.where(side == 0, 0.0, rim)
    after = jnp.where(side == 0, rim, 0.0)
    filler = jnp.zeros((2 * wide, LANES - 2 * HALF), jnp.float32)
    shifted = jnp.concatenate([before, mid, after, filler], axis=1).astype(jnp.bfloat16)
    both = jnp.concatenate([mid.astype(jnp.bfloat16), shifted], axis=1)
    chunks = both.shape[1] // LANES
    line_spectra = jnp.dot(line_table_of, both, preferred_element_type=jnp.float32)
    line_spectra = line_spectra.astype(jnp.bfloat16)
    pieces = []
    for row in range(row_patches):
        top = row * 2 * PATCH
        for chunk in range(chunks):
            cut = slice(chunk * LANES, (chunk + 1) * LANES)
            real = line_spectra[top : top + PATCH, cut]
            imag = line_spectra[top + PATCH : top + 2 * PATCH, cut]
            pieces.append(jnp.concatenate([real, imag], axis=1))
    patches = jnp.concatenate(pieces, axis=0)
    spectrum_ref[...] = jnp.dot(patches, forward, preferred_element_type=jnp.float32)
    powers = []
    for block in range(row_patches * chunks):
        rows = slice(block * PATCH, (block + 1) * PATCH)
        real = spectrum_ref[rows, :LANES]
        imag = spectrum_ref[rows, LANES:]
        power = real * real + imag * imag
        power = power + pltpu.roll(power, 1, 0) + pltpu.roll(power, PATCH - 1, 0)
        powers.append(power.astype(jnp.bfloat16))
    smooth = jnp.dot(jnp.concatenate(powers, axis=0), ring, preferred_element_type=jnp.float32)
    gain = lax.rsqrt(lax.rsqrt(smooth * (1.0 / (9.0 * PATCH * PATCH)) + 1.0))
    shaped = jnp.concatenate(
        [spectrum_ref[:, :LANES] * gain, spectrum_ref[:, LANES:] * gain], axis=1
    ).astype(jnp.bfloat16)
    range_back = jnp.dot(shaped, inverse, preferred_element_type=jnp.float32)
    range_back = range_back.astype(jnp.bfloat16)
    window = jnp.concatenate([window] * chunks, axis=1)
    totals = [[None] * (row_patches - 1) for _ in range(2)]
    for row in range(row_patches):
        stacked = []
        for chunk in range(chunks):
            top = (row * chunks + chunk) * PATCH
            block = range_back[top : top + PATCH]
            stacked.append(jnp.concatenate([block[:, :LANES], block[:, LANES:]], axis=0))
        stacked = jnp.concatenate(stacked, axis=1)
        patch_out = jnp.dot(back, stacked, preferred_element_type=jnp.float32) * window
        for part in range(2):
            upper = patch_out[part * PATCH : part * PATCH + HALF]
            lower = patch_out[part * PATCH + HALF : (part + 1) * PATCH]
            if row > 0:
                totals[part][row - 1] = totals[part][row - 1] + upper
            if row < row_patches - 1:
                totals[part][row] = lower
    total = jnp.concatenate([block for part in totals for block in part], axis=0)
    return total[:, :width] + total[:, width + HALF : 2 * width + HALF]


def own_kernel(table_ref, first_ref, second_ref, out_ref, spectrum_ref):
    own = (first_ref, second_ref)
    lines = out_ref.shape[1]
    result = filtered_of(own, own, table_ref, spectrum_ref, lines)
    for part in range(2):
        out_ref[part] = result[part * lines : (part + 1) * lines]


def other_kernel(match_ref, table_ref, filtered_own_ref, first_ref, second_ref, *refs):
    out_ref, result_ref, spectrum_ref, sems = refs[-4:]
    match_count, _, _, lines, _ = out_ref.shape
    date = lax.axis_index("date")
    dates = match_ref.shape[1]

    def slot_of(match):
        return lax.rem(match_ref[match, date] - date + dates, dates)

    def copy_of(match, source):
        return pltpu.make_async_copy(source, out_ref.at[match, :, 0], sems.at[match])

    for match in range(match_count):

        @pl.when(slot_of(match) == 0)
        def _():
            copy_of(match, filtered_own_ref).start()

    for slot in range(1, dates):
        other = refs[2 * slot - 2 : 2 * slot]
        result = filtered_of((first_ref, second_ref), other, table_ref, spectrum_ref, lines)
        for part in range(2):
            result_ref[slot - 1, part] = result[part * lines : (part + 1) * lines]
    for match in range(match_count):
        slot = slot_of(match)

        @pl.when(slot > 0)
        def _():
            copy_of(match, result_ref.at[lax.max(slot - 1, 0)]).start()

    for match in range(match_count):
        copy_of(match, filtered_own_ref).wait()


def all_tables(row_patches):
    forward = fourier_table(1.0, 1.0)
    inverse = fourier_table(-1.0, 1.0 / PATCH)
    back = inverse.reshape(2, PATCH, 2, PATCH).transpose(2, 3, 0, 1).reshape(2 * PATCH, 2 * PATCH)
    window = window_table()[:PATCH, :PATCH]
    splits = []
    for _ in range(3):
        splits.append(window.astype(jnp.bfloat16).astype(np.float32))
        window = window - splits[-1]
    natural = np.arange((row_patches + 1) * HALF)
    wide = len(natural)
    inner = natural[REACH : wide - REACH]
    orders = [
        np.concatenate([natural[:REACH], inner, natural[wide - REACH :]]),
        np.concatenate([natural[wide - REACH :], inner, natural[:REACH]]),
    ]
    lines = line_table(forward, row_patches).reshape(-1, 2, wide)
    rows = [lines[:, :, order].reshape(-1, 2 * wide) for order in orders] + [
        paired(forward),
        paired(inverse),
        np.concatenate([back, ring_table()], axis=1),
        np.concatenate([*splits, np.zeros_like(window)], axis=1),
    ]
    return np.concatenate(rows, axis=0).astype(jnp.bfloat16)


def split_tables(table_ref, row_patches):
    size = row_patches * 2 * PATCH
    start = pl.multiple_of(jnp.where(is_above(0), 0, size), size)
    line_table_of = table_ref[pl.ds(start, size), :]
    at = 2 * size
    forward = table_ref[at : at + 4 * PATCH, :]
    at += 4 * PATCH
    inverse = table_ref[at : at + 4 * PATCH, :]
    at += 4 * PATCH
    back = table_ref[at : at + LANES, :LANES]
    ring = table_ref[at : at + LANES, LANES:]
    at += LANES
    splits = table_ref[at : at + PATCH, :].astype(jnp.float32)
    window = splits[:, :PATCH] + splits[:, PATCH : 2 * PATCH] + splits[:, 2 * PATCH : 3 * PATCH]
    window = jnp.concatenate([window, window], axis=1)
    window = jnp.concatenate([window, window], axis=0)
    return line_table_of, forward, inverse, back, ring, window


def per_device(image_stack, tap_weights, offsets, matchings):
    _, _, lines, width = image_stack.shape
    match_count = matchings.shape[0]
    other = lax.ppermute(image_stack, "rg", [(0, 1), (1, 0)]).reshape(2, lines, width)
    arguments = (
        image_stack.reshape(2, lines, width),
        tap_weights.reshape(TAPS, lines),
        offsets,
    )
    raw = pl.pallas_call(
        load_kernel,
        out_shape=tuple(pltpu.VMEM(a.shape, a.dtype) for a in arguments),
        in_specs=[HBM] * 3,
        out_specs=(VMEM,) * 3,
        scratch_shapes=[pltpu.SemaphoreType.DMA((3,))],
        compiler_params=PARAMS,
        name="load",
    )(*(pltpu.with_memory_space_constraint(a, pltpu.HBM) for a in arguments))
    raw = (raw[0], other, *raw[1:])
    message = jax.ShapeDtypeStruct((2 * REACH + HALF, width), jnp.bfloat16)
    messages = pl.pallas_call(
        pack_kernel,
        out_shape=(message, message),
        in_specs=[VMEM] * 4,
        out_specs=(VMEM, VMEM),
        compiler_params=PARAMS,
        name="pack",
    )(*raw)
    peers = lax.axis_size("az")

    def swapped(value, start):
        paired_with = {i: i + 1 for i in range(start, peers - 1, 2)}
        paired_with.update({j: i for i, j in paired_with.items()})
        pairs = [
            (2 * i + core, 2 * paired_with[i] + core if i in paired_with else 2 * i + 1 - core)
            for i in range(peers)
            for core in range(2)
        ]
        return lax.ppermute(value, ("az", "rg"), pairs)

    messages = [swapped(messages[turn], turn) for turn in range(2)]
    inner = pl.pallas_call(
        inner_kernel,
        out_shape=jax.ShapeDtypeStruct((2, lines - 2 * RIM, width + HALF), jnp.float32),
        in_specs=[VMEM] * 4,
        out_specs=VMEM,
        compiler_params=PARAMS,
        name="inner",
    )(*raw)
    own = []
    for turn in range(2):
        made = (*own, inner)[:1] if turn else (inner,)
        call = pl.pallas_call(
            functools.partial(side_kernel, turn),
            out_shape=piece_shape(REACH + (0 if turn else lines - 2 * RIM), width),
            in_specs=[VMEM] * (5 + len(made)),
            out_specs=VMEM,
            compiler_params=PARAMS,
            name="side_" + "ab"[turn],
        )
        own.append(call(*raw, messages[turn], *made))
    dates = lax.axis_size("date")

    def from_date(piece, slot):
        return lax.ppermute(piece, "date", [((i + slot) % dates, i) for i in range(dates)])

    others = [from_date(piece, slot) for slot in range(1, dates) for piece in own]
    row_patches = lines // HALF + 1
    chunks = (width + width + LANES) // LANES
    tables = jnp.asarray(all_tables(row_patches))
    spectrum = pltpu.VMEM((row_patches * chunks * PATCH, 2 * LANES), jnp.float32)
    filtered_own = pl.pallas_call(
        own_kernel,
        out_shape=jax.ShapeDtypeStruct((2, lines, width), jnp.float32),
        in_specs=[VMEM] * 3,
        out_specs=VMEM,
        scratch_shapes=[spectrum],
        compiler_params=PARAMS,
        name="filter_own",
    )(tables, *own)
    return pl.pallas_call(
        other_kernel,
        out_shape=jax.ShapeDtypeStruct((match_count, 2, 1, lines, width), jnp.float32),
        in_specs=[SMEM] + [VMEM] * (4 + len(others)),
        out_specs=HBM,
        scratch_shapes=[
            pltpu.VMEM((dates - 1, 2, lines, width), jnp.float32),
            spectrum,
            pltpu.SemaphoreType.DMA((match_count,)),
        ],
        compiler_params=PARAMS,
        name="filter_other",
    )(matchings, tables, filtered_own, *own, *others)


def solution(mesh):
    placed = (
        P(None, ("parts", "date"), "az", "rg"),
        P(None, ("parts", "date"), "az"),
        P(("parts", "date"), "az"),
        P(),
    )
    return jax.shard_map(
        per_device,
        mesh=mesh,
        in_specs=placed,
        out_specs=P(None, None, ("parts", "date"), "az", "rg"),
        check_vma=False,
    )
```

time: 16.5 us -> 16.9 us (1.024)
  starting transfers between devices: 5.29 us -> 5.55 us
    ppermute x1 -> x2, waiting for transfers between devices: 2.14 us -> 2.6 us  [from_date(): lax.ppermute(piece, 'date', [((i + slot) % dates, i) for i in range(dates)])]
    ppermute x2, waiting for transfers between devices: 2.4 us -> 2.09 us  [swapped(): return lax.ppermute(value, ('az', 'rg'), pairs)]
    pallas_call x2 -> x4, Pallas kernels: 2.2 us -> 2.48 us  [the longest x1 1.23 us: per_device(): pl.pallas_call(own_kernel, out_shape=jax.ShapeDtypeStruct((2, lines, widt...]
    ppermute x1 -> x2, starting transfers between devices: 1.84 us -> 2.1 us  [from_date(): lax.ppermute(piece, 'date', [((i + slot) % dates, i) for i in range(dates)])]
    pallas_call x1, Pallas kernels: 2.73 us -> 2.49 us  [per_device(): pl.pallas_call(other_kernel, out_shape=jax.ShapeDtypeStruct((match_count,...]
  transfers between devices with their start and end apart: 4 -> 5, of which waited for: 3 -> 3; matrix products, arithmetic and copies ran while one was open for 1% -> 1% of each run, Pallas kernels for 14% -> 20%
where the time goes in v9:
time: 16.9 us; the launch traced here: 16.7 us
  Pallas kernels  6.06 us (36%)
  starting transfers between devices  5.55 us (33%)
  waiting for transfers between devices  4.95 us (29%)
    ppermute x2, starting transfers between devices, swapped(): return lax.ppermute(value, ('az', 'rg'), pairs)  3 us
    ppermute x2, waiting for transfers between devices, from_date(): lax.ppermute(piece, 'date', [((i + slot) % dates, i) for i in range(dates)])  2.6 us
    pallas_call x1, Pallas kernels, per_device(): pl.pallas_call(other_kernel, out_shape=jax.ShapeDtypeStruct((match_count,...  2.49 us
    ppermute x2, starting transfers between devices, from_date(): lax.ppermute(piece, 'date', [((i + slot) % dates, i) for i in range(dates)])  2.1 us
    ppermute x2, waiting for transfers between devices, swapped(): return lax.ppermute(value, ('az', 'rg'), pairs)  2.09 us
    pallas_call x1, Pallas kernels, per_device(): pl.pallas_call(own_kernel, out_shape=jax.ShapeDtypeStruct((2, lines, widt...  1.23 us
    pallas_call x2, Pallas kernels, per_device(): own.append(call(*raw, messages[turn], *made))  0.94 us
    pallas_call x1, Pallas kernels, per_device(): pl.pallas_call(load_kernel, out_shape=tuple((pltpu.VMEM(a.shape, a.dtype)...  0.93 us
  transfers between devices with their start and end apart: 5, of which 3 were waited for; matrix products, arithmetic and copies ran while one was open for 1% of the time, Pallas kernels for 20%

profile of v9, /device:TPU:0, one launch (start us, length us, event | category | flops | bytes accessed | tf_op | source)
XLA Modules:
  0.0 16.7 jit_solution(9973330841983748535)
XLA Ops:
  0.0 0.5 %collective-permute-start = (f32[2,1,64,256]{3,2,0,1:T(8,128)}, f32[2,1,64,256]{3,2,0,1:T(8,128)S(1)}, u32[]{:S(2)}, u32[]{:S(2)}) collective-permute-start(f32[2,1,64,256]{3,2,0,1:T(8,128)} %bitcast.8), channel_id=1, source_target_pairs={{0,1},{1,0},{2,3},{3,2},{4,5},{5,4},{6,7},{7,6},{8,9},{9,8},{10,11... | collective-permute-start | bytes 393224 | tf_op jit(solution)/shard_map/ppermute | solution.py:415
  0.5 0.9 %load.1 = (f32[2,64,256]{2,1,0:T(8,128)S(1)}, f32[8,64]{1,0:T(8,128)S(1)}, s32[1,64]{1,0:T(1,128)S(1)}) custom-call(f32[2,64,256]{2,1,0:T(8,128)} %bitcast.9, f32[8,64]{1,0:T(8,128)} %bitcast.10, s32[1,64]{1,0:T(1,128)} %refs_2_.1), custom_call_target="tpu_custom_call" | custom-call | tf_op jit(solution)/shard_map/load/pallas_call | solution.py:421
  1.4 0.3 %collective-permute-done = f32[2,1,64,256]{3,2,0,1:T(8,128)S(1)} collective-permute-done((f32[2,1,64,256]{3,2,0,1:T(8,128)}, f32[2,1,64,256]{3,2,0,1:T(8,128)S(1)}, u32[]{:S(2)}, u32[]{:S(2)}) %collective-permute-start) | collective-permute-done | bytes 131104 | tf_op jit(solution)/shard_map/ppermute | solution.py:415
  1.7 0.2 pack.1
  1.8 0.0 copy-start
  1.8 3.0 %collective-permute-start.1 = (bf16[128,256]{1,0:T(8,128)(2,1)S(1)}, bf16[128,256]{1,0:T(8,128)(2,1)S(1)}, u32[]{:S(2)}, u32[]{:S(2)}) collective-permute-start(bf16[128,256]{1,0:T(8,128)(2,1)S(1)} %get-tuple-element.13), channel_id=1, source_target_pairs={{0,4},{1,5},{4,0},{5,1},{8,12},{9,13},{12,8},{13,9},{2,6},{3,7},{6... | collective-permute-start | bytes 196616 | tf_op jit(solution)/shard_map/ppermute | solution.py:450
  4.8 0.0 collective-permute-start.2
  4.8 0.3 %inner.1.refs_0_ = f32[2,32,288]{2,1,0:T(8,128)S(1)} custom-call(f32[2,64,256]{2,1,0:T(8,128)S(1)} %get-tuple-element.10.image_ref, f32[2,64,256]{2,1,0:T(8,128)S(1)} %bitcast.5, f32[8,64]{1,0:T(8,128)S(1)} %get-tuple-element.11.taps_ref, s32[1,64]{1,0:T(1,128)S(1)} %get-tuple-element.12.offsets_ref), custom_call_target="tpu_custom_call" | custom-call | tf_op jit(solution)/shard_map/inner/pallas_call | solution.py:453
  5.1 2.1 %collective-permute-done.1.message_ref = bf16[128,256]{1,0:T(8,128)(2,1)S(1)} collective-permute-done((bf16[128,256]{1,0:T(8,128)(2,1)S(1)}, bf16[128,256]{1,0:T(8,128)(2,1)S(1)}, u32[]{:S(2)}, u32[]{:S(2)}) %collective-permute-start.1) | collective-permute-done | bytes 65568 | tf_op jit(solution)/shard_map/ppermute | solution.py:450
  7.2 0.5 %side_a.1.refs_0_.first_ref = bf16[192,256]{1,0:T(8,128)(2,1)S(1)} custom-call(f32[2,64,256]{2,1,0:T(8,128)S(1)} %get-tuple-element.10.image_ref, f32[2,64,256]{2,1,0:T(8,128)S(1)} %bitcast.6, f32[8,64]{1,0:T(8,128)S(1)} %get-tuple-element.11.taps_ref, s32[1,64]{1,0:T(1,128)S(1)} %get-tuple-element.12.offsets_ref, ...), custom_call_target="tpu_custom_call" | custom-call | tf_op jit(solution)/shard_map/side_a/pallas_call | solution.py:472
  7.7 0.0 copy-start.1
  7.7 1.8 %collective-permute-start.3 = (bf16[192,256]{1,0:T(8,128)(2,1)S(1)}, bf16[192,256]{1,0:T(8,128)(2,1)S(1)}, u32[]{:S(2)}, u32[]{:S(2)}) collective-permute-start(bf16[192,256]{1,0:T(8,128)(2,1)S(1)} %side_a.1.refs_0_.first_ref), channel_id=1, source_target_pairs={{2,0},{0,2},{3,1},{1,3},{6,4},{4,6},{7,5},{5,7},{10,8},{8,10},{11,... | collective-permute-start | bytes 294920 | tf_op jit(solution)/shard_map/ppermute | solution.py:476
  9.5 0.0 collective-permute-done.2.message_ref
  9.5 0.5 %side_b.1.second_ref = bf16[112,256]{1,0:T(8,128)(2,1)S(1)} custom-call(f32[2,64,256]{2,1,0:T(8,128)S(1)} %get-tuple-element.10.image_ref, f32[2,64,256]{2,1,0:T(8,128)S(1)} %bitcast.7, f32[8,64]{1,0:T(8,128)S(1)} %get-tuple-element.11.taps_ref, s32[1,64]{1,0:T(1,128)S(1)} %get-tuple-element.12.offsets_ref, ...), custom_call_target="tpu_custom_call" | custom-call | tf_op jit(solution)/shard_map/side_b/pallas_call | solution.py:472
  10.0 0.3 %collective-permute-start.4 = (bf16[112,256]{1,0:T(8,128)(2,1)S(1)}, bf16[112,256]{1,0:T(8,128)(2,1)S(1)}, u32[]{:S(2)}, u32[]{:S(2)}) collective-permute-start(bf16[112,256]{1,0:T(8,128)(2,1)S(1)} %side_b.1.second_ref), channel_id=1, source_target_pairs={{2,0},{0,2},{3,1},{1,3},{6,4},{4,6},{7,5},{5,7},{10,8},{8,10},{11,... | collective-permute-start | bytes 172040 | tf_op jit(solution)/shard_map/ppermute | solution.py:476
  10.3 0.0 copy-done.1
  10.3 0.1 copy.7.match_ref
  10.4 0.0 copy-done
  10.4 1.2 %filter_own.1.filtered_own_ref = f32[2,64,256]{2,1,0:T(8,128)S(1)} custom-call(bf16[1472,256]{1,0:T(8,128)(2,1)S(1)} %copy-done, bf16[192,256]{1,0:T(8,128)(2,1)S(1)} %side_a.1.refs_0_.first_ref, bf16[112,256]{1,0:T(8,128)(2,1)S(1)} %side_b.1.second_ref), custom_call_target="tpu_custom_call" | custom-call | tf_op jit(solution)/shard_map/filter_own/pallas_call | solution.py:483
  11.6 2.6 %collective-permute-done.4.refs_1_ = bf16[112,256]{1,0:T(8,128)(2,1)S(1)} collective-permute-done((bf16[112,256]{1,0:T(8,128)(2,1)S(1)}, bf16[112,256]{1,0:T(8,128)(2,1)S(1)}, u32[]{:S(2)}, u32[]{:S(2)}) %collective-permute-start.4) | collective-permute-done | bytes 57376 | tf_op jit(solution)/shard_map/ppermute | solution.py:476
  14.2 0.0 collective-permute-done.3.refs_0_
  14.2 2.5 %filter_other.1 = f32[3,2,1,64,256]{4,3,2,1,0:T(8,128)} custom-call(s32[3,2]{1,0:T(4,128)S(1)} %copy.7.match_ref, bf16[1472,256]{1,0:T(8,128)(2,1)S(1)} %copy-done, f32[2,64,256]{2,1,0:T(8,128)S(1)} %filter_own.1.filtered_own_ref, bf16[192,256]{1,0:T(8,128)(2,1)S(1)} %side_a.1.refs_0_.first_ref, bf16[112,256]{1,0:T(8,128)(2,1)S(1)} %side_b.1.second_ref, ...), custom_call_target="tpu_custom_call" | custom-call | tf_op jit(solution)/shard_map/filter_other/pallas_call | solution.py:492
Async XLA Ops:
  0.0 1.6 %collective-permute-start = (f32[2,1,64,256]{3,2,0,1:T(8,128)}, f32[2,1,64,256]{3,2,0,1:T(8,128)S(1)}, u32[]{:S(2)}, u32[]{:S(2)}) collective-permute-start(f32[2,1,64,256]{3,2,0,1:T(8,128)} %bitcast.8), channel_id=1, source_target_pairs={{0,1},{1,0},{2,3},{3,2},{4,5},{5,4},{6,7},{7,6},{8,9},{9,8},{10,11... | collective-permute-start | bytes 393224 | tf_op jit(solution)/shard_map/ppermute | solution.py:415
  1.8 8.6 %copy-start = (bf16[1472,256]{1,0:T(8,128)(2,1)S(1)}, bf16[1472,256]{1,0:T(8,128)(2,1)}, u32[]{:S(2)}) copy-start(bf16[1472,256]{1,0:T(8,128)(2,1)} %constant.2.clone.table_ref) | copy-start | bytes 2260996
  1.8 5.4 %collective-permute-start.1 = (bf16[128,256]{1,0:T(8,128)(2,1)S(1)}, bf16[128,256]{1,0:T(8,128)(2,1)S(1)}, u32[]{:S(2)}, u32[]{:S(2)}) collective-permute-start(bf16[128,256]{1,0:T(8,128)(2,1)S(1)} %get-tuple-element.13), channel_id=1, source_target_pairs={{0,4},{1,5},{4,0},{5,1},{8,12},{9,13},{12,8},{13,9},{2,6},{3,7},{6... | collective-permute-start | bytes 196616 | tf_op jit(solution)/shard_map/ppermute | solution.py:450
  4.8 4.7 %collective-permute-start.2 = (bf16[128,256]{1,0:T(8,128)(2,1)S(1)}, bf16[128,256]{1,0:T(8,128)(2,1)S(1)}, u32[]{:S(2)}, u32[]{:S(2)}) collective-permute-start(bf16[128,256]{1,0:T(8,128)(2,1)S(1)} %get-tuple-element.14), channel_id=1, source_target_pairs={{0,1},{1,0},{4,8},{5,9},{8,4},{9,5},{12,13},{13,12},{2,3},{3,2},{6... | collective-permute-start | bytes 196616 | tf_op jit(solution)/shard_map/ppermute | solution.py:450
  7.7 2.6 %copy-start.1 = (s32[3,2]{0,1:T(2,128)S(1)}, s32[3,2]{0,1:T(2,128)}, u32[]{:S(2)}) copy-start(s32[3,2]{0,1:T(2,128)} %param.8) | copy-start | bytes 76
  7.7 6.5 %collective-permute-start.3 = (bf16[192,256]{1,0:T(8,128)(2,1)S(1)}, bf16[192,256]{1,0:T(8,128)(2,1)S(1)}, u32[]{:S(2)}, u32[]{:S(2)}) collective-permute-start(bf16[192,256]{1,0:T(8,128)(2,1)S(1)} %side_a.1.refs_0_.first_ref), channel_id=1, source_target_pairs={{2,0},{0,2},{3,1},{1,3},{6,4},{4,6},{7,5},{5,7},{10,8},{8,10},{11,... | collective-permute-start | bytes 294920 | tf_op jit(solution)/shard_map/ppermute | solution.py:476
  10.0 4.2 %collective-permute-start.4 = (bf16[112,256]{1,0:T(8,128)(2,1)S(1)}, bf16[112,256]{1,0:T(8,128)(2,1)S(1)}, u32[]{:S(2)}, u32[]{:S(2)}) collective-permute-start(bf16[112,256]{1,0:T(8,128)(2,1)S(1)} %side_b.1.second_ref), channel_id=1, source_target_pairs={{2,0},{0,2},{3,1},{1,3},{6,4},{4,6},{7,5},{5,7},{10,8},{8,10},{11,... | collective-permute-start | bytes 172040 | tf_op jit(solution)/shard_map/ppermute | solution.py:476

commit v10 on v9

--- a/solution.py
+++ b/solution.py
@@ -16,7 +16,7 @@
 RIM = SHIFT_MAX + TAPS // 2
 REACH = HALF + RIM
 LANES = 128
-EDGE_STEP = 16
+STEP = 16
 VMEM_LIMIT = 48 * 1024 * 1024
 
 VMEM = pl.BlockSpec(memory_space=pltpu.VMEM)
@@ -74,6 +74,15 @@
     )
 
 
+def side_by_side(values):
+    values = jnp.concatenate(values, axis=0)
+    return jnp.concatenate([values[i : i + STEP] for i in range(0, values.shape[0], STEP)], axis=1)
+
+
+def one_below(block, first, last):
+    return jnp.concatenate([block[:, i * HALF : (i + 1) * HALF] for i in range(first, last)], axis=0)
+
+
 def load_kernel(*refs):
     count = (len(refs) - 1) // 2
     copies = [
@@ -87,25 +96,20 @@
 
 def pack_kernel(image_ref, other_ref, taps_ref, offsets_ref, even_ref, odd_ref):
     lines = image_ref.shape[1]
-    width = image_ref.shape[2]
     side = lax.axis_index("rg")
     taps = taps_ref[...]
     taps_high = taps.astype(jnp.bfloat16).astype(jnp.float32)
-    taps_low = taps - taps_high
-    shifts = jnp.broadcast_to(offsets_ref[...].astype(jnp.float32), (TAPS, lines))
+    taps = jnp.concatenate([taps_high, taps - taps_high], axis=0)
+    shifts = jnp.broadcast_to(offsets_ref[...].astype(jnp.float32), taps.shape)
 
     def write(out_ref, line_start, tap_start):
         rows = slice(line_start, line_start + REACH)
         for part in range(2):
             cut = slice(part * REACH, (part + 1) * REACH)
             out_ref[cut, :] = image_ref[part, rows, :].astype(jnp.bfloat16)
-        edges = jnp.concatenate([edge_of(other_ref, part, side, rows) for part in range(2)], axis=0)
+        edges = [edge_of(other_ref, part, side, rows) for part in range(2)]
         cut = slice(tap_start, tap_start + HALF)
-        block = jnp.concatenate([taps_high[:, cut], taps_low[:, cut], shifts[:, cut]], axis=1)
-        block = jnp.concatenate([block, jnp.zeros((HALF - TAPS, 3 * HALF), jnp.float32)], axis=0)
-        cuts = [edges[i * HALF : (i + 1) * HALF] for i in range(3)]
-        filler = jnp.zeros((HALF, width - 6 * HALF), jnp.float32)
-        block = jnp.concatenate([block, *cuts, filler], axis=1)
+        block = side_by_side([*edges, taps[:, cut], shifts[:, cut]])
         out_ref[2 * REACH :, :] = block.astype(jnp.bfloat16)
 
     parity = lax.rem(lax.axis_index("az"), 2)
@@ -147,35 +151,12 @@
     return lax.dot_general(high_low(weights), rows, over_rows, preferred_element_type=jnp.float32)
 
 
-def edge_rows(lines, width):
-    rows = EDGE_STEP
-    while 2 * lines // rows * HALF > width:
-        rows *= 2
-    return rows
-
-
-def piece_shape(lines, width):
-    return jax.ShapeDtypeStruct((2 * lines + edge_rows(lines, width), width), jnp.bfloat16)
-
-
-def write_piece(out_ref, parts, width):
+def write_piece(out_ref, parts, more_edge, width):
     lines = parts[0].shape[0]
-    rows = edge_rows(lines, width)
     for part, value in enumerate(parts):
         out_ref[part * lines : (part + 1) * lines, :] = value[:, :width].astype(jnp.bfloat16)
-    edges = jnp.concatenate([value[:, width:] for value in parts], axis=0)
-    slots = [edges[at : at + rows] for at in range(0, 2 * lines, rows)]
-    slots.append(jnp.zeros((rows, width - len(slots) * HALF), jnp.float32))
-    out_ref[2 * lines :, :] = jnp.concatenate(slots, axis=1).astype(jnp.bfloat16)
-
-
-def read_piece(ref, lines):
-    rows = ref.shape[0] - 2 * lines
-    block = ref[2 * lines :, :].astype(jnp.float32)
-    slots = [block[:, i * HALF : (i + 1) * HALF] for i in range(2 * lines // rows)]
-    edges = jnp.concatenate(slots, axis=0)
-    tiles = ref[: 2 * lines, :].astype(jnp.float32)
-    return [(v[:lines], v[lines:]) for v in (tiles, edges)]
+    edges = side_by_side([value[:REACH, width:] for value in parts] + [more_edge])
+    out_ref[2 * lines :, :] = edges.astype(jnp.bfloat16)
 
 
 def inner_kernel(image_ref, other_ref, taps_ref, offsets_ref, out_ref):
@@ -192,7 +173,9 @@
         out_ref[part] = apply_band(weights, rows)
 
 
-def side_kernel(turn, image_ref, other_ref, taps_ref, offsets_ref, message_ref, *refs):
+def side_kernel(
+    turn, image_ref, other_ref, taps_ref, offsets_ref, message_ref, inner_ref, *refs
+):
     out_ref = refs[-1]
     lines = image_ref.shape[1]
     width = image_ref.shape[2]
@@ -203,11 +186,11 @@
     message = message_ref[...]
     message = jnp.where(alone, jnp.zeros_like(message), message)
     block = message[2 * REACH :, :].astype(jnp.float32)
-    head = block[:TAPS]
-    rim_taps = head[:, :HALF] + head[:, HALF : 2 * HALF]
-    rim_shift = head[:1, 2 * HALF : 3 * HALF]
-    rim_edges = [block[:, i * HALF : (i + 1) * HALF] for i in range(3, 6)]
-    rim_edges = jnp.concatenate(rim_edges, axis=0).astype(jnp.bfloat16)
+    steps = 2 * REACH // STEP
+    rim_edges = one_below(block, 0, steps).astype(jnp.bfloat16)
+    rim_taps = one_below(block, steps, steps + 1)
+    rim_taps = rim_taps[:TAPS] + rim_taps[TAPS:]
+    rim_shift = one_below(block, steps + 1, steps + 2)[:1]
 
     def per_line(own, rim):
         upper = jnp.concatenate([rim, own[:, :RIM]], axis=1)
@@ -236,9 +219,9 @@
         rim = jnp.concatenate([message[cut, :], rim_edges[cut]], axis=1)
         total = apply_band(weights, jnp.concatenate([rim, own], axis=0))
         if turn == 0:
-            total = jnp.concatenate([total, refs[0][part]], axis=0)
+            total = jnp.concatenate([total, inner_ref[part]], axis=0)
         parts.append(total)
-    write_piece(out_ref, parts, width)
+    write_piece(out_ref, parts, inner_ref[turn, :, width:], width)
 
 
 def cross(own_parts, other_parts):
@@ -250,15 +233,25 @@
 
 
 def tile_of(first_ref, second_ref, lines):
-    first = read_piece(first_ref, REACH + lines - 2 * RIM)
-    second = read_piece(second_ref, REACH)
-    return [
-        tuple(jnp.concatenate([a, b], axis=0) for a, b in zip(*which))
-        for which in zip(first, second)
-    ]
-
-
-def filtered_of(own_refs, other_refs, table_ref, spectrum_ref, lines):
+    inner = lines - 2 * RIM
+    step, more = REACH // STEP, inner // STEP
+
+    def split(ref, count):
+        tiles = ref[: 2 * count, :].astype(jnp.float32)
+        block = ref[2 * count :, :].astype(jnp.float32)
+        edges = [one_below(block, part * step, (part + 1) * step) for part in range(2)]
+        return (tiles[:count], tiles[count:]), edges, one_below(block, 2 * step, 2 * step + more)
+
+    first = split(first_ref, REACH + inner)
+    second = split(second_ref, REACH)
+    tiles, edges = [], []
+    for part, middle in enumerate((first[2], second[2])):
+        tiles.append(jnp.concatenate([first[0][part], second[0][part]], axis=0))
+        edges.append(jnp.concatenate([first[1][part], middle, second[1][part]], axis=0))
+    return tiles, edges
+
+
+def filtered_of(own_refs, other_refs, table_ref, spectrum_ref, lines, emit):
     width = own_refs[0].shape[1]
     wide = lines + 2 * HALF
     row_patches = lines // HALF + 1
@@ -302,7 +295,7 @@
     range_back = jnp.dot(shaped, inverse, preferred_element_type=jnp.float32)
     range_back = range_back.astype(jnp.bfloat16)
     window = jnp.concatenate([window] * chunks, axis=1)
-    totals = [[None] * (row_patches - 1) for _ in range(2)]
+    earlier = None
     for row in range(row_patches):
         stacked = []
         for chunk in range(chunks):
@@ -311,23 +304,24 @@
             stacked.append(jnp.concatenate([block[:, :LANES], block[:, LANES:]], axis=0))
         stacked = jnp.concatenate(stacked, axis=1)
         patch_out = jnp.dot(back, stacked, preferred_element_type=jnp.float32) * window
-        for part in range(2):
-            upper = patch_out[part * PATCH : part * PATCH + HALF]
-            lower = patch_out[part * PATCH + HALF : (part + 1) * PATCH]
-            if row > 0:
-                totals[part][row - 1] = totals[part][row - 1] + upper
-            if row < row_patches - 1:
-                totals[part][row] = lower
-    total = jnp.concatenate([block for part in totals for block in part], axis=0)
-    return total[:, :width] + total[:, width + HALF : 2 * width + HALF]
+        uppers = [patch_out[part * PATCH : part * PATCH + HALF] for part in range(2)]
+        if row > 0:
+            total = jnp.concatenate(uppers, axis=0) + earlier
+            total = total[:, :width] + total[:, width + HALF : 2 * width + HALF]
+            emit(row - 1, total)
+        lowers = [patch_out[part * PATCH + HALF : (part + 1) * PATCH] for part in range(2)]
+        earlier = jnp.concatenate(lowers, axis=0)
+
+
+def keep(ref, row, total):
+    for part in range(2):
+        ref[part, row * HALF : (row + 1) * HALF] = total[part * HALF : (part + 1) * HALF]
 
 
 def own_kernel(table_ref, first_ref, second_ref, out_ref, spectrum_ref):
     own = (first_ref, second_ref)
     lines = out_ref.shape[1]
-    result = filtered_of(own, own, table_ref, spectrum_ref, lines)
-    for part in range(2):
-        out_ref[part] = result[part * lines : (part + 1) * lines]
+    filtered_of(own, own, table_ref, spectrum_ref, lines, functools.partial(keep, out_ref))
 
 
 def other_kernel(match_ref, table_ref, filtered_own_ref, first_ref, second_ref, *refs):
@@ -335,33 +329,35 @@
     match_count, _, _, lines, _ = out_ref.shape
     date = lax.axis_index("date")
     dates = match_ref.shape[1]
-
-    def slot_of(match):
-        return lax.rem(match_ref[match, date] - date + dates, dates)
-
-    def copy_of(match, source):
-        return pltpu.make_async_copy(source, out_ref.at[match, :, 0], sems.at[match])
-
-    for match in range(match_count):
-
-        @pl.when(slot_of(match) == 0)
-        def _():
-            copy_of(match, filtered_own_ref).start()
-
+    rows = lines // HALF
+
+    def copy_of(match, row, source_ref):
+        cut = slice(row * HALF, (row + 1) * HALF)
+        target = out_ref.at[match, :, 0, cut]
+        return pltpu.make_async_copy(source_ref.at[:, cut], target, sems.at[match, row])
+
+    def send(slot, row, source_ref):
+        for match in range(match_count):
+            wanted = lax.rem(match_ref[match, date] - date + dates, dates)
+
+            @pl.when(wanted == slot)
+            def _():
+                copy_of(match, row, source_ref).start()
+
+    for row in range(rows):
+        send(0, row, filtered_own_ref)
     for slot in range(1, dates):
         other = refs[2 * slot - 2 : 2 * slot]
-        result = filtered_of((first_ref, second_ref), other, table_ref, spectrum_ref, lines)
-        for part in range(2):
-            result_ref[slot - 1, part] = result[part * lines : (part + 1) * lines]
+        target_ref = result_ref.at[slot - 1]
+
+        def emit(row, total):
+            keep(target_ref, row, total)
+            send(slot, row, target_ref)
+
+        filtered_of((first_ref, second_ref), other, table_ref, spectrum_ref, lines, emit)
     for match in range(match_count):
-        slot = slot_of(match)
-
-        @pl.when(slot > 0)
-        def _():
-            copy_of(match, result_ref.at[lax.max(slot - 1, 0)]).start()
-
-    for match in range(match_count):
-        copy_of(match, filtered_own_ref).wait()
+        for row in range(rows):
+            copy_of(match, row, filtered_own_ref).wait()
 
 
 def all_tables(row_patches):
@@ -428,7 +424,7 @@
         name="load",
     )(*(pltpu.with_memory_space_constraint(a, pltpu.HBM) for a in arguments))
     raw = (raw[0], other, *raw[1:])
-    message = jax.ShapeDtypeStruct((2 * REACH + HALF, width), jnp.bfloat16)
+    message = jax.ShapeDtypeStruct((2 * REACH + STEP, width), jnp.bfloat16)
     messages = pl.pallas_call(
         pack_kernel,
         out_shape=(message, message),
@@ -460,16 +456,16 @@
     )(*raw)
     own = []
     for turn in range(2):
-        made = (*own, inner)[:1] if turn else (inner,)
+        count = REACH + (0 if turn else lines - 2 * RIM)
         call = pl.pallas_call(
             functools.partial(side_kernel, turn),
-            out_shape=piece_shape(REACH + (0 if turn else lines - 2 * RIM), width),
-            in_specs=[VMEM] * (5 + len(made)),
+            out_shape=jax.ShapeDtypeStruct((2 * count + STEP, width), jnp.bfloat16),
+            in_specs=[VMEM] * (6 + len(own)),
             out_specs=VMEM,
             compiler_params=PARAMS,
             name="side_" + "ab"[turn],
         )
-        own.append(call(*raw, messages[turn], *made))
+        own.append(call(*raw, messages[turn], inner, *own))
     dates = lax.axis_size("date")
 
     def from_date(piece, slot):
@@ -497,7 +493,7 @@
         scratch_shapes=[
             pltpu.VMEM((dates - 1, 2, lines, width), jnp.float32),
             spectrum,
-            pltpu.SemaphoreType.DMA((match_count,)),
+            pltpu.SemaphoreType.DMA((match_count, lines // HALF)),
         ],
         compiler_params=PARAMS,
         name="filter_other",

time: 16.9 us -> 16.8 us (level)
  Pallas kernels: 6.06 us -> 6.36 us
  waiting for transfers between devices: 4.95 us -> 4.68 us
    pallas_call x1, Pallas kernels: 2.49 us -> 2.75 us  [per_device(): pl.pallas_call(other_kernel, out_shape=jax.ShapeDtypeStruct((match_count,...]
    pallas_call x1, Pallas kernels: 1.23 us -> 1.41 us  [per_device(): pl.pallas_call(own_kernel, out_shape=jax.ShapeDtypeStruct((2, lines, widt...]
    ppermute x2, waiting for transfers between devices: 2.09 us -> 1.91 us  [swapped(): return lax.ppermute(value, ('az', 'rg'), pairs)]
  transfers between devices with their start and end apart: 5 -> 5, of which waited for: 3 -> 3; matrix products, arithmetic and copies ran while one was open for 1% -> 1% of each run, Pallas kernels for 20% -> 21%
where the time goes in v10:
time: 16.8 us; the launch traced here: 16.7 us
  Pallas kernels  6.36 us (38%)
  starting transfers between devices  5.51 us (33%)
  waiting for transfers between devices  4.68 us (28%)
    ppermute x2, starting transfers between devices, swapped(): return lax.ppermute(value, ('az', 'rg'), pairs)  3 us
    pallas_call x1, Pallas kernels, per_device(): pl.pallas_call(other_kernel, out_shape=jax.ShapeDtypeStruct((match_count,...  2.75 us
    ppermute x2, waiting for transfers between devices, from_date(): lax.ppermute(piece, 'date', [((i + slot) % dates, i) for i in range(dates)])  2.51 us
    ppermute x2, starting transfers between devices, from_date(): lax.ppermute(piece, 'date', [((i + slot) % dates, i) for i in range(dates)])  2.06 us
    ppermute x2, waiting for transfers between devices, swapped(): return lax.ppermute(value, ('az', 'rg'), pairs)  1.91 us
    pallas_call x1, Pallas kernels, per_device(): pl.pallas_call(own_kernel, out_shape=jax.ShapeDtypeStruct((2, lines, widt...  1.41 us
    pallas_call x1, Pallas kernels, per_device(): pl.pallas_call(load_kernel, out_shape=tuple((pltpu.VMEM(a.shape, a.dtype)...  0.93 us
    pallas_call x2, Pallas kernels, per_device(): own.append(call(*raw, messages[turn], inner, *own))  0.8 us
  transfers between devices with their start and end apart: 5, of which 3 were waited for; matrix products, arithmetic and copies ran while one was open for 1% of the time, Pallas kernels for 21%

profile of v10, /device:TPU:0, one launch (start us, length us, event | category | flops | bytes accessed | tf_op | source)
XLA Modules:
  0.0 16.7 jit_solution(14774332218611306599)
XLA Ops:
  0.0 0.5 %collective-permute-start = (f32[2,1,64,256]{3,2,0,1:T(8,128)}, f32[2,1,64,256]{3,2,0,1:T(8,128)S(1)}, u32[]{:S(2)}, u32[]{:S(2)}) collective-permute-start(f32[2,1,64,256]{3,2,0,1:T(8,128)} %bitcast.8), channel_id=1, source_target_pairs={{0,1},{1,0},{2,3},{3,2},{4,5},{5,4},{6,7},{7,6},{8,9},{9,8},{10,11... | collective-permute-start | bytes 393224 | tf_op jit(solution)/shard_map/ppermute | solution.py:411
  0.5 0.9 %load.1 = (f32[2,64,256]{2,1,0:T(8,128)S(1)}, f32[8,64]{1,0:T(8,128)S(1)}, s32[1,64]{1,0:T(1,128)S(1)}) custom-call(f32[2,64,256]{2,1,0:T(8,128)} %bitcast.9, f32[8,64]{1,0:T(8,128)} %bitcast.10, s32[1,64]{1,0:T(1,128)} %refs_2_.1), custom_call_target="tpu_custom_call" | custom-call | tf_op jit(solution)/shard_map/load/pallas_call | solution.py:417
  1.4 0.3 %collective-permute-done = f32[2,1,64,256]{3,2,0,1:T(8,128)S(1)} collective-permute-done((f32[2,1,64,256]{3,2,0,1:T(8,128)}, f32[2,1,64,256]{3,2,0,1:T(8,128)S(1)}, u32[]{:S(2)}, u32[]{:S(2)}) %collective-permute-start) | collective-permute-done | bytes 131104 | tf_op jit(solution)/shard_map/ppermute | solution.py:411
  1.7 0.2 pack.1
  1.8 0.0 copy-start
  1.8 3.0 %collective-permute-start.1 = (bf16[112,256]{1,0:T(8,128)(2,1)S(1)}, bf16[112,256]{1,0:T(8,128)(2,1)S(1)}, u32[]{:S(2)}, u32[]{:S(2)}) collective-permute-start(bf16[112,256]{1,0:T(8,128)(2,1)S(1)} %get-tuple-element.13), channel_id=1, source_target_pairs={{0,4},{1,5},{4,0},{5,1},{8,12},{9,13},{12,8},{13,9},{2,6},{3,7},{6... | collective-permute-start | bytes 172040 | tf_op jit(solution)/shard_map/ppermute | solution.py:446
  4.8 0.0 collective-permute-start.2
  4.8 0.3 %inner.1.inner_ref = f32[2,32,288]{2,1,0:T(8,128)S(1)} custom-call(f32[2,64,256]{2,1,0:T(8,128)S(1)} %get-tuple-element.10.image_ref, f32[2,64,256]{2,1,0:T(8,128)S(1)} %bitcast.5, f32[8,64]{1,0:T(8,128)S(1)} %get-tuple-element.11.taps_ref, s32[1,64]{1,0:T(1,128)S(1)} %get-tuple-element.12.offsets_ref), custom_call_target="tpu_custom_call" | custom-call | tf_op jit(solution)/shard_map/inner/pallas_call | solution.py:449
  5.1 1.9 %collective-permute-done.1.message_ref = bf16[112,256]{1,0:T(8,128)(2,1)S(1)} collective-permute-done((bf16[112,256]{1,0:T(8,128)(2,1)S(1)}, bf16[112,256]{1,0:T(8,128)(2,1)S(1)}, u32[]{:S(2)}, u32[]{:S(2)}) %collective-permute-start.1) | collective-permute-done | bytes 57376 | tf_op jit(solution)/shard_map/ppermute | solution.py:446
  7.1 0.4 %side_a.1.refs_0_.first_ref = bf16[176,256]{1,0:T(8,128)(2,1)S(1)} custom-call(f32[2,64,256]{2,1,0:T(8,128)S(1)} %get-tuple-element.10.image_ref, f32[2,64,256]{2,1,0:T(8,128)S(1)} %bitcast.6, f32[8,64]{1,0:T(8,128)S(1)} %get-tuple-element.11.taps_ref, s32[1,64]{1,0:T(1,128)S(1)} %get-tuple-element.12.offsets_ref, ...), custom_call_target="tpu_custom_call" | custom-call | tf_op jit(solution)/shard_map/side_a/pallas_call | solution.py:468
  7.5 0.0 copy-start.1
  7.5 1.9 %collective-permute-start.3 = (bf16[176,256]{1,0:T(8,128)(2,1)S(1)}, bf16[176,256]{1,0:T(8,128)(2,1)S(1)}, u32[]{:S(2)}, u32[]{:S(2)}) collective-permute-start(bf16[176,256]{1,0:T(8,128)(2,1)S(1)} %side_a.1.refs_0_.first_ref), channel_id=1, source_target_pairs={{2,0},{0,2},{3,1},{1,3},{6,4},{4,6},{7,5},{5,7},{10,8},{8,10},{11,... | collective-permute-start | bytes 270344 | tf_op jit(solution)/shard_map/ppermute | solution.py:472
  9.3 0.0 collective-permute-done.2.message_ref
  9.4 0.4 %side_b.1.second_ref = bf16[112,256]{1,0:T(8,128)(2,1)S(1)} custom-call(f32[2,64,256]{2,1,0:T(8,128)S(1)} %get-tuple-element.10.image_ref, f32[2,64,256]{2,1,0:T(8,128)S(1)} %bitcast.7, f32[8,64]{1,0:T(8,128)S(1)} %get-tuple-element.11.taps_ref, s32[1,64]{1,0:T(1,128)S(1)} %get-tuple-element.12.offsets_ref, ...), custom_call_target="tpu_custom_call" | custom-call | tf_op jit(solution)/shard_map/side_b/pallas_call | solution.py:468
  9.8 0.2 %collective-permute-start.4 = (bf16[112,256]{1,0:T(8,128)(2,1)S(1)}, bf16[112,256]{1,0:T(8,128)(2,1)S(1)}, u32[]{:S(2)}, u32[]{:S(2)}) collective-permute-start(bf16[112,256]{1,0:T(8,128)(2,1)S(1)} %side_b.1.second_ref), channel_id=1, source_target_pairs={{2,0},{0,2},{3,1},{1,3},{6,4},{4,6},{7,5},{5,7},{10,8},{8,10},{11,... | collective-permute-start | bytes 172040 | tf_op jit(solution)/shard_map/ppermute | solution.py:472
  9.9 0.0 copy-done.1
  9.9 0.1 copy.7.match_ref
  10.0 0.0 copy-done
  10.0 1.4 %filter_own.1.filtered_own_ref = f32[2,64,256]{2,1,0:T(8,128)S(1)} custom-call(bf16[1472,256]{1,0:T(8,128)(2,1)S(1)} %copy-done, bf16[176,256]{1,0:T(8,128)(2,1)S(1)} %side_a.1.refs_0_.first_ref, bf16[112,256]{1,0:T(8,128)(2,1)S(1)} %side_b.1.second_ref), custom_call_target="tpu_custom_call" | custom-call | tf_op jit(solution)/shard_map/filter_own/pallas_call | solution.py:479
  11.4 2.5 %collective-permute-done.4.refs_1_ = bf16[112,256]{1,0:T(8,128)(2,1)S(1)} collective-permute-done((bf16[112,256]{1,0:T(8,128)(2,1)S(1)}, bf16[112,256]{1,0:T(8,128)(2,1)S(1)}, u32[]{:S(2)}, u32[]{:S(2)}) %collective-permute-start.4) | collective-permute-done | bytes 57376 | tf_op jit(solution)/shard_map/ppermute | solution.py:472
  13.9 0.0 collective-permute-done.3.refs_0_
  13.9 2.8 %filter_other.1 = f32[3,2,1,64,256]{4,3,2,1,0:T(8,128)} custom-call(s32[3,2]{1,0:T(4,128)S(1)} %copy.7.match_ref, bf16[1472,256]{1,0:T(8,128)(2,1)S(1)} %copy-done, f32[2,64,256]{2,1,0:T(8,128)S(1)} %filter_own.1.filtered_own_ref, bf16[176,256]{1,0:T(8,128)(2,1)S(1)} %side_a.1.refs_0_.first_ref, bf16[112,256]{1,0:T(8,128)(2,1)S(1)} %side_b.1.second_ref, ...), custom_call_target="tpu_custom_call" | custom-call | tf_op jit(solution)/shard_map/filter_other/pallas_call | solution.py:488
Async XLA Ops:
  0.0 1.6 %collective-permute-start = (f32[2,1,64,256]{3,2,0,1:T(8,128)}, f32[2,1,64,256]{3,2,0,1:T(8,128)S(1)}, u32[]{:S(2)}, u32[]{:S(2)}) collective-permute-start(f32[2,1,64,256]{3,2,0,1:T(8,128)} %bitcast.8), channel_id=1, source_target_pairs={{0,1},{1,0},{2,3},{3,2},{4,5},{5,4},{6,7},{7,6},{8,9},{9,8},{10,11... | collective-permute-start | bytes 393224 | tf_op jit(solution)/shard_map/ppermute | solution.py:411
  1.8 8.2 %copy-start = (bf16[1472,256]{1,0:T(8,128)(2,1)S(1)}, bf16[1472,256]{1,0:T(8,128)(2,1)}, u32[]{:S(2)}) copy-start(bf16[1472,256]{1,0:T(8,128)(2,1)} %constant.2.clone.table_ref) | copy-start | bytes 2260996
  1.8 5.2 %collective-permute-start.1 = (bf16[112,256]{1,0:T(8,128)(2,1)S(1)}, bf16[112,256]{1,0:T(8,128)(2,1)S(1)}, u32[]{:S(2)}, u32[]{:S(2)}) collective-permute-start(bf16[112,256]{1,0:T(8,128)(2,1)S(1)} %get-tuple-element.13), channel_id=1, source_target_pairs={{0,4},{1,5},{4,0},{5,1},{8,12},{9,13},{12,8},{13,9},{2,6},{3,7},{6... | collective-permute-start | bytes 172040 | tf_op jit(solution)/shard_map/ppermute | solution.py:446
  4.8 4.5 %collective-permute-start.2 = (bf16[112,256]{1,0:T(8,128)(2,1)S(1)}, bf16[112,256]{1,0:T(8,128)(2,1)S(1)}, u32[]{:S(2)}, u32[]{:S(2)}) collective-permute-start(bf16[112,256]{1,0:T(8,128)(2,1)S(1)} %get-tuple-element.14), channel_id=1, source_target_pairs={{0,1},{1,0},{4,8},{5,9},{8,4},{9,5},{12,13},{13,12},{2,3},{3,2},{6... | collective-permute-start | bytes 172040 | tf_op jit(solution)/shard_map/ppermute | solution.py:446
  7.5 2.5 %copy-start.1 = (s32[3,2]{0,1:T(2,128)S(1)}, s32[3,2]{0,1:T(2,128)}, u32[]{:S(2)}) copy-start(s32[3,2]{0,1:T(2,128)} %param.8) | copy-start | bytes 76
  7.5 6.5 %collective-permute-start.3 = (bf16[176,256]{1,0:T(8,128)(2,1)S(1)}, bf16[176,256]{1,0:T(8,128)(2,1)S(1)}, u32[]{:S(2)}, u32[]{:S(2)}) collective-permute-start(bf16[176,256]{1,0:T(8,128)(2,1)S(1)} %side_a.1.refs_0_.first_ref), channel_id=1, source_target_pairs={{2,0},{0,2},{3,1},{1,3},{6,4},{4,6},{7,5},{5,7},{10,8},{8,10},{11,... | collective-permute-start | bytes 270344 | tf_op jit(solution)/shard_map/ppermute | solution.py:472
  9.8 4.2 %collective-permute-start.4 = (bf16[112,256]{1,0:T(8,128)(2,1)S(1)}, bf16[112,256]{1,0:T(8,128)(2,1)S(1)}, u32[]{:S(2)}, u32[]{:S(2)}) collective-permute-start(bf16[112,256]{1,0:T(8,128)(2,1)S(1)} %side_b.1.second_ref), channel_id=1, source_target_pairs={{2,0},{0,2},{3,1},{1,3},{6,4},{4,6},{7,5},{5,7},{10,8},{8,10},{11,... | collective-permute-start | bytes 172040 | tf_op jit(solution)/shard_map/ppermute | solution.py:472

commit v11 on v10

--- a/solution.py
+++ b/solution.py
@@ -94,35 +94,45 @@
         copy.wait()
 
 
-def pack_kernel(image_ref, other_ref, taps_ref, offsets_ref, even_ref, odd_ref):
+def pack_kernel(image_ref, other_ref, taps_ref, offsets_ref, even_ref, odd_ref, own_ref):
     lines = image_ref.shape[1]
+    width = image_ref.shape[2]
     side = lax.axis_index("rg")
     taps = taps_ref[...]
     taps_high = taps.astype(jnp.bfloat16).astype(jnp.float32)
     taps = jnp.concatenate([taps_high, taps - taps_high], axis=0)
     shifts = jnp.broadcast_to(offsets_ref[...].astype(jnp.float32), taps.shape)
 
-    def write(out_ref, line_start, tap_start):
-        rows = slice(line_start, line_start + REACH)
+    def write(out_ref, line_start, count, weights):
+        rows = slice(line_start, line_start + count)
         for part in range(2):
-            cut = slice(part * REACH, (part + 1) * REACH)
+            cut = slice(part * count, (part + 1) * count)
             out_ref[cut, :] = image_ref[part, rows, :].astype(jnp.bfloat16)
-        edges = [edge_of(other_ref, part, side, rows) for part in range(2)]
-        cut = slice(tap_start, tap_start + HALF)
-        block = side_by_side([*edges, taps[:, cut], shifts[:, cut]])
-        out_ref[2 * REACH :, :] = block.astype(jnp.bfloat16)
+        edges = side_by_side([edge_of(other_ref, part, side, rows) for part in range(2)])
+        block = jnp.concatenate([edges, *weights], axis=1)
+        for at in range(0, block.shape[1], width):
+            top = 2 * count + at // width * STEP
+            out_ref[top : top + STEP, :] = block[:, at : at + width].astype(jnp.bfloat16)
+
+    def write_side(out_ref, first):
+        cut = slice(0, HALF) if first else slice(lines - HALF, lines)
+        start = 0 if first else lines - REACH
+        write(out_ref, start, REACH, [taps[:, cut], shifts[:, cut]])
 
     parity = lax.rem(lax.axis_index("az"), 2)
 
     @pl.when(parity == 0)
     def _():
-        write(even_ref, lines - REACH, lines - HALF)
-        write(odd_ref, 0, 0)
+        write_side(even_ref, False)
+        write_side(odd_ref, True)
 
     @pl.when(parity == 1)
     def _():
-        write(even_ref, 0, 0)
-        write(odd_ref, lines - REACH, lines - HALF)
+        write_side(even_ref, True)
+        write_side(odd_ref, False)
+
+    filler = jnp.zeros((STEP, width - 2 * lines), jnp.float32)
+    write(own_ref, 0, lines, [taps, shifts, filler])
 
 
 def is_above(turn):
@@ -151,35 +161,50 @@
     return lax.dot_general(high_low(weights), rows, over_rows, preferred_element_type=jnp.float32)
 
 
-def write_piece(out_ref, parts, more_edge, width):
-    lines = parts[0].shape[0]
-    for part, value in enumerate(parts):
-        out_ref[part * lines : (part + 1) * lines, :] = value[:, :width].astype(jnp.bfloat16)
-    edges = side_by_side([value[:REACH, width:] for value in parts] + [more_edge])
-    out_ref[2 * lines :, :] = edges.astype(jnp.bfloat16)
-
-
-def inner_kernel(image_ref, other_ref, taps_ref, offsets_ref, out_ref):
-    lines = image_ref.shape[1]
-    width = image_ref.shape[2]
-    side = lax.axis_index("rg")
+class Own:
+    def __init__(self, image_ref, other_ref, taps_ref, offsets_ref):
+        self.image_ref, self.other_ref = image_ref, other_ref
+        self.lines, self.width = image_ref.shape[1:]
+        self.taps = taps_ref[...]
+        self.shift = offsets_ref[...].astype(jnp.float32)
+
+    def rows(self, part, cut):
+        edge = edge_of(self.other_ref, part, lax.axis_index("rg"), cut)
+        return high_low(jnp.concatenate([self.image_ref[part, cut, :], edge], axis=1))
+
+
+class Partner:
+    def __init__(self, ref):
+        self.ref = ref
+        self.width = ref.shape[1]
+        self.lines = lines = (ref.shape[0] - 2 * STEP) // 2
+        steps = 2 * lines // STEP
+        self.edges = one_below(ref[2 * lines : 2 * lines + STEP, :].astype(jnp.float32), 0, steps)
+        block = ref[2 * lines + STEP :, :].astype(jnp.float32)
+        self.taps = block[:TAPS, :lines] + block[TAPS : 2 * TAPS, :lines]
+        self.shift = block[:1, lines : 2 * lines]
+
+    def rows(self, part, cut):
+        rows = slice(part * self.lines + cut.start, part * self.lines + cut.stop)
+        edge = self.edges[rows].astype(jnp.bfloat16)
+        return jnp.concatenate([self.ref[rows, :], edge], axis=1)
+
+
+def inner_lines(source):
+    lines = source.lines
     cut = slice(RIM, lines - RIM)
-    source = lax.broadcasted_iota(jnp.int32, (lines, lines - 2 * RIM), 0)
-    weights = band(taps_ref[:, cut], offsets_ref[:, cut], RIM, source)
-    weights = jnp.concatenate([weights, weights], axis=0)
+    ids = lax.broadcasted_iota(jnp.int32, (lines, lines - 2 * RIM), 0)
+    weights = band(source.taps[:, cut], source.shift[:, cut].astype(jnp.int32), RIM, ids)
+    parts = []
     for part in range(2):
-        edge = edge_of(other_ref, part, side, slice(0, lines))
-        rows = high_low(jnp.concatenate([image_ref[part], edge], axis=1))
-        out_ref[part] = apply_band(weights, rows)
-
-
-def side_kernel(
-    turn, image_ref, other_ref, taps_ref, offsets_ref, message_ref, inner_ref, *refs
-):
-    out_ref = refs[-1]
-    lines = image_ref.shape[1]
-    width = image_ref.shape[2]
-    side = lax.axis_index("rg")
+        rows = source.rows(part, slice(0, lines))
+        repeats = rows.shape[0] // lines
+        parts.append(apply_band(jnp.concatenate([weights] * repeats, axis=0), rows))
+    return parts
+
+
+def side_lines(turn, source, message_ref):
+    lines = source.lines
     place = lax.axis_index("az")
     above = is_above(turn)
     alone = jnp.where(above, place == 0, place == lax.axis_size("az") - 1)
@@ -197,31 +222,39 @@
         lower = jnp.concatenate([own[:, lines - RIM :], rim], axis=1)
         return jnp.where(above, upper, lower)
 
-    taps = per_line(taps_ref[...], rim_taps)
-    shift = per_line(offsets_ref[...].astype(jnp.float32), rim_shift).astype(jnp.int32)
+    taps = per_line(source.taps, rim_taps)
+    shift = per_line(source.shift, rim_shift).astype(jnp.int32)
     first_line = jnp.where(above, -HALF, lines - RIM)
     near = 2 * RIM
     first_own = jnp.where(above, 0, lines - near)
     first_rim = jnp.where(above, -REACH, lines)
-    source = lax.broadcasted_iota(jnp.int32, (REACH + near, REACH), 0)
-    source = jnp.where(source < REACH, source + first_rim, source - REACH + first_own)
-    weights = band(taps, shift, first_line, source)
-    weights = jnp.concatenate([weights, weights[REACH:]], axis=0)
+    ids = lax.broadcasted_iota(jnp.int32, (REACH + near, REACH), 0)
+    ids = jnp.where(ids < REACH, ids + first_rim, ids - REACH + first_own)
+    weights = band(taps, shift, first_line, ids)
     parts = []
     for part in range(2):
-        upper, lower = slice(0, near), slice(lines - near, lines)
-        edge = jnp.where(
-            above, edge_of(other_ref, part, side, upper), edge_of(other_ref, part, side, lower)
-        )
-        own = jnp.where(above, image_ref[part, upper, :], image_ref[part, lower, :])
-        own = high_low(jnp.concatenate([own, edge], axis=1))
+        upper = source.rows(part, slice(0, near))
+        own = jnp.where(above, upper, source.rows(part, slice(lines - near, lines)))
+        repeats = own.shape[0] // near
+        both = jnp.concatenate([weights] + [weights[REACH:]] * (repeats - 1), axis=0)
         cut = slice(part * REACH, (part + 1) * REACH)
         rim = jnp.concatenate([message[cut, :], rim_edges[cut]], axis=1)
-        total = apply_band(weights, jnp.concatenate([rim, own], axis=0))
-        if turn == 0:
-            total = jnp.concatenate([total, inner_ref[part]], axis=0)
-        parts.append(total)
-    write_piece(out_ref, parts, inner_ref[turn, :, width:], width)
+        parts.append(apply_band(both, jnp.concatenate([rim, own], axis=0)))
+    return parts
+
+
+def inner_kernel(make, *refs):
+    for part, value in enumerate(inner_lines(make(*refs[:-1]))):
+        refs[-1][part] = value.astype(jnp.bfloat16)
+
+
+def side_kernel(turn, make, *refs):
+    for part, value in enumerate(side_lines(turn, make(*refs[:-2]), refs[-2])):
+        refs[-1][part] = value.astype(jnp.bfloat16)
+
+
+def pass_kernel(message_ref, *refs):
+    refs[-1][...] = message_ref[...]
 
 
 def cross(own_parts, other_parts):
@@ -232,33 +265,21 @@
     return real, imag
 
 
-def tile_of(first_ref, second_ref, lines):
-    inner = lines - 2 * RIM
-    step, more = REACH // STEP, inner // STEP
-
-    def split(ref, count):
-        tiles = ref[: 2 * count, :].astype(jnp.float32)
-        block = ref[2 * count :, :].astype(jnp.float32)
-        edges = [one_below(block, part * step, (part + 1) * step) for part in range(2)]
-        return (tiles[:count], tiles[count:]), edges, one_below(block, 2 * step, 2 * step + more)
-
-    first = split(first_ref, REACH + inner)
-    second = split(second_ref, REACH)
-    tiles, edges = [], []
-    for part, middle in enumerate((first[2], second[2])):
-        tiles.append(jnp.concatenate([first[0][part], second[0][part]], axis=0))
-        edges.append(jnp.concatenate([first[1][part], middle, second[1][part]], axis=0))
-    return tiles, edges
-
-
-def filtered_of(own_refs, other_refs, table_ref, spectrum_ref, lines, emit):
-    width = own_refs[0].shape[1]
+def tile_of(pieces, width):
+    parts = [
+        jnp.concatenate([piece[part].astype(jnp.float32) for piece in pieces], axis=0)
+        for part in range(2)
+    ]
+    return [part[:, :width] for part in parts], [part[:, width:] for part in parts]
+
+
+def filtered_of(own_pieces, other_pieces, table_ref, spectrum_ref, lines, width):
     wide = lines + 2 * HALF
     row_patches = lines // HALF + 1
     side = lax.axis_index("rg")
     line_table_of, forward, inverse, back, ring, window = split_tables(table_ref, row_patches)
-    own_tile, own_edge = tile_of(*own_refs, lines)
-    other_tile, other_edge = tile_of(*other_refs, lines)
+    own_tile, own_edge = tile_of(own_pieces, width)
+    other_tile, other_edge = tile_of(other_pieces, width)
     mid = jnp.concatenate(cross(own_tile, other_tile), axis=0)
     rim = jnp.concatenate(cross(own_edge, other_edge), axis=0)
     before = jnp.where(side == 0, 0.0, rim)
@@ -295,7 +316,7 @@
     range_back = jnp.dot(shaped, inverse, preferred_element_type=jnp.float32)
     range_back = range_back.astype(jnp.bfloat16)
     window = jnp.concatenate([window] * chunks, axis=1)
-    earlier = None
+    totals = [[None] * (row_patches - 1) for _ in range(2)]
     for row in range(row_patches):
         stacked = []
         for chunk in range(chunks):
@@ -304,60 +325,56 @@
             stacked.append(jnp.concatenate([block[:, :LANES], block[:, LANES:]], axis=0))
         stacked = jnp.concatenate(stacked, axis=1)
         patch_out = jnp.dot(back, stacked, preferred_element_type=jnp.float32) * window
-        uppers = [patch_out[part * PATCH : part * PATCH + HALF] for part in range(2)]
-        if row > 0:
-            total = jnp.concatenate(uppers, axis=0) + earlier
-            total = total[:, :width] + total[:, width + HALF : 2 * width + HALF]
-            emit(row - 1, total)
-        lowers = [patch_out[part * PATCH + HALF : (part + 1) * PATCH] for part in range(2)]
-        earlier = jnp.concatenate(lowers, axis=0)
-
-
-def keep(ref, row, total):
+        for part in range(2):
+            upper = patch_out[part * PATCH : part * PATCH + HALF]
+            lower = patch_out[part * PATCH + HALF : (part + 1) * PATCH]
+            if row > 0:
+                totals[part][row - 1] = totals[part][row - 1] + upper
+            if row < row_patches - 1:
+                totals[part][row] = lower
+    total = jnp.concatenate([block for part in totals for block in part], axis=0)
+    return total[:, :width] + total[:, width + HALF : 2 * width + HALF]
+
+
+def own_kernel(table_ref, first_ref, inner_ref, second_ref, out_ref, spectrum_ref):
+    own = (first_ref, inner_ref, second_ref)
+    _, lines, width = out_ref.shape
+    result = filtered_of(own, own, table_ref, spectrum_ref, lines, width)
     for part in range(2):
-        ref[part, row * HALF : (row + 1) * HALF] = total[part * HALF : (part + 1) * HALF]
-
-
-def own_kernel(table_ref, first_ref, second_ref, out_ref, spectrum_ref):
-    own = (first_ref, second_ref)
-    lines = out_ref.shape[1]
-    filtered_of(own, own, table_ref, spectrum_ref, lines, functools.partial(keep, out_ref))
-
-
-def other_kernel(match_ref, table_ref, filtered_own_ref, first_ref, second_ref, *refs):
+        out_ref[part] = result[part * lines : (part + 1) * lines]
+
+
+def other_kernel(
+    match_ref, table_ref, filtered_own_ref, first_ref, inner_ref, second_ref, *refs
+):
     out_ref, result_ref, spectrum_ref, sems = refs[-4:]
-    match_count, _, _, lines, _ = out_ref.shape
+    match_count, _, _, lines, width = out_ref.shape
     date = lax.axis_index("date")
     dates = match_ref.shape[1]
-    rows = lines // HALF
-
-    def copy_of(match, row, source_ref):
-        cut = slice(row * HALF, (row + 1) * HALF)
-        target = out_ref.at[match, :, 0, cut]
-        return pltpu.make_async_copy(source_ref.at[:, cut], target, sems.at[match, row])
-
-    def send(slot, row, source_ref):
+
+    def send(slot, source_ref):
         for match in range(match_count):
             wanted = lax.rem(match_ref[match, date] - date + dates, dates)
 
             @pl.when(wanted == slot)
             def _():
-                copy_of(match, row, source_ref).start()
-
-    for row in range(rows):
-        send(0, row, filtered_own_ref)
+                copy_of(match, source_ref).start()
+
+    def copy_of(match, source_ref):
+        return pltpu.make_async_copy(source_ref, out_ref.at[match, :, 0], sems.at[match])
+
+    send(0, filtered_own_ref)
+    own = (first_ref, inner_ref, second_ref)
     for slot in range(1, dates):
-        other = refs[2 * slot - 2 : 2 * slot]
-        target_ref = result_ref.at[slot - 1]
-
-        def emit(row, total):
-            keep(target_ref, row, total)
-            send(slot, row, target_ref)
-
-        filtered_of((first_ref, second_ref), other, table_ref, spectrum_ref, lines, emit)
+        near_ref, middle_ref, raw_ref, message_ref = refs[4 * slot - 4 : 4 * slot]
+        last = [v.astype(jnp.bfloat16) for v in side_lines(1, Partner(raw_ref), message_ref)]
+        other = (near_ref, middle_ref, last)
+        result = filtered_of(own, other, table_ref, spectrum_ref, lines, width)
+        for part in range(2):
+            result_ref[slot - 1, part] = result[part * lines : (part + 1) * lines]
+        send(slot, result_ref.at[slot - 1])
     for match in range(match_count):
-        for row in range(rows):
-            copy_of(match, row, filtered_own_ref).wait()
+        copy_of(match, filtered_own_ref).wait()
 
 
 def all_tables(row_patches):
@@ -425,14 +442,25 @@
     )(*(pltpu.with_memory_space_constraint(a, pltpu.HBM) for a in arguments))
     raw = (raw[0], other, *raw[1:])
     message = jax.ShapeDtypeStruct((2 * REACH + STEP, width), jnp.bfloat16)
-    messages = pl.pallas_call(
+    *messages, own_raw = pl.pallas_call(
         pack_kernel,
-        out_shape=(message, message),
+        out_shape=(
+            message,
+            message,
+            jax.ShapeDtypeStruct((2 * lines + 2 * STEP, width), jnp.bfloat16),
+        ),
         in_specs=[VMEM] * 4,
-        out_specs=(VMEM, VMEM),
+        out_specs=(VMEM,) * 3,
         compiler_params=PARAMS,
         name="pack",
     )(*raw)
+    dates = lax.axis_size("date")
+
+    def from_date(piece, slot):
+        return lax.ppermute(piece, "date", [((i + slot) % dates, i) for i in range(dates)])
+
+    slots = range(1, dates)
+    raws = [from_date(own_raw, slot) for slot in slots]
     peers = lax.axis_size("az")
 
     def swapped(value, start):
@@ -446,32 +474,50 @@
         return lax.ppermute(value, ("az", "rg"), pairs)
 
     messages = [swapped(messages[turn], turn) for turn in range(2)]
-    inner = pl.pallas_call(
-        inner_kernel,
-        out_shape=jax.ShapeDtypeStruct((2, lines - 2 * RIM, width + HALF), jnp.float32),
-        in_specs=[VMEM] * 4,
-        out_specs=VMEM,
-        compiler_params=PARAMS,
-        name="inner",
-    )(*raw)
-    own = []
-    for turn in range(2):
-        count = REACH + (0 if turn else lines - 2 * RIM)
-        call = pl.pallas_call(
-            functools.partial(side_kernel, turn),
-            out_shape=jax.ShapeDtypeStruct((2 * count + STEP, width), jnp.bfloat16),
-            in_specs=[VMEM] * (6 + len(own)),
+    def resampled(kernel, count, name, *args):
+        return pl.pallas_call(
+            kernel,
+            out_shape=jax.ShapeDtypeStruct((2, count, width + HALF), jnp.bfloat16),
+            in_specs=[VMEM] * len(args),
             out_specs=VMEM,
             compiler_params=PARAMS,
-            name="side_" + "ab"[turn],
+            name=name,
+        )(*args)
+
+    between = lines - 2 * RIM
+    inner = resampled(functools.partial(inner_kernel, Own), between, "own_inner", *raw)
+
+    def own_side(turn):
+        name = "own_side_" + "ab"[turn]
+        kernel = functools.partial(side_kernel, turn, Own)
+        return resampled(kernel, REACH, name, *raw, messages[turn])
+
+    def forwarded(turn, *made):
+        message = pl.pallas_call(
+            pass_kernel,
+            out_shape=jax.ShapeDtypeStruct(messages[turn].shape, jnp.bfloat16),
+            in_specs=[VMEM] * (1 + len(made)),
+            out_specs=VMEM,
+            compiler_params=PARAMS,
+            name="pass_" + "ab"[turn],
+        )(messages[turn], *made)
+        return [from_date(message, slot) for slot in slots]
+
+    nears = forwarded(0, inner)
+    first = own_side(0)
+    middles = [
+        resampled(functools.partial(inner_kernel, Partner), between, "partner_inner", partner)
+        for partner in raws
+    ]
+    fars = forwarded(1, first, *middles)
+    second = own_side(1)
+    own = (first, inner, second)
+    others = []
+    for partner, near, middle, far in zip(raws, nears, middles, fars):
+        near = resampled(
+            functools.partial(side_kernel, 0, Partner), REACH, "partner_side_a", partner, near
         )
-        own.append(call(*raw, messages[turn], inner, *own))
-    dates = lax.axis_size("date")
-
-    def from_date(piece, slot):
-        return lax.ppermute(piece, "date", [((i + slot) % dates, i) for i in range(dates)])
-
-    others = [from_date(piece, slot) for slot in range(1, dates) for piece in own]
+        others += [near, middle, partner, far]
     row_patches = lines // HALF + 1
     chunks = (width + width + LANES) // LANES
     tables = jnp.asarray(all_tables(row_patches))
@@ -479,7 +525,7 @@
     filtered_own = pl.pallas_call(
         own_kernel,
         out_shape=jax.ShapeDtypeStruct((2, lines, width), jnp.float32),
-        in_specs=[VMEM] * 3,
+        in_specs=[VMEM] * 4,
         out_specs=VMEM,
         scratch_shapes=[spectrum],
         compiler_params=PARAMS,
@@ -488,12 +534,12 @@
     return pl.pallas_call(
         other_kernel,
         out_shape=jax.ShapeDtypeStruct((match_count, 2, 1, lines, width), jnp.float32),
-        in_specs=[SMEM] + [VMEM] * (4 + len(others)),
+        in_specs=[SMEM] + [VMEM] * (5 + len(others)),
         out_specs=HBM,
         scratch_shapes=[
             pltpu.VMEM((dates - 1, 2, lines, width), jnp.float32),
             spectrum,
-            pltpu.SemaphoreType.DMA((match_count, lines // HALF)),
+            pltpu.SemaphoreType.DMA((match_count,)),
         ],
         compiler_params=PARAMS,
         name="filter_other",

time: 16.8 us -> 16.9 us (level)
  waiting for transfers between devices: 4.68 us -> 2.78 us
  starting transfers between devices: 5.51 us -> 6.99 us
  Pallas kernels: 6.36 us -> 6.78 us
    ppermute x2 -> x3, starting transfers between devices: 2.06 us -> 4.96 us  [from_date(): lax.ppermute(piece, 'date', [((i + slot) % dates, i) for i in range(dates)])]
    ppermute x2 -> x3, waiting for transfers between devices: 2.51 us -> 0.25 us  [from_date(): lax.ppermute(piece, 'date', [((i + slot) % dates, i) for i in range(dates)])]
    ppermute x2, starting transfers between devices: 3 us -> 1.58 us  [swapped(): return lax.ppermute(value, ('az', 'rg'), pairs)]
    pallas_call x4 -> x8, Pallas kernels: 1.27 us -> 1.89 us  [the longest x5 1.57 us: resampled(): pl.pallas_call(kernel, out_shape=jax.ShapeDtypeStruct((2, count, width +...]
    ppermute x2, waiting for transfers between devices: 1.91 us -> 2.28 us  [swapped(): return lax.ppermute(value, ('az', 'rg'), pairs)]
    pallas_call x1, Pallas kernels: 1.41 us -> 1.19 us  [per_device(): pl.pallas_call(own_kernel, out_shape=jax.ShapeDtypeStruct((2, lines, widt...]
  transfers between devices with their start and end apart: 5 -> 6, of which waited for: 3 -> 3; matrix products, arithmetic and copies ran while one was open for 1% -> 1% of each run, Pallas kernels for 21% -> 22%
where the time goes in v11:
time: 16.9 us; the launch traced here: 16.8 us
  starting transfers between devices  6.99 us (41%)
  Pallas kernels  6.78 us (40%)
  waiting for transfers between devices  2.78 us (16%)
    ppermute x3, starting transfers between devices, from_date(): lax.ppermute(piece, 'date', [((i + slot) % dates, i) for i in range(dates)])  4.96 us
    pallas_call x1, Pallas kernels, per_device(): pl.pallas_call(other_kernel, out_shape=jax.ShapeDtypeStruct((match_count,...  2.76 us
    ppermute x2, waiting for transfers between devices, swapped(): return lax.ppermute(value, ('az', 'rg'), pairs)  2.28 us
    ppermute x2, starting transfers between devices, swapped(): return lax.ppermute(value, ('az', 'rg'), pairs)  1.58 us
    pallas_call x5, Pallas kernels, resampled(): pl.pallas_call(kernel, out_shape=jax.ShapeDtypeStruct((2, count, width +...  1.57 us
    pallas_call x1, Pallas kernels, per_device(): pl.pallas_call(own_kernel, out_shape=jax.ShapeDtypeStruct((2, lines, widt...  1.19 us
    pallas_call x1, Pallas kernels, per_device(): pl.pallas_call(load_kernel, out_shape=tuple((pltpu.VMEM(a.shape, a.dtype)...  0.93 us
    ppermute x1, starting transfers between devices, per_device(): lax.ppermute(image_stack, 'rg', [(0, 1), (1, 0)]).reshape(2, lines, width)  0.45 us
  transfers between devices with their start and end apart: 6, of which 3 were waited for; matrix products, arithmetic and copies ran while one was open for 1% of the time, Pallas kernels for 22%

profile of v11, /device:TPU:0, one launch (start us, length us, event | category | flops | bytes accessed | tf_op | source)
XLA Modules:
  0.0 16.8 jit_solution(6651604621033521977)
XLA Ops:
  0.0 0.5 %collective-permute-start = (f32[2,1,64,256]{3,2,0,1:T(8,128)}, f32[2,1,64,256]{3,2,0,1:T(8,128)S(1)}, u32[]{:S(2)}, u32[]{:S(2)}) collective-permute-start(f32[2,1,64,256]{3,2,0,1:T(8,128)} %bitcast.8), channel_id=1, source_target_pairs={{0,1},{1,0},{2,3},{3,2},{4,5},{5,4},{6,7},{7,6},{8,9},{9,8},{10,11... | collective-permute-start | bytes 393224 | tf_op jit(solution)/shard_map/ppermute | solution.py:428
  0.5 0.9 %load.1 = (f32[2,64,256]{2,1,0:T(8,128)S(1)}, f32[8,64]{1,0:T(8,128)S(1)}, s32[1,64]{1,0:T(1,128)S(1)}) custom-call(f32[2,64,256]{2,1,0:T(8,128)} %bitcast.9, f32[8,64]{1,0:T(8,128)} %bitcast.10, s32[1,64]{1,0:T(1,128)} %refs_2_.1), custom_call_target="tpu_custom_call" | custom-call | tf_op jit(solution)/shard_map/load/pallas_call | solution.py:434
  1.4 0.3 %collective-permute-done = f32[2,1,64,256]{3,2,0,1:T(8,128)S(1)} collective-permute-done((f32[2,1,64,256]{3,2,0,1:T(8,128)}, f32[2,1,64,256]{3,2,0,1:T(8,128)S(1)}, u32[]{:S(2)}, u32[]{:S(2)}) %collective-permute-start) | collective-permute-done | bytes 131104 | tf_op jit(solution)/shard_map/ppermute | solution.py:428
  1.7 0.3 %pack.1 = (bf16[112,256]{1,0:T(8,128)(2,1)S(1)}, bf16[112,256]{1,0:T(8,128)(2,1)S(1)}, bf16[160,256]{1,0:T(8,128)(2,1)S(1)}) custom-call(f32[2,64,256]{2,1,0:T(8,128)S(1)} %get-tuple-element.11.image_ref.refs_0_, f32[2,64,256]{2,1,0:T(8,128)S(1)} %bitcast.4, f32[8,64]{1,0:T(8,128)S(1)} %get-tuple-element.12.taps_ref.refs_2_, ...), custom_call_target="tpu_custom_call" | custom-call | tf_op jit(solution)/shard_map/pack/pallas_call | solution.py:445
  2.0 2.9 %collective-permute-start.3 = (bf16[160,256]{1,0:T(8,128)(2,1)S(1)}, bf16[160,256]{1,0:T(8,128)(2,1)S(1)}, u32[]{:S(2)}, u32[]{:S(2)}) collective-permute-start(bf16[160,256]{1,0:T(8,128)(2,1)S(1)} %get-tuple-element.16), channel_id=1, source_target_pairs={{2,0},{0,2},{3,1},{1,3},{6,4},{4,6},{7,5},{5,7},{10,8},{8,10},{11,... | collective-permute-start | bytes 245768 | tf_op jit(solution)/shard_map/ppermute | solution.py:460
  4.8 1.6 %collective-permute-start.1 = (bf16[112,256]{1,0:T(8,128)(2,1)S(1)}, bf16[112,256]{1,0:T(8,128)(2,1)S(1)}, u32[]{:S(2)}, u32[]{:S(2)}) collective-permute-start(bf16[112,256]{1,0:T(8,128)(2,1)S(1)} %get-tuple-element.14), channel_id=1, source_target_pairs={{0,4},{1,5},{4,0},{5,1},{8,12},{9,13},{12,8},{13,9},{2,6},{3,7},{6... | collective-permute-start | bytes 172040 | tf_op jit(solution)/shard_map/ppermute | solution.py:474
  6.4 0.0 copy-start
  6.4 0.0 collective-permute-start.2
  6.4 0.3 %own_inner.1.inner_ref.refs_0_ = bf16[2,32,288]{2,1,0:T(8,128)(2,1)S(1)} custom-call(f32[2,64,256]{2,1,0:T(8,128)S(1)} %get-tuple-element.11.image_ref.refs_0_, f32[2,64,256]{2,1,0:T(8,128)S(1)} %bitcast.5, f32[8,64]{1,0:T(8,128)S(1)} %get-tuple-element.12.taps_ref.refs_2_, s32[1,64]{1,0:T(1,128)S(1)} %get-tuple-element.13.offsets_ref.refs_3_), custom_call_target="tpu_custom_call" | custom-call | tf_op jit(solution)/shard_map/own_inner/pallas_call | solution.py:478
  6.7 2.3 %collective-permute-done.1.refs_4_.message_ref = bf16[112,256]{1,0:T(8,128)(2,1)S(1)} collective-permute-done((bf16[112,256]{1,0:T(8,128)(2,1)S(1)}, bf16[112,256]{1,0:T(8,128)(2,1)S(1)}, u32[]{:S(2)}, u32[]{:S(2)}) %collective-permute-start.1) | collective-permute-done | bytes 57376 | tf_op jit(solution)/shard_map/ppermute | solution.py:474
  9.0 0.1 collective-permute-start.4
  9.1 0.3 %own_side_a.1.first_ref.refs_0_ = bf16[2,48,288]{2,1,0:T(8,128)(2,1)S(1)} custom-call(f32[2,64,256]{2,1,0:T(8,128)S(1)} %get-tuple-element.11.image_ref.refs_0_, f32[2,64,256]{2,1,0:T(8,128)S(1)} %bitcast.6, f32[8,64]{1,0:T(8,128)S(1)} %get-tuple-element.12.taps_ref.refs_2_, s32[1,64]{1,0:T(1,128)S(1)} %get-tuple-element.13.offsets_ref.refs_3_, ...), custom_call_target="tpu_custom_call" | custom-call | tf_op jit(solution)/shard_map/own_side_a/pallas_call | solution.py:478
  9.4 0.0 collective-permute-done.3.refs_0_.refs_2_
  9.4 0.3 %partner_inner.1.refs_1_ = bf16[2,32,288]{2,1,0:T(8,128)(2,1)S(1)} custom-call(bf16[160,256]{1,0:T(8,128)(2,1)S(1)} %collective-permute-done.3.refs_0_.refs_2_), custom_call_target="tpu_custom_call" | custom-call | tf_op jit(solution)/shard_map/partner_inner/pallas_call | solution.py:478
  9.7 0.0 copy-start.1
  9.7 0.0 collective-permute-done.2.refs_4_.message_ref
  9.8 2.0 %collective-permute-start.5 = (bf16[112,256]{1,0:T(8,128)(2,1)S(1)}, bf16[112,256]{1,0:T(8,128)(2,1)S(1)}, u32[]{:S(2)}, u32[]{:S(2)}) collective-permute-start(bf16[112,256]{1,0:T(8,128)(2,1)S(1)} %pass_b.1), channel_id=1, source_target_pairs={{2,0},{0,2},{3,1},{1,3},{6,4},{4,6},{7,5},{5,7},{10,8},{8,10},{11,... | collective-permute-start | bytes 172040 | tf_op jit(solution)/shard_map/ppermute | solution.py:460
  11.8 0.0 copy-done.1
  11.8 0.1 copy.7.match_ref
  11.9 0.3 %own_side_b.1.second_ref = bf16[2,48,288]{2,1,0:T(8,128)(2,1)S(1)} custom-call(f32[2,64,256]{2,1,0:T(8,128)S(1)} %get-tuple-element.11.image_ref.refs_0_, f32[2,64,256]{2,1,0:T(8,128)S(1)} %bitcast.7, f32[8,64]{1,0:T(8,128)S(1)} %get-tuple-element.12.taps_ref.refs_2_, s32[1,64]{1,0:T(1,128)S(1)} %get-tuple-element.13.offsets_ref.refs_3_, ...), custom_call_target="tpu_custom_call" | custom-call | tf_op jit(solution)/shard_map/own_side_b/pallas_call | solution.py:478
  12.2 0.0 copy-done
  12.2 1.2 %filter_own.1.filtered_own_ref = f32[2,64,256]{2,1,0:T(8,128)S(1)} custom-call(bf16[1472,256]{1,0:T(8,128)(2,1)S(1)} %copy-done, bf16[2,48,288]{2,1,0:T(8,128)(2,1)S(1)} %own_side_a.1.first_ref.refs_0_, bf16[2,32,288]{2,1,0:T(8,128)(2,1)S(1)} %own_inner.1.inner_ref.refs_0_, bf16[2,48,288]{2,1,0:T(8,128)(2,1)S(1)} %own_side_b.1.second_ref), custom_call_target="tpu_custom_call" | custom-call | tf_op jit(solution)/shard_map/filter_own/pallas_call | solution.py:525
  13.4 0.0 collective-permute-done.4.refs_1_
  13.4 0.3 %partner_side_a.1.refs_0_ = bf16[2,48,288]{2,1,0:T(8,128)(2,1)S(1)} custom-call(bf16[160,256]{1,0:T(8,128)(2,1)S(1)} %collective-permute-done.3.refs_0_.refs_2_, bf16[112,256]{1,0:T(8,128)(2,1)S(1)} %collective-permute-done.4.refs_1_), custom_call_target="tpu_custom_call" | custom-call | tf_op jit(solution)/shard_map/partner_side_a/pallas_call | solution.py:478
  13.8 0.2 %collective-permute-done.5.refs_3_ = bf16[112,256]{1,0:T(8,128)(2,1)S(1)} collective-permute-done((bf16[112,256]{1,0:T(8,128)(2,1)S(1)}, bf16[112,256]{1,0:T(8,128)(2,1)S(1)}, u32[]{:S(2)}, u32[]{:S(2)}) %collective-permute-start.5) | collective-permute-done | bytes 57376 | tf_op jit(solution)/shard_map/ppermute | solution.py:460
  14.0 2.8 %filter_other.1 = f32[3,2,1,64,256]{4,3,2,1,0:T(8,128)} custom-call(s32[3,2]{1,0:T(4,128)S(1)} %copy.7.match_ref, bf16[1472,256]{1,0:T(8,128)(2,1)S(1)} %copy-done, f32[2,64,256]{2,1,0:T(8,128)S(1)} %filter_own.1.filtered_own_ref, bf16[2,48,288]{2,1,0:T(8,128)(2,1)S(1)} %own_side_a.1.first_ref.refs_0_, bf16[2,32,288]{2,1,0:T(8,128)(2,1)S(1)} %own_inner.1.inner_ref.refs_0_, ...), custom_call_target="tpu_custom_call" | custom-call | tf_op jit(solution)/shard_map/filter_other/pallas_call | solution.py:534
  (2 shorter events, 0.0 us)
Async XLA Ops:
  0.0 1.6 %collective-permute-start = (f32[2,1,64,256]{3,2,0,1:T(8,128)}, f32[2,1,64,256]{3,2,0,1:T(8,128)S(1)}, u32[]{:S(2)}, u32[]{:S(2)}) collective-permute-start(f32[2,1,64,256]{3,2,0,1:T(8,128)} %bitcast.8), channel_id=1, source_target_pairs={{0,1},{1,0},{2,3},{3,2},{4,5},{5,4},{6,7},{7,6},{8,9},{9,8},{10,11... | collective-permute-start | bytes 393224 | tf_op jit(solution)/shard_map/ppermute | solution.py:428
  2.0 7.5 %collective-permute-start.3 = (bf16[160,256]{1,0:T(8,128)(2,1)S(1)}, bf16[160,256]{1,0:T(8,128)(2,1)S(1)}, u32[]{:S(2)}, u32[]{:S(2)}) collective-permute-start(bf16[160,256]{1,0:T(8,128)(2,1)S(1)} %get-tuple-element.16), channel_id=1, source_target_pairs={{2,0},{0,2},{3,1},{1,3},{6,4},{4,6},{7,5},{5,7},{10,8},{8,10},{11,... | collective-permute-start | bytes 245768 | tf_op jit(solution)/shard_map/ppermute | solution.py:460
  4.8 4.2 %collective-permute-start.1 = (bf16[112,256]{1,0:T(8,128)(2,1)S(1)}, bf16[112,256]{1,0:T(8,128)(2,1)S(1)}, u32[]{:S(2)}, u32[]{:S(2)}) collective-permute-start(bf16[112,256]{1,0:T(8,128)(2,1)S(1)} %get-tuple-element.14), channel_id=1, source_target_pairs={{0,4},{1,5},{4,0},{5,1},{8,12},{9,13},{12,8},{13,9},{2,6},{3,7},{6... | collective-permute-start | bytes 172040 | tf_op jit(solution)/shard_map/ppermute | solution.py:474
  6.4 5.8 %copy-start = (bf16[1472,256]{1,0:T(8,128)(2,1)S(1)}, bf16[1472,256]{1,0:T(8,128)(2,1)}, u32[]{:S(2)}) copy-start(bf16[1472,256]{1,0:T(8,128)(2,1)} %constant.2.clone.table_ref) | copy-start | bytes 2260996
  6.4 3.3 %collective-permute-start.2 = (bf16[112,256]{1,0:T(8,128)(2,1)S(1)}, bf16[112,256]{1,0:T(8,128)(2,1)S(1)}, u32[]{:S(2)}, u32[]{:S(2)}) collective-permute-start(bf16[112,256]{1,0:T(8,128)(2,1)S(1)} %get-tuple-element.15), channel_id=1, source_target_pairs={{0,1},{1,0},{4,8},{5,9},{8,4},{9,5},{12,13},{13,12},{2,3},{3,2},{6... | collective-permute-start | bytes 172040 | tf_op jit(solution)/shard_map/ppermute | solution.py:474
  9.0 4.4 %collective-permute-start.4 = (bf16[112,256]{1,0:T(8,128)(2,1)S(1)}, bf16[112,256]{1,0:T(8,128)(2,1)S(1)}, u32[]{:S(2)}, u32[]{:S(2)}) collective-permute-start(bf16[112,256]{1,0:T(8,128)(2,1)S(1)} %pass_a.1), channel_id=1, source_target_pairs={{2,0},{0,2},{3,1},{1,3},{6,4},{4,6},{7,5},{5,7},{10,8},{8,10},{11,... | collective-permute-start | bytes 172040 | tf_op jit(solution)/shard_map/ppermute | solution.py:460
  9.7 2.0 %copy-start.1 = (s32[3,2]{0,1:T(2,128)S(1)}, s32[3,2]{0,1:T(2,128)}, u32[]{:S(2)}) copy-start(s32[3,2]{0,1:T(2,128)} %param.8) | copy-start | bytes 76
  9.8 4.2 %collective-permute-start.5 = (bf16[112,256]{1,0:T(8,128)(2,1)S(1)}, bf16[112,256]{1,0:T(8,128)(2,1)S(1)}, u32[]{:S(2)}, u32[]{:S(2)}) collective-permute-start(bf16[112,256]{1,0:T(8,128)(2,1)S(1)} %pass_b.1), channel_id=1, source_target_pairs={{2,0},{0,2},{3,1},{1,3},{6,4},{4,6},{7,5},{5,7},{10,8},{8,10},{11,... | collective-permute-start | bytes 172040 | tf_op jit(solution)/shard_map/ppermute | solution.py:460

commit v12 on v10

--- a/solution.py
+++ b/solution.py
@@ -20,7 +20,6 @@
 VMEM_LIMIT = 48 * 1024 * 1024
 
 VMEM = pl.BlockSpec(memory_space=pltpu.VMEM)
-SMEM = pl.BlockSpec(memory_space=pltpu.SMEM)
 HBM = pl.BlockSpec(memory_space=pltpu.HBM)
 PARAMS = pltpu.CompilerParams(vmem_limit_bytes=VMEM_LIMIT)
 
@@ -251,7 +250,7 @@
     return tiles, edges
 
 
-def filtered_of(own_refs, other_refs, table_ref, spectrum_ref, lines, emit):
+def filtered_of(own_refs, other_refs, table_ref, spectrum_ref, lines, meanwhile=None):
     width = own_refs[0].shape[1]
     wide = lines + 2 * HALF
     row_patches = lines // HALF + 1
@@ -279,6 +278,8 @@
             pieces.append(jnp.concatenate([real, imag], axis=1))
     patches = jnp.concatenate(pieces, axis=0)
     spectrum_ref[...] = jnp.dot(patches, forward, preferred_element_type=jnp.float32)
+    if meanwhile is not None:
+        meanwhile()
     powers = []
     for block in range(row_patches * chunks):
         rows = slice(block * PATCH, (block + 1) * PATCH)
@@ -295,7 +296,7 @@
     range_back = jnp.dot(shaped, inverse, preferred_element_type=jnp.float32)
     range_back = range_back.astype(jnp.bfloat16)
     window = jnp.concatenate([window] * chunks, axis=1)
-    earlier = None
+    totals = [[None] * (row_patches - 1) for _ in range(2)]
     for row in range(row_patches):
         stacked = []
         for chunk in range(chunks):
@@ -304,60 +305,64 @@
             stacked.append(jnp.concatenate([block[:, :LANES], block[:, LANES:]], axis=0))
         stacked = jnp.concatenate(stacked, axis=1)
         patch_out = jnp.dot(back, stacked, preferred_element_type=jnp.float32) * window
-        uppers = [patch_out[part * PATCH : part * PATCH + HALF] for part in range(2)]
-        if row > 0:
-            total = jnp.concatenate(uppers, axis=0) + earlier
-            total = total[:, :width] + total[:, width + HALF : 2 * width + HALF]
-            emit(row - 1, total)
-        lowers = [patch_out[part * PATCH + HALF : (part + 1) * PATCH] for part in range(2)]
-        earlier = jnp.concatenate(lowers, axis=0)
-
-
-def keep(ref, row, total):
+        for part in range(2):
+            upper = patch_out[part * PATCH : part * PATCH + HALF]
+            lower = patch_out[part * PATCH + HALF : (part + 1) * PATCH]
+            if row > 0:
+                totals[part][row - 1] = totals[part][row - 1] + upper
+            if row < row_patches - 1:
+                totals[part][row] = lower
+    total = jnp.concatenate([block for part in totals for block in part], axis=0)
+    return total[:, :width] + total[:, width + HALF : 2 * width + HALF]
+
+
+def keep(ref, result):
+    lines = ref.shape[1]
     for part in range(2):
-        ref[part, row * HALF : (row + 1) * HALF] = total[part * HALF : (part + 1) * HALF]
+        ref[part] = result[part * lines : (part + 1) * lines]
 
 
 def own_kernel(table_ref, first_ref, second_ref, out_ref, spectrum_ref):
     own = (first_ref, second_ref)
-    lines = out_ref.shape[1]
-    filtered_of(own, own, table_ref, spectrum_ref, lines, functools.partial(keep, out_ref))
-
-
-def other_kernel(match_ref, table_ref, filtered_own_ref, first_ref, second_ref, *refs):
-    out_ref, result_ref, spectrum_ref, sems = refs[-4:]
+    keep(out_ref, filtered_of(own, own, table_ref, spectrum_ref, out_ref.shape[1]))
+
+
+def other_kernel(matchings_ref, table_ref, filtered_own_ref, first_ref, second_ref, *refs):
+    out_ref, match_ref, result_ref, spectrum_ref, sems = refs[-5:]
     match_count, _, _, lines, _ = out_ref.shape
     date = lax.axis_index("date")
     dates = match_ref.shape[1]
-    rows = lines // HALF
-
-    def copy_of(match, row, source_ref):
-        cut = slice(row * HALF, (row + 1) * HALF)
-        target = out_ref.at[match, :, 0, cut]
-        return pltpu.make_async_copy(source_ref.at[:, cut], target, sems.at[match, row])
-
-    def send(slot, row, source_ref):
+    fetch = pltpu.make_async_copy(matchings_ref, match_ref, sems.at[match_count])
+    fetch.start()
+
+    def copy_of(match, source_ref):
+        return pltpu.make_async_copy(source_ref, out_ref.at[match, :, 0], sems.at[match])
+
+    def send(slot, source_ref):
         for match in range(match_count):
             wanted = lax.rem(match_ref[match, date] - date + dates, dates)
 
             @pl.when(wanted == slot)
             def _():
-                copy_of(match, row, source_ref).start()
-
-    for row in range(rows):
-        send(0, row, filtered_own_ref)
+                copy_of(match, source_ref).start()
+
+    def meanwhile():
+        fetch.wait()
+        send(0, filtered_own_ref)
+
     for slot in range(1, dates):
-        other = refs[2 * slot - 2 : 2 * slot]
-        target_ref = result_ref.at[slot - 1]
-
-        def emit(row, total):
-            keep(target_ref, row, total)
-            send(slot, row, target_ref)
-
-        filtered_of((first_ref, second_ref), other, table_ref, spectrum_ref, lines, emit)
+        result = filtered_of(
+            (first_ref, second_ref),
+            refs[2 * slot - 2 : 2 * slot],
+            table_ref,
+            spectrum_ref,
+            lines,
+            meanwhile if slot == 1 else None,
+        )
+        keep(result_ref.at[slot - 1], result)
+        send(slot, result_ref.at[slot - 1])
     for match in range(match_count):
-        for row in range(rows):
-            copy_of(match, row, filtered_own_ref).wait()
+        copy_of(match, filtered_own_ref).wait()
 
 
 def all_tables(row_patches):
@@ -488,16 +493,17 @@
     return pl.pallas_call(
         other_kernel,
         out_shape=jax.ShapeDtypeStruct((match_count, 2, 1, lines, width), jnp.float32),
-        in_specs=[SMEM] + [VMEM] * (4 + len(others)),
+        in_specs=[HBM] + [VMEM] * (4 + len(others)),
         out_specs=HBM,
         scratch_shapes=[
+            pltpu.SMEM(matchings.shape, jnp.int32),
             pltpu.VMEM((dates - 1, 2, lines, width), jnp.float32),
             spectrum,
-            pltpu.SemaphoreType.DMA((match_count, lines // HALF)),
+            pltpu.SemaphoreType.DMA((match_count + 1,)),
         ],
         compiler_params=PARAMS,
         name="filter_other",
-    )(matchings, tables, filtered_own, *own, *others)
+    )(pltpu.with_memory_space_constraint(matchings, pltpu.HBM), tables, filtered_own, *own, *others)
 
 
 def solution(mesh):

time: 16.8 us -> 16.5 us (0.982); the launches traced: 16.7 us -> 16.7 us
  local copies, waits for them, and re-layouts: 0.1 us -> 0.69 us
  waiting for transfers between devices: 4.68 us -> 4.09 us
    unnamed x5, local copies, waits for them, and re-layouts: 0.1 us -> 0.69 us
    ppermute x2, waiting for transfers between devices: 2.51 us -> 1.92 us  [from_date(): lax.ppermute(piece, 'date', [((i + slot) % dates, i) for i in range(dates)])]
  transfers between devices with their start and end apart: 5 -> 5, of which waited for: 3 -> 3; matrix products, arithmetic and copies ran while one was open for 1% -> 4% of each run, Pallas kernels for 21% -> 21%
where the time goes in v12:
time: 16.5 us; the launch traced here: 16.7 us
  Pallas kernels  6.34 us (38%)
  starting transfers between devices  5.51 us (33%)
  waiting for transfers between devices  4.09 us (25%)
  local copies, waits for them, and re-layouts  0.69 us (4%)
    ppermute x2, starting transfers between devices, swapped(): return lax.ppermute(value, ('az', 'rg'), pairs)  3 us
    pallas_call x1, Pallas kernels, per_device(): pl.pallas_call(other_kernel, out_shape=jax.ShapeDtypeStruct((match_count,...  2.74 us
    ppermute x2, starting transfers between devices, from_date(): lax.ppermute(piece, 'date', [((i + slot) % dates, i) for i in range(dates)])  2.06 us
    ppermute x2, waiting for transfers between devices, from_date(): lax.ppermute(piece, 'date', [((i + slot) % dates, i) for i in range(dates)])  1.92 us
    ppermute x2, waiting for transfers between devices, swapped(): return lax.ppermute(value, ('az', 'rg'), pairs)  1.91 us
    pallas_call x1, Pallas kernels, per_device(): pl.pallas_call(own_kernel, out_shape=jax.ShapeDtypeStruct((2, lines, widt...  1.41 us
    pallas_call x1, Pallas kernels, per_device(): pl.pallas_call(load_kernel, out_shape=tuple((pltpu.VMEM(a.shape, a.dtype)...  0.93 us
    pallas_call x2, Pallas kernels, per_device(): own.append(call(*raw, messages[turn], inner, *own))  0.8 us
  transfers between devices with their start and end apart: 5, of which 3 were waited for; matrix products, arithmetic and copies ran while one was open for 4% of the time, Pallas kernels for 21%

profile of v12, /device:TPU:0, one launch (start us, length us, event | category | flops | bytes accessed | tf_op | source)
XLA Modules:
  0.0 16.7 jit_solution(4394180678445315384)
XLA Ops:
  0.0 0.5 %collective-permute-start = (f32[2,1,64,256]{3,2,0,1:T(8,128)}, f32[2,1,64,256]{3,2,0,1:T(8,128)S(1)}, u32[]{:S(2)}, u32[]{:S(2)}) collective-permute-start(f32[2,1,64,256]{3,2,0,1:T(8,128)} %bitcast.8), channel_id=1, source_target_pairs={{0,1},{1,0},{2,3},{3,2},{4,5},{5,4},{6,7},{7,6},{8,9},{9,8},{10,11... | collective-permute-start | bytes 393224 | tf_op jit(solution)/shard_map/ppermute | solution.py:416
  0.5 0.9 %load.1 = (f32[2,64,256]{2,1,0:T(8,128)S(1)}, f32[8,64]{1,0:T(8,128)S(1)}, s32[1,64]{1,0:T(1,128)S(1)}) custom-call(f32[2,64,256]{2,1,0:T(8,128)} %bitcast.9, f32[8,64]{1,0:T(8,128)} %bitcast.10, s32[1,64]{1,0:T(1,128)} %refs_2_.1), custom_call_target="tpu_custom_call" | custom-call | tf_op jit(solution)/shard_map/load/pallas_call | solution.py:422
  1.4 0.3 %collective-permute-done = f32[2,1,64,256]{3,2,0,1:T(8,128)S(1)} collective-permute-done((f32[2,1,64,256]{3,2,0,1:T(8,128)}, f32[2,1,64,256]{3,2,0,1:T(8,128)S(1)}, u32[]{:S(2)}, u32[]{:S(2)}) %collective-permute-start) | collective-permute-done | bytes 131104 | tf_op jit(solution)/shard_map/ppermute | solution.py:416
  1.7 0.2 pack.1
  1.8 0.0 copy-start
  1.8 3.0 %collective-permute-start.1 = (bf16[112,256]{1,0:T(8,128)(2,1)S(1)}, bf16[112,256]{1,0:T(8,128)(2,1)S(1)}, u32[]{:S(2)}, u32[]{:S(2)}) collective-permute-start(bf16[112,256]{1,0:T(8,128)(2,1)S(1)} %get-tuple-element.13), channel_id=1, source_target_pairs={{0,4},{1,5},{4,0},{5,1},{8,12},{9,13},{12,8},{13,9},{2,6},{3,7},{6... | collective-permute-start | bytes 172040 | tf_op jit(solution)/shard_map/ppermute | solution.py:451
  4.8 0.0 collective-permute-start.2
  4.8 0.3 %inner.1.inner_ref = f32[2,32,288]{2,1,0:T(8,128)S(1)} custom-call(f32[2,64,256]{2,1,0:T(8,128)S(1)} %get-tuple-element.10.image_ref, f32[2,64,256]{2,1,0:T(8,128)S(1)} %bitcast.5, f32[8,64]{1,0:T(8,128)S(1)} %get-tuple-element.11.taps_ref, s32[1,64]{1,0:T(1,128)S(1)} %get-tuple-element.12.offsets_ref), custom_call_target="tpu_custom_call" | custom-call | tf_op jit(solution)/shard_map/inner/pallas_call | solution.py:454
  5.1 1.9 %collective-permute-done.1.message_ref = bf16[112,256]{1,0:T(8,128)(2,1)S(1)} collective-permute-done((bf16[112,256]{1,0:T(8,128)(2,1)S(1)}, bf16[112,256]{1,0:T(8,128)(2,1)S(1)}, u32[]{:S(2)}, u32[]{:S(2)}) %collective-permute-start.1) | collective-permute-done | bytes 57376 | tf_op jit(solution)/shard_map/ppermute | solution.py:451
  7.1 0.4 %side_a.1.refs_0_.first_ref = bf16[176,256]{1,0:T(8,128)(2,1)S(1)} custom-call(f32[2,64,256]{2,1,0:T(8,128)S(1)} %get-tuple-element.10.image_ref, f32[2,64,256]{2,1,0:T(8,128)S(1)} %bitcast.6, f32[8,64]{1,0:T(8,128)S(1)} %get-tuple-element.11.taps_ref, s32[1,64]{1,0:T(1,128)S(1)} %get-tuple-element.12.offsets_ref, ...), custom_call_target="tpu_custom_call" | custom-call | tf_op jit(solution)/shard_map/side_a/pallas_call | solution.py:473
  7.5 0.0 copy-start.1
  7.5 1.9 %collective-permute-start.3 = (bf16[176,256]{1,0:T(8,128)(2,1)S(1)}, bf16[176,256]{1,0:T(8,128)(2,1)S(1)}, u32[]{:S(2)}, u32[]{:S(2)}) collective-permute-start(bf16[176,256]{1,0:T(8,128)(2,1)S(1)} %side_a.1.refs_0_.first_ref), channel_id=1, source_target_pairs={{2,0},{0,2},{3,1},{1,3},{6,4},{4,6},{7,5},{5,7},{10,8},{8,10},{11,... | collective-permute-start | bytes 270344 | tf_op jit(solution)/shard_map/ppermute | solution.py:477
  9.3 0.0 collective-permute-done.2.message_ref
  9.4 0.4 %side_b.1.second_ref = bf16[112,256]{1,0:T(8,128)(2,1)S(1)} custom-call(f32[2,64,256]{2,1,0:T(8,128)S(1)} %get-tuple-element.10.image_ref, f32[2,64,256]{2,1,0:T(8,128)S(1)} %bitcast.7, f32[8,64]{1,0:T(8,128)S(1)} %get-tuple-element.11.taps_ref, s32[1,64]{1,0:T(1,128)S(1)} %get-tuple-element.12.offsets_ref, ...), custom_call_target="tpu_custom_call" | custom-call | tf_op jit(solution)/shard_map/side_b/pallas_call | solution.py:473
  9.8 0.2 %collective-permute-start.4 = (bf16[112,256]{1,0:T(8,128)(2,1)S(1)}, bf16[112,256]{1,0:T(8,128)(2,1)S(1)}, u32[]{:S(2)}, u32[]{:S(2)}) collective-permute-start(bf16[112,256]{1,0:T(8,128)(2,1)S(1)} %side_b.1.second_ref), channel_id=1, source_target_pairs={{2,0},{0,2},{3,1},{1,3},{6,4},{4,6},{7,5},{5,7},{10,8},{8,10},{11,... | collective-permute-start | bytes 172040 | tf_op jit(solution)/shard_map/ppermute | solution.py:477
  9.9 0.0 copy-done.1
  9.9 0.7 %copy.7.matchings_ref = s32[3,2]{1,0:T(4,128)} copy(s32[3,2]{0,1:T(2,128)S(1)} %copy-done.1) | data formatting | bytes 48 | tf_op args[3]
  10.6 0.0 copy-done
  10.6 1.4 %filter_own.1.filtered_own_ref = f32[2,64,256]{2,1,0:T(8,128)S(1)} custom-call(bf16[1472,256]{1,0:T(8,128)(2,1)S(1)} %copy-done, bf16[176,256]{1,0:T(8,128)(2,1)S(1)} %side_a.1.refs_0_.first_ref, bf16[112,256]{1,0:T(8,128)(2,1)S(1)} %side_b.1.second_ref), custom_call_target="tpu_custom_call" | custom-call | tf_op jit(solution)/shard_map/filter_own/pallas_call | solution.py:484
  12.0 1.9 %collective-permute-done.4.refs_1_ = bf16[112,256]{1,0:T(8,128)(2,1)S(1)} collective-permute-done((bf16[112,256]{1,0:T(8,128)(2,1)S(1)}, bf16[112,256]{1,0:T(8,128)(2,1)S(1)}, u32[]{:S(2)}, u32[]{:S(2)}) %collective-permute-start.4) | collective-permute-done | bytes 57376 | tf_op jit(solution)/shard_map/ppermute | solution.py:477
  13.9 0.0 collective-permute-done.3.refs_0_
  13.9 2.7 %filter_other.1 = f32[3,2,1,64,256]{4,3,2,1,0:T(8,128)} custom-call(s32[3,2]{1,0:T(4,128)} %copy.7.matchings_ref, bf16[1472,256]{1,0:T(8,128)(2,1)S(1)} %copy-done, f32[2,64,256]{2,1,0:T(8,128)S(1)} %filter_own.1.filtered_own_ref, bf16[176,256]{1,0:T(8,128)(2,1)S(1)} %side_a.1.refs_0_.first_ref, bf16[112,256]{1,0:T(8,128)(2,1)S(1)} %side_b.1.second_ref, ...), custom_call_target="tpu_custom_call" | custom-call | tf_op jit(solution)/shard_map/filter_other/pallas_call | solution.py:493
Async XLA Ops:
  0.0 1.6 %collective-permute-start = (f32[2,1,64,256]{3,2,0,1:T(8,128)}, f32[2,1,64,256]{3,2,0,1:T(8,128)S(1)}, u32[]{:S(2)}, u32[]{:S(2)}) collective-permute-start(f32[2,1,64,256]{3,2,0,1:T(8,128)} %bitcast.8), channel_id=1, source_target_pairs={{0,1},{1,0},{2,3},{3,2},{4,5},{5,4},{6,7},{7,6},{8,9},{9,8},{10,11... | collective-permute-start | bytes 393224 | tf_op jit(solution)/shard_map/ppermute | solution.py:416
  1.8 8.8 %copy-start = (bf16[1472,256]{1,0:T(8,128)(2,1)S(1)}, bf16[1472,256]{1,0:T(8,128)(2,1)}, u32[]{:S(2)}) copy-start(bf16[1472,256]{1,0:T(8,128)(2,1)} %constant.2.clone.table_ref) | copy-start | bytes 2260996
  1.8 5.2 %collective-permute-start.1 = (bf16[112,256]{1,0:T(8,128)(2,1)S(1)}, bf16[112,256]{1,0:T(8,128)(2,1)S(1)}, u32[]{:S(2)}, u32[]{:S(2)}) collective-permute-start(bf16[112,256]{1,0:T(8,128)(2,1)S(1)} %get-tuple-element.13), channel_id=1, source_target_pairs={{0,4},{1,5},{4,0},{5,1},{8,12},{9,13},{12,8},{13,9},{2,6},{3,7},{6... | collective-permute-start | bytes 172040 | tf_op jit(solution)/shard_map/ppermute | solution.py:451
  4.8 4.5 %collective-permute-start.2 = (bf16[112,256]{1,0:T(8,128)(2,1)S(1)}, bf16[112,256]{1,0:T(8,128)(2,1)S(1)}, u32[]{:S(2)}, u32[]{:S(2)}) collective-permute-start(bf16[112,256]{1,0:T(8,128)(2,1)S(1)} %get-tuple-element.14), channel_id=1, source_target_pairs={{0,1},{1,0},{4,8},{5,9},{8,4},{9,5},{12,13},{13,12},{2,3},{3,2},{6... | collective-permute-start | bytes 172040 | tf_op jit(solution)/shard_map/ppermute | solution.py:451
  7.5 2.5 %copy-start.1 = (s32[3,2]{0,1:T(2,128)S(1)}, s32[3,2]{0,1:T(2,128)}, u32[]{:S(2)}) copy-start(s32[3,2]{0,1:T(2,128)} %param.8) | copy-start | bytes 76
  7.5 6.5 %collective-permute-start.3 = (bf16[176,256]{1,0:T(8,128)(2,1)S(1)}, bf16[176,256]{1,0:T(8,128)(2,1)S(1)}, u32[]{:S(2)}, u32[]{:S(2)}) collective-permute-start(bf16[176,256]{1,0:T(8,128)(2,1)S(1)} %side_a.1.refs_0_.first_ref), channel_id=1, source_target_pairs={{2,0},{0,2},{3,1},{1,3},{6,4},{4,6},{7,5},{5,7},{10,8},{8,10},{11,... | collective-permute-start | bytes 270344 | tf_op jit(solution)/shard_map/ppermute | solution.py:477
  9.8 4.2 %collective-permute-start.4 = (bf16[112,256]{1,0:T(8,128)(2,1)S(1)}, bf16[112,256]{1,0:T(8,128)(2,1)S(1)}, u32[]{:S(2)}, u32[]{:S(2)}) collective-permute-start(bf16[112,256]{1,0:T(8,128)(2,1)S(1)} %side_b.1.second_ref), channel_id=1, source_target_pairs={{2,0},{0,2},{3,1},{1,3},{6,4},{4,6},{7,5},{5,7},{10,8},{8,10},{11,... | collective-permute-start | bytes 172040 | tf_op jit(solution)/shard_map/ppermute | solution.py:477

commit v13 on v12

--- a/solution.py
+++ b/solution.py
@@ -20,6 +20,7 @@
 VMEM_LIMIT = 48 * 1024 * 1024
 
 VMEM = pl.BlockSpec(memory_space=pltpu.VMEM)
+SMEM = pl.BlockSpec(memory_space=pltpu.SMEM)
 HBM = pl.BlockSpec(memory_space=pltpu.HBM)
 PARAMS = pltpu.CompilerParams(vmem_limit_bytes=VMEM_LIMIT)
 
@@ -150,12 +151,19 @@
     return lax.dot_general(high_low(weights), rows, over_rows, preferred_element_type=jnp.float32)
 
 
-def write_piece(out_ref, parts, more_edge, width):
+def write_piece(out_ref, parts, width):
     lines = parts[0].shape[0]
     for part, value in enumerate(parts):
         out_ref[part * lines : (part + 1) * lines, :] = value[:, :width].astype(jnp.bfloat16)
-    edges = side_by_side([value[:REACH, width:] for value in parts] + [more_edge])
+    edges = side_by_side([value[:, width:] for value in parts])
     out_ref[2 * lines :, :] = edges.astype(jnp.bfloat16)
+
+
+def read_piece(ref):
+    lines = (ref.shape[0] - STEP) // 2
+    tiles = ref[: 2 * lines, :].astype(jnp.float32)
+    edges = one_below(ref[2 * lines :, :].astype(jnp.float32), 0, 2 * lines // STEP)
+    return [(v[:lines], v[lines:]) for v in (tiles, edges)]
 
 
 def inner_kernel(image_ref, other_ref, taps_ref, offsets_ref, out_ref):
@@ -217,10 +225,11 @@
         cut = slice(part * REACH, (part + 1) * REACH)
         rim = jnp.concatenate([message[cut, :], rim_edges[cut]], axis=1)
         total = apply_band(weights, jnp.concatenate([rim, own], axis=0))
-        if turn == 0:
-            total = jnp.concatenate([total, inner_ref[part]], axis=0)
-        parts.append(total)
-    write_piece(out_ref, parts, inner_ref[turn, :, width:], width)
+        between = inner_ref.shape[1] // 2
+        upper = jnp.concatenate([total, inner_ref[part, :between]], axis=0)
+        lower = jnp.concatenate([inner_ref[part, between:], total], axis=0)
+        parts.append(jnp.where(above, upper, lower))
+    write_piece(out_ref, parts, width)
 
 
 def cross(own_parts, other_parts):
@@ -231,43 +240,28 @@
     return real, imag
 
 
-def tile_of(first_ref, second_ref, lines):
-    inner = lines - 2 * RIM
-    step, more = REACH // STEP, inner // STEP
-
-    def split(ref, count):
-        tiles = ref[: 2 * count, :].astype(jnp.float32)
-        block = ref[2 * count :, :].astype(jnp.float32)
-        edges = [one_below(block, part * step, (part + 1) * step) for part in range(2)]
-        return (tiles[:count], tiles[count:]), edges, one_below(block, 2 * step, 2 * step + more)
-
-    first = split(first_ref, REACH + inner)
-    second = split(second_ref, REACH)
-    tiles, edges = [], []
-    for part, middle in enumerate((first[2], second[2])):
-        tiles.append(jnp.concatenate([first[0][part], second[0][part]], axis=0))
-        edges.append(jnp.concatenate([first[1][part], middle, second[1][part]], axis=0))
-    return tiles, edges
-
-
-def filtered_of(own_refs, other_refs, table_ref, spectrum_ref, lines, meanwhile=None):
-    width = own_refs[0].shape[1]
-    wide = lines + 2 * HALF
-    row_patches = lines // HALF + 1
+def interferogram(own_ref, other_ref):
     side = lax.axis_index("rg")
-    line_table_of, forward, inverse, back, ring, window = split_tables(table_ref, row_patches)
-    own_tile, own_edge = tile_of(*own_refs, lines)
-    other_tile, other_edge = tile_of(*other_refs, lines)
+    own_tile, own_edge = read_piece(own_ref)
+    other_tile, other_edge = read_piece(other_ref)
     mid = jnp.concatenate(cross(own_tile, other_tile), axis=0)
     rim = jnp.concatenate(cross(own_edge, other_edge), axis=0)
     before = jnp.where(side == 0, 0.0, rim)
     after = jnp.where(side == 0, rim, 0.0)
-    filler = jnp.zeros((2 * wide, LANES - 2 * HALF), jnp.float32)
+    filler = jnp.zeros((mid.shape[0], LANES - 2 * HALF), jnp.float32)
     shifted = jnp.concatenate([before, mid, after, filler], axis=1).astype(jnp.bfloat16)
-    both = jnp.concatenate([mid.astype(jnp.bfloat16), shifted], axis=1)
-    chunks = both.shape[1] // LANES
-    line_spectra = jnp.dot(line_table_of, both, preferred_element_type=jnp.float32)
+    return jnp.concatenate([mid.astype(jnp.bfloat16), shifted], axis=1)
+
+
+def line_sum(turn, tables, own_ref, other_ref):
+    both = interferogram(own_ref, other_ref)
+    return jnp.dot(tables.lines(turn), both, preferred_element_type=jnp.float32)
+
+
+def filtered_of(line_spectra, tables, spectrum_ref, row_patches, width):
     line_spectra = line_spectra.astype(jnp.bfloat16)
+    chunks = line_spectra.shape[1] // LANES
+    forward, inverse, back, ring, window = tables.core()
     pieces = []
     for row in range(row_patches):
         top = row * 2 * PATCH
@@ -278,8 +272,6 @@
             pieces.append(jnp.concatenate([real, imag], axis=1))
     patches = jnp.concatenate(pieces, axis=0)
     spectrum_ref[...] = jnp.dot(patches, forward, preferred_element_type=jnp.float32)
-    if meanwhile is not None:
-        meanwhile()
     powers = []
     for block in range(row_patches * chunks):
         rows = slice(block * PATCH, (block + 1) * PATCH)
@@ -323,17 +315,26 @@
 
 
 def own_kernel(table_ref, first_ref, second_ref, out_ref, spectrum_ref):
-    own = (first_ref, second_ref)
-    keep(out_ref, filtered_of(own, own, table_ref, spectrum_ref, out_ref.shape[1]))
-
-
-def other_kernel(matchings_ref, table_ref, filtered_own_ref, first_ref, second_ref, *refs):
-    out_ref, match_ref, result_ref, spectrum_ref, sems = refs[-5:]
-    match_count, _, _, lines, _ = out_ref.shape
+    _, lines, width = out_ref.shape
+    row_patches = lines // HALF + 1
+    tables = Tables(table_ref, row_patches)
+    both = [interferogram(ref, ref) for ref in (first_ref, second_ref)]
+    weights = jnp.concatenate([tables.lines(turn) for turn in range(2)], axis=1)
+    total = jnp.dot(weights, jnp.concatenate(both, axis=0), preferred_element_type=jnp.float32)
+    keep(out_ref, filtered_of(total, tables, spectrum_ref, row_patches, width))
+
+
+def first_kernel(row_patches, table_ref, own_ref, other_ref, out_ref):
+    out_ref[...] = line_sum(0, Tables(table_ref, row_patches), own_ref, other_ref)
+
+
+def other_kernel(match_ref, table_ref, filtered_own_ref, own_ref, *refs):
+    out_ref, result_ref, spectrum_ref, sems = refs[-4:]
+    match_count, _, _, lines, width = out_ref.shape
+    row_patches = lines // HALF + 1
     date = lax.axis_index("date")
     dates = match_ref.shape[1]
-    fetch = pltpu.make_async_copy(matchings_ref, match_ref, sems.at[match_count])
-    fetch.start()
+    tables = Tables(table_ref, row_patches)
 
     def copy_of(match, source_ref):
         return pltpu.make_async_copy(source_ref, out_ref.at[match, :, 0], sems.at[match])
@@ -346,19 +347,11 @@
             def _():
                 copy_of(match, source_ref).start()
 
-    def meanwhile():
-        fetch.wait()
-        send(0, filtered_own_ref)
-
+    send(0, filtered_own_ref)
     for slot in range(1, dates):
-        result = filtered_of(
-            (first_ref, second_ref),
-            refs[2 * slot - 2 : 2 * slot],
-            table_ref,
-            spectrum_ref,
-            lines,
-            meanwhile if slot == 1 else None,
-        )
+        first_ref, other_ref = refs[2 * slot - 2 : 2 * slot]
+        total = first_ref[...] + line_sum(1, tables, own_ref, other_ref)
+        result = filtered_of(total, tables, spectrum_ref, row_patches, width)
         keep(result_ref.at[slot - 1], result)
         send(slot, result_ref.at[slot - 1])
     for match in range(match_count):
@@ -374,15 +367,10 @@
     for _ in range(3):
         splits.append(window.astype(jnp.bfloat16).astype(np.float32))
         window = window - splits[-1]
-    natural = np.arange((row_patches + 1) * HALF)
-    wide = len(natural)
-    inner = natural[REACH : wide - REACH]
-    orders = [
-        np.concatenate([natural[:REACH], inner, natural[wide - REACH :]]),
-        np.concatenate([natural[wide - REACH :], inner, natural[:REACH]]),
-    ]
-    lines = line_table(forward, row_patches).reshape(-1, 2, wide)
-    rows = [lines[:, :, order].reshape(-1, 2 * wide) for order in orders] + [
+    half = (row_patches + 1) * HALF // 2
+    lines = line_table(forward, row_patches).reshape(-1, 2, 2, half)
+    halves = [lines[:, :, at].reshape(-1, 2 * half) for at in range(2)]
+    rows = [np.concatenate([value, np.zeros_like(value)], axis=1) for value in halves] + [
         paired(forward),
         paired(inverse),
         np.concatenate([back, ring_table()], axis=1),
@@ -391,23 +379,29 @@
     return np.concatenate(rows, axis=0).astype(jnp.bfloat16)
 
 
-def split_tables(table_ref, row_patches):
-    size = row_patches * 2 * PATCH
-    start = pl.multiple_of(jnp.where(is_above(0), 0, size), size)
-    line_table_of = table_ref[pl.ds(start, size), :]
-    at = 2 * size
-    forward = table_ref[at : at + 4 * PATCH, :]
-    at += 4 * PATCH
-    inverse = table_ref[at : at + 4 * PATCH, :]
-    at += 4 * PATCH
-    back = table_ref[at : at + LANES, :LANES]
-    ring = table_ref[at : at + LANES, LANES:]
-    at += LANES
-    splits = table_ref[at : at + PATCH, :].astype(jnp.float32)
-    window = splits[:, :PATCH] + splits[:, PATCH : 2 * PATCH] + splits[:, 2 * PATCH : 3 * PATCH]
-    window = jnp.concatenate([window, window], axis=1)
-    window = jnp.concatenate([window, window], axis=0)
-    return line_table_of, forward, inverse, back, ring, window
+class Tables:
+    def __init__(self, ref, row_patches):
+        self.ref = ref
+        self.size = row_patches * 2 * PATCH
+
+    def lines(self, turn):
+        start = pl.multiple_of(jnp.where(is_above(turn), 0, self.size), self.size)
+        return self.ref[pl.ds(start, self.size), :LANES]
+
+    def core(self):
+        ref, at = self.ref, 2 * self.size
+        forward = ref[at : at + 4 * PATCH, :]
+        at += 4 * PATCH
+        inverse = ref[at : at + 4 * PATCH, :]
+        at += 4 * PATCH
+        back = ref[at : at + LANES, :LANES]
+        ring = ref[at : at + LANES, LANES:]
+        at += LANES
+        splits = ref[at : at + PATCH, :].astype(jnp.float32)
+        window = splits[:, :PATCH] + splits[:, PATCH : 2 * PATCH] + splits[:, 2 * PATCH : 3 * PATCH]
+        window = jnp.concatenate([window, window], axis=1)
+        window = jnp.concatenate([window, window], axis=0)
+        return forward, inverse, back, ring, window
 
 
 def per_device(image_stack, tap_weights, offsets, matchings):
@@ -461,7 +455,7 @@
     )(*raw)
     own = []
     for turn in range(2):
-        count = REACH + (0 if turn else lines - 2 * RIM)
+        count = lines // 2 + HALF
         call = pl.pallas_call(
             functools.partial(side_kernel, turn),
             out_shape=jax.ShapeDtypeStruct((2 * count + STEP, width), jnp.bfloat16),
@@ -490,20 +484,30 @@
         compiler_params=PARAMS,
         name="filter_own",
     )(tables, *own)
+    pieces = []
+    for first, second in zip(others[::2], others[1::2]):
+        total = pl.pallas_call(
+            functools.partial(first_kernel, row_patches),
+            out_shape=jax.ShapeDtypeStruct((row_patches * 2 * PATCH, chunks * LANES), jnp.float32),
+            in_specs=[VMEM] * 3,
+            out_specs=VMEM,
+            compiler_params=PARAMS,
+            name="filter_first",
+        )(tables, own[0], first)
+        pieces += [total, second]
     return pl.pallas_call(
         other_kernel,
         out_shape=jax.ShapeDtypeStruct((match_count, 2, 1, lines, width), jnp.float32),
-        in_specs=[HBM] + [VMEM] * (4 + len(others)),
+        in_specs=[SMEM] + [VMEM] * (3 + len(pieces)),
         out_specs=HBM,
         scratch_shapes=[
-            pltpu.SMEM(matchings.shape, jnp.int32),
             pltpu.VMEM((dates - 1, 2, lines, width), jnp.float32),
             spectrum,
-            pltpu.SemaphoreType.DMA((match_count + 1,)),
+            pltpu.SemaphoreType.DMA((match_count,)),
         ],
         compiler_params=PARAMS,
         name="filter_other",
-    )(pltpu.with_memory_space_constraint(matchings, pltpu.HBM), tables, filtered_own, *own, *others)
+    )(matchings, tables, filtered_own, own[1], *pieces)
 
 
 def solution(mesh):

time: 16.5 us -> 16.8 us (1.018); the launches traced: 16.7 us -> 16.7 us
  local copies, waits for them, and re-layouts: 0.69 us -> 0.1 us
  waiting for transfers between devices: 4.09 us -> 4.68 us
    unnamed x5, local copies, waits for them, and re-layouts: 0.69 us -> 0.1 us
    ppermute x2, waiting for transfers between devices: 1.92 us -> 2.51 us  [from_date(): lax.ppermute(piece, 'date', [((i + slot) % dates, i) for i in range(dates)])]
    pallas_call x0 -> x1, Pallas kernels: none -> 0.35 us  [per_device(): pl.pallas_call(functools.partial(first_kernel, row_patches), out_shape=ja...]
    pallas_call x1, Pallas kernels: 2.74 us -> 2.47 us  [per_device(): pl.pallas_call(other_kernel, out_shape=jax.ShapeDtypeStruct((match_count,...]
    pallas_call x1, Pallas kernels: 1.41 us -> 1.23 us  [per_device(): pl.pallas_call(own_kernel, out_shape=jax.ShapeDtypeStruct((2, lines, widt...]
  transfers between devices with their start and end apart: 5 -> 5, of which waited for: 3 -> 4; matrix products, arithmetic and copies ran while one was open for 4% -> 1% of each run, Pallas kernels for 21% -> 22%
where the time goes in v13:
time: 16.8 us; the launch traced here: 16.7 us
  Pallas kernels  6.25 us (37%)
  starting transfers between devices  5.57 us (33%)
  waiting for transfers between devices  4.68 us (28%)
    ppermute x2, starting transfers between devices, swapped(): return lax.ppermute(value, ('az', 'rg'), pairs)  3 us
    ppermute x2, waiting for transfers between devices, from_date(): lax.ppermute(piece, 'date', [((i + slot) % dates, i) for i in range(dates)])  2.51 us
    pallas_call x1, Pallas kernels, per_device(): pl.pallas_call(other_kernel, out_shape=jax.ShapeDtypeStruct((match_count,...  2.47 us
    ppermute x2, starting transfers between devices, from_date(): lax.ppermute(piece, 'date', [((i + slot) % dates, i) for i in range(dates)])  2.12 us
    ppermute x2, waiting for transfers between devices, swapped(): return lax.ppermute(value, ('az', 'rg'), pairs)  1.91 us
    pallas_call x1, Pallas kernels, per_device(): pl.pallas_call(own_kernel, out_shape=jax.ShapeDtypeStruct((2, lines, widt...  1.23 us
    pallas_call x1, Pallas kernels, per_device(): pl.pallas_call(load_kernel, out_shape=tuple((pltpu.VMEM(a.shape, a.dtype)...  0.93 us
    pallas_call x2, Pallas kernels, per_device(): own.append(call(*raw, messages[turn], inner, *own))  0.81 us
  transfers between devices with their start and end apart: 5, of which 4 were waited for; matrix products, arithmetic and copies ran while one was open for 1% of the time, Pallas kernels for 22%

profile of v13, /device:TPU:0, one launch (start us, length us, event | category | flops | bytes accessed | tf_op | source)
XLA Modules:
  0.0 16.7 jit_solution(3640207748518130690)
XLA Ops:
  0.0 0.5 %collective-permute-start = (f32[2,1,64,256]{3,2,0,1:T(8,128)}, f32[2,1,64,256]{3,2,0,1:T(8,128)S(1)}, u32[]{:S(2)}, u32[]{:S(2)}) collective-permute-start(f32[2,1,64,256]{3,2,0,1:T(8,128)} %bitcast.8), channel_id=1, source_target_pairs={{0,1},{1,0},{2,3},{3,2},{4,5},{5,4},{6,7},{7,6},{8,9},{9,8},{10,11... | collective-permute-start | bytes 393224 | tf_op jit(solution)/shard_map/ppermute | solution.py:410
  0.5 0.9 %load.1 = (f32[2,64,256]{2,1,0:T(8,128)S(1)}, f32[8,64]{1,0:T(8,128)S(1)}, s32[1,64]{1,0:T(1,128)S(1)}) custom-call(f32[2,64,256]{2,1,0:T(8,128)} %bitcast.9, f32[8,64]{1,0:T(8,128)} %bitcast.10, s32[1,64]{1,0:T(1,128)} %refs_2_.1), custom_call_target="tpu_custom_call" | custom-call | tf_op jit(solution)/shard_map/load/pallas_call | solution.py:416
  1.4 0.3 %collective-permute-done = f32[2,1,64,256]{3,2,0,1:T(8,128)S(1)} collective-permute-done((f32[2,1,64,256]{3,2,0,1:T(8,128)}, f32[2,1,64,256]{3,2,0,1:T(8,128)S(1)}, u32[]{:S(2)}, u32[]{:S(2)}) %collective-permute-start) | collective-permute-done | bytes 131104 | tf_op jit(solution)/shard_map/ppermute | solution.py:410
  1.7 0.2 pack.1
  1.8 0.0 copy-start
  1.8 3.0 %collective-permute-start.1 = (bf16[112,256]{1,0:T(8,128)(2,1)S(1)}, bf16[112,256]{1,0:T(8,128)(2,1)S(1)}, u32[]{:S(2)}, u32[]{:S(2)}) collective-permute-start(bf16[112,256]{1,0:T(8,128)(2,1)S(1)} %get-tuple-element.13), channel_id=1, source_target_pairs={{0,4},{1,5},{4,0},{5,1},{8,12},{9,13},{12,8},{13,9},{2,6},{3,7},{6... | collective-permute-start | bytes 172040 | tf_op jit(solution)/shard_map/ppermute | solution.py:445
  4.8 0.0 collective-permute-start.2
  4.8 0.3 %inner.1.inner_ref = f32[2,32,288]{2,1,0:T(8,128)S(1)} custom-call(f32[2,64,256]{2,1,0:T(8,128)S(1)} %get-tuple-element.10.image_ref, f32[2,64,256]{2,1,0:T(8,128)S(1)} %bitcast.5, f32[8,64]{1,0:T(8,128)S(1)} %get-tuple-element.11.taps_ref, s32[1,64]{1,0:T(1,128)S(1)} %get-tuple-element.12.offsets_ref), custom_call_target="tpu_custom_call" | custom-call | tf_op jit(solution)/shard_map/inner/pallas_call | solution.py:448
  5.1 1.9 %collective-permute-done.1.message_ref = bf16[112,256]{1,0:T(8,128)(2,1)S(1)} collective-permute-done((bf16[112,256]{1,0:T(8,128)(2,1)S(1)}, bf16[112,256]{1,0:T(8,128)(2,1)S(1)}, u32[]{:S(2)}, u32[]{:S(2)}) %collective-permute-start.1) | collective-permute-done | bytes 57376 | tf_op jit(solution)/shard_map/ppermute | solution.py:445
  7.1 0.4 %side_a.1.refs_0_.first_ref.own_ref = bf16[144,256]{1,0:T(8,128)(2,1)S(1)} custom-call(f32[2,64,256]{2,1,0:T(8,128)S(1)} %get-tuple-element.10.image_ref, f32[2,64,256]{2,1,0:T(8,128)S(1)} %bitcast.6, f32[8,64]{1,0:T(8,128)S(1)} %get-tuple-element.11.taps_ref, s32[1,64]{1,0:T(1,128)S(1)} %get-tuple-element.12.offsets_ref, ...), custom_call_target="tpu_custom_call" | custom-call | tf_op jit(solution)/shard_map/side_a/pallas_call | solution.py:467
  7.5 0.0 copy-start.1
  7.5 1.9 %collective-permute-start.3 = (bf16[144,256]{1,0:T(8,128)(2,1)S(1)}, bf16[144,256]{1,0:T(8,128)(2,1)S(1)}, u32[]{:S(2)}, u32[]{:S(2)}) collective-permute-start(bf16[144,256]{1,0:T(8,128)(2,1)S(1)} %side_a.1.refs_0_.first_ref.own_ref), channel_id=1, source_target_pairs={{2,0},{0,2},{3,1},{1,3},{6,4},{4,6},{7,5},{5,7},{10,8},{8,10},{11,... | collective-permute-start | bytes 221192 | tf_op jit(solution)/shard_map/ppermute | solution.py:471
  9.4 0.0 collective-permute-done.2.message_ref
  9.4 0.4 %side_b.1.second_ref.own_ref = bf16[144,256]{1,0:T(8,128)(2,1)S(1)} custom-call(f32[2,64,256]{2,1,0:T(8,128)S(1)} %get-tuple-element.10.image_ref, f32[2,64,256]{2,1,0:T(8,128)S(1)} %bitcast.7, f32[8,64]{1,0:T(8,128)S(1)} %get-tuple-element.11.taps_ref, s32[1,64]{1,0:T(1,128)S(1)} %get-tuple-element.12.offsets_ref, ...), custom_call_target="tpu_custom_call" | custom-call | tf_op jit(solution)/shard_map/side_b/pallas_call | solution.py:467
  9.8 0.2 %collective-permute-start.4 = (bf16[144,256]{1,0:T(8,128)(2,1)S(1)}, bf16[144,256]{1,0:T(8,128)(2,1)S(1)}, u32[]{:S(2)}, u32[]{:S(2)}) collective-permute-start(bf16[144,256]{1,0:T(8,128)(2,1)S(1)} %side_b.1.second_ref.own_ref), channel_id=1, source_target_pairs={{2,0},{0,2},{3,1},{1,3},{6,4},{4,6},{7,5},{5,7},{10,8},{8,10},{11,... | collective-permute-start | bytes 221192 | tf_op jit(solution)/shard_map/ppermute | solution.py:471
  10.0 0.0 copy-done.1
  10.0 0.1 copy.7.match_ref
  10.1 0.0 copy-done
  10.1 1.2 %filter_own.1.filtered_own_ref = f32[2,64,256]{2,1,0:T(8,128)S(1)} custom-call(bf16[1472,256]{1,0:T(8,128)(2,1)S(1)} %copy-done, bf16[144,256]{1,0:T(8,128)(2,1)S(1)} %side_a.1.refs_0_.first_ref.own_ref, bf16[144,256]{1,0:T(8,128)(2,1)S(1)} %side_b.1.second_ref.own_ref), custom_call_target="tpu_custom_call" | custom-call | tf_op jit(solution)/shard_map/filter_own/pallas_call | solution.py:478
  11.3 1.3 %collective-permute-done.3.other_ref = bf16[144,256]{1,0:T(8,128)(2,1)S(1)} collective-permute-done((bf16[144,256]{1,0:T(8,128)(2,1)S(1)}, bf16[144,256]{1,0:T(8,128)(2,1)S(1)}, u32[]{:S(2)}, u32[]{:S(2)}) %collective-permute-start.3) | collective-permute-done | bytes 73760 | tf_op jit(solution)/shard_map/ppermute | solution.py:471
  12.6 0.3 %filter_first.1.refs_0_ = f32[384,640]{1,0:T(8,128)S(1)} custom-call(bf16[1472,256]{1,0:T(8,128)(2,1)S(1)} %copy-done, bf16[144,256]{1,0:T(8,128)(2,1)S(1)} %side_a.1.refs_0_.first_ref.own_ref, bf16[144,256]{1,0:T(8,128)(2,1)S(1)} %collective-permute-done.3.other_ref), custom_call_target="tpu_custom_call" | custom-call | tf_op jit(solution)/shard_map/filter_first/pallas_call | solution.py:489
  13.0 1.2 %collective-permute-done.4.refs_1_ = bf16[144,256]{1,0:T(8,128)(2,1)S(1)} collective-permute-done((bf16[144,256]{1,0:T(8,128)(2,1)S(1)}, bf16[144,256]{1,0:T(8,128)(2,1)S(1)}, u32[]{:S(2)}, u32[]{:S(2)}) %collective-permute-start.4) | collective-permute-done | bytes 73760 | tf_op jit(solution)/shard_map/ppermute | solution.py:471
  14.2 2.5 %filter_other.1 = f32[3,2,1,64,256]{4,3,2,1,0:T(8,128)} custom-call(s32[3,2]{1,0:T(4,128)S(1)} %copy.7.match_ref, bf16[1472,256]{1,0:T(8,128)(2,1)S(1)} %copy-done, f32[2,64,256]{2,1,0:T(8,128)S(1)} %filter_own.1.filtered_own_ref, bf16[144,256]{1,0:T(8,128)(2,1)S(1)} %side_b.1.second_ref.own_ref, f32[384,640]{1,0:T(8,128)S(1)} %filter_first.1.refs_0_, ...), custom_call_target="tpu_custom_call" | custom-call | tf_op jit(solution)/shard_map/filter_other/pallas_call | solution.py:498
Async XLA Ops:
  0.0 1.6 %collective-permute-start = (f32[2,1,64,256]{3,2,0,1:T(8,128)}, f32[2,1,64,256]{3,2,0,1:T(8,128)S(1)}, u32[]{:S(2)}, u32[]{:S(2)}) collective-permute-start(f32[2,1,64,256]{3,2,0,1:T(8,128)} %bitcast.8), channel_id=1, source_target_pairs={{0,1},{1,0},{2,3},{3,2},{4,5},{5,4},{6,7},{7,6},{8,9},{9,8},{10,11... | collective-permute-start | bytes 393224 | tf_op jit(solution)/shard_map/ppermute | solution.py:410
  1.8 8.3 %copy-start = (bf16[1472,256]{1,0:T(8,128)(2,1)S(1)}, bf16[1472,256]{1,0:T(8,128)(2,1)}, u32[]{:S(2)}) copy-start(bf16[1472,256]{1,0:T(8,128)(2,1)} %constant.2.clone.table_ref) | copy-start | bytes 2260996
  1.8 5.2 %collective-permute-start.1 = (bf16[112,256]{1,0:T(8,128)(2,1)S(1)}, bf16[112,256]{1,0:T(8,128)(2,1)S(1)}, u32[]{:S(2)}, u32[]{:S(2)}) collective-permute-start(bf16[112,256]{1,0:T(8,128)(2,1)S(1)} %get-tuple-element.13), channel_id=1, source_target_pairs={{0,4},{1,5},{4,0},{5,1},{8,12},{9,13},{12,8},{13,9},{2,6},{3,7},{6... | collective-permute-start | bytes 172040 | tf_op jit(solution)/shard_map/ppermute | solution.py:445
  4.8 4.6 %collective-permute-start.2 = (bf16[112,256]{1,0:T(8,128)(2,1)S(1)}, bf16[112,256]{1,0:T(8,128)(2,1)S(1)}, u32[]{:S(2)}, u32[]{:S(2)}) collective-permute-start(bf16[112,256]{1,0:T(8,128)(2,1)S(1)} %get-tuple-element.14), channel_id=1, source_target_pairs={{0,1},{1,0},{4,8},{5,9},{8,4},{9,5},{12,13},{13,12},{2,3},{3,2},{6... | collective-permute-start | bytes 172040 | tf_op jit(solution)/shard_map/ppermute | solution.py:445
  7.5 2.5 %copy-start.1 = (s32[3,2]{0,1:T(2,128)S(1)}, s32[3,2]{0,1:T(2,128)}, u32[]{:S(2)}) copy-start(s32[3,2]{0,1:T(2,128)} %param.8) | copy-start | bytes 76
  7.5 5.1 %collective-permute-start.3 = (bf16[144,256]{1,0:T(8,128)(2,1)S(1)}, bf16[144,256]{1,0:T(8,128)(2,1)S(1)}, u32[]{:S(2)}, u32[]{:S(2)}) collective-permute-start(bf16[144,256]{1,0:T(8,128)(2,1)S(1)} %side_a.1.refs_0_.first_ref.own_ref), channel_id=1, source_target_pairs={{2,0},{0,2},{3,1},{1,3},{6,4},{4,6},{7,5},{5,7},{10,8},{8,10},{11,... | collective-permute-start | bytes 221192 | tf_op jit(solution)/shard_map/ppermute | solution.py:471
  9.8 4.4 %collective-permute-start.4 = (bf16[144,256]{1,0:T(8,128)(2,1)S(1)}, bf16[144,256]{1,0:T(8,128)(2,1)S(1)}, u32[]{:S(2)}, u32[]{:S(2)}) collective-permute-start(bf16[144,256]{1,0:T(8,128)(2,1)S(1)} %side_b.1.second_ref.own_ref), channel_id=1, source_target_pairs={{2,0},{0,2},{3,1},{1,3},{6,4},{4,6},{7,5},{5,7},{10,8},{8,10},{11,... | collective-permute-start | bytes 221192 | tf_op jit(solution)/shard_map/ppermute | solution.py:471

commit v14 on v13

--- a/solution.py
+++ b/solution.py
@@ -155,7 +155,9 @@
     lines = parts[0].shape[0]
     for part, value in enumerate(parts):
         out_ref[part * lines : (part + 1) * lines, :] = value[:, :width].astype(jnp.bfloat16)
-    edges = side_by_side([value[:, width:] for value in parts])
+    filler = jnp.zeros((STEP * width // HALF - 2 * lines, HALF), jnp.float32)
+    edges = [value[:, width:] for value in parts]
+    edges = side_by_side(edges + [filler] if filler.shape[0] else edges)
     out_ref[2 * lines :, :] = edges.astype(jnp.bfloat16)
 
 
@@ -174,10 +176,12 @@
     source = lax.broadcasted_iota(jnp.int32, (lines, lines - 2 * RIM), 0)
     weights = band(taps_ref[:, cut], offsets_ref[:, cut], RIM, source)
     weights = jnp.concatenate([weights, weights], axis=0)
+    parts = []
     for part in range(2):
         edge = edge_of(other_ref, part, side, slice(0, lines))
         rows = high_low(jnp.concatenate([image_ref[part], edge], axis=1))
-        out_ref[part] = apply_band(weights, rows)
+        parts.append(apply_band(weights, rows))
+    write_piece(out_ref, parts, width)
 
 
 def side_kernel(
@@ -224,12 +228,12 @@
         own = high_low(jnp.concatenate([own, edge], axis=1))
         cut = slice(part * REACH, (part + 1) * REACH)
         rim = jnp.concatenate([message[cut, :], rim_edges[cut]], axis=1)
-        total = apply_band(weights, jnp.concatenate([rim, own], axis=0))
-        between = inner_ref.shape[1] // 2
-        upper = jnp.concatenate([total, inner_ref[part, :between]], axis=0)
-        lower = jnp.concatenate([inner_ref[part, between:], total], axis=0)
-        parts.append(jnp.where(above, upper, lower))
+        parts.append(apply_band(weights, jnp.concatenate([rim, own], axis=0)))
     write_piece(out_ref, parts, width)
+
+
+def pass_kernel(piece_ref, *refs):
+    refs[-1][...] = piece_ref[...]
 
 
 def cross(own_parts, other_parts):
@@ -253,9 +257,15 @@
     return jnp.concatenate([mid.astype(jnp.bfloat16), shifted], axis=1)
 
 
-def line_sum(turn, tables, own_ref, other_ref):
+def first_sum(tables, own_refs, other_refs):
+    both = [interferogram(own, other) for own, other in zip(own_refs, other_refs)]
+    both = jnp.concatenate(both, axis=0)
+    return jnp.dot(tables.first(), both, preferred_element_type=jnp.float32)
+
+
+def second_sum(tables, own_ref, other_ref):
     both = interferogram(own_ref, other_ref)
-    return jnp.dot(tables.lines(turn), both, preferred_element_type=jnp.float32)
+    return jnp.dot(tables.second(), both, preferred_element_type=jnp.float32)
 
 
 def filtered_of(line_spectra, tables, spectrum_ref, row_patches, width):
@@ -314,18 +324,18 @@
         ref[part] = result[part * lines : (part + 1) * lines]
 
 
-def own_kernel(table_ref, first_ref, second_ref, out_ref, spectrum_ref):
+def own_kernel(table_ref, first_ref, inner_ref, second_ref, out_ref, spectrum_ref):
     _, lines, width = out_ref.shape
     row_patches = lines // HALF + 1
     tables = Tables(table_ref, row_patches)
-    both = [interferogram(ref, ref) for ref in (first_ref, second_ref)]
-    weights = jnp.concatenate([tables.lines(turn) for turn in range(2)], axis=1)
-    total = jnp.dot(weights, jnp.concatenate(both, axis=0), preferred_element_type=jnp.float32)
+    first = (first_ref, inner_ref)
+    total = first_sum(tables, first, first) + second_sum(tables, second_ref, second_ref)
     keep(out_ref, filtered_of(total, tables, spectrum_ref, row_patches, width))
 
 
-def first_kernel(row_patches, table_ref, own_ref, other_ref, out_ref):
-    out_ref[...] = line_sum(0, Tables(table_ref, row_patches), own_ref, other_ref)
+def first_kernel(row_patches, table_ref, first_ref, inner_ref, other_ref, middle_ref, out_ref):
+    tables = Tables(table_ref, row_patches)
+    out_ref[...] = first_sum(tables, (first_ref, inner_ref), (other_ref, middle_ref))
 
 
 def other_kernel(match_ref, table_ref, filtered_own_ref, own_ref, *refs):
@@ -345,12 +355,12 @@
 
             @pl.when(wanted == slot)
             def _():
-                copy_of(match, source_ref).start()
+                copy_of(match, source_ref).start(priority=match % 2)
 
     send(0, filtered_own_ref)
     for slot in range(1, dates):
         first_ref, other_ref = refs[2 * slot - 2 : 2 * slot]
-        total = first_ref[...] + line_sum(1, tables, own_ref, other_ref)
+        total = first_ref[...] + second_sum(tables, own_ref, other_ref)
         result = filtered_of(total, tables, spectrum_ref, row_patches, width)
         keep(result_ref.at[slot - 1], result)
         send(slot, result_ref.at[slot - 1])
@@ -367,10 +377,17 @@
     for _ in range(3):
         splits.append(window.astype(jnp.bfloat16).astype(np.float32))
         window = window - splits[-1]
-    half = (row_patches + 1) * HALF // 2
-    lines = line_table(forward, row_patches).reshape(-1, 2, 2, half)
-    halves = [lines[:, :, at].reshape(-1, 2 * half) for at in range(2)]
-    rows = [np.concatenate([value, np.zeros_like(value)], axis=1) for value in halves] + [
+    wide = (row_patches + 1) * HALF
+    natural = np.arange(wide)
+    upper, inner, lower = natural[:REACH], natural[REACH : wide - REACH], natural[wide - REACH :]
+    lines = line_table(forward, row_patches).reshape(-1, 2, wide)
+
+    def columns(*orders):
+        cut = [lines[:, :, order].reshape(len(lines), -1) for order in orders]
+        cut = np.concatenate(cut, axis=1)
+        return np.pad(cut, ((0, 0), (0, 4 * PATCH - cut.shape[1])))
+
+    rows = [columns(upper, inner), columns(lower, inner), columns(lower), columns(upper)] + [
         paired(forward),
         paired(inverse),
         np.concatenate([back, ring_table()], axis=1),
@@ -384,12 +401,19 @@
         self.ref = ref
         self.size = row_patches * 2 * PATCH
 
-    def lines(self, turn):
-        start = pl.multiple_of(jnp.where(is_above(turn), 0, self.size), self.size)
-        return self.ref[pl.ds(start, self.size), :LANES]
+    def first(self):
+        inner = self.size // (2 * PATCH) * HALF + HALF - 2 * REACH
+        return self.of_side(0)[:, : 2 * (REACH + inner)]
+
+    def second(self):
+        return self.of_side(2)[:, : 2 * REACH]
+
+    def of_side(self, block):
+        start = jnp.where(is_above(0), block * self.size, (block + 1) * self.size)
+        return self.ref[pl.ds(pl.multiple_of(start, self.size), self.size), :]
 
     def core(self):
-        ref, at = self.ref, 2 * self.size
+        ref, at = self.ref, 4 * self.size
         forward = ref[at : at + 4 * PATCH, :]
         at += 4 * PATCH
         inverse = ref[at : at + 4 * PATCH, :]
@@ -445,32 +469,46 @@
         return lax.ppermute(value, ("az", "rg"), pairs)
 
     messages = [swapped(messages[turn], turn) for turn in range(2)]
+    def piece_of(count):
+        return jax.ShapeDtypeStruct((2 * count + STEP, width), jnp.bfloat16)
+
     inner = pl.pallas_call(
         inner_kernel,
-        out_shape=jax.ShapeDtypeStruct((2, lines - 2 * RIM, width + HALF), jnp.float32),
+        out_shape=piece_of(lines - 2 * RIM),
         in_specs=[VMEM] * 4,
         out_specs=VMEM,
         compiler_params=PARAMS,
         name="inner",
     )(*raw)
-    own = []
+    sides = []
     for turn in range(2):
-        count = lines // 2 + HALF
         call = pl.pallas_call(
             functools.partial(side_kernel, turn),
-            out_shape=jax.ShapeDtypeStruct((2 * count + STEP, width), jnp.bfloat16),
-            in_specs=[VMEM] * (6 + len(own)),
+            out_shape=piece_of(REACH),
+            in_specs=[VMEM] * (6 + len(sides)),
             out_specs=VMEM,
             compiler_params=PARAMS,
             name="side_" + "ab"[turn],
         )
-        own.append(call(*raw, messages[turn], inner, *own))
+        sides.append(call(*raw, messages[turn], inner, *sides))
+    own = (sides[0], inner, sides[1])
     dates = lax.axis_size("date")
 
     def from_date(piece, slot):
         return lax.ppermute(piece, "date", [((i + slot) % dates, i) for i in range(dates)])
 
-    others = [from_date(piece, slot) for slot in range(1, dates) for piece in own]
+    slots = range(1, dates)
+    middles = [from_date(inner, slot) for slot in slots]
+    firsts = [from_date(sides[0], slot) for slot in slots]
+    last = pl.pallas_call(
+        pass_kernel,
+        out_shape=piece_of(REACH),
+        in_specs=[VMEM] * (1 + len(middles)),
+        out_specs=VMEM,
+        compiler_params=PARAMS,
+        name="pass",
+    )(sides[1], *middles)
+    seconds = [from_date(last, slot) for slot in slots]
     row_patches = lines // HALF + 1
     chunks = (width + width + LANES) // LANES
     tables = jnp.asarray(all_tables(row_patches))
@@ -478,22 +516,22 @@
     filtered_own = pl.pallas_call(
         own_kernel,
         out_shape=jax.ShapeDtypeStruct((2, lines, width), jnp.float32),
-        in_specs=[VMEM] * 3,
+        in_specs=[VMEM] * 4,
         out_specs=VMEM,
         scratch_shapes=[spectrum],
         compiler_params=PARAMS,
         name="filter_own",
     )(tables, *own)
     pieces = []
-    for first, second in zip(others[::2], others[1::2]):
+    for first, middle, second in zip(firsts, middles, seconds):
         total = pl.pallas_call(
             functools.partial(first_kernel, row_patches),
             out_shape=jax.ShapeDtypeStruct((row_patches * 2 * PATCH, chunks * LANES), jnp.float32),
-            in_specs=[VMEM] * 3,
+            in_specs=[VMEM] * 5,
             out_specs=VMEM,
             compiler_params=PARAMS,
             name="filter_first",
-        )(tables, own[0], first)
+        )(tables, *own[:2], first, middle)
         pieces += [total, second]
     return pl.pallas_call(
         other_kernel,
@@ -507,7 +545,7 @@
         ],
         compiler_params=PARAMS,
         name="filter_other",
-    )(matchings, tables, filtered_own, own[1], *pieces)
+    )(matchings, tables, filtered_own, own[2], *pieces)
 
 
 def solution(mesh):

time: 16.8 us -> 16.6 us (0.988)
  waiting for transfers between devices: 4.68 us -> 2.03 us
  starting transfers between devices: 5.57 us -> 7.81 us
  Pallas kernels: 6.25 us -> 6.49 us
    ppermute x2 -> x3, starting transfers between devices: 2.12 us -> 4.36 us  [from_date(): lax.ppermute(piece, 'date', [((i + slot) % dates, i) for i in range(dates)])]
    ppermute x2, waiting for transfers between devices: 1.91 us -> 0.36 us  [swapped(): return lax.ppermute(value, ('az', 'rg'), pairs)]
    ppermute x2 -> x3, waiting for transfers between devices: 2.51 us -> 1.42 us  [from_date(): lax.ppermute(piece, 'date', [((i + slot) % dates, i) for i in range(dates)])]
    pallas_call x3 -> x4, Pallas kernels: 1.12 us -> 1.15 us  [the longest x2 0.8 us: per_device(): sides.append(call(*raw, messages[turn], inner, *sides))]
  transfers between devices with their start and end apart: 5 -> 6, of which waited for: 4 -> 3; matrix products, arithmetic and copies ran while one was open for 1% -> 1% of each run, Pallas kernels for 22% -> 23%
where the time goes in v14:
time: 16.6 us; the launch traced here: 16.5 us
  starting transfers between devices  7.81 us (47%)
  Pallas kernels  6.49 us (39%)
  waiting for transfers between devices  2.03 us (12%)
    ppermute x3, starting transfers between devices, from_date(): lax.ppermute(piece, 'date', [((i + slot) % dates, i) for i in range(dates)])  4.36 us
    ppermute x2, starting transfers between devices, swapped(): return lax.ppermute(value, ('az', 'rg'), pairs)  3 us
    pallas_call x1, Pallas kernels, per_device(): pl.pallas_call(other_kernel, out_shape=jax.ShapeDtypeStruct((match_count,...  2.49 us
    ppermute x3, waiting for transfers between devices, from_date(): lax.ppermute(piece, 'date', [((i + slot) % dates, i) for i in range(dates)])  1.42 us
    pallas_call x1, Pallas kernels, per_device(): pl.pallas_call(own_kernel, out_shape=jax.ShapeDtypeStruct((2, lines, widt...  1.34 us
    pallas_call x1, Pallas kernels, per_device(): pl.pallas_call(load_kernel, out_shape=tuple((pltpu.VMEM(a.shape, a.dtype)...  0.93 us
    pallas_call x2, Pallas kernels, per_device(): sides.append(call(*raw, messages[turn], inner, *sides))  0.8 us
    ppermute x1, starting transfers between devices, per_device(): lax.ppermute(image_stack, 'rg', [(0, 1), (1, 0)]).reshape(2, lines, width)  0.45 us
  transfers between devices with their start and end apart: 6, of which 3 were waited for; matrix products, arithmetic and copies ran while one was open for 1% of the time, Pallas kernels for 23%

profile of v14, /device:TPU:0, one launch (start us, length us, event | category | flops | bytes accessed | tf_op | source)
XLA Modules:
  0.0 16.5 jit_solution(13072534584813153093)
XLA Ops:
  0.0 0.0 copy-start
  0.0 0.0 copy-start.1
  0.0 0.5 %collective-permute-start = (f32[2,1,64,256]{3,2,0,1:T(8,128)}, f32[2,1,64,256]{3,2,0,1:T(8,128)S(1)}, u32[]{:S(2)}, u32[]{:S(2)}) collective-permute-start(f32[2,1,64,256]{3,2,0,1:T(8,128)} %bitcast.8), channel_id=1, source_target_pairs={{0,1},{1,0},{2,3},{3,2},{4,5},{5,4},{6,7},{7,6},{8,9},{9,8},{10,11... | collective-permute-start | bytes 393224 | tf_op jit(solution)/shard_map/ppermute | solution.py:434
  0.5 0.9 %load.1 = (f32[2,64,256]{2,1,0:T(8,128)S(1)}, f32[8,64]{1,0:T(8,128)S(1)}, s32[1,64]{1,0:T(1,128)S(1)}) custom-call(f32[2,64,256]{2,1,0:T(8,128)} %bitcast.9, f32[8,64]{1,0:T(8,128)} %bitcast.10, s32[1,64]{1,0:T(1,128)} %refs_2_.1), custom_call_target="tpu_custom_call" | custom-call | tf_op jit(solution)/shard_map/load/pallas_call | solution.py:440
  1.4 0.3 %collective-permute-done = f32[2,1,64,256]{3,2,0,1:T(8,128)S(1)} collective-permute-done((f32[2,1,64,256]{3,2,0,1:T(8,128)}, f32[2,1,64,256]{3,2,0,1:T(8,128)S(1)}, u32[]{:S(2)}, u32[]{:S(2)}) %collective-permute-start) | collective-permute-done | bytes 131104 | tf_op jit(solution)/shard_map/ppermute | solution.py:434
  1.7 0.2 pack.1
  1.8 3.0 %collective-permute-start.1 = (bf16[112,256]{1,0:T(8,128)(2,1)S(1)}, bf16[112,256]{1,0:T(8,128)(2,1)S(1)}, u32[]{:S(2)}, u32[]{:S(2)}) collective-permute-start(bf16[112,256]{1,0:T(8,128)(2,1)S(1)} %get-tuple-element.13), channel_id=1, source_target_pairs={{0,4},{1,5},{4,0},{5,1},{8,12},{9,13},{12,8},{13,9},{2,6},{3,7},{6... | collective-permute-start | bytes 172040 | tf_op jit(solution)/shard_map/ppermute | solution.py:469
  4.8 0.0 collective-permute-start.2
  4.8 0.3 %inner.1.inner_ref = bf16[80,256]{1,0:T(8,128)(2,1)S(1)} custom-call(f32[2,64,256]{2,1,0:T(8,128)S(1)} %get-tuple-element.10.image_ref, f32[2,64,256]{2,1,0:T(8,128)S(1)} %bitcast.5, f32[8,64]{1,0:T(8,128)S(1)} %get-tuple-element.11.taps_ref, s32[1,64]{1,0:T(1,128)S(1)} %get-tuple-element.12.offsets_ref), custom_call_target="tpu_custom_call" | custom-call | tf_op jit(solution)/shard_map/inner/pallas_call | solution.py:475
  5.2 1.5 %collective-permute-start.4 = (bf16[80,256]{1,0:T(8,128)(2,1)S(1)}, bf16[80,256]{1,0:T(8,128)(2,1)S(1)}, u32[]{:S(2)}, u32[]{:S(2)}) collective-permute-start(bf16[80,256]{1,0:T(8,128)(2,1)S(1)} %inner.1.inner_ref), channel_id=1, source_target_pairs={{2,0},{0,2},{3,1},{1,3},{6,4},{4,6},{7,5},{5,7},{10,8},{8,10},{11,... | collective-permute-start | bytes 122888 | tf_op jit(solution)/shard_map/ppermute | solution.py:498
  6.7 0.4 %collective-permute-done.1.message_ref = bf16[112,256]{1,0:T(8,128)(2,1)S(1)} collective-permute-done((bf16[112,256]{1,0:T(8,128)(2,1)S(1)}, bf16[112,256]{1,0:T(8,128)(2,1)S(1)}, u32[]{:S(2)}, u32[]{:S(2)}) %collective-permute-start.1) | collective-permute-done | bytes 57376 | tf_op jit(solution)/shard_map/ppermute | solution.py:469
  7.0 0.4 %side_a.1.refs_0_.first_ref = bf16[112,256]{1,0:T(8,128)(2,1)S(1)} custom-call(f32[2,64,256]{2,1,0:T(8,128)S(1)} %get-tuple-element.10.image_ref, f32[2,64,256]{2,1,0:T(8,128)S(1)} %bitcast.6, f32[8,64]{1,0:T(8,128)S(1)} %get-tuple-element.11.taps_ref, s32[1,64]{1,0:T(1,128)S(1)} %get-tuple-element.12.offsets_ref, ...), custom_call_target="tpu_custom_call" | custom-call | tf_op jit(solution)/shard_map/side_a/pallas_call | solution.py:493
  7.4 1.9 %collective-permute-start.3 = (bf16[112,256]{1,0:T(8,128)(2,1)S(1)}, bf16[112,256]{1,0:T(8,128)(2,1)S(1)}, u32[]{:S(2)}, u32[]{:S(2)}) collective-permute-start(bf16[112,256]{1,0:T(8,128)(2,1)S(1)} %side_a.1.refs_0_.first_ref), channel_id=1, source_target_pairs={{2,0},{0,2},{3,1},{1,3},{6,4},{4,6},{7,5},{5,7},{10,8},{8,10},{11,... | collective-permute-start | bytes 172040 | tf_op jit(solution)/shard_map/ppermute | solution.py:498
  9.3 0.0 collective-permute-done.2.message_ref
  9.3 0.4 %side_b.1.second_ref.piece_ref.own_ref = bf16[112,256]{1,0:T(8,128)(2,1)S(1)} custom-call(f32[2,64,256]{2,1,0:T(8,128)S(1)} %get-tuple-element.10.image_ref, f32[2,64,256]{2,1,0:T(8,128)S(1)} %bitcast.7, f32[8,64]{1,0:T(8,128)S(1)} %get-tuple-element.11.taps_ref, s32[1,64]{1,0:T(1,128)S(1)} %get-tuple-element.12.offsets_ref, ...), custom_call_target="tpu_custom_call" | custom-call | tf_op jit(solution)/shard_map/side_b/pallas_call | solution.py:493
  9.7 0.0 collective-permute-done.4.middle_ref.refs_0_
  9.7 1.0 %collective-permute-start.5 = (bf16[112,256]{1,0:T(8,128)(2,1)S(1)}, bf16[112,256]{1,0:T(8,128)(2,1)S(1)}, u32[]{:S(2)}, u32[]{:S(2)}) collective-permute-start(bf16[112,256]{1,0:T(8,128)(2,1)S(1)} %pass.1), channel_id=1, source_target_pairs={{2,0},{0,2},{3,1},{1,3},{6,4},{4,6},{7,5},{5,7},{10,8},{8,10},{11,... | collective-permute-start | bytes 172040 | tf_op jit(solution)/shard_map/ppermute | solution.py:498
  10.7 0.0 copy-done.1
  10.7 0.1 copy.7.match_ref
  10.8 0.0 copy-done
  10.8 1.3 %filter_own.1.filtered_own_ref = f32[2,64,256]{2,1,0:T(8,128)S(1)} custom-call(bf16[2240,256]{1,0:T(8,128)(2,1)S(1)} %copy-done, bf16[112,256]{1,0:T(8,128)(2,1)S(1)} %side_a.1.refs_0_.first_ref, bf16[80,256]{1,0:T(8,128)(2,1)S(1)} %inner.1.inner_ref, bf16[112,256]{1,0:T(8,128)(2,1)S(1)} %side_b.1.second_ref.piece_ref.own_ref), custom_call_target="tpu_custom_call" | custom-call | tf_op jit(solution)/shard_map/filter_own/pallas_call | solution.py:516
  12.1 0.0 collective-permute-done.3.other_ref
  12.2 0.4 %filter_first.1.refs_0_ = f32[384,640]{1,0:T(8,128)S(1)} custom-call(bf16[2240,256]{1,0:T(8,128)(2,1)S(1)} %copy-done, bf16[112,256]{1,0:T(8,128)(2,1)S(1)} %side_a.1.refs_0_.first_ref, bf16[80,256]{1,0:T(8,128)(2,1)S(1)} %inner.1.inner_ref, bf16[112,256]{1,0:T(8,128)(2,1)S(1)} %collective-permute-done.3.other_ref, ...), custom_call_target="tpu_custom_call" | custom-call | tf_op jit(solution)/shard_map/filter_first/pallas_call | solution.py:527
  12.6 1.4 %collective-permute-done.5.refs_1_ = bf16[112,256]{1,0:T(8,128)(2,1)S(1)} collective-permute-done((bf16[112,256]{1,0:T(8,128)(2,1)S(1)}, bf16[112,256]{1,0:T(8,128)(2,1)S(1)}, u32[]{:S(2)}, u32[]{:S(2)}) %collective-permute-start.5) | collective-permute-done | bytes 57376 | tf_op jit(solution)/shard_map/ppermute | solution.py:498
  14.0 2.5 %filter_other.1 = f32[3,2,1,64,256]{4,3,2,1,0:T(8,128)} custom-call(s32[3,2]{1,0:T(4,128)S(1)} %copy.7.match_ref, bf16[2240,256]{1,0:T(8,128)(2,1)S(1)} %copy-done, f32[2,64,256]{2,1,0:T(8,128)S(1)} %filter_own.1.filtered_own_ref, bf16[112,256]{1,0:T(8,128)(2,1)S(1)} %side_b.1.second_ref.piece_ref.own_ref, f32[384,640]{1,0:T(8,128)S(1)} %filter_first.1.refs_0_, ...), custom_call_target="tpu_custom_call" | custom-call | tf_op jit(solution)/shard_map/filter_other/pallas_call | solution.py:536
  (1 shorter events, 0.0 us)
Async XLA Ops:
  0.0 10.8 %copy-start = (bf16[2240,256]{1,0:T(8,128)(2,1)S(1)}, bf16[2240,256]{1,0:T(8,128)(2,1)}, u32[]{:S(2)}) copy-start(bf16[2240,256]{1,0:T(8,128)(2,1)} %constant.2.clone.table_ref) | copy-start | bytes 3440644
  0.0 10.7 %copy-start.1 = (s32[3,2]{0,1:T(2,128)S(1)}, s32[3,2]{0,1:T(2,128)}, u32[]{:S(2)}) copy-start(s32[3,2]{0,1:T(2,128)} %param.8) | copy-start | bytes 76
  0.0 1.6 %collective-permute-start = (f32[2,1,64,256]{3,2,0,1:T(8,128)}, f32[2,1,64,256]{3,2,0,1:T(8,128)S(1)}, u32[]{:S(2)}, u32[]{:S(2)}) collective-permute-start(f32[2,1,64,256]{3,2,0,1:T(8,128)} %bitcast.8), channel_id=1, source_target_pairs={{0,1},{1,0},{2,3},{3,2},{4,5},{5,4},{6,7},{7,6},{8,9},{9,8},{10,11... | collective-permute-start | bytes 393224 | tf_op jit(solution)/shard_map/ppermute | solution.py:434
  1.8 5.2 %collective-permute-start.1 = (bf16[112,256]{1,0:T(8,128)(2,1)S(1)}, bf16[112,256]{1,0:T(8,128)(2,1)S(1)}, u32[]{:S(2)}, u32[]{:S(2)}) collective-permute-start(bf16[112,256]{1,0:T(8,128)(2,1)S(1)} %get-tuple-element.13), channel_id=1, source_target_pairs={{0,4},{1,5},{4,0},{5,1},{8,12},{9,13},{12,8},{13,9},{2,6},{3,7},{6... | collective-permute-start | bytes 172040 | tf_op jit(solution)/shard_map/ppermute | solution.py:469
  4.8 4.5 %collective-permute-start.2 = (bf16[112,256]{1,0:T(8,128)(2,1)S(1)}, bf16[112,256]{1,0:T(8,128)(2,1)S(1)}, u32[]{:S(2)}, u32[]{:S(2)}) collective-permute-start(bf16[112,256]{1,0:T(8,128)(2,1)S(1)} %get-tuple-element.14), channel_id=1, source_target_pairs={{0,1},{1,0},{4,8},{5,9},{8,4},{9,5},{12,13},{13,12},{2,3},{3,2},{6... | collective-permute-start | bytes 172040 | tf_op jit(solution)/shard_map/ppermute | solution.py:469
  5.2 4.6 %collective-permute-start.4 = (bf16[80,256]{1,0:T(8,128)(2,1)S(1)}, bf16[80,256]{1,0:T(8,128)(2,1)S(1)}, u32[]{:S(2)}, u32[]{:S(2)}) collective-permute-start(bf16[80,256]{1,0:T(8,128)(2,1)S(1)} %inner.1.inner_ref), channel_id=1, source_target_pairs={{2,0},{0,2},{3,1},{1,3},{6,4},{4,6},{7,5},{5,7},{10,8},{8,10},{11,... | collective-permute-start | bytes 122888 | tf_op jit(solution)/shard_map/ppermute | solution.py:498
  7.4 4.7 %collective-permute-start.3 = (bf16[112,256]{1,0:T(8,128)(2,1)S(1)}, bf16[112,256]{1,0:T(8,128)(2,1)S(1)}, u32[]{:S(2)}, u32[]{:S(2)}) collective-permute-start(bf16[112,256]{1,0:T(8,128)(2,1)S(1)} %side_a.1.refs_0_.first_ref), channel_id=1, source_target_pairs={{2,0},{0,2},{3,1},{1,3},{6,4},{4,6},{7,5},{5,7},{10,8},{8,10},{11,... | collective-permute-start | bytes 172040 | tf_op jit(solution)/shard_map/ppermute | solution.py:498
  9.7 4.2 %collective-permute-start.5 = (bf16[112,256]{1,0:T(8,128)(2,1)S(1)}, bf16[112,256]{1,0:T(8,128)(2,1)S(1)}, u32[]{:S(2)}, u32[]{:S(2)}) collective-permute-start(bf16[112,256]{1,0:T(8,128)(2,1)S(1)} %pass.1), channel_id=1, source_target_pairs={{2,0},{0,2},{3,1},{1,3},{6,4},{4,6},{7,5},{5,7},{10,8},{8,10},{11,... | collective-permute-start | bytes 172040 | tf_op jit(solution)/shard_map/ppermute | solution.py:498

commit v15 on v13

--- a/solution.py
+++ b/solution.py
@@ -159,10 +159,11 @@
     out_ref[2 * lines :, :] = edges.astype(jnp.bfloat16)
 
 
-def read_piece(ref):
-    lines = (ref.shape[0] - STEP) // 2
-    tiles = ref[: 2 * lines, :].astype(jnp.float32)
-    edges = one_below(ref[2 * lines :, :].astype(jnp.float32), 0, 2 * lines // STEP)
+def read_piece(ref, first, count):
+    lines = (count - STEP) // 2
+    middle = first + 2 * lines
+    tiles = ref[first:middle, :].astype(jnp.float32)
+    edges = one_below(ref[middle : first + count, :].astype(jnp.float32), 0, 2 * lines // STEP)
     return [(v[:lines], v[lines:]) for v in (tiles, edges)]
 
 
@@ -170,9 +171,8 @@
     lines = image_ref.shape[1]
     width = image_ref.shape[2]
     side = lax.axis_index("rg")
-    cut = slice(RIM, lines - RIM)
-    source = lax.broadcasted_iota(jnp.int32, (lines, lines - 2 * RIM), 0)
-    weights = band(taps_ref[:, cut], offsets_ref[:, cut], RIM, source)
+    source = lax.broadcasted_iota(jnp.int32, (lines, lines), 0)
+    weights = band(taps_ref[...], offsets_ref[...], 0, source)
     weights = jnp.concatenate([weights, weights], axis=0)
     for part in range(2):
         edge = edge_of(other_ref, part, side, slice(0, lines))
@@ -180,18 +180,11 @@
         out_ref[part] = apply_band(weights, rows)
 
 
-def side_kernel(
-    turn, image_ref, other_ref, taps_ref, offsets_ref, message_ref, inner_ref, *refs
-):
-    out_ref = refs[-1]
+def side_lines(turn, image_ref, other_ref, taps_ref, offsets_ref, message_ref):
     lines = image_ref.shape[1]
-    width = image_ref.shape[2]
     side = lax.axis_index("rg")
-    place = lax.axis_index("az")
     above = is_above(turn)
-    alone = jnp.where(above, place == 0, place == lax.axis_size("az") - 1)
     message = message_ref[...]
-    message = jnp.where(alone, jnp.zeros_like(message), message)
     block = message[2 * REACH :, :].astype(jnp.float32)
     steps = 2 * REACH // STEP
     rim_edges = one_below(block, 0, steps).astype(jnp.bfloat16)
@@ -224,12 +217,45 @@
         own = high_low(jnp.concatenate([own, edge], axis=1))
         cut = slice(part * REACH, (part + 1) * REACH)
         rim = jnp.concatenate([message[cut, :], rim_edges[cut]], axis=1)
-        total = apply_band(weights, jnp.concatenate([rim, own], axis=0))
-        between = inner_ref.shape[1] // 2
-        upper = jnp.concatenate([total, inner_ref[part, :between]], axis=0)
-        lower = jnp.concatenate([inner_ref[part, between:], total], axis=0)
-        parts.append(jnp.where(above, upper, lower))
-    write_piece(out_ref, parts, width)
+        parts.append(apply_band(weights, jnp.concatenate([rim, own], axis=0)))
+    return parts
+
+
+def side_kernel(turn, *refs):
+    image_ref, other_ref, taps_ref, offsets_ref, message_ref, inner_ref = refs[:6]
+    out_ref = refs[-1]
+    width = image_ref.shape[2]
+    place = lax.axis_index("az")
+    above = is_above(turn)
+    alone = jnp.where(above, place == 0, place == lax.axis_size("az") - 1)
+    if turn == 1:
+        count = refs[6].shape[0]
+        out_ref[:count, :] = refs[6][...]
+        out_ref = out_ref.at[count:]
+
+    lines = inner_ref.shape[1]
+    half = lines // 2 + HALF
+
+    @pl.when(alone)
+    def _():
+        halves = []
+        for part in range(2):
+            blank = jnp.zeros((HALF, inner_ref.shape[2]), jnp.float32)
+            upper = jnp.concatenate([blank, inner_ref[part, : half - HALF]], axis=0)
+            lower = jnp.concatenate([inner_ref[part, lines - half + HALF :], blank], axis=0)
+            halves.append(jnp.where(above, upper, lower))
+        write_piece(out_ref, halves, width)
+
+    @pl.when(jnp.logical_not(alone))
+    def _():
+        halves = []
+        for part, total in enumerate(side_lines(turn, *refs[:5])):
+            near = inner_ref[part, RIM : half - HALF]
+            upper = jnp.concatenate([total, near], axis=0)
+            near = inner_ref[part, lines - half + HALF : lines - RIM]
+            lower = jnp.concatenate([near, total], axis=0)
+            halves.append(jnp.where(above, upper, lower))
+        write_piece(out_ref, halves, width)
 
 
 def cross(own_parts, other_parts):
@@ -240,10 +266,10 @@
     return real, imag
 
 
-def interferogram(own_ref, other_ref):
+def interferogram(own_ref, other_ref, first, count):
     side = lax.axis_index("rg")
-    own_tile, own_edge = read_piece(own_ref)
-    other_tile, other_edge = read_piece(other_ref)
+    own_tile, own_edge = read_piece(own_ref, first, count)
+    other_tile, other_edge = read_piece(other_ref, first, count)
     mid = jnp.concatenate(cross(own_tile, other_tile), axis=0)
     rim = jnp.concatenate(cross(own_edge, other_edge), axis=0)
     before = jnp.where(side == 0, 0.0, rim)
@@ -253,9 +279,12 @@
     return jnp.concatenate([mid.astype(jnp.bfloat16), shifted], axis=1)
 
 
-def line_sum(turn, tables, own_ref, other_ref):
-    both = interferogram(own_ref, other_ref)
-    return jnp.dot(tables.lines(turn), both, preferred_element_type=jnp.float32)
+def line_sum(tables, own_ref, other_ref):
+    count = own_ref.shape[0] // 2
+    both = [interferogram(own_ref, other_ref, turn * count, count) for turn in range(2)]
+    weights = jnp.concatenate([tables.lines(turn) for turn in range(2)], axis=1)
+    both = jnp.concatenate(both, axis=0)
+    return jnp.dot(weights, both, preferred_element_type=jnp.float32)
 
 
 def filtered_of(line_spectra, tables, spectrum_ref, row_patches, width):
@@ -314,18 +343,12 @@
         ref[part] = result[part * lines : (part + 1) * lines]
 
 
-def own_kernel(table_ref, first_ref, second_ref, out_ref, spectrum_ref):
+def own_kernel(table_ref, own_ref, out_ref, spectrum_ref):
     _, lines, width = out_ref.shape
     row_patches = lines // HALF + 1
     tables = Tables(table_ref, row_patches)
-    both = [interferogram(ref, ref) for ref in (first_ref, second_ref)]
-    weights = jnp.concatenate([tables.lines(turn) for turn in range(2)], axis=1)
-    total = jnp.dot(weights, jnp.concatenate(both, axis=0), preferred_element_type=jnp.float32)
+    total = line_sum(tables, own_ref, own_ref)
     keep(out_ref, filtered_of(total, tables, spectrum_ref, row_patches, width))
-
-
-def first_kernel(row_patches, table_ref, own_ref, other_ref, out_ref):
-    out_ref[...] = line_sum(0, Tables(table_ref, row_patches), own_ref, other_ref)
 
 
 def other_kernel(match_ref, table_ref, filtered_own_ref, own_ref, *refs):
@@ -349,8 +372,7 @@
 
     send(0, filtered_own_ref)
     for slot in range(1, dates):
-        first_ref, other_ref = refs[2 * slot - 2 : 2 * slot]
-        total = first_ref[...] + line_sum(1, tables, own_ref, other_ref)
+        total = line_sum(tables, own_ref, refs[slot - 1])
         result = filtered_of(total, tables, spectrum_ref, row_patches, width)
         keep(result_ref.at[slot - 1], result)
         send(slot, result_ref.at[slot - 1])
@@ -447,30 +469,31 @@
     messages = [swapped(messages[turn], turn) for turn in range(2)]
     inner = pl.pallas_call(
         inner_kernel,
-        out_shape=jax.ShapeDtypeStruct((2, lines - 2 * RIM, width + HALF), jnp.float32),
+        out_shape=jax.ShapeDtypeStruct((2, lines, width + HALF), jnp.float32),
         in_specs=[VMEM] * 4,
         out_specs=VMEM,
         compiler_params=PARAMS,
         name="inner",
     )(*raw)
-    own = []
+    pieces = []
+    count = 2 * (lines // 2 + HALF) + STEP
     for turn in range(2):
-        count = lines // 2 + HALF
         call = pl.pallas_call(
             functools.partial(side_kernel, turn),
-            out_shape=jax.ShapeDtypeStruct((2 * count + STEP, width), jnp.bfloat16),
-            in_specs=[VMEM] * (6 + len(own)),
+            out_shape=jax.ShapeDtypeStruct(((turn + 1) * count, width), jnp.bfloat16),
+            in_specs=[VMEM] * (6 + turn),
             out_specs=VMEM,
             compiler_params=PARAMS,
             name="side_" + "ab"[turn],
         )
-        own.append(call(*raw, messages[turn], inner, *own))
+        pieces.append(call(*raw, messages[turn], inner, *pieces))
+    own = pieces[1]
     dates = lax.axis_size("date")
 
     def from_date(piece, slot):
         return lax.ppermute(piece, "date", [((i + slot) % dates, i) for i in range(dates)])
 
-    others = [from_date(piece, slot) for slot in range(1, dates) for piece in own]
+    others = [from_date(own, slot) for slot in range(1, dates)]
     row_patches = lines // HALF + 1
     chunks = (width + width + LANES) // LANES
     tables = jnp.asarray(all_tables(row_patches))
@@ -478,27 +501,16 @@
     filtered_own = pl.pallas_call(
         own_kernel,
         out_shape=jax.ShapeDtypeStruct((2, lines, width), jnp.float32),
-        in_specs=[VMEM] * 3,
+        in_specs=[VMEM] * 2,
         out_specs=VMEM,
         scratch_shapes=[spectrum],
         compiler_params=PARAMS,
         name="filter_own",
-    )(tables, *own)
-    pieces = []
-    for first, second in zip(others[::2], others[1::2]):
-        total = pl.pallas_call(
-            functools.partial(first_kernel, row_patches),
-            out_shape=jax.ShapeDtypeStruct((row_patches * 2 * PATCH, chunks * LANES), jnp.float32),
-            in_specs=[VMEM] * 3,
-            out_specs=VMEM,
-            compiler_params=PARAMS,
-            name="filter_first",
-        )(tables, own[0], first)
-        pieces += [total, second]
+    )(tables, own)
     return pl.pallas_call(
         other_kernel,
         out_shape=jax.ShapeDtypeStruct((match_count, 2, 1, lines, width), jnp.float32),
-        in_specs=[SMEM] + [VMEM] * (3 + len(pieces)),
+        in_specs=[SMEM] + [VMEM] * (3 + len(others)),
         out_specs=HBM,
         scratch_shapes=[
             pltpu.VMEM((dates - 1, 2, lines, width), jnp.float32),
@@ -507,7 +519,7 @@
         ],
         compiler_params=PARAMS,
         name="filter_other",
-    )(matchings, tables, filtered_own, own[1], *pieces)
+    )(matchings, tables, filtered_own, own, *others)
 
 
 def solution(mesh):

time: 16.8 us -> 15.8 us (0.940); the launches traced: 16.7 us -> 15.5 us
  Pallas kernels: 6.25 us -> 5.56 us
  waiting for transfers between devices: 4.68 us -> 4.39 us
  starting transfers between devices: 5.57 us -> 5.35 us
    pallas_call x4 -> x3, Pallas kernels: 1.46 us -> 0.77 us  [the longest x2 0.5 us: per_device(): pieces.append(call(*raw, messages[turn], inner, *pieces))]
    ppermute x2 -> x1, waiting for transfers between devices: 2.51 us -> 2.19 us  [from_date(): lax.ppermute(piece, 'date', [((i + slot) % dates, i) for i in range(dates)])]
    ppermute x2 -> x1, starting transfers between devices: 2.12 us -> 1.9 us  [from_date(): lax.ppermute(piece, 'date', [((i + slot) % dates, i) for i in range(dates)])]
  transfers between devices with their start and end apart: 5 -> 4, of which waited for: 4 -> 3; matrix products, arithmetic and copies ran while one was open for 1% -> 1% of each run, Pallas kernels for 22% -> 18%
where the time goes in v15:
time: 15.8 us; the launch traced here: 15.5 us
  Pallas kernels  5.56 us (35%)
  starting transfers between devices  5.35 us (34%)
  waiting for transfers between devices  4.39 us (28%)
    ppermute x2, starting transfers between devices, swapped(): return lax.ppermute(value, ('az', 'rg'), pairs)  3 us
    pallas_call x1, Pallas kernels, per_device(): pl.pallas_call(other_kernel, out_shape=jax.ShapeDtypeStruct((match_count,...  2.48 us
    ppermute x1, waiting for transfers between devices, from_date(): lax.ppermute(piece, 'date', [((i + slot) % dates, i) for i in range(dates)])  2.19 us
    ppermute x2, waiting for transfers between devices, swapped(): return lax.ppermute(value, ('az', 'rg'), pairs)  1.94 us
    ppermute x1, starting transfers between devices, from_date(): lax.ppermute(piece, 'date', [((i + slot) % dates, i) for i in range(dates)])  1.9 us
    pallas_call x1, Pallas kernels, per_device(): pl.pallas_call(own_kernel, out_shape=jax.ShapeDtypeStruct((2, lines, widt...  1.23 us
    pallas_call x1, Pallas kernels, per_device(): pl.pallas_call(load_kernel, out_shape=tuple((pltpu.VMEM(a.shape, a.dtype)...  0.93 us
    pallas_call x2, Pallas kernels, per_device(): pieces.append(call(*raw, messages[turn], inner, *pieces))  0.5 us
  transfers between devices with their start and end apart: 4, of which 3 were waited for; matrix products, arithmetic and copies ran while one was open for 1% of the time, Pallas kernels for 18%

profile of v15, /device:TPU:0, one launch (start us, length us, event | category | flops | bytes accessed | tf_op | source)
XLA Modules:
  0.0 15.5 jit_solution(18079454293290125416)
XLA Ops:
  0.0 0.5 %collective-permute-start = (f32[2,1,64,256]{3,2,0,1:T(8,128)}, f32[2,1,64,256]{3,2,0,1:T(8,128)S(1)}, u32[]{:S(2)}, u32[]{:S(2)}) collective-permute-start(f32[2,1,64,256]{3,2,0,1:T(8,128)} %bitcast.8), channel_id=1, source_target_pairs={{0,1},{1,0},{2,3},{3,2},{4,5},{5,4},{6,7},{7,6},{8,9},{9,8},{10,11... | collective-permute-start | bytes 393224 | tf_op jit(solution)/shard_map/ppermute | solution.py:432
  0.5 0.9 %load.1 = (f32[2,64,256]{2,1,0:T(8,128)S(1)}, f32[8,64]{1,0:T(8,128)S(1)}, s32[1,64]{1,0:T(1,128)S(1)}) custom-call(f32[2,64,256]{2,1,0:T(8,128)} %bitcast.9, f32[8,64]{1,0:T(8,128)} %bitcast.10, s32[1,64]{1,0:T(1,128)} %refs_2_.1), custom_call_target="tpu_custom_call" | custom-call | tf_op jit(solution)/shard_map/load/pallas_call | solution.py:438
  1.4 0.3 %collective-permute-done = f32[2,1,64,256]{3,2,0,1:T(8,128)S(1)} collective-permute-done((f32[2,1,64,256]{3,2,0,1:T(8,128)}, f32[2,1,64,256]{3,2,0,1:T(8,128)S(1)}, u32[]{:S(2)}, u32[]{:S(2)}) %collective-permute-start) | collective-permute-done | bytes 131104 | tf_op jit(solution)/shard_map/ppermute | solution.py:432
  1.7 0.2 %pack.1 = (bf16[112,256]{1,0:T(8,128)(2,1)S(1)}, bf16[112,256]{1,0:T(8,128)(2,1)S(1)}) custom-call(f32[2,64,256]{2,1,0:T(8,128)S(1)} %get-tuple-element.10.image_ref.refs_0_, f32[2,64,256]{2,1,0:T(8,128)S(1)} %bitcast.4, f32[8,64]{1,0:T(8,128)S(1)} %get-tuple-element.11.taps_ref.refs_2_, s32[1,64]{1,0:T(1,128)S(1)} %get-tuple-element.12.offsets_ref.refs_3_), custom_call_target="tpu_custom_call" | custom-call | tf_op jit(solution)/shard_map/pack/pallas_call | solution.py:449
  1.8 3.0 %collective-permute-start.2 = (bf16[112,256]{1,0:T(8,128)(2,1)S(1)}, bf16[112,256]{1,0:T(8,128)(2,1)S(1)}, u32[]{:S(2)}, u32[]{:S(2)}) collective-permute-start(bf16[112,256]{1,0:T(8,128)(2,1)S(1)} %get-tuple-element.14), channel_id=1, source_target_pairs={{0,4},{1,5},{4,0},{5,1},{8,12},{9,13},{12,8},{13,9},{2,6},{3,7},{6... | collective-permute-start | bytes 172040 | tf_op jit(solution)/shard_map/ppermute | solution.py:467
  4.8 0.0 collective-permute-start.1
  4.8 0.3 %inner.1.refs_5_ = f32[2,64,288]{2,1,0:T(8,128)S(1)} custom-call(f32[2,64,256]{2,1,0:T(8,128)S(1)} %get-tuple-element.10.image_ref.refs_0_, f32[2,64,256]{2,1,0:T(8,128)S(1)} %bitcast.5, f32[8,64]{1,0:T(8,128)S(1)} %get-tuple-element.11.taps_ref.refs_2_, s32[1,64]{1,0:T(1,128)S(1)} %get-tuple-element.12.offsets_ref.refs_3_), custom_call_target="tpu_custom_call" | custom-call | tf_op jit(solution)/shard_map/inner/pallas_call | solution.py:470
  5.1 0.0 copy-start
  5.1 1.9 %collective-permute-done.2.refs_4_ = bf16[112,256]{1,0:T(8,128)(2,1)S(1)} collective-permute-done((bf16[112,256]{1,0:T(8,128)(2,1)S(1)}, bf16[112,256]{1,0:T(8,128)(2,1)S(1)}, u32[]{:S(2)}, u32[]{:S(2)}) %collective-permute-start.2) | collective-permute-done | bytes 57376 | tf_op jit(solution)/shard_map/ppermute | solution.py:467
  7.0 0.4 %side_a.1.refs_6_ = bf16[144,256]{1,0:T(8,128)(2,1)S(1)} custom-call(f32[2,64,256]{2,1,0:T(8,128)S(1)} %get-tuple-element.10.image_ref.refs_0_, f32[2,64,256]{2,1,0:T(8,128)S(1)} %bitcast.6, f32[8,64]{1,0:T(8,128)S(1)} %get-tuple-element.11.taps_ref.refs_2_, s32[1,64]{1,0:T(1,128)S(1)} %get-tuple-element.12.offsets_ref.refs_3_, ...), custom_call_target="tpu_custom_call" | custom-call | tf_op jit(solution)/shard_map/side_a/pallas_call | solution.py:489
  7.4 0.0 copy-start.1
  7.4 0.0 collective-permute-done.1.refs_4_
  7.4 0.1 side_b.1.own_ref
  7.6 1.9 %collective-permute-start.3 = (bf16[288,256]{1,0:T(8,128)(2,1)S(1)}, bf16[288,256]{1,0:T(8,128)(2,1)S(1)}, u32[]{:S(2)}, u32[]{:S(2)}) collective-permute-start(bf16[288,256]{1,0:T(8,128)(2,1)S(1)} %side_b.1.own_ref), channel_id=1, source_target_pairs={{2,0},{0,2},{3,1},{1,3},{6,4},{4,6},{7,5},{5,7},{10,8},{8,10},{11,... | collective-permute-start | bytes 442376 | tf_op jit(solution)/shard_map/ppermute | solution.py:494
  9.5 0.0 copy-done.1
  9.5 0.1 copy.7.match_ref
  9.5 0.0 copy-done
  9.6 1.2 %filter_own.1.filtered_own_ref = f32[2,64,256]{2,1,0:T(8,128)S(1)} custom-call(bf16[1472,256]{1,0:T(8,128)(2,1)S(1)} %copy-done, bf16[288,256]{1,0:T(8,128)(2,1)S(1)} %side_b.1.own_ref), custom_call_target="tpu_custom_call" | custom-call | tf_op jit(solution)/shard_map/filter_own/pallas_call | solution.py:501
  10.8 2.2 %collective-permute-done.3.refs_0_ = bf16[288,256]{1,0:T(8,128)(2,1)S(1)} collective-permute-done((bf16[288,256]{1,0:T(8,128)(2,1)S(1)}, bf16[288,256]{1,0:T(8,128)(2,1)S(1)}, u32[]{:S(2)}, u32[]{:S(2)}) %collective-permute-start.3) | collective-permute-done | bytes 147488 | tf_op jit(solution)/shard_map/ppermute | solution.py:494
  13.0 2.5 %filter_other.1 = f32[3,2,1,64,256]{4,3,2,1,0:T(8,128)} custom-call(s32[3,2]{1,0:T(4,128)S(1)} %copy.7.match_ref, bf16[1472,256]{1,0:T(8,128)(2,1)S(1)} %copy-done, f32[2,64,256]{2,1,0:T(8,128)S(1)} %filter_own.1.filtered_own_ref, bf16[288,256]{1,0:T(8,128)(2,1)S(1)} %side_b.1.own_ref, bf16[288,256]{1,0:T(8,128)(2,1)S(1)} %collective-permute-done.3.refs_0_), custom_call_target="tpu_custom_call" | custom-call | tf_op jit(solution)/shard_map/filter_other/pallas_call | solution.py:510
Async XLA Ops:
  0.0 1.6 %collective-permute-start = (f32[2,1,64,256]{3,2,0,1:T(8,128)}, f32[2,1,64,256]{3,2,0,1:T(8,128)S(1)}, u32[]{:S(2)}, u32[]{:S(2)}) collective-permute-start(f32[2,1,64,256]{3,2,0,1:T(8,128)} %bitcast.8), channel_id=1, source_target_pairs={{0,1},{1,0},{2,3},{3,2},{4,5},{5,4},{6,7},{7,6},{8,9},{9,8},{10,11... | collective-permute-start | bytes 393224 | tf_op jit(solution)/shard_map/ppermute | solution.py:432
  1.8 5.2 %collective-permute-start.2 = (bf16[112,256]{1,0:T(8,128)(2,1)S(1)}, bf16[112,256]{1,0:T(8,128)(2,1)S(1)}, u32[]{:S(2)}, u32[]{:S(2)}) collective-permute-start(bf16[112,256]{1,0:T(8,128)(2,1)S(1)} %get-tuple-element.14), channel_id=1, source_target_pairs={{0,4},{1,5},{4,0},{5,1},{8,12},{9,13},{12,8},{13,9},{2,6},{3,7},{6... | collective-permute-start | bytes 172040 | tf_op jit(solution)/shard_map/ppermute | solution.py:467
  4.8 2.6 %collective-permute-start.1 = (bf16[112,256]{1,0:T(8,128)(2,1)S(1)}, bf16[112,256]{1,0:T(8,128)(2,1)S(1)}, u32[]{:S(2)}, u32[]{:S(2)}) collective-permute-start(bf16[112,256]{1,0:T(8,128)(2,1)S(1)} %get-tuple-element.13), channel_id=1, source_target_pairs={{0,1},{1,0},{4,8},{5,9},{8,4},{9,5},{12,13},{13,12},{2,3},{3,2},{6... | collective-permute-start | bytes 172040 | tf_op jit(solution)/shard_map/ppermute | solution.py:467
  5.1 4.5 %copy-start = (bf16[1472,256]{1,0:T(8,128)(2,1)S(1)}, bf16[1472,256]{1,0:T(8,128)(2,1)}, u32[]{:S(2)}) copy-start(bf16[1472,256]{1,0:T(8,128)(2,1)} %constant.2.clone.table_ref) | copy-start | bytes 2260996
  7.4 2.0 %copy-start.1 = (s32[3,2]{0,1:T(2,128)S(1)}, s32[3,2]{0,1:T(2,128)}, u32[]{:S(2)}) copy-start(s32[3,2]{0,1:T(2,128)} %param.8) | copy-start | bytes 76
  7.6 5.4 %collective-permute-start.3 = (bf16[288,256]{1,0:T(8,128)(2,1)S(1)}, bf16[288,256]{1,0:T(8,128)(2,1)S(1)}, u32[]{:S(2)}, u32[]{:S(2)}) collective-permute-start(bf16[288,256]{1,0:T(8,128)(2,1)S(1)} %side_b.1.own_ref), channel_id=1, source_target_pairs={{2,0},{0,2},{3,1},{1,3},{6,4},{4,6},{7,5},{5,7},{10,8},{8,10},{11,... | collective-permute-start | bytes 442376 | tf_op jit(solution)/shard_map/ppermute | solution.py:494

commit v16 on v15

--- a/solution.py
+++ b/solution.py
@@ -291,38 +291,43 @@
     line_spectra = line_spectra.astype(jnp.bfloat16)
     chunks = line_spectra.shape[1] // LANES
     forward, inverse, back, ring, window = tables.core()
-    pieces = []
-    for row in range(row_patches):
+    step = chunks * PATCH
+    spans = [slice(row * step, (row + 1) * step) for row in range(row_patches)]
+    for row, span in enumerate(spans):
         top = row * 2 * PATCH
+        pieces = []
         for chunk in range(chunks):
             cut = slice(chunk * LANES, (chunk + 1) * LANES)
             real = line_spectra[top : top + PATCH, cut]
             imag = line_spectra[top + PATCH : top + 2 * PATCH, cut]
             pieces.append(jnp.concatenate([real, imag], axis=1))
-    patches = jnp.concatenate(pieces, axis=0)
-    spectrum_ref[...] = jnp.dot(patches, forward, preferred_element_type=jnp.float32)
-    powers = []
-    for block in range(row_patches * chunks):
-        rows = slice(block * PATCH, (block + 1) * PATCH)
-        real = spectrum_ref[rows, :LANES]
-        imag = spectrum_ref[rows, LANES:]
-        power = real * real + imag * imag
-        power = power + pltpu.roll(power, 1, 0) + pltpu.roll(power, PATCH - 1, 0)
-        powers.append(power.astype(jnp.bfloat16))
-    smooth = jnp.dot(jnp.concatenate(powers, axis=0), ring, preferred_element_type=jnp.float32)
-    gain = lax.rsqrt(lax.rsqrt(smooth * (1.0 / (9.0 * PATCH * PATCH)) + 1.0))
-    shaped = jnp.concatenate(
-        [spectrum_ref[:, :LANES] * gain, spectrum_ref[:, LANES:] * gain], axis=1
-    ).astype(jnp.bfloat16)
-    range_back = jnp.dot(shaped, inverse, preferred_element_type=jnp.float32)
-    range_back = range_back.astype(jnp.bfloat16)
+        patches = jnp.concatenate(pieces, axis=0)
+        spectrum_ref[span, :] = jnp.dot(patches, forward, preferred_element_type=jnp.float32)
+    smooths = []
+    for span in spans:
+        powers = []
+        for start in range(span.start, span.stop, PATCH):
+            real = spectrum_ref[start : start + PATCH, :LANES]
+            imag = spectrum_ref[start : start + PATCH, LANES:]
+            power = real * real + imag * imag
+            power = power + pltpu.roll(power, 1, 0) + pltpu.roll(power, PATCH - 1, 0)
+            powers.append(power.astype(jnp.bfloat16))
+        powers = jnp.concatenate(powers, axis=0)
+        smooths.append(jnp.dot(powers, ring, preferred_element_type=jnp.float32))
+    range_backs = []
+    for span, smooth in zip(spans, smooths):
+        gain = lax.rsqrt(lax.rsqrt(smooth * (1.0 / (9.0 * PATCH * PATCH)) + 1.0))
+        shaped = jnp.concatenate(
+            [spectrum_ref[span, :LANES] * gain, spectrum_ref[span, LANES:] * gain], axis=1
+        ).astype(jnp.bfloat16)
+        range_back = jnp.dot(shaped, inverse, preferred_element_type=jnp.float32)
+        range_backs.append(range_back.astype(jnp.bfloat16))
     window = jnp.concatenate([window] * chunks, axis=1)
     totals = [[None] * (row_patches - 1) for _ in range(2)]
     for row in range(row_patches):
         stacked = []
         for chunk in range(chunks):
-            top = (row * chunks + chunk) * PATCH
-            block = range_back[top : top + PATCH]
+            block = range_backs[row][chunk * PATCH : (chunk + 1) * PATCH]
             stacked.append(jnp.concatenate([block[:, :LANES], block[:, LANES:]], axis=0))
         stacked = jnp.concatenate(stacked, axis=1)
         patch_out = jnp.dot(back, stacked, preferred_element_type=jnp.float32) * window

time: 15.8 us -> 15.7 us (level)
  Pallas kernels: 5.56 us -> 5.37 us
  transfers between devices with their start and end apart: 4 -> 4, of which waited for: 3 -> 3; matrix products, arithmetic and copies ran while one was open for 1% -> 1% of each run, Pallas kernels for 18% -> 17%
where the time goes in v16:
time: 15.7 us; the launch traced here: 15.4 us
  Pallas kernels  5.37 us (34%)
  starting transfers between devices  5.35 us (34%)
  waiting for transfers between devices  4.52 us (29%)
    ppermute x2, starting transfers between devices, swapped(): return lax.ppermute(value, ('az', 'rg'), pairs)  3 us
    pallas_call x1, Pallas kernels, per_device(): pl.pallas_call(other_kernel, out_shape=jax.ShapeDtypeStruct((match_count,...  2.41 us
    ppermute x1, waiting for transfers between devices, from_date(): lax.ppermute(piece, 'date', [((i + slot) % dates, i) for i in range(dates)])  2.32 us
    ppermute x2, waiting for transfers between devices, swapped(): return lax.ppermute(value, ('az', 'rg'), pairs)  1.94 us
    ppermute x1, starting transfers between devices, from_date(): lax.ppermute(piece, 'date', [((i + slot) % dates, i) for i in range(dates)])  1.9 us
    pallas_call x1, Pallas kernels, per_device(): pl.pallas_call(own_kernel, out_shape=jax.ShapeDtypeStruct((2, lines, widt...  1.1 us
    pallas_call x1, Pallas kernels, per_device(): pl.pallas_call(load_kernel, out_shape=tuple((pltpu.VMEM(a.shape, a.dtype)...  0.93 us
    pallas_call x2, Pallas kernels, per_device(): pieces.append(call(*raw, messages[turn], inner, *pieces))  0.5 us
  transfers between devices with their start and end apart: 4, of which 3 were waited for; matrix products, arithmetic and copies ran while one was open for 1% of the time, Pallas kernels for 17%

profile of v16, /device:TPU:0, one launch (start us, length us, event | category | flops | bytes accessed | tf_op | source)
XLA Modules:
  0.0 15.4 jit_solution(17018793586820122490)
XLA Ops:
  0.0 0.5 %collective-permute-start = (f32[2,1,64,256]{3,2,0,1:T(8,128)}, f32[2,1,64,256]{3,2,0,1:T(8,128)S(1)}, u32[]{:S(2)}, u32[]{:S(2)}) collective-permute-start(f32[2,1,64,256]{3,2,0,1:T(8,128)} %bitcast.8), channel_id=1, source_target_pairs={{0,1},{1,0},{2,3},{3,2},{4,5},{5,4},{6,7},{7,6},{8,9},{9,8},{10,11... | collective-permute-start | bytes 393224 | tf_op jit(solution)/shard_map/ppermute | solution.py:437
  0.5 0.9 %load.1 = (f32[2,64,256]{2,1,0:T(8,128)S(1)}, f32[8,64]{1,0:T(8,128)S(1)}, s32[1,64]{1,0:T(1,128)S(1)}) custom-call(f32[2,64,256]{2,1,0:T(8,128)} %bitcast.9, f32[8,64]{1,0:T(8,128)} %bitcast.10, s32[1,64]{1,0:T(1,128)} %refs_2_.1), custom_call_target="tpu_custom_call" | custom-call | tf_op jit(solution)/shard_map/load/pallas_call | solution.py:443
  1.4 0.3 %collective-permute-done = f32[2,1,64,256]{3,2,0,1:T(8,128)S(1)} collective-permute-done((f32[2,1,64,256]{3,2,0,1:T(8,128)}, f32[2,1,64,256]{3,2,0,1:T(8,128)S(1)}, u32[]{:S(2)}, u32[]{:S(2)}) %collective-permute-start) | collective-permute-done | bytes 131104 | tf_op jit(solution)/shard_map/ppermute | solution.py:437
  1.7 0.2 %pack.1 = (bf16[112,256]{1,0:T(8,128)(2,1)S(1)}, bf16[112,256]{1,0:T(8,128)(2,1)S(1)}) custom-call(f32[2,64,256]{2,1,0:T(8,128)S(1)} %get-tuple-element.10.image_ref.refs_0_, f32[2,64,256]{2,1,0:T(8,128)S(1)} %bitcast.4, f32[8,64]{1,0:T(8,128)S(1)} %get-tuple-element.11.taps_ref.refs_2_, s32[1,64]{1,0:T(1,128)S(1)} %get-tuple-element.12.offsets_ref.refs_3_), custom_call_target="tpu_custom_call" | custom-call | tf_op jit(solution)/shard_map/pack/pallas_call | solution.py:454
  1.8 3.0 %collective-permute-start.2 = (bf16[112,256]{1,0:T(8,128)(2,1)S(1)}, bf16[112,256]{1,0:T(8,128)(2,1)S(1)}, u32[]{:S(2)}, u32[]{:S(2)}) collective-permute-start(bf16[112,256]{1,0:T(8,128)(2,1)S(1)} %get-tuple-element.14), channel_id=1, source_target_pairs={{0,4},{1,5},{4,0},{5,1},{8,12},{9,13},{12,8},{13,9},{2,6},{3,7},{6... | collective-permute-start | bytes 172040 | tf_op jit(solution)/shard_map/ppermute | solution.py:472
  4.8 0.0 collective-permute-start.1
  4.8 0.3 %inner.1.refs_5_ = f32[2,64,288]{2,1,0:T(8,128)S(1)} custom-call(f32[2,64,256]{2,1,0:T(8,128)S(1)} %get-tuple-element.10.image_ref.refs_0_, f32[2,64,256]{2,1,0:T(8,128)S(1)} %bitcast.5, f32[8,64]{1,0:T(8,128)S(1)} %get-tuple-element.11.taps_ref.refs_2_, s32[1,64]{1,0:T(1,128)S(1)} %get-tuple-element.12.offsets_ref.refs_3_), custom_call_target="tpu_custom_call" | custom-call | tf_op jit(solution)/shard_map/inner/pallas_call | solution.py:475
  5.1 0.0 copy-start
  5.1 1.9 %collective-permute-done.2.refs_4_ = bf16[112,256]{1,0:T(8,128)(2,1)S(1)} collective-permute-done((bf16[112,256]{1,0:T(8,128)(2,1)S(1)}, bf16[112,256]{1,0:T(8,128)(2,1)S(1)}, u32[]{:S(2)}, u32[]{:S(2)}) %collective-permute-start.2) | collective-permute-done | bytes 57376 | tf_op jit(solution)/shard_map/ppermute | solution.py:472
  7.0 0.4 %side_a.1.refs_6_ = bf16[144,256]{1,0:T(8,128)(2,1)S(1)} custom-call(f32[2,64,256]{2,1,0:T(8,128)S(1)} %get-tuple-element.10.image_ref.refs_0_, f32[2,64,256]{2,1,0:T(8,128)S(1)} %bitcast.6, f32[8,64]{1,0:T(8,128)S(1)} %get-tuple-element.11.taps_ref.refs_2_, s32[1,64]{1,0:T(1,128)S(1)} %get-tuple-element.12.offsets_ref.refs_3_, ...), custom_call_target="tpu_custom_call" | custom-call | tf_op jit(solution)/shard_map/side_a/pallas_call | solution.py:494
  7.4 0.0 copy-start.1
  7.4 0.0 collective-permute-done.1.refs_4_
  7.4 0.1 side_b.1.own_ref
  7.6 1.9 %collective-permute-start.3 = (bf16[288,256]{1,0:T(8,128)(2,1)S(1)}, bf16[288,256]{1,0:T(8,128)(2,1)S(1)}, u32[]{:S(2)}, u32[]{:S(2)}) collective-permute-start(bf16[288,256]{1,0:T(8,128)(2,1)S(1)} %side_b.1.own_ref), channel_id=1, source_target_pairs={{2,0},{0,2},{3,1},{1,3},{6,4},{4,6},{7,5},{5,7},{10,8},{8,10},{11,... | collective-permute-start | bytes 442376 | tf_op jit(solution)/shard_map/ppermute | solution.py:499
  9.5 0.0 copy-done.1
  9.5 0.1 copy.7.match_ref
  9.5 0.0 copy-done
  9.6 1.1 %filter_own.1.filtered_own_ref = f32[2,64,256]{2,1,0:T(8,128)S(1)} custom-call(bf16[1472,256]{1,0:T(8,128)(2,1)S(1)} %copy-done, bf16[288,256]{1,0:T(8,128)(2,1)S(1)} %side_b.1.own_ref), custom_call_target="tpu_custom_call" | custom-call | tf_op jit(solution)/shard_map/filter_own/pallas_call | solution.py:506
  10.7 2.3 %collective-permute-done.3.refs_0_ = bf16[288,256]{1,0:T(8,128)(2,1)S(1)} collective-permute-done((bf16[288,256]{1,0:T(8,128)(2,1)S(1)}, bf16[288,256]{1,0:T(8,128)(2,1)S(1)}, u32[]{:S(2)}, u32[]{:S(2)}) %collective-permute-start.3) | collective-permute-done | bytes 147488 | tf_op jit(solution)/shard_map/ppermute | solution.py:499
  13.0 2.4 %filter_other.1 = f32[3,2,1,64,256]{4,3,2,1,0:T(8,128)} custom-call(s32[3,2]{1,0:T(4,128)S(1)} %copy.7.match_ref, bf16[1472,256]{1,0:T(8,128)(2,1)S(1)} %copy-done, f32[2,64,256]{2,1,0:T(8,128)S(1)} %filter_own.1.filtered_own_ref, bf16[288,256]{1,0:T(8,128)(2,1)S(1)} %side_b.1.own_ref, bf16[288,256]{1,0:T(8,128)(2,1)S(1)} %collective-permute-done.3.refs_0_), custom_call_target="tpu_custom_call" | custom-call | tf_op jit(solution)/shard_map/filter_other/pallas_call | solution.py:515
Async XLA Ops:
  0.0 1.6 %collective-permute-start = (f32[2,1,64,256]{3,2,0,1:T(8,128)}, f32[2,1,64,256]{3,2,0,1:T(8,128)S(1)}, u32[]{:S(2)}, u32[]{:S(2)}) collective-permute-start(f32[2,1,64,256]{3,2,0,1:T(8,128)} %bitcast.8), channel_id=1, source_target_pairs={{0,1},{1,0},{2,3},{3,2},{4,5},{5,4},{6,7},{7,6},{8,9},{9,8},{10,11... | collective-permute-start | bytes 393224 | tf_op jit(solution)/shard_map/ppermute | solution.py:437
  1.8 5.2 %collective-permute-start.2 = (bf16[112,256]{1,0:T(8,128)(2,1)S(1)}, bf16[112,256]{1,0:T(8,128)(2,1)S(1)}, u32[]{:S(2)}, u32[]{:S(2)}) collective-permute-start(bf16[112,256]{1,0:T(8,128)(2,1)S(1)} %get-tuple-element.14), channel_id=1, source_target_pairs={{0,4},{1,5},{4,0},{5,1},{8,12},{9,13},{12,8},{13,9},{2,6},{3,7},{6... | collective-permute-start | bytes 172040 | tf_op jit(solution)/shard_map/ppermute | solution.py:472
  4.8 2.6 %collective-permute-start.1 = (bf16[112,256]{1,0:T(8,128)(2,1)S(1)}, bf16[112,256]{1,0:T(8,128)(2,1)S(1)}, u32[]{:S(2)}, u32[]{:S(2)}) collective-permute-start(bf16[112,256]{1,0:T(8,128)(2,1)S(1)} %get-tuple-element.13), channel_id=1, source_target_pairs={{0,1},{1,0},{4,8},{5,9},{8,4},{9,5},{12,13},{13,12},{2,3},{3,2},{6... | collective-permute-start | bytes 172040 | tf_op jit(solution)/shard_map/ppermute | solution.py:472
  5.1 4.5 %copy-start = (bf16[1472,256]{1,0:T(8,128)(2,1)S(1)}, bf16[1472,256]{1,0:T(8,128)(2,1)}, u32[]{:S(2)}) copy-start(bf16[1472,256]{1,0:T(8,128)(2,1)} %constant.2.clone.table_ref) | copy-start | bytes 2260996
  7.4 2.0 %copy-start.1 = (s32[3,2]{0,1:T(2,128)S(1)}, s32[3,2]{0,1:T(2,128)}, u32[]{:S(2)}) copy-start(s32[3,2]{0,1:T(2,128)} %param.8) | copy-start | bytes 76
  7.6 5.4 %collective-permute-start.3 = (bf16[288,256]{1,0:T(8,128)(2,1)S(1)}, bf16[288,256]{1,0:T(8,128)(2,1)S(1)}, u32[]{:S(2)}, u32[]{:S(2)}) collective-permute-start(bf16[288,256]{1,0:T(8,128)(2,1)S(1)} %side_b.1.own_ref), channel_id=1, source_target_pairs={{2,0},{0,2},{3,1},{1,3},{6,4},{4,6},{7,5},{5,7},{10,8},{8,10},{11,... | collective-permute-start | bytes 442376 | tf_op jit(solution)/shard_map/ppermute | solution.py:499

commit v17 on v16

--- a/solution.py
+++ b/solution.py
@@ -266,10 +266,15 @@
     return real, imag
 
 
-def interferogram(own_ref, other_ref, first, count):
+def both_halves(ref):
+    count = ref.shape[0] // 2
+    return [read_piece(ref, turn * count, count) for turn in range(2)]
+
+
+def interferogram(own, other):
     side = lax.axis_index("rg")
-    own_tile, own_edge = read_piece(own_ref, first, count)
-    other_tile, other_edge = read_piece(other_ref, first, count)
+    own_tile, own_edge = own
+    other_tile, other_edge = other
     mid = jnp.concatenate(cross(own_tile, other_tile), axis=0)
     rim = jnp.concatenate(cross(own_edge, other_edge), axis=0)
     before = jnp.where(side == 0, 0.0, rim)
@@ -279,9 +284,8 @@
     return jnp.concatenate([mid.astype(jnp.bfloat16), shifted], axis=1)
 
 
-def line_sum(tables, own_ref, other_ref):
-    count = own_ref.shape[0] // 2
-    both = [interferogram(own_ref, other_ref, turn * count, count) for turn in range(2)]
+def line_sum(tables, own, other):
+    both = [interferogram(*halves) for halves in zip(own, other)]
     weights = jnp.concatenate([tables.lines(turn) for turn in range(2)], axis=1)
     both = jnp.concatenate(both, axis=0)
     return jnp.dot(weights, both, preferred_element_type=jnp.float32)
@@ -348,15 +352,20 @@
         ref[part] = result[part * lines : (part + 1) * lines]
 
 
-def own_kernel(table_ref, own_ref, out_ref, spectrum_ref):
+def own_kernel(table_ref, own_ref, out_ref, tile_ref, edge_ref, spectrum_ref):
     _, lines, width = out_ref.shape
     row_patches = lines // HALF + 1
     tables = Tables(table_ref, row_patches)
-    total = line_sum(tables, own_ref, own_ref)
+    own = both_halves(own_ref)
+    for turn, (tile, edge) in enumerate(own):
+        for part in range(2):
+            tile_ref[turn, part] = tile[part]
+            edge_ref[turn, part] = edge[part]
+    total = line_sum(tables, own, own)
     keep(out_ref, filtered_of(total, tables, spectrum_ref, row_patches, width))
 
 
-def other_kernel(match_ref, table_ref, filtered_own_ref, own_ref, *refs):
+def other_kernel(match_ref, table_ref, filtered_own_ref, tile_ref, edge_ref, *refs):
     out_ref, result_ref, spectrum_ref, sems = refs[-4:]
     match_count, _, _, lines, width = out_ref.shape
     row_patches = lines // HALF + 1
@@ -376,8 +385,11 @@
                 copy_of(match, source_ref).start()
 
     send(0, filtered_own_ref)
+    own = [
+        [(ref[turn, 0], ref[turn, 1]) for ref in (tile_ref, edge_ref)] for turn in range(2)
+    ]
     for slot in range(1, dates):
-        total = line_sum(tables, own_ref, refs[slot - 1])
+        total = line_sum(tables, own, both_halves(refs[slot - 1]))
         result = filtered_of(total, tables, spectrum_ref, row_patches, width)
         keep(result_ref.at[slot - 1], result)
         send(slot, result_ref.at[slot - 1])
@@ -503,11 +515,16 @@
     chunks = (width + width + LANES) // LANES
     tables = jnp.asarray(all_tables(row_patches))
     spectrum = pltpu.VMEM((row_patches * chunks * PATCH, 2 * LANES), jnp.float32)
-    filtered_own = pl.pallas_call(
+    half = lines // 2 + HALF
+    filtered_own, *own_parts = pl.pallas_call(
         own_kernel,
-        out_shape=jax.ShapeDtypeStruct((2, lines, width), jnp.float32),
+        out_shape=(
+            jax.ShapeDtypeStruct((2, lines, width), jnp.float32),
+            jax.ShapeDtypeStruct((2, 2, half, width), jnp.float32),
+            jax.ShapeDtypeStruct((2, 2, half, HALF), jnp.float32),
+        ),
         in_specs=[VMEM] * 2,
-        out_specs=VMEM,
+        out_specs=(VMEM,) * 3,
         scratch_shapes=[spectrum],
         compiler_params=PARAMS,
         name="filter_own",
@@ -515,7 +532,7 @@
     return pl.pallas_call(
         other_kernel,
         out_shape=jax.ShapeDtypeStruct((match_count, 2, 1, lines, width), jnp.float32),
-        in_specs=[SMEM] + [VMEM] * (3 + len(others)),
+        in_specs=[SMEM] + [VMEM] * (4 + len(others)),
         out_specs=HBM,
         scratch_shapes=[
             pltpu.VMEM((dates - 1, 2, lines, width), jnp.float32),
@@ -524,7 +541,7 @@
         ],
         compiler_params=PARAMS,
         name="filter_other",
-    )(matchings, tables, filtered_own, own, *others)
+    )(matchings, tables, filtered_own, *own_parts, *others)
 
 
 def solution(mesh):

time: 15.7 us -> 15.6 us (level)
  transfers between devices with their start and end apart: 4 -> 4, of which waited for: 3 -> 3; matrix products, arithmetic and copies ran while one was open for 1% -> 1% of each run, Pallas kernels for 17% -> 18%
where the time goes in v17:
time: 15.6 us; the launch traced here: 15.3 us
  starting transfers between devices  5.35 us (34%)
  Pallas kernels  5.31 us (34%)
  waiting for transfers between devices  4.52 us (29%)
    ppermute x2, starting transfers between devices, swapped(): return lax.ppermute(value, ('az', 'rg'), pairs)  3 us
    pallas_call x1, Pallas kernels, per_device(): pl.pallas_call(other_kernel, out_shape=jax.ShapeDtypeStruct((match_count,...  2.35 us
    ppermute x1, waiting for transfers between devices, from_date(): lax.ppermute(piece, 'date', [((i + slot) % dates, i) for i in range(dates)])  2.32 us
    ppermute x2, waiting for transfers between devices, swapped(): return lax.ppermute(value, ('az', 'rg'), pairs)  1.94 us
    ppermute x1, starting transfers between devices, from_date(): lax.ppermute(piece, 'date', [((i + slot) % dates, i) for i in range(dates)])  1.9 us
    pallas_call x1, Pallas kernels, per_device(): pl.pallas_call(own_kernel, out_shape=(jax.ShapeDtypeStruct((2, lines, wid...  1.1 us
    pallas_call x1, Pallas kernels, per_device(): pl.pallas_call(load_kernel, out_shape=tuple((pltpu.VMEM(a.shape, a.dtype)...  0.93 us
    pallas_call x2, Pallas kernels, per_device(): pieces.append(call(*raw, messages[turn], inner, *pieces))  0.5 us
  transfers between devices with their start and end apart: 4, of which 3 were waited for; matrix products, arithmetic and copies ran while one was open for 1% of the time, Pallas kernels for 18%

profile of v17, /device:TPU:0, one launch (start us, length us, event | category | flops | bytes accessed | tf_op | source)
XLA Modules:
  0.0 15.3 jit_solution(4653990228243230743)
XLA Ops:
  0.0 0.5 %collective-permute-start = (f32[2,1,64,256]{3,2,0,1:T(8,128)}, f32[2,1,64,256]{3,2,0,1:T(8,128)S(1)}, u32[]{:S(2)}, u32[]{:S(2)}) collective-permute-start(f32[2,1,64,256]{3,2,0,1:T(8,128)} %bitcast.8), channel_id=1, source_target_pairs={{0,1},{1,0},{2,3},{3,2},{4,5},{5,4},{6,7},{7,6},{8,9},{9,8},{10,11... | collective-permute-start | bytes 393224 | tf_op jit(solution)/shard_map/ppermute | solution.py:449
  0.5 0.9 %load.1 = (f32[2,64,256]{2,1,0:T(8,128)S(1)}, f32[8,64]{1,0:T(8,128)S(1)}, s32[1,64]{1,0:T(1,128)S(1)}) custom-call(f32[2,64,256]{2,1,0:T(8,128)} %bitcast.9, f32[8,64]{1,0:T(8,128)} %bitcast.10, s32[1,64]{1,0:T(1,128)} %refs_2_.1), custom_call_target="tpu_custom_call" | custom-call | tf_op jit(solution)/shard_map/load/pallas_call | solution.py:455
  1.4 0.3 %collective-permute-done = f32[2,1,64,256]{3,2,0,1:T(8,128)S(1)} collective-permute-done((f32[2,1,64,256]{3,2,0,1:T(8,128)}, f32[2,1,64,256]{3,2,0,1:T(8,128)S(1)}, u32[]{:S(2)}, u32[]{:S(2)}) %collective-permute-start) | collective-permute-done | bytes 131104 | tf_op jit(solution)/shard_map/ppermute | solution.py:449
  1.7 0.2 %pack.1 = (bf16[112,256]{1,0:T(8,128)(2,1)S(1)}, bf16[112,256]{1,0:T(8,128)(2,1)S(1)}) custom-call(f32[2,64,256]{2,1,0:T(8,128)S(1)} %get-tuple-element.13.image_ref.refs_0_, f32[2,64,256]{2,1,0:T(8,128)S(1)} %bitcast.4, f32[8,64]{1,0:T(8,128)S(1)} %get-tuple-element.14.taps_ref.refs_2_, s32[1,64]{1,0:T(1,128)S(1)} %get-tuple-element.15.offsets_ref.refs_3_), custom_call_target="tpu_custom_call" | custom-call | tf_op jit(solution)/shard_map/pack/pallas_call | solution.py:466
  1.8 3.0 %collective-permute-start.2 = (bf16[112,256]{1,0:T(8,128)(2,1)S(1)}, bf16[112,256]{1,0:T(8,128)(2,1)S(1)}, u32[]{:S(2)}, u32[]{:S(2)}) collective-permute-start(bf16[112,256]{1,0:T(8,128)(2,1)S(1)} %get-tuple-element.17), channel_id=1, source_target_pairs={{0,4},{1,5},{4,0},{5,1},{8,12},{9,13},{12,8},{13,9},{2,6},{3,7},{6... | collective-permute-start | bytes 172040 | tf_op jit(solution)/shard_map/ppermute | solution.py:484
  4.8 0.0 collective-permute-start.1
  4.8 0.3 %inner.1.refs_5_ = f32[2,64,288]{2,1,0:T(8,128)S(1)} custom-call(f32[2,64,256]{2,1,0:T(8,128)S(1)} %get-tuple-element.13.image_ref.refs_0_, f32[2,64,256]{2,1,0:T(8,128)S(1)} %bitcast.5, f32[8,64]{1,0:T(8,128)S(1)} %get-tuple-element.14.taps_ref.refs_2_, s32[1,64]{1,0:T(1,128)S(1)} %get-tuple-element.15.offsets_ref.refs_3_), custom_call_target="tpu_custom_call" | custom-call | tf_op jit(solution)/shard_map/inner/pallas_call | solution.py:487
  5.1 0.0 copy-start
  5.1 1.9 %collective-permute-done.2.refs_4_ = bf16[112,256]{1,0:T(8,128)(2,1)S(1)} collective-permute-done((bf16[112,256]{1,0:T(8,128)(2,1)S(1)}, bf16[112,256]{1,0:T(8,128)(2,1)S(1)}, u32[]{:S(2)}, u32[]{:S(2)}) %collective-permute-start.2) | collective-permute-done | bytes 57376 | tf_op jit(solution)/shard_map/ppermute | solution.py:484
  7.0 0.4 %side_a.1.refs_6_ = bf16[144,256]{1,0:T(8,128)(2,1)S(1)} custom-call(f32[2,64,256]{2,1,0:T(8,128)S(1)} %get-tuple-element.13.image_ref.refs_0_, f32[2,64,256]{2,1,0:T(8,128)S(1)} %bitcast.6, f32[8,64]{1,0:T(8,128)S(1)} %get-tuple-element.14.taps_ref.refs_2_, s32[1,64]{1,0:T(1,128)S(1)} %get-tuple-element.15.offsets_ref.refs_3_, ...), custom_call_target="tpu_custom_call" | custom-call | tf_op jit(solution)/shard_map/side_a/pallas_call | solution.py:506
  7.4 0.0 copy-start.1
  7.4 0.0 collective-permute-done.1.refs_4_
  7.4 0.1 side_b.1.own_ref
  7.6 1.9 %collective-permute-start.3 = (bf16[288,256]{1,0:T(8,128)(2,1)S(1)}, bf16[288,256]{1,0:T(8,128)(2,1)S(1)}, u32[]{:S(2)}, u32[]{:S(2)}) collective-permute-start(bf16[288,256]{1,0:T(8,128)(2,1)S(1)} %side_b.1.own_ref), channel_id=1, source_target_pairs={{2,0},{0,2},{3,1},{1,3},{6,4},{4,6},{7,5},{5,7},{10,8},{8,10},{11,... | collective-permute-start | bytes 442376 | tf_op jit(solution)/shard_map/ppermute | solution.py:511
  9.5 0.0 copy-done.1
  9.5 0.1 copy.7.match_ref
  9.5 0.0 copy-done
  9.6 1.1 %filter_own.1 = (f32[2,64,256]{2,1,0:T(8,128)S(1)}, f32[2,2,64,256]{3,2,1,0:T(8,128)S(1)}, f32[2,2,64,32]{3,2,1,0:T(8,128)S(1)}) custom-call(bf16[1472,256]{1,0:T(8,128)(2,1)S(1)} %copy-done, bf16[288,256]{1,0:T(8,128)(2,1)S(1)} %side_b.1.own_ref), custom_call_target="tpu_custom_call" | custom-call | tf_op jit(solution)/shard_map/filter_own/pallas_call | solution.py:519
  10.7 2.3 %collective-permute-done.3.refs_0_ = bf16[288,256]{1,0:T(8,128)(2,1)S(1)} collective-permute-done((bf16[288,256]{1,0:T(8,128)(2,1)S(1)}, bf16[288,256]{1,0:T(8,128)(2,1)S(1)}, u32[]{:S(2)}, u32[]{:S(2)}) %collective-permute-start.3) | collective-permute-done | bytes 147488 | tf_op jit(solution)/shard_map/ppermute | solution.py:511
  13.0 2.4 %filter_other.1 = f32[3,2,1,64,256]{4,3,2,1,0:T(8,128)} custom-call(s32[3,2]{1,0:T(4,128)S(1)} %copy.7.match_ref, bf16[1472,256]{1,0:T(8,128)(2,1)S(1)} %copy-done, f32[2,64,256]{2,1,0:T(8,128)S(1)} %get-tuple-element.18.filtered_own_ref, f32[2,2,64,256]{3,2,1,0:T(8,128)S(1)} %get-tuple-element.19.tile_ref, f32[2,2,64,32]{3,2,1,0:T(8,128)S(1)} %get-tuple-element.20.edge_ref, ...), custom_call_target="tpu_custom_call" | custom-call | tf_op jit(solution)/shard_map/filter_other/pallas_call | solution.py:532
Async XLA Ops:
  0.0 1.6 %collective-permute-start = (f32[2,1,64,256]{3,2,0,1:T(8,128)}, f32[2,1,64,256]{3,2,0,1:T(8,128)S(1)}, u32[]{:S(2)}, u32[]{:S(2)}) collective-permute-start(f32[2,1,64,256]{3,2,0,1:T(8,128)} %bitcast.8), channel_id=1, source_target_pairs={{0,1},{1,0},{2,3},{3,2},{4,5},{5,4},{6,7},{7,6},{8,9},{9,8},{10,11... | collective-permute-start | bytes 393224 | tf_op jit(solution)/shard_map/ppermute | solution.py:449
  1.8 5.2 %collective-permute-start.2 = (bf16[112,256]{1,0:T(8,128)(2,1)S(1)}, bf16[112,256]{1,0:T(8,128)(2,1)S(1)}, u32[]{:S(2)}, u32[]{:S(2)}) collective-permute-start(bf16[112,256]{1,0:T(8,128)(2,1)S(1)} %get-tuple-element.17), channel_id=1, source_target_pairs={{0,4},{1,5},{4,0},{5,1},{8,12},{9,13},{12,8},{13,9},{2,6},{3,7},{6... | collective-permute-start | bytes 172040 | tf_op jit(solution)/shard_map/ppermute | solution.py:484
  4.8 2.6 %collective-permute-start.1 = (bf16[112,256]{1,0:T(8,128)(2,1)S(1)}, bf16[112,256]{1,0:T(8,128)(2,1)S(1)}, u32[]{:S(2)}, u32[]{:S(2)}) collective-permute-start(bf16[112,256]{1,0:T(8,128)(2,1)S(1)} %get-tuple-element.16), channel_id=1, source_target_pairs={{0,1},{1,0},{4,8},{5,9},{8,4},{9,5},{12,13},{13,12},{2,3},{3,2},{6... | collective-permute-start | bytes 172040 | tf_op jit(solution)/shard_map/ppermute | solution.py:484
  5.1 4.5 %copy-start = (bf16[1472,256]{1,0:T(8,128)(2,1)S(1)}, bf16[1472,256]{1,0:T(8,128)(2,1)}, u32[]{:S(2)}) copy-start(bf16[1472,256]{1,0:T(8,128)(2,1)} %constant.2.clone.table_ref) | copy-start | bytes 2260996
  7.4 2.0 %copy-start.1 = (s32[3,2]{0,1:T(2,128)S(1)}, s32[3,2]{0,1:T(2,128)}, u32[]{:S(2)}) copy-start(s32[3,2]{0,1:T(2,128)} %param.8) | copy-start | bytes 76
  7.6 5.4 %collective-permute-start.3 = (bf16[288,256]{1,0:T(8,128)(2,1)S(1)}, bf16[288,256]{1,0:T(8,128)(2,1)S(1)}, u32[]{:S(2)}, u32[]{:S(2)}) collective-permute-start(bf16[288,256]{1,0:T(8,128)(2,1)S(1)} %side_b.1.own_ref), channel_id=1, source_target_pairs={{2,0},{0,2},{3,1},{1,3},{6,4},{4,6},{7,5},{5,7},{10,8},{8,10},{11,... | collective-permute-start | bytes 442376 | tf_op jit(solution)/shard_map/ppermute | solution.py:511

commit v18 on v17

--- a/solution.py
+++ b/solution.py
@@ -291,7 +291,7 @@
     return jnp.dot(weights, both, preferred_element_type=jnp.float32)
 
 
-def filtered_of(line_spectra, tables, spectrum_ref, row_patches, width):
+def filtered_of(line_spectra, tables, spectrum_ref, row_patches, width, emit):
     line_spectra = line_spectra.astype(jnp.bfloat16)
     chunks = line_spectra.shape[1] // LANES
     forward, inverse, back, ring, window = tables.core()
@@ -327,7 +327,7 @@
         range_back = jnp.dot(shaped, inverse, preferred_element_type=jnp.float32)
         range_backs.append(range_back.astype(jnp.bfloat16))
     window = jnp.concatenate([window] * chunks, axis=1)
-    totals = [[None] * (row_patches - 1) for _ in range(2)]
+    earlier = None
     for row in range(row_patches):
         stacked = []
         for chunk in range(chunks):
@@ -335,21 +335,17 @@
             stacked.append(jnp.concatenate([block[:, :LANES], block[:, LANES:]], axis=0))
         stacked = jnp.concatenate(stacked, axis=1)
         patch_out = jnp.dot(back, stacked, preferred_element_type=jnp.float32) * window
-        for part in range(2):
-            upper = patch_out[part * PATCH : part * PATCH + HALF]
-            lower = patch_out[part * PATCH + HALF : (part + 1) * PATCH]
-            if row > 0:
-                totals[part][row - 1] = totals[part][row - 1] + upper
-            if row < row_patches - 1:
-                totals[part][row] = lower
-    total = jnp.concatenate([block for part in totals for block in part], axis=0)
-    return total[:, :width] + total[:, width + HALF : 2 * width + HALF]
-
-
-def keep(ref, result):
-    lines = ref.shape[1]
+        uppers = [patch_out[part * PATCH : part * PATCH + HALF] for part in range(2)]
+        if row > 0:
+            total = jnp.concatenate(uppers, axis=0) + earlier
+            emit(row - 1, total[:, :width] + total[:, width + HALF : 2 * width + HALF])
+        lowers = [patch_out[part * PATCH + HALF : (part + 1) * PATCH] for part in range(2)]
+        earlier = jnp.concatenate(lowers, axis=0)
+
+
+def keep(ref, row, total):
     for part in range(2):
-        ref[part] = result[part * lines : (part + 1) * lines]
+        ref[part, row * HALF : (row + 1) * HALF] = total[part * HALF : (part + 1) * HALF]
 
 
 def own_kernel(table_ref, own_ref, out_ref, tile_ref, edge_ref, spectrum_ref):
@@ -362,7 +358,8 @@
             tile_ref[turn, part] = tile[part]
             edge_ref[turn, part] = edge[part]
     total = line_sum(tables, own, own)
-    keep(out_ref, filtered_of(total, tables, spectrum_ref, row_patches, width))
+    emit = functools.partial(keep, out_ref)
+    filtered_of(total, tables, spectrum_ref, row_patches, width, emit)
 
 
 def other_kernel(match_ref, table_ref, filtered_own_ref, tile_ref, edge_ref, *refs):
@@ -373,28 +370,38 @@
     dates = match_ref.shape[1]
     tables = Tables(table_ref, row_patches)
 
-    def copy_of(match, source_ref):
-        return pltpu.make_async_copy(source_ref, out_ref.at[match, :, 0], sems.at[match])
-
-    def send(slot, source_ref):
+    rows = lines // HALF
+
+    def copy_of(match, row, source_ref):
+        cut = slice(row * HALF, (row + 1) * HALF)
+        target = out_ref.at[match, :, 0, cut]
+        return pltpu.make_async_copy(source_ref.at[:, cut], target, sems.at[match, row])
+
+    def send(slot, row, source_ref):
         for match in range(match_count):
             wanted = lax.rem(match_ref[match, date] - date + dates, dates)
 
             @pl.when(wanted == slot)
             def _():
-                copy_of(match, source_ref).start()
-
-    send(0, filtered_own_ref)
+                copy_of(match, row, source_ref).start()
+
+    for row in range(rows):
+        send(0, row, filtered_own_ref)
     own = [
         [(ref[turn, 0], ref[turn, 1]) for ref in (tile_ref, edge_ref)] for turn in range(2)
     ]
     for slot in range(1, dates):
         total = line_sum(tables, own, both_halves(refs[slot - 1]))
-        result = filtered_of(total, tables, spectrum_ref, row_patches, width)
-        keep(result_ref.at[slot - 1], result)
-        send(slot, result_ref.at[slot - 1])
+        target_ref = result_ref.at[slot - 1]
+
+        def emit(row, total):
+            keep(target_ref, row, total)
+            send(slot, row, target_ref)
+
+        filtered_of(total, tables, spectrum_ref, row_patches, width, emit)
     for match in range(match_count):
-        copy_of(match, filtered_own_ref).wait()
+        for row in range(rows):
+            copy_of(match, row, filtered_own_ref).wait()
 
 
 def all_tables(row_patches):
@@ -537,7 +544,7 @@
         scratch_shapes=[
             pltpu.VMEM((dates - 1, 2, lines, width), jnp.float32),
             spectrum,
-            pltpu.SemaphoreType.DMA((match_count,)),
+            pltpu.SemaphoreType.DMA((match_count, lines // HALF)),
         ],
         compiler_params=PARAMS,
         name="filter_other",

time: 15.6 us -> 15.6 us (level)
  no operation moved by 1% of the time
where the time goes in v18:
time: 15.6 us; the launch traced here: 15.3 us
  starting transfers between devices  5.35 us (34%)
  Pallas kernels  5.31 us (34%)
  waiting for transfers between devices  4.52 us (29%)
    ppermute x2, starting transfers between devices, swapped(): return lax.ppermute(value, ('az', 'rg'), pairs)  3 us
    pallas_call x1, Pallas kernels, per_device(): pl.pallas_call(other_kernel, out_shape=jax.ShapeDtypeStruct((match_count,...  2.35 us
    ppermute x1, waiting for transfers between devices, from_date(): lax.ppermute(piece, 'date', [((i + slot) % dates, i) for i in range(dates)])  2.32 us
    ppermute x2, waiting for transfers between devices, swapped(): return lax.ppermute(value, ('az', 'rg'), pairs)  1.94 us
    ppermute x1, starting transfers between devices, from_date(): lax.ppermute(piece, 'date', [((i + slot) % dates, i) for i in range(dates)])  1.9 us
    pallas_call x1, Pallas kernels, per_device(): pl.pallas_call(own_kernel, out_shape=(jax.ShapeDtypeStruct((2, lines, wid...  1.1 us
    pallas_call x1, Pallas kernels, per_device(): pl.pallas_call(load_kernel, out_shape=tuple((pltpu.VMEM(a.shape, a.dtype)...  0.93 us
    pallas_call x2, Pallas kernels, per_device(): pieces.append(call(*raw, messages[turn], inner, *pieces))  0.5 us
  transfers between devices with their start and end apart: 4, of which 3 were waited for; matrix products, arithmetic and copies ran while one was open for 1% of the time, Pallas kernels for 18%

profile of v18, /device:TPU:0, one launch (start us, length us, event | category | flops | bytes accessed | tf_op | source)
XLA Modules:
  0.0 15.3 jit_solution(2372918214812083346)
XLA Ops:
  0.0 0.5 %collective-permute-start = (f32[2,1,64,256]{3,2,0,1:T(8,128)}, f32[2,1,64,256]{3,2,0,1:T(8,128)S(1)}, u32[]{:S(2)}, u32[]{:S(2)}) collective-permute-start(f32[2,1,64,256]{3,2,0,1:T(8,128)} %bitcast.8), channel_id=1, source_target_pairs={{0,1},{1,0},{2,3},{3,2},{4,5},{5,4},{6,7},{7,6},{8,9},{9,8},{10,11... | collective-permute-start | bytes 393224 | tf_op jit(solution)/shard_map/ppermute | solution.py:456
  0.5 0.9 %load.1 = (f32[2,64,256]{2,1,0:T(8,128)S(1)}, f32[8,64]{1,0:T(8,128)S(1)}, s32[1,64]{1,0:T(1,128)S(1)}) custom-call(f32[2,64,256]{2,1,0:T(8,128)} %bitcast.9, f32[8,64]{1,0:T(8,128)} %bitcast.10, s32[1,64]{1,0:T(1,128)} %refs_2_.1), custom_call_target="tpu_custom_call" | custom-call | tf_op jit(solution)/shard_map/load/pallas_call | solution.py:462
  1.4 0.3 %collective-permute-done = f32[2,1,64,256]{3,2,0,1:T(8,128)S(1)} collective-permute-done((f32[2,1,64,256]{3,2,0,1:T(8,128)}, f32[2,1,64,256]{3,2,0,1:T(8,128)S(1)}, u32[]{:S(2)}, u32[]{:S(2)}) %collective-permute-start) | collective-permute-done | bytes 131104 | tf_op jit(solution)/shard_map/ppermute | solution.py:456
  1.7 0.2 %pack.1 = (bf16[112,256]{1,0:T(8,128)(2,1)S(1)}, bf16[112,256]{1,0:T(8,128)(2,1)S(1)}) custom-call(f32[2,64,256]{2,1,0:T(8,128)S(1)} %get-tuple-element.13.image_ref.refs_0_, f32[2,64,256]{2,1,0:T(8,128)S(1)} %bitcast.4, f32[8,64]{1,0:T(8,128)S(1)} %get-tuple-element.14.taps_ref.refs_2_, s32[1,64]{1,0:T(1,128)S(1)} %get-tuple-element.15.offsets_ref.refs_3_), custom_call_target="tpu_custom_call" | custom-call | tf_op jit(solution)/shard_map/pack/pallas_call | solution.py:473
  1.8 3.0 %collective-permute-start.2 = (bf16[112,256]{1,0:T(8,128)(2,1)S(1)}, bf16[112,256]{1,0:T(8,128)(2,1)S(1)}, u32[]{:S(2)}, u32[]{:S(2)}) collective-permute-start(bf16[112,256]{1,0:T(8,128)(2,1)S(1)} %get-tuple-element.17), channel_id=1, source_target_pairs={{0,4},{1,5},{4,0},{5,1},{8,12},{9,13},{12,8},{13,9},{2,6},{3,7},{6... | collective-permute-start | bytes 172040 | tf_op jit(solution)/shard_map/ppermute | solution.py:491
  4.8 0.0 collective-permute-start.1
  4.8 0.3 %inner.1.refs_5_ = f32[2,64,288]{2,1,0:T(8,128)S(1)} custom-call(f32[2,64,256]{2,1,0:T(8,128)S(1)} %get-tuple-element.13.image_ref.refs_0_, f32[2,64,256]{2,1,0:T(8,128)S(1)} %bitcast.5, f32[8,64]{1,0:T(8,128)S(1)} %get-tuple-element.14.taps_ref.refs_2_, s32[1,64]{1,0:T(1,128)S(1)} %get-tuple-element.15.offsets_ref.refs_3_), custom_call_target="tpu_custom_call" | custom-call | tf_op jit(solution)/shard_map/inner/pallas_call | solution.py:494
  5.1 0.0 copy-start
  5.1 1.9 %collective-permute-done.2.refs_4_ = bf16[112,256]{1,0:T(8,128)(2,1)S(1)} collective-permute-done((bf16[112,256]{1,0:T(8,128)(2,1)S(1)}, bf16[112,256]{1,0:T(8,128)(2,1)S(1)}, u32[]{:S(2)}, u32[]{:S(2)}) %collective-permute-start.2) | collective-permute-done | bytes 57376 | tf_op jit(solution)/shard_map/ppermute | solution.py:491
  7.0 0.4 %side_a.1.refs_6_ = bf16[144,256]{1,0:T(8,128)(2,1)S(1)} custom-call(f32[2,64,256]{2,1,0:T(8,128)S(1)} %get-tuple-element.13.image_ref.refs_0_, f32[2,64,256]{2,1,0:T(8,128)S(1)} %bitcast.6, f32[8,64]{1,0:T(8,128)S(1)} %get-tuple-element.14.taps_ref.refs_2_, s32[1,64]{1,0:T(1,128)S(1)} %get-tuple-element.15.offsets_ref.refs_3_, ...), custom_call_target="tpu_custom_call" | custom-call | tf_op jit(solution)/shard_map/side_a/pallas_call | solution.py:513
  7.4 0.0 copy-start.1
  7.4 0.0 collective-permute-done.1.refs_4_
  7.4 0.1 side_b.1.own_ref
  7.6 1.9 %collective-permute-start.3 = (bf16[288,256]{1,0:T(8,128)(2,1)S(1)}, bf16[288,256]{1,0:T(8,128)(2,1)S(1)}, u32[]{:S(2)}, u32[]{:S(2)}) collective-permute-start(bf16[288,256]{1,0:T(8,128)(2,1)S(1)} %side_b.1.own_ref), channel_id=1, source_target_pairs={{2,0},{0,2},{3,1},{1,3},{6,4},{4,6},{7,5},{5,7},{10,8},{8,10},{11,... | collective-permute-start | bytes 442376 | tf_op jit(solution)/shard_map/ppermute | solution.py:518
  9.5 0.0 copy-done.1
  9.5 0.1 copy.7.match_ref
  9.5 0.0 copy-done
  9.6 1.1 %filter_own.1 = (f32[2,64,256]{2,1,0:T(8,128)S(1)}, f32[2,2,64,256]{3,2,1,0:T(8,128)S(1)}, f32[2,2,64,32]{3,2,1,0:T(8,128)S(1)}) custom-call(bf16[1472,256]{1,0:T(8,128)(2,1)S(1)} %copy-done, bf16[288,256]{1,0:T(8,128)(2,1)S(1)} %side_b.1.own_ref), custom_call_target="tpu_custom_call" | custom-call | tf_op jit(solution)/shard_map/filter_own/pallas_call | solution.py:526
  10.7 2.3 %collective-permute-done.3.refs_0_ = bf16[288,256]{1,0:T(8,128)(2,1)S(1)} collective-permute-done((bf16[288,256]{1,0:T(8,128)(2,1)S(1)}, bf16[288,256]{1,0:T(8,128)(2,1)S(1)}, u32[]{:S(2)}, u32[]{:S(2)}) %collective-permute-start.3) | collective-permute-done | bytes 147488 | tf_op jit(solution)/shard_map/ppermute | solution.py:518
  13.0 2.4 %filter_other.1 = f32[3,2,1,64,256]{4,3,2,1,0:T(8,128)} custom-call(s32[3,2]{1,0:T(4,128)S(1)} %copy.7.match_ref, bf16[1472,256]{1,0:T(8,128)(2,1)S(1)} %copy-done, f32[2,64,256]{2,1,0:T(8,128)S(1)} %get-tuple-element.18.filtered_own_ref, f32[2,2,64,256]{3,2,1,0:T(8,128)S(1)} %get-tuple-element.19.tile_ref, f32[2,2,64,32]{3,2,1,0:T(8,128)S(1)} %get-tuple-element.20.edge_ref, ...), custom_call_target="tpu_custom_call" | custom-call | tf_op jit(solution)/shard_map/filter_other/pallas_call | solution.py:539
Async XLA Ops:
  0.0 1.6 %collective-permute-start = (f32[2,1,64,256]{3,2,0,1:T(8,128)}, f32[2,1,64,256]{3,2,0,1:T(8,128)S(1)}, u32[]{:S(2)}, u32[]{:S(2)}) collective-permute-start(f32[2,1,64,256]{3,2,0,1:T(8,128)} %bitcast.8), channel_id=1, source_target_pairs={{0,1},{1,0},{2,3},{3,2},{4,5},{5,4},{6,7},{7,6},{8,9},{9,8},{10,11... | collective-permute-start | bytes 393224 | tf_op jit(solution)/shard_map/ppermute | solution.py:456
  1.8 5.2 %collective-permute-start.2 = (bf16[112,256]{1,0:T(8,128)(2,1)S(1)}, bf16[112,256]{1,0:T(8,128)(2,1)S(1)}, u32[]{:S(2)}, u32[]{:S(2)}) collective-permute-start(bf16[112,256]{1,0:T(8,128)(2,1)S(1)} %get-tuple-element.17), channel_id=1, source_target_pairs={{0,4},{1,5},{4,0},{5,1},{8,12},{9,13},{12,8},{13,9},{2,6},{3,7},{6... | collective-permute-start | bytes 172040 | tf_op jit(solution)/shard_map/ppermute | solution.py:491
  4.8 2.6 %collective-permute-start.1 = (bf16[112,256]{1,0:T(8,128)(2,1)S(1)}, bf16[112,256]{1,0:T(8,128)(2,1)S(1)}, u32[]{:S(2)}, u32[]{:S(2)}) collective-permute-start(bf16[112,256]{1,0:T(8,128)(2,1)S(1)} %get-tuple-element.16), channel_id=1, source_target_pairs={{0,1},{1,0},{4,8},{5,9},{8,4},{9,5},{12,13},{13,12},{2,3},{3,2},{6... | collective-permute-start | bytes 172040 | tf_op jit(solution)/shard_map/ppermute | solution.py:491
  5.1 4.5 %copy-start = (bf16[1472,256]{1,0:T(8,128)(2,1)S(1)}, bf16[1472,256]{1,0:T(8,128)(2,1)}, u32[]{:S(2)}) copy-start(bf16[1472,256]{1,0:T(8,128)(2,1)} %constant.2.clone.table_ref) | copy-start | bytes 2260996
  7.4 2.0 %copy-start.1 = (s32[3,2]{0,1:T(2,128)S(1)}, s32[3,2]{0,1:T(2,128)}, u32[]{:S(2)}) copy-start(s32[3,2]{0,1:T(2,128)} %param.8) | copy-start | bytes 76
  7.6 5.4 %collective-permute-start.3 = (bf16[288,256]{1,0:T(8,128)(2,1)S(1)}, bf16[288,256]{1,0:T(8,128)(2,1)S(1)}, u32[]{:S(2)}, u32[]{:S(2)}) collective-permute-start(bf16[288,256]{1,0:T(8,128)(2,1)S(1)} %side_b.1.own_ref), channel_id=1, source_target_pairs={{2,0},{0,2},{3,1},{1,3},{6,4},{4,6},{7,5},{5,7},{10,8},{8,10},{11,... | collective-permute-start | bytes 442376 | tf_op jit(solution)/shard_map/ppermute | solution.py:518

commit v19 on v18

--- a/solution.py
+++ b/solution.py
@@ -307,40 +307,40 @@
             pieces.append(jnp.concatenate([real, imag], axis=1))
         patches = jnp.concatenate(pieces, axis=0)
         spectrum_ref[span, :] = jnp.dot(patches, forward, preferred_element_type=jnp.float32)
-    smooths = []
-    for span in spans:
-        powers = []
-        for start in range(span.start, span.stop, PATCH):
-            real = spectrum_ref[start : start + PATCH, :LANES]
-            imag = spectrum_ref[start : start + PATCH, LANES:]
-            power = real * real + imag * imag
-            power = power + pltpu.roll(power, 1, 0) + pltpu.roll(power, PATCH - 1, 0)
-            powers.append(power.astype(jnp.bfloat16))
-        powers = jnp.concatenate(powers, axis=0)
-        smooths.append(jnp.dot(powers, ring, preferred_element_type=jnp.float32))
-    range_backs = []
-    for span, smooth in zip(spans, smooths):
-        gain = lax.rsqrt(lax.rsqrt(smooth * (1.0 / (9.0 * PATCH * PATCH)) + 1.0))
-        shaped = jnp.concatenate(
-            [spectrum_ref[span, :LANES] * gain, spectrum_ref[span, LANES:] * gain], axis=1
-        ).astype(jnp.bfloat16)
-        range_back = jnp.dot(shaped, inverse, preferred_element_type=jnp.float32)
-        range_backs.append(range_back.astype(jnp.bfloat16))
     window = jnp.concatenate([window] * chunks, axis=1)
-    earlier = None
-    for row in range(row_patches):
-        stacked = []
-        for chunk in range(chunks):
-            block = range_backs[row][chunk * PATCH : (chunk + 1) * PATCH]
-            stacked.append(jnp.concatenate([block[:, :LANES], block[:, LANES:]], axis=0))
-        stacked = jnp.concatenate(stacked, axis=1)
-        patch_out = jnp.dot(back, stacked, preferred_element_type=jnp.float32) * window
-        uppers = [patch_out[part * PATCH : part * PATCH + HALF] for part in range(2)]
-        if row > 0:
-            total = jnp.concatenate(uppers, axis=0) + earlier
-            emit(row - 1, total[:, :width] + total[:, width + HALF : 2 * width + HALF])
-        lowers = [patch_out[part * PATCH + HALF : (part + 1) * PATCH] for part in range(2)]
-        earlier = jnp.concatenate(lowers, axis=0)
+    earlier, range_backs = None, []
+    for group in (spans[:-1], spans[-1:]):
+        smooths = []
+        for span in group:
+            powers = []
+            for start in range(span.start, span.stop, PATCH):
+                real = spectrum_ref[start : start + PATCH, :LANES]
+                imag = spectrum_ref[start : start + PATCH, LANES:]
+                power = real * real + imag * imag
+                power = power + pltpu.roll(power, 1, 0) + pltpu.roll(power, PATCH - 1, 0)
+                powers.append(power.astype(jnp.bfloat16))
+            powers = jnp.concatenate(powers, axis=0)
+            smooths.append(jnp.dot(powers, ring, preferred_element_type=jnp.float32))
+        for span, smooth in zip(group, smooths):
+            gain = lax.rsqrt(lax.rsqrt(smooth * (1.0 / (9.0 * PATCH * PATCH)) + 1.0))
+            shaped = jnp.concatenate(
+                [spectrum_ref[span, :LANES] * gain, spectrum_ref[span, LANES:] * gain], axis=1
+            ).astype(jnp.bfloat16)
+            range_back = jnp.dot(shaped, inverse, preferred_element_type=jnp.float32)
+            range_backs.append(range_back.astype(jnp.bfloat16))
+        for row in range(len(range_backs) - len(group), len(range_backs)):
+            stacked = []
+            for chunk in range(chunks):
+                block = range_backs[row][chunk * PATCH : (chunk + 1) * PATCH]
+                stacked.append(jnp.concatenate([block[:, :LANES], block[:, LANES:]], axis=0))
+            stacked = jnp.concatenate(stacked, axis=1)
+            patch_out = jnp.dot(back, stacked, preferred_element_type=jnp.float32) * window
+            uppers = [patch_out[part * PATCH : part * PATCH + HALF] for part in range(2)]
+            if row > 0:
+                total = jnp.concatenate(uppers, axis=0) + earlier
+                emit(row - 1, total[:, :width] + total[:, width + HALF : 2 * width + HALF])
+            lowers = [patch_out[part * PATCH + HALF : (part + 1) * PATCH] for part in range(2)]
+            earlier = jnp.concatenate(lowers, axis=0)
 
 
 def keep(ref, row, total):

time: 15.6 us -> 15.9 us (1.019)
  the two profiles are of different devices: /device:TPU:0 before, /device:TPU:18 now
where the time goes in v19:
time: 15.9 us; the launch traced here: 15.6 us
  waiting for transfers between devices  7.2 us (45%)
  Pallas kernels  6.08 us (38%)
  starting transfers between devices  2.21 us (14%)
    ppermute x2, waiting for transfers between devices, swapped(): return lax.ppermute(value, ('az', 'rg'), pairs)  3.5 us
    ppermute x1, waiting for transfers between devices, from_date(): lax.ppermute(piece, 'date', [((i + slot) % dates, i) for i in range(dates)])  3.08 us
    pallas_call x1, Pallas kernels, per_device(): pl.pallas_call(other_kernel, out_shape=jax.ShapeDtypeStruct((match_count,...  2.51 us
    ppermute x2, starting transfers between devices, swapped(): return lax.ppermute(value, ('az', 'rg'), pairs)  1.64 us
    pallas_call x1, Pallas kernels, per_device(): pl.pallas_call(own_kernel, out_shape=(jax.ShapeDtypeStruct((2, lines, wid...  1.42 us
    pallas_call x1, Pallas kernels, per_device(): pl.pallas_call(load_kernel, out_shape=tuple((pltpu.VMEM(a.shape, a.dtype)...  0.93 us
    pallas_call x2, Pallas kernels, per_device(): pieces.append(call(*raw, messages[turn], inner, *pieces))  0.79 us
    ppermute x1, waiting for transfers between devices, per_device(): lax.ppermute(image_stack, 'rg', [(0, 1), (1, 0)]).reshape(2, lines, width)  0.61 us
  transfers between devices with their start and end apart: 4, of which 4 were waited for; matrix products, arithmetic and copies ran while one was open for 1% of the time, Pallas kernels for 19%

profile of v19, /device:TPU:18, one launch (start us, length us, event | category | flops | bytes accessed | tf_op | source)
XLA Modules:
  0.0 15.6 jit_solution(16758552355761544589)
XLA Ops:
  0.0 0.0 collective-permute-start
  0.0 0.9 %load.1 = (f32[2,64,256]{2,1,0:T(8,128)S(1)}, f32[8,64]{1,0:T(8,128)S(1)}, s32[1,64]{1,0:T(1,128)S(1)}) custom-call(f32[2,64,256]{2,1,0:T(8,128)} %bitcast.9, f32[8,64]{1,0:T(8,128)} %bitcast.10, s32[1,64]{1,0:T(1,128)} %refs_2_.1), custom_call_target="tpu_custom_call" | custom-call | tf_op jit(solution)/shard_map/load/pallas_call | solution.py:462
  0.9 0.6 %collective-permute-done = f32[2,1,64,256]{3,2,0,1:T(8,128)S(1)} collective-permute-done((f32[2,1,64,256]{3,2,0,1:T(8,128)}, f32[2,1,64,256]{3,2,0,1:T(8,128)S(1)}, u32[]{:S(2)}, u32[]{:S(2)}) %collective-permute-start) | collective-permute-done | bytes 131104 | tf_op jit(solution)/shard_map/ppermute | solution.py:456
  1.6 0.2 %pack.1 = (bf16[112,256]{1,0:T(8,128)(2,1)S(1)}, bf16[112,256]{1,0:T(8,128)(2,1)S(1)}) custom-call(f32[2,64,256]{2,1,0:T(8,128)S(1)} %get-tuple-element.13.image_ref.refs_0_, f32[2,64,256]{2,1,0:T(8,128)S(1)} %bitcast.4, f32[8,64]{1,0:T(8,128)S(1)} %get-tuple-element.14.taps_ref.refs_2_, s32[1,64]{1,0:T(1,128)S(1)} %get-tuple-element.15.offsets_ref.refs_3_), custom_call_target="tpu_custom_call" | custom-call | tf_op jit(solution)/shard_map/pack/pallas_call | solution.py:473
  1.7 1.6 %collective-permute-start.2 = (bf16[112,256]{1,0:T(8,128)(2,1)S(1)}, bf16[112,256]{1,0:T(8,128)(2,1)S(1)}, u32[]{:S(2)}, u32[]{:S(2)}) collective-permute-start(bf16[112,256]{1,0:T(8,128)(2,1)S(1)} %get-tuple-element.17), channel_id=1, source_target_pairs={{0,4},{1,5},{4,0},{5,1},{8,12},{9,13},{12,8},{13,9},{2,6},{3,7},{6... | collective-permute-start | bytes 172040 | tf_op jit(solution)/shard_map/ppermute | solution.py:491
  3.4 0.0 collective-permute-start.1
  3.4 0.3 %inner.1.refs_5_ = f32[2,64,288]{2,1,0:T(8,128)S(1)} custom-call(f32[2,64,256]{2,1,0:T(8,128)S(1)} %get-tuple-element.13.image_ref.refs_0_, f32[2,64,256]{2,1,0:T(8,128)S(1)} %bitcast.5, f32[8,64]{1,0:T(8,128)S(1)} %get-tuple-element.14.taps_ref.refs_2_, s32[1,64]{1,0:T(1,128)S(1)} %get-tuple-element.15.offsets_ref.refs_3_), custom_call_target="tpu_custom_call" | custom-call | tf_op jit(solution)/shard_map/inner/pallas_call | solution.py:494
  3.6 0.0 copy-start
  3.7 2.3 %collective-permute-done.2.refs_4_ = bf16[112,256]{1,0:T(8,128)(2,1)S(1)} collective-permute-done((bf16[112,256]{1,0:T(8,128)(2,1)S(1)}, bf16[112,256]{1,0:T(8,128)(2,1)S(1)}, u32[]{:S(2)}, u32[]{:S(2)}) %collective-permute-start.2) | collective-permute-done | bytes 57376 | tf_op jit(solution)/shard_map/ppermute | solution.py:491
  6.0 0.4 %side_a.1.refs_6_ = bf16[144,256]{1,0:T(8,128)(2,1)S(1)} custom-call(f32[2,64,256]{2,1,0:T(8,128)S(1)} %get-tuple-element.13.image_ref.refs_0_, f32[2,64,256]{2,1,0:T(8,128)S(1)} %bitcast.6, f32[8,64]{1,0:T(8,128)S(1)} %get-tuple-element.14.taps_ref.refs_2_, s32[1,64]{1,0:T(1,128)S(1)} %get-tuple-element.15.offsets_ref.refs_3_, ...), custom_call_target="tpu_custom_call" | custom-call | tf_op jit(solution)/shard_map/side_a/pallas_call | solution.py:513
  6.4 0.0 copy-start.1
  6.4 1.2 %collective-permute-done.1.refs_4_ = bf16[112,256]{1,0:T(8,128)(2,1)S(1)} collective-permute-done((bf16[112,256]{1,0:T(8,128)(2,1)S(1)}, bf16[112,256]{1,0:T(8,128)(2,1)S(1)}, u32[]{:S(2)}, u32[]{:S(2)}) %collective-permute-start.1) | collective-permute-done | bytes 57376 | tf_op jit(solution)/shard_map/ppermute | solution.py:491
  7.5 0.4 %side_b.1.own_ref = bf16[288,256]{1,0:T(8,128)(2,1)S(1)} custom-call(f32[2,64,256]{2,1,0:T(8,128)S(1)} %get-tuple-element.13.image_ref.refs_0_, f32[2,64,256]{2,1,0:T(8,128)S(1)} %bitcast.7, f32[8,64]{1,0:T(8,128)S(1)} %get-tuple-element.14.taps_ref.refs_2_, s32[1,64]{1,0:T(1,128)S(1)} %get-tuple-element.15.offsets_ref.refs_3_, ...), custom_call_target="tpu_custom_call" | custom-call | tf_op jit(solution)/shard_map/side_b/pallas_call | solution.py:513
  7.9 0.6 %collective-permute-start.3 = (bf16[288,256]{1,0:T(8,128)(2,1)S(1)}, bf16[288,256]{1,0:T(8,128)(2,1)S(1)}, u32[]{:S(2)}, u32[]{:S(2)}) collective-permute-start(bf16[288,256]{1,0:T(8,128)(2,1)S(1)} %side_b.1.own_ref), channel_id=1, source_target_pairs={{2,0},{0,2},{3,1},{1,3},{6,4},{4,6},{7,5},{5,7},{10,8},{8,10},{11,... | collective-permute-start | bytes 442376 | tf_op jit(solution)/shard_map/ppermute | solution.py:518
  8.5 0.0 copy-done.1
  8.5 0.1 copy.7.match_ref
  8.6 0.0 copy-done
  8.6 1.4 %filter_own.1 = (f32[2,64,256]{2,1,0:T(8,128)S(1)}, f32[2,2,64,256]{3,2,1,0:T(8,128)S(1)}, f32[2,2,64,32]{3,2,1,0:T(8,128)S(1)}) custom-call(bf16[1472,256]{1,0:T(8,128)(2,1)S(1)} %copy-done, bf16[288,256]{1,0:T(8,128)(2,1)S(1)} %side_b.1.own_ref), custom_call_target="tpu_custom_call" | custom-call | tf_op jit(solution)/shard_map/filter_own/pallas_call | solution.py:526
  10.0 3.1 %collective-permute-done.3.refs_0_ = bf16[288,256]{1,0:T(8,128)(2,1)S(1)} collective-permute-done((bf16[288,256]{1,0:T(8,128)(2,1)S(1)}, bf16[288,256]{1,0:T(8,128)(2,1)S(1)}, u32[]{:S(2)}, u32[]{:S(2)}) %collective-permute-start.3) | collective-permute-done | bytes 147488 | tf_op jit(solution)/shard_map/ppermute | solution.py:518
  13.1 2.5 %filter_other.1 = f32[3,2,1,64,256]{4,3,2,1,0:T(8,128)} custom-call(s32[3,2]{1,0:T(4,128)S(1)} %copy.7.match_ref, bf16[1472,256]{1,0:T(8,128)(2,1)S(1)} %copy-done, f32[2,64,256]{2,1,0:T(8,128)S(1)} %get-tuple-element.18.filtered_own_ref, f32[2,2,64,256]{3,2,1,0:T(8,128)S(1)} %get-tuple-element.19.tile_ref, f32[2,2,64,32]{3,2,1,0:T(8,128)S(1)} %get-tuple-element.20.edge_ref, ...), custom_call_target="tpu_custom_call" | custom-call | tf_op jit(solution)/shard_map/filter_other/pallas_call | solution.py:539
Async XLA Ops:
  0.0 1.6 %collective-permute-start = (f32[2,1,64,256]{3,2,0,1:T(8,128)}, f32[2,1,64,256]{3,2,0,1:T(8,128)S(1)}, u32[]{:S(2)}, u32[]{:S(2)}) collective-permute-start(f32[2,1,64,256]{3,2,0,1:T(8,128)} %bitcast.8), channel_id=1, source_target_pairs={{0,1},{1,0},{2,3},{3,2},{4,5},{5,4},{6,7},{7,6},{8,9},{9,8},{10,11... | collective-permute-start | bytes 393224 | tf_op jit(solution)/shard_map/ppermute | solution.py:456
  1.7 4.2 %collective-permute-start.2 = (bf16[112,256]{1,0:T(8,128)(2,1)S(1)}, bf16[112,256]{1,0:T(8,128)(2,1)S(1)}, u32[]{:S(2)}, u32[]{:S(2)}) collective-permute-start(bf16[112,256]{1,0:T(8,128)(2,1)S(1)} %get-tuple-element.17), channel_id=1, source_target_pairs={{0,4},{1,5},{4,0},{5,1},{8,12},{9,13},{12,8},{13,9},{2,6},{3,7},{6... | collective-permute-start | bytes 172040 | tf_op jit(solution)/shard_map/ppermute | solution.py:491
  3.4 4.2 %collective-permute-start.1 = (bf16[112,256]{1,0:T(8,128)(2,1)S(1)}, bf16[112,256]{1,0:T(8,128)(2,1)S(1)}, u32[]{:S(2)}, u32[]{:S(2)}) collective-permute-start(bf16[112,256]{1,0:T(8,128)(2,1)S(1)} %get-tuple-element.16), channel_id=1, source_target_pairs={{0,1},{1,0},{4,8},{5,9},{8,4},{9,5},{12,13},{13,12},{2,3},{3,2},{6... | collective-permute-start | bytes 172040 | tf_op jit(solution)/shard_map/ppermute | solution.py:491
  3.6 5.0 %copy-start = (bf16[1472,256]{1,0:T(8,128)(2,1)S(1)}, bf16[1472,256]{1,0:T(8,128)(2,1)}, u32[]{:S(2)}) copy-start(bf16[1472,256]{1,0:T(8,128)(2,1)} %constant.2.clone.table_ref) | copy-start | bytes 2260996
  6.4 2.1 %copy-start.1 = (s32[3,2]{0,1:T(2,128)S(1)}, s32[3,2]{0,1:T(2,128)}, u32[]{:S(2)}) copy-start(s32[3,2]{0,1:T(2,128)} %param.8) | copy-start | bytes 76
  7.9 5.2 %collective-permute-start.3 = (bf16[288,256]{1,0:T(8,128)(2,1)S(1)}, bf16[288,256]{1,0:T(8,128)(2,1)S(1)}, u32[]{:S(2)}, u32[]{:S(2)}) collective-permute-start(bf16[288,256]{1,0:T(8,128)(2,1)S(1)} %side_b.1.own_ref), channel_id=1, source_target_pairs={{2,0},{0,2},{3,1},{1,3},{6,4},{4,6},{7,5},{5,7},{10,8},{8,10},{11,... | collective-permute-start | bytes 442376 | tf_op jit(solution)/shard_map/ppermute | solution.py:518

commit v20 on v18

--- a/solution.py
+++ b/solution.py
@@ -94,7 +94,7 @@
         copy.wait()
 
 
-def pack_kernel(image_ref, other_ref, taps_ref, offsets_ref, even_ref, odd_ref):
+def pack_kernel(turn, image_ref, other_ref, taps_ref, offsets_ref, out_ref):
     lines = image_ref.shape[1]
     side = lax.axis_index("rg")
     taps = taps_ref[...]
@@ -112,17 +112,15 @@
         block = side_by_side([*edges, taps[:, cut], shifts[:, cut]])
         out_ref[2 * REACH :, :] = block.astype(jnp.bfloat16)
 
-    parity = lax.rem(lax.axis_index("az"), 2)
-
-    @pl.when(parity == 0)
+    above = is_above(turn)
+
+    @pl.when(above)
     def _():
-        write(even_ref, lines - REACH, lines - HALF)
-        write(odd_ref, 0, 0)
-
-    @pl.when(parity == 1)
+        write(out_ref, 0, 0)
+
+    @pl.when(jnp.logical_not(above))
     def _():
-        write(even_ref, 0, 0)
-        write(odd_ref, lines - REACH, lines - HALF)
+        write(out_ref, lines - REACH, lines - HALF)
 
 
 def is_above(turn):
@@ -470,14 +468,17 @@
     )(*(pltpu.with_memory_space_constraint(a, pltpu.HBM) for a in arguments))
     raw = (raw[0], other, *raw[1:])
     message = jax.ShapeDtypeStruct((2 * REACH + STEP, width), jnp.bfloat16)
-    messages = pl.pallas_call(
-        pack_kernel,
-        out_shape=(message, message),
-        in_specs=[VMEM] * 4,
-        out_specs=(VMEM, VMEM),
-        compiler_params=PARAMS,
-        name="pack",
-    )(*raw)
+    messages = [
+        pl.pallas_call(
+            functools.partial(pack_kernel, turn),
+            out_shape=message,
+            in_specs=[VMEM] * 4,
+            out_specs=VMEM,
+            compiler_params=PARAMS,
+            name="pack_" + "ab"[turn],
+        )(*raw)
+        for turn in range(2)
+    ]
     peers = lax.axis_size("az")
 
     def swapped(value, start):

time: 15.6 us -> 15.8 us (1.013)
  the two profiles are of different devices: /device:TPU:0 before, /device:TPU:16 now
where the time goes in v20:
time: 15.8 us; the launch traced here: 15.6 us
  waiting for transfers between devices  6.55 us (41%)
  Pallas kernels  5.77 us (37%)
  starting transfers between devices  3.13 us (20%)
    ppermute x2, waiting for transfers between devices, swapped(): return lax.ppermute(value, ('az', 'rg'), pairs)  3.48 us
    ppermute x1, waiting for transfers between devices, from_date(): lax.ppermute(piece, 'date', [((i + slot) % dates, i) for i in range(dates)])  2.45 us
    pallas_call x1, Pallas kernels, per_device(): pl.pallas_call(other_kernel, out_shape=jax.ShapeDtypeStruct((match_count,...  2.38 us
    ppermute x2, starting transfers between devices, swapped(): return lax.ppermute(value, ('az', 'rg'), pairs)  1.6 us
    ppermute x1, starting transfers between devices, from_date(): lax.ppermute(piece, 'date', [((i + slot) % dates, i) for i in range(dates)])  1.53 us
    pallas_call x1, Pallas kernels, per_device(): pl.pallas_call(own_kernel, out_shape=(jax.ShapeDtypeStruct((2, lines, wid...  1.1 us
    pallas_call x1, Pallas kernels, per_device(): pl.pallas_call(load_kernel, out_shape=tuple((pltpu.VMEM(a.shape, a.dtype)...  0.93 us
    pallas_call x2, Pallas kernels, per_device(): pieces.append(call(*raw, messages[turn], inner, *pieces))  0.79 us
  transfers between devices with their start and end apart: 4, of which 4 were waited for; matrix products, arithmetic and copies ran while one was open for 1% of the time, Pallas kernels for 18%

profile of v20, /device:TPU:16, one launch (start us, length us, event | category | flops | bytes accessed | tf_op | source)
XLA Modules:
  0.0 15.6 jit_solution(3995436673793061890)
XLA Ops:
  0.0 0.0 collective-permute-start
  0.0 0.9 %load.1 = (f32[2,64,256]{2,1,0:T(8,128)S(1)}, f32[8,64]{1,0:T(8,128)S(1)}, s32[1,64]{1,0:T(1,128)S(1)}) custom-call(f32[2,64,256]{2,1,0:T(8,128)} %bitcast.10, f32[8,64]{1,0:T(8,128)} %bitcast.11, s32[1,64]{1,0:T(1,128)} %refs_2_.1), custom_call_target="tpu_custom_call" | custom-call | tf_op jit(solution)/shard_map/load/pallas_call | solution.py:460
  0.9 0.6 %collective-permute-done = f32[2,1,64,256]{3,2,0,1:T(8,128)S(1)} collective-permute-done((f32[2,1,64,256]{3,2,0,1:T(8,128)}, f32[2,1,64,256]{3,2,0,1:T(8,128)S(1)}, u32[]{:S(2)}, u32[]{:S(2)}) %collective-permute-start) | collective-permute-done | bytes 131104 | tf_op jit(solution)/shard_map/ppermute | solution.py:454
  1.6 0.2 pack_a.1
  1.7 1.6 %collective-permute-start.2 = (bf16[112,256]{1,0:T(8,128)(2,1)S(1)}, bf16[112,256]{1,0:T(8,128)(2,1)S(1)}, u32[]{:S(2)}, u32[]{:S(2)}) collective-permute-start(bf16[112,256]{1,0:T(8,128)(2,1)S(1)} %pack_a.1), channel_id=1, source_target_pairs={{0,4},{1,5},{4,0},{5,1},{8,12},{9,13},{12,8},{13,9},{2,6},{3,7},{6... | collective-permute-start | bytes 172040 | tf_op jit(solution)/shard_map/ppermute | solution.py:492
  3.3 0.1 pack_b.1
  3.4 0.0 collective-permute-start.1
  3.5 0.3 %inner.1.refs_5_ = f32[2,64,288]{2,1,0:T(8,128)S(1)} custom-call(f32[2,64,256]{2,1,0:T(8,128)S(1)} %get-tuple-element.11.image_ref.refs_0_, f32[2,64,256]{2,1,0:T(8,128)S(1)} %bitcast.6, f32[8,64]{1,0:T(8,128)S(1)} %get-tuple-element.12.taps_ref.refs_2_, s32[1,64]{1,0:T(1,128)S(1)} %get-tuple-element.13.offsets_ref.refs_3_), custom_call_target="tpu_custom_call" | custom-call | tf_op jit(solution)/shard_map/inner/pallas_call | solution.py:495
  3.7 0.0 copy-start
  3.8 2.1 %collective-permute-done.2.refs_4_ = bf16[112,256]{1,0:T(8,128)(2,1)S(1)} collective-permute-done((bf16[112,256]{1,0:T(8,128)(2,1)S(1)}, bf16[112,256]{1,0:T(8,128)(2,1)S(1)}, u32[]{:S(2)}, u32[]{:S(2)}) %collective-permute-start.2) | collective-permute-done | bytes 57376 | tf_op jit(solution)/shard_map/ppermute | solution.py:492
  5.9 0.4 %side_a.1.refs_6_ = bf16[144,256]{1,0:T(8,128)(2,1)S(1)} custom-call(f32[2,64,256]{2,1,0:T(8,128)S(1)} %get-tuple-element.11.image_ref.refs_0_, f32[2,64,256]{2,1,0:T(8,128)S(1)} %bitcast.7, f32[8,64]{1,0:T(8,128)S(1)} %get-tuple-element.12.taps_ref.refs_2_, s32[1,64]{1,0:T(1,128)S(1)} %get-tuple-element.13.offsets_ref.refs_3_, ...), custom_call_target="tpu_custom_call" | custom-call | tf_op jit(solution)/shard_map/side_a/pallas_call | solution.py:514
  6.3 0.0 copy-start.1
  6.3 1.3 %collective-permute-done.1.refs_4_ = bf16[112,256]{1,0:T(8,128)(2,1)S(1)} collective-permute-done((bf16[112,256]{1,0:T(8,128)(2,1)S(1)}, bf16[112,256]{1,0:T(8,128)(2,1)S(1)}, u32[]{:S(2)}, u32[]{:S(2)}) %collective-permute-start.1) | collective-permute-done | bytes 57376 | tf_op jit(solution)/shard_map/ppermute | solution.py:492
  7.6 0.4 %side_b.1.own_ref = bf16[288,256]{1,0:T(8,128)(2,1)S(1)} custom-call(f32[2,64,256]{2,1,0:T(8,128)S(1)} %get-tuple-element.11.image_ref.refs_0_, f32[2,64,256]{2,1,0:T(8,128)S(1)} %bitcast.8, f32[8,64]{1,0:T(8,128)S(1)} %get-tuple-element.12.taps_ref.refs_2_, s32[1,64]{1,0:T(1,128)S(1)} %get-tuple-element.13.offsets_ref.refs_3_, ...), custom_call_target="tpu_custom_call" | custom-call | tf_op jit(solution)/shard_map/side_b/pallas_call | solution.py:514
  8.0 1.5 %collective-permute-start.3 = (bf16[288,256]{1,0:T(8,128)(2,1)S(1)}, bf16[288,256]{1,0:T(8,128)(2,1)S(1)}, u32[]{:S(2)}, u32[]{:S(2)}) collective-permute-start(bf16[288,256]{1,0:T(8,128)(2,1)S(1)} %side_b.1.own_ref), channel_id=1, source_target_pairs={{2,0},{0,2},{3,1},{1,3},{6,4},{4,6},{7,5},{5,7},{10,8},{8,10},{11,... | collective-permute-start | bytes 442376 | tf_op jit(solution)/shard_map/ppermute | solution.py:519
  9.6 0.0 copy-done.1
  9.6 0.1 copy.7.match_ref
  9.7 0.0 copy-done
  9.7 1.1 %filter_own.1 = (f32[2,64,256]{2,1,0:T(8,128)S(1)}, f32[2,2,64,256]{3,2,1,0:T(8,128)S(1)}, f32[2,2,64,32]{3,2,1,0:T(8,128)S(1)}) custom-call(bf16[1472,256]{1,0:T(8,128)(2,1)S(1)} %copy-done, bf16[288,256]{1,0:T(8,128)(2,1)S(1)} %side_b.1.own_ref), custom_call_target="tpu_custom_call" | custom-call | tf_op jit(solution)/shard_map/filter_own/pallas_call | solution.py:527
  10.8 2.5 %collective-permute-done.3.refs_0_ = bf16[288,256]{1,0:T(8,128)(2,1)S(1)} collective-permute-done((bf16[288,256]{1,0:T(8,128)(2,1)S(1)}, bf16[288,256]{1,0:T(8,128)(2,1)S(1)}, u32[]{:S(2)}, u32[]{:S(2)}) %collective-permute-start.3) | collective-permute-done | bytes 147488 | tf_op jit(solution)/shard_map/ppermute | solution.py:519
  13.2 2.4 %filter_other.1 = f32[3,2,1,64,256]{4,3,2,1,0:T(8,128)} custom-call(s32[3,2]{1,0:T(4,128)S(1)} %copy.7.match_ref, bf16[1472,256]{1,0:T(8,128)(2,1)S(1)} %copy-done, f32[2,64,256]{2,1,0:T(8,128)S(1)} %get-tuple-element.14.filtered_own_ref, f32[2,2,64,256]{3,2,1,0:T(8,128)S(1)} %get-tuple-element.15.tile_ref, f32[2,2,64,32]{3,2,1,0:T(8,128)S(1)} %get-tuple-element.16.edge_ref, ...), custom_call_target="tpu_custom_call" | custom-call | tf_op jit(solution)/shard_map/filter_other/pallas_call | solution.py:540
Async XLA Ops:
  0.0 1.6 %collective-permute-start = (f32[2,1,64,256]{3,2,0,1:T(8,128)}, f32[2,1,64,256]{3,2,0,1:T(8,128)S(1)}, u32[]{:S(2)}, u32[]{:S(2)}) collective-permute-start(f32[2,1,64,256]{3,2,0,1:T(8,128)} %bitcast.9), channel_id=1, source_target_pairs={{0,1},{1,0},{2,3},{3,2},{4,5},{5,4},{6,7},{7,6},{8,9},{9,8},{10,11... | collective-permute-start | bytes 393224 | tf_op jit(solution)/shard_map/ppermute | solution.py:454
  1.7 4.2 %collective-permute-start.2 = (bf16[112,256]{1,0:T(8,128)(2,1)S(1)}, bf16[112,256]{1,0:T(8,128)(2,1)S(1)}, u32[]{:S(2)}, u32[]{:S(2)}) collective-permute-start(bf16[112,256]{1,0:T(8,128)(2,1)S(1)} %pack_a.1), channel_id=1, source_target_pairs={{0,4},{1,5},{4,0},{5,1},{8,12},{9,13},{12,8},{13,9},{2,6},{3,7},{6... | collective-permute-start | bytes 172040 | tf_op jit(solution)/shard_map/ppermute | solution.py:492
  3.4 4.2 %collective-permute-start.1 = (bf16[112,256]{1,0:T(8,128)(2,1)S(1)}, bf16[112,256]{1,0:T(8,128)(2,1)S(1)}, u32[]{:S(2)}, u32[]{:S(2)}) collective-permute-start(bf16[112,256]{1,0:T(8,128)(2,1)S(1)} %pack_b.1), channel_id=1, source_target_pairs={{0,1},{1,0},{4,8},{5,9},{8,4},{9,5},{12,13},{13,12},{2,3},{3,2},{6... | collective-permute-start | bytes 172040 | tf_op jit(solution)/shard_map/ppermute | solution.py:492
  3.7 5.9 %copy-start = (bf16[1472,256]{1,0:T(8,128)(2,1)S(1)}, bf16[1472,256]{1,0:T(8,128)(2,1)}, u32[]{:S(2)}) copy-start(bf16[1472,256]{1,0:T(8,128)(2,1)} %constant.2.clone.table_ref) | copy-start | bytes 2260996
  6.3 3.3 %copy-start.1 = (s32[3,2]{0,1:T(2,128)S(1)}, s32[3,2]{0,1:T(2,128)}, u32[]{:S(2)}) copy-start(s32[3,2]{0,1:T(2,128)} %param.8) | copy-start | bytes 76
  8.0 5.2 %collective-permute-start.3 = (bf16[288,256]{1,0:T(8,128)(2,1)S(1)}, bf16[288,256]{1,0:T(8,128)(2,1)S(1)}, u32[]{:S(2)}, u32[]{:S(2)}) collective-permute-start(bf16[288,256]{1,0:T(8,128)(2,1)S(1)} %side_b.1.own_ref), channel_id=1, source_target_pairs={{2,0},{0,2},{3,1},{1,3},{6,4},{4,6},{7,5},{5,7},{10,8},{8,10},{11,... | collective-permute-start | bytes 442376 | tf_op jit(solution)/shard_map/ppermute | solution.py:519
